TPU v7x, 32 devices: a whole 2x2x4 slice. The times are simulated.
32 devices in a mesh: frames: 4 (over y, x), rows: 2 (over core), batch: 4 (over z).
Axes of the slice: x: 2, y: 2, z: 4, core: 2. Of those that a mesh axis runs over, the one named last changes fastest.
Arguments:
- video: bfloat16 [32, 32, 128, 320], P(('batch', 'frames'), 'rows'), parts along dimension 0, may hold values from -6 to 6
- w_spatial: bfloat16 [3, 3, 320, 320], replicated, may hold values from -0.109375 to 0.109375
- b_spatial: float32 [320], replicated, may hold values from -3 to 3
- w_temporal: bfloat16 [3, 320, 320], replicated, may hold values from -0.1875 to 0.1875
- b_temporal: float32 [320], replicated, may hold values from -3 to 3
Outputs:
- downsampled: bfloat16 [16, 32, 128, 320], P(('batch', 'frames'), 'rows'), parts along dimension 0
There are 4 independent parts, one for each index of `batch`. A program takes and returns all parts, laid end to end along the dimension named above; an argument that names none is the same for every part. Nothing has to cross between parts.
All inputs are finite; a program needn't handle non-finite values.
Results may differ from a plain program's by a relative error of at most 0.0042.
Values may be sent and summed in bfloat16 or wider, within the bound.
No kernel may reach another device: no remote copies, remote signals or barrier semaphores. Data moves between devices by JAX's collectives and lax.ppermute only.
A program may use at most 64 MiB of HBM per device.

v0:
```python
import jax
import jax.numpy as jnp
from jax import lax
from jax.sharding import PartitionSpec as P


def with_halo(cells, sides, width):
    for axis, dim in sides:
        count = lax.axis_size(axis)
        ends = count - 1
        head = lax.slice_in_dim(cells, 0, width, axis=dim)
        tail = lax.slice_in_dim(cells, cells.shape[dim] - width, cells.shape[dim], axis=dim)
        cells = jnp.concatenate(
            [
                lax.ppermute(tail, axis, [(i, (i + 1) % count) for i in range(ends)]),
                cells,
                lax.ppermute(head, axis, [((i + 1) % count, i) for i in range(ends)]),
            ],
            axis=dim,
        )
    return cells


def shifted(block, axis, distance):
    devices = range(lax.axis_size(axis))
    route = [(i - distance, i) for i in devices if i - distance in devices]
    return lax.ppermute(block, axis, route)


def temporal_mix(prev_frames, even_frames, odd_frames, w_temporal, b_temporal):
    total = jnp.dot(prev_frames, w_temporal[0], preferred_element_type=jnp.float32)
    total = total + jnp.dot(even_frames, w_temporal[1], preferred_element_type=jnp.float32)
    total = total + jnp.dot(odd_frames, w_temporal[2], preferred_element_type=jnp.float32)
    return (total + b_temporal).astype(jnp.bfloat16)


def spatial_conv(padded, kernel, b_spatial, row_count, width, channels):
    frame_count = padded.shape[0]
    columns = jnp.concatenate(
        [padded[:, :, 0:width], padded[:, :, 1 : width + 1], padded[:, :, 2 : width + 2]], axis=-1
    )
    summed = jnp.zeros((frame_count, row_count, width, channels), jnp.float32) + b_spatial
    for row_tap in range(3):
        summed = summed + jnp.dot(
            columns[:, row_tap : row_tap + row_count],
            kernel[row_tap],
            preferred_element_type=jnp.float32,
        )
    return jax.nn.silu(summed).astype(jnp.bfloat16)


def per_device(video, w_spatial, b_spatial, w_temporal, b_temporal):
    frame_count, row_count, width, channels = video.shape
    kernel = w_spatial.reshape(3, 3 * channels, channels)
    padded = with_halo(video, (("rows", 1),), 1)
    padded = jnp.pad(padded, ((0, 0), (0, 0), (1, 1), (0, 0)))
    last_frame = spatial_conv(
        padded[frame_count - 1 :], kernel, b_spatial, row_count, width, channels
    )
    incoming = shifted(last_frame, "frames", 1)
    earlier = spatial_conv(padded[: frame_count - 1], kernel, b_spatial, row_count, width, channels)
    activated = jnp.concatenate([earlier, last_frame], axis=0)
    even_frames = activated[0::2]
    odd_frames = activated[1::2]
    prev_frames = jnp.concatenate([incoming, odd_frames[:-1]], axis=0)
    return temporal_mix(prev_frames, even_frames, odd_frames, w_temporal, b_temporal)


def solution(mesh):
    in_specs = (P(("batch", "frames"), "rows", None, None), P(), P(), P(), P())
    out_specs = P(("batch", "frames"), "rows", None, None)
    return jax.shard_map(
        per_device, mesh=mesh, in_specs=in_specs, out_specs=out_specs, check_vma=False
    )
```

profile of v0, /device:TPU:20, one launch (start us, length us, event | category | flops | bytes accessed | tf_op | source)
XLA Modules:
  0.0 57.6 jit_solution(13644041092569717370)
XLA Ops:
  0.0 0.0 copy-start.1
  0.0 1.2 %fusion.19 = (bf16[2,1,128,320]{2,3,1,0:T(8,128)(2,1)S(1)}, bf16[2,1,128,320]{2,3,1,0:T(8,128)(2,1)S(1)}) fusion(bf16[2,16,128,320]{2,3,1,0:T(8,128)(2,1)} %param.5), kind=kLoop, calls=%fused_computation.37 | loop fusion | bytes 655360 | tf_op jit(solution)/shard_map/slice | solution.py:11
  1.2 1.7 %collective-permute-start = (bf16[2,1,128,320]{2,3,1,0:T(8,128)(2,1)S(1)}, bf16[2,1,128,320]{2,3,1,0:T(8,128)(2,1)S(1)}, u32[]{:S(2)}, u32[]{:S(2)}) collective-permute-start(bf16[2,1,128,320]{2,3,1,0:T(8,128)(2,1)S(1)} %get-tuple-element.12), channel_id=1, source_target_pairs={{0,4},{1,5},{2,6},{3,7},{8,12},{9,13},{10,14},{11,15},{16,20},{17,... | collective-permute-start | bytes 491528 | tf_op jit(solution)/shard_map/ppermute | solution.py:15
  2.9 1.3 %collective-permute-start.1 = (bf16[2,1,128,320]{2,3,1,0:T(8,128)(2,1)S(1)}, bf16[2,1,128,320]{2,3,1,0:T(8,128)(2,1)S(1)}, u32[]{:S(2)}, u32[]{:S(2)}) collective-permute-start(bf16[2,1,128,320]{2,3,1,0:T(8,128)(2,1)S(1)} %get-tuple-element.11), channel_id=1, source_target_pairs={{4,0},{5,1},{6,2},{7,3},{12,8},{13,9},{14,10},{15,11},{20,16},{21,... | collective-permute-start | bytes 491528 | tf_op jit(solution)/shard_map/ppermute | solution.py:17
  4.2 1.8 %fusion.20 = (bf16[1,3,320,320]{3,2,1,0:T(8,128)(2,1)S(1)}, bf16[1,3,320,320]{3,2,1,0:T(8,128)(2,1)S(1)}, bf16[1,3,320,320]{3,2,1,0:T(8,128)(2,1)S(1)}) fusion(bf16[3,3,320,320]{3,2,1,0:T(8,128)(2,1)} %param.6), kind=kLoop, calls=%fused_computation.38 | loop fusion | bytes 3686400 | tf_op jit(solution)/shard_map/slice | solution.py:46
  6.0 0.0 collective-permute-done
  6.0 0.0 copy-done.1
  6.1 0.3 constant_dynamic-update-slice_fusion.1
  6.4 0.0 collective-permute-done.1
  6.5 1.9 %pad_slice_fusion.1 = (bf16[1,18,128,320]{2,3,1,0:T(8,128)(2,1)S(1)}, bf16[1,18,128,320]{2,3,1,0:T(8,128)(2,1)S(1)}, bf16[1,18,128,320]{2,3,1,0:T(8,128)(2,1)S(1...) fusion(bf16[2,18,128,320]{2,3,1,0:T(8,128)(2,1)S(1)} %constant_, ...), kind=kLoop, calls=%fused_computation.1 | loop fusion | bytes 14745600 | tf_op jit(solution)/shard_map/slice | solution.py:40
  8.4 0.4 pad_maximum_fusion
  8.8 1.6 %fusion.4 = f32[16,128,320]{1,2,0:T(8,128)S(1)} fusion(bf16[960,320,1]{1,0,2:T(8,128)(2,1)S(1)} %bitcast.68, bf16[1,18,128,960]{2,3,1,0:T(8,128)(2,1)S(1)} %pad_maximum_fusion), kind=kOutput, calls=%fused_computation.15 | convolution fusion | flops 1258291200 | bytes 7290880 | tf_op jit(solution)/shard_map/dot_general | solution.py:44
  10.3 1.6 %fusion.5 = f32[16,128,320]{1,2,0:T(8,128)S(1)} fusion(bf16[960,320,1]{1,0,2:T(8,128)(2,1)S(1)} %bitcast.66, bf16[1,18,128,960]{2,3,1,0:T(8,128)(2,1)S(1)} %pad_maximum_fusion), kind=kOutput, calls=%fused_computation.17 | convolution fusion | flops 1258291200 | bytes 7290880 | tf_op jit(solution)/shard_map/dot_general | solution.py:44
  11.9 0.4 pad_maximum_fusion.1
  12.3 0.0 copy-start
  12.3 0.0 copy-start.3
  12.3 3.1 %fusion.1 = f32[16,128,320]{1,2,0:T(8,128)} fusion(bf16[960,320,1]{1,0,2:T(8,128)(2,1)S(1)} %bitcast.69, bf16[1,18,128,960]{2,3,1,0:T(8,128)(2,1)S(1)} %pad_maximum_fusion.1), kind=kOutput, calls=%fused_computation.9 | convolution fusion | flops 1258291200 | bytes 7290880 | tf_op jit(solution)/shard_map/dot_general | solution.py:44
  15.4 0.0 copy-done.3
  15.4 3.3 %multiply_convert_fusion.1 = bf16[16,128,320]{1,2,0:T(8,128)(2,1)} fusion(f32[16,128,320]{1,2,0:T(8,128)S(1)} %fusion.4, f32[16,128,320]{1,2,0:T(8,128)S(1)} %fusion.5, bf16[960,320,1]{1,0,2:T(8,128)(2,1)S(1)} %bitcast.64, bf16[1,18,128,960]{2,3,1,0:T(8,128)(2,1)S(1)} %pad_maximum_fusion, f32[320]{0:T(512)S(1)} %copy-done.3), kind=kOutput, calls=%fused_computation.20 | convolution fusion | flops 1263534080 | bytes 11225088 | tf_op jit(solution)/shard_map/dot_general | solution.py:44
  18.7 3.6 %collective-permute-start.2 = (bf16[1,16,128,320]{2,3,1,0:T(8,128)(2,1)}, bf16[1,16,128,320]{2,3,1,0:T(8,128)(2,1)}, u32[]{:S(2)}, u32[]{:S(2)}) collective-permute-start(bf16[1,16,128,320]{2,3,1,0:T(8,128)(2,1)} %bitcast.9), channel_id=1, source_target_pairs={{0,8},{8,16},{16,24},{1,9},{9,17},{17,25},{2,10},{10,18},{18,26},{... | collective-permute-start | bytes 3932168 | tf_op jit(solution)/shard_map/ppermute | solution.py:27
  22.3 0.0 copy-done
  22.3 3.0 %fusion.2 = f32[16,128,320]{1,2,0:T(8,128)} fusion(bf16[960,320,1]{1,0,2:T(8,128)(2,1)S(1)} %bitcast.67, bf16[1,18,128,960]{2,3,1,0:T(8,128)(2,1)S(1)} %pad_maximum_fusion.1), kind=kOutput, calls=%fused_computation.11 | convolution fusion | flops 1258291200 | bytes 7290880 | tf_op jit(solution)/shard_map/dot_general | solution.py:44
  25.3 2.3 %fusion.11 = f32[16,128,320]{1,2,0:T(8,128)S(1)} fusion(bf16[16,128,320]{1,2,0:T(8,128)(2,1)} %multiply_convert_fusion.1, bf16[3,320,320]{2,1,0:T(8,128)(2,1)} %param.8), kind=kOutput, calls=%fused_computation.26 | convolution fusion | flops 419430400 | bytes 4177920 | tf_op jit(solution)/shard_map/dot_general | solution.py:33
  27.7 0.0 copy-start.2
  27.7 8.1 %fusion.6 = f32[16,128,320]{1,2,0:T(8,128)} fusion(f32[16,128,320]{1,2,0:T(8,128)} %fusion.1, f32[16,128,320]{1,2,0:T(8,128)} %fusion.2, bf16[960,320,1]{1,0,2:T(8,128)(2,1)S(1)} %bitcast.65, bf16[1,18,128,960]{2,3,1,0:T(8,128)(2,1)} %copy-done, f32[320]{0:T(512)S(1)} %copy-done.3, bf16[3,320,320]{2,1,0:T(8,128)(2,1)} %param.8), kind=kOutput, calls=%fused_computation.21 | convolution fusion | flops 1682964480 | bytes 12657920 | tf_op jit(solution)/shard_map/dot_general | solution.py:32
  35.8 17.5 %collective-permute-done.2 = bf16[1,16,128,320]{2,3,1,0:T(8,128)(2,1)} collective-permute-done((bf16[1,16,128,320]{2,3,1,0:T(8,128)(2,1)}, bf16[1,16,128,320]{2,3,1,0:T(8,128)(2,1)}, u32[]{:S(2)}, u32[]{:S(2)}) %collective-permute-start.2) | collective-permute-done | bytes 1310752 | tf_op jit(solution)/shard_map/ppermute | solution.py:27
  53.3 0.0 copy-done.2
  53.3 4.3 %fusion.7 = bf16[1,16,128,320]{2,3,1,0:T(8,128)(2,1)} fusion(f32[16,128,320]{1,2,0:T(8,128)S(1)} %fusion.11, f32[16,128,320]{1,2,0:T(8,128)} %fusion.6, bf16[1,16,128,320]{2,3,1,0:T(8,128)(2,1)} %collective-permute-done.2, f32[320]{0:T(512)S(1)} %copy-done.2, bf16[3,320,320]{2,1,0:T(8,128)(2,1)} %param.8), kind=kOutput, calls=%fused_computation.22 | convolution fusion | flops 422051840 | bytes 8111360 | tf_op jit(solution)/shard_map/dot_general | solution.py:31
  (2 shorter events, 0.0 us)
Async XLA Ops:
  0.0 6.1 %copy-start.1 = (bf16[2,16,128,320]{2,3,1,0:T(8,128)(2,1)S(1)}, bf16[2,16,128,320]{2,3,1,0:T(8,128)(2,1)}, u32[]{:S(2)}) copy-start(bf16[2,16,128,320]{2,3,1,0:T(8,128)(2,1)} %param.5) | copy-start | bytes 7864324
  1.2 4.8 %collective-permute-start = (bf16[2,1,128,320]{2,3,1,0:T(8,128)(2,1)S(1)}, bf16[2,1,128,320]{2,3,1,0:T(8,128)(2,1)S(1)}, u32[]{:S(2)}, u32[]{:S(2)}) collective-permute-start(bf16[2,1,128,320]{2,3,1,0:T(8,128)(2,1)S(1)} %get-tuple-element.12), channel_id=1, source_target_pairs={{0,4},{1,5},{2,6},{3,7},{8,12},{9,13},{10,14},{11,15},{16,20},{17,... | collective-permute-start | bytes 491528 | tf_op jit(solution)/shard_map/ppermute | solution.py:15
  2.9 3.5 %collective-permute-start.1 = (bf16[2,1,128,320]{2,3,1,0:T(8,128)(2,1)S(1)}, bf16[2,1,128,320]{2,3,1,0:T(8,128)(2,1)S(1)}, u32[]{:S(2)}, u32[]{:S(2)}) collective-permute-start(bf16[2,1,128,320]{2,3,1,0:T(8,128)(2,1)S(1)} %get-tuple-element.11), channel_id=1, source_target_pairs={{4,0},{5,1},{6,2},{7,3},{12,8},{13,9},{14,10},{15,11},{20,16},{21,... | collective-permute-start | bytes 491528 | tf_op jit(solution)/shard_map/ppermute | solution.py:17
  12.3 10.0 %copy-start = (bf16[1,18,128,960]{2,3,1,0:T(8,128)(2,1)}, bf16[1,18,128,960]{2,3,1,0:T(8,128)(2,1)S(1)}, u32[]{:S(2)}) copy-start(bf16[1,18,128,960]{2,3,1,0:T(8,128)(2,1)S(1)} %pad_maximum_fusion.1) | copy-start | bytes 13271044
  12.3 3.1 %copy-start.3 = (f32[320]{0:T(512)S(1)}, f32[320]{0:T(512)}, u32[]{:S(2)}) copy-start(f32[320]{0:T(512)} %param.7) | copy-start | bytes 3844
  18.7 34.6 %collective-permute-start.2 = (bf16[1,16,128,320]{2,3,1,0:T(8,128)(2,1)}, bf16[1,16,128,320]{2,3,1,0:T(8,128)(2,1)}, u32[]{:S(2)}, u32[]{:S(2)}) collective-permute-start(bf16[1,16,128,320]{2,3,1,0:T(8,128)(2,1)} %bitcast.9), channel_id=1, source_target_pairs={{0,8},{8,16},{16,24},{1,9},{9,17},{17,25},{2,10},{10,18},{18,26},{... | collective-permute-start | bytes 3932168 | tf_op jit(solution)/shard_map/ppermute | solution.py:27
  27.7 25.6 %copy-start.2 = (f32[320]{0:T(512)S(1)}, f32[320]{0:T(512)}, u32[]{:S(2)}) copy-start(f32[320]{0:T(512)} %param.9) | copy-start | bytes 3844
where the time goes:
time: 58.2 us; the launch traced here: 57.6 us
  matrix products  27.4 us (47%)
  waiting for transfers between devices  17.5 us (30%)
  starting transfers between devices  6.61 us (11%)
  local copies, waits for them, and re-layouts  5.3 us (9%)
  other arithmetic  0.7 us (1%)
    ppermute x1, waiting for transfers between devices, shifted(): return lax.ppermute(block, axis, route)  17.5 us
    dot_general x5, matrix products, spatial_conv(): jnp.dot(columns[:, row_tap:row_tap + row_count], kernel[row_tap], preferr...  12.6 us
    dot_general x1, matrix products, temporal_mix(): jnp.dot(even_frames, w_temporal[1], preferred_element_type=jnp.float32)  8.11 us
    dot_general x1, matrix products, temporal_mix(): jnp.dot(prev_frames, w_temporal[0], preferred_element_type=jnp.float32)  4.35 us
    ppermute x1, starting transfers between devices, shifted(): return lax.ppermute(block, axis, route)  3.57 us
    dot_general x1, matrix products, temporal_mix(): jnp.dot(odd_frames, w_temporal[2], preferred_element_type=jnp.float32)  2.32 us
    slice x1, local copies, waits for them, and re-layouts, spatial_conv(): padded[:, :, 0:width]  1.94 us
    slice x1, local copies, waits for them, and re-layouts, spatial_conv(): kernel[row_tap]  1.79 us
  transfers between devices with their start and end apart: 3, of which 1 were waited for; matrix products, arithmetic and copies ran while one was open for 27% of the time, Pallas kernels for 0%

commit v1 on v0

v1 whole, which is shorter than its diff:
```python
import functools

import jax
import jax.numpy as jnp
from jax import lax
from jax.experimental import pallas as pl
from jax.experimental.pallas import tpu as pltpu
from jax.sharding import PartitionSpec as P

F32 = jnp.float32
BF16 = jnp.bfloat16
VMEM = pl.BlockSpec(memory_space=pltpu.VMEM)
ANY = pl.BlockSpec(memory_space=pl.ANY)
PARAMS = pltpu.CompilerParams(vmem_limit_bytes=20 * 2**20)


def ring(axis):
    count = lax.axis_size(axis)
    return [(i, (i + 1) % count) for i in range(count)]


def neighbour_rows(top, bottom):
    count = lax.axis_size("rows")
    if count == 2:
        mine = jnp.where(lax.axis_index("rows") == 0, bottom, top)
        got = lax.ppermute(mine, "rows", ring("rows"))
        return got, got
    above = lax.ppermute(bottom, "rows", ring("rows"))
    below = lax.ppermute(top, "rows", [(b, a) for a, b in ring("rows")])
    return above, below


def silu(v):
    half = 0.5 * v
    return half + half * jnp.tanh(half)


def prepare_kernel(ws_ref, bs_ref, wt_ref, bt_ref, conv_ref, mix_ref, cb_ref, mb_ref):
    taps, channels = ws_ref.shape[0], ws_ref.shape[2]
    for j in range(taps):
        block = ws_ref[:, j].reshape(taps * channels, channels)
        conv_ref[j * channels : (j + 1) * channels, :] = block.T
    mix_ref[...] = wt_ref[...].reshape(taps * channels, channels).T
    width = cb_ref.shape[1]
    cb_ref[...] = jnp.broadcast_to(bs_ref[...], (width, channels)).T
    mb_ref[...] = jnp.broadcast_to(bt_ref[...], (width, channels)).T


def conv_rows(columns, conv, bias, channels, width):
    stacked = jnp.concatenate(columns, axis=1)
    products = jnp.dot(conv, stacked, preferred_element_type=F32)
    lane = lax.broadcasted_iota(jnp.int32, (1, width), 1)
    rows = []
    for q in range(len(columns)):
        part = products[:, q * width : (q + 1) * width]
        left = jnp.where(lane == 0, 0.0, pltpu.roll(part[:channels], 1, 1))
        right = jnp.where(lane == width - 1, 0.0, pltpu.roll(part[2 * channels :], width - 1, 1))
        rows.append(silu(left + part[channels : 2 * channels] + right + bias).astype(BF16))
    return jnp.concatenate(rows, axis=1)


def own_kernel(x_ref, above_ref, below_ref, conv_ref, mix_ref, cb_ref, mb_ref, out_ref, xs, *, group):
    frames, rows, channels, width = x_ref.shape
    index, count = lax.axis_index("rows"), lax.axis_size("rows")
    zero = jnp.zeros((channels, width), BF16)
    for f in range(frames):
        xs[f, 0] = jnp.where(index > 0, above_ref[f, 0], zero)
        xs[f, rows + 1] = jnp.where(index < count - 1, below_ref[f, 0], zero)
    xs[:, 1 : rows + 1] = x_ref[...]

    def body(p, carry):
        h = p * group
        parts = []
        for f in range(frames):
            columns = [xs[f, pl.ds(h + q, 3)].reshape(3 * channels, width) for q in range(group)]
            parts.append(conv_rows(columns, conv_ref[...], cb_ref[...], channels, width))
        mixed = jnp.dot(mix_ref[:, channels:], jnp.concatenate(parts, axis=0), preferred_element_type=F32)
        for q in range(group):
            out_ref[h + q] = mixed[:, q * width : (q + 1) * width] + mb_ref[...]
        return carry

    lax.fori_loop(0, rows // group, body, 0)


def incoming_kernel(*refs, pieces, groups, seeded):
    refs = list(refs)
    own_ref, conv_ref, mix_ref, cb_ref = refs[:4]
    above_ref, below_ref = refs[4:6]
    piece_refs = refs[6 : 6 + len(pieces)]
    out_ref, stage, sem = refs[-3:]
    rows, channels, width = own_ref.shape
    index, count = lax.axis_index("rows"), lax.axis_size("rows")
    first = lax.axis_index("frames") == 0
    zero = jnp.zeros((channels, width), BF16)
    where = {}
    for ref, held in zip(piece_refs, pieces):
        for k, r in enumerate(held):
            where[r] = (ref, k)

    def row(r):
        if r < 0:
            return jnp.where(index > 0, above_ref[0], zero)
        if r >= rows:
            return jnp.where(index < count - 1, below_ref[0], zero)
        ref, k = where[r]
        return ref[k]

    copies = []
    slot = 0
    for start, size in groups:
        columns = [
            jnp.concatenate([row(start + q + i - 1) for i in range(3)], axis=0) for q in range(size)
        ]
        act = conv_rows(columns, conv_ref[...], cb_ref[...], channels, width)
        act = jnp.where(first, jnp.zeros_like(act), act)
        mixed = jnp.dot(mix_ref[:, :channels], act, preferred_element_type=F32)
        for q in range(size):
            total = own_ref[start + q] + mixed[:, q * width : (q + 1) * width]
            stage[slot + q] = total.astype(BF16)
        copy = pltpu.make_async_copy(
            stage.at[pl.ds(slot, size)], out_ref.at[pl.ds(start, size)], sem.at[len(copies)]
        )
        copy.start()
        copies.append(copy)
        slot += size
    for copy in copies:
        copy.wait()


def incoming_rows(out, own, weights, edges, arrived, groups):
    conv, mix, cb = weights
    rows, channels, width = own.shape
    pieces = [held for held, _ in arrived]
    operands = [own, conv, mix, cb, *edges] + [array for _, array in arrived]
    in_specs = [VMEM] * len(operands)
    aliases = {}
    if out is not None:
        aliases = {len(operands): 0}
        operands.append(out)
        in_specs.append(ANY)
    return pl.pallas_call(
        functools.partial(incoming_kernel, pieces=pieces, groups=groups, seeded=out is not None),
        out_shape=jax.ShapeDtypeStruct(own.shape, BF16),
        in_specs=in_specs,
        out_specs=ANY,
        input_output_aliases=aliases,
        scratch_shapes=[
            pltpu.VMEM((sum(size for _, size in groups), channels, width), BF16),
            pltpu.SemaphoreType.DMA((len(groups),)),
        ],
        compiler_params=PARAMS,
    )(*operands)


def per_device(video, w_spatial, b_spatial, w_temporal, b_temporal):
    frames, rows, width, channels = video.shape
    x = jnp.transpose(video, (0, 1, 3, 2))
    last = x[frames - 1]

    chunk_rows = [[0, 1, 2, 13, 14, 15], list(range(3, 11)), [11, 12]]

    def chunk(held):
        runs = []
        for r in held:
            if runs and runs[-1][1] == r:
                runs[-1][1] = r + 1
            else:
                runs.append([r, r + 1])
        return jnp.concatenate([last[a:b] for a, b in runs], axis=0)

    arrived = [(held, lax.ppermute(chunk(held), "frames", ring("frames"))) for held in chunk_rows]
    above, below = neighbour_rows(x[:, :1], x[:, rows - 1 :])
    edges = neighbour_rows(arrived[0][1][:1], arrived[0][1][-1:])

    square = jax.ShapeDtypeStruct((3 * channels, 3 * channels), BF16)
    flat = jax.ShapeDtypeStruct((channels, 3 * channels), BF16)
    bias = jax.ShapeDtypeStruct((channels, width), F32)
    conv, mix, cb, mb = pl.pallas_call(
        prepare_kernel,
        out_shape=(square, flat, bias, bias),
        in_specs=[VMEM] * 4,
        out_specs=(VMEM,) * 4,
        compiler_params=PARAMS,
    )(w_spatial, b_spatial.reshape(1, channels), w_temporal, b_temporal.reshape(1, channels))

    own = pl.pallas_call(
        functools.partial(own_kernel, group=4),
        out_shape=jax.ShapeDtypeStruct((rows, channels, width), F32),
        in_specs=[VMEM] * 7,
        out_specs=VMEM,
        scratch_shapes=[pltpu.VMEM((frames, rows + 2, channels, width), BF16)],
        compiler_params=PARAMS,
    )(x, above, below, conv, mix, cb, mb)

    weights = (conv, mix, cb)
    out = incoming_rows(None, own, weights, edges, arrived[:1], [(0, 2), (14, 2)])
    out = incoming_rows(out, own, weights, edges, arrived[:2], [(2, 4), (6, 4)])
    out = incoming_rows(out, own, weights, edges, arrived, [(10, 4)])
    return jnp.transpose(out[None], (0, 1, 3, 2))


def solution(mesh):
    in_specs = (P(("batch", "frames"), "rows", None, None), P(), P(), P(), P())
    out_specs = P(("batch", "frames"), "rows", None, None)
    return jax.shard_map(
        per_device, mesh=mesh, in_specs=in_specs, out_specs=out_specs, check_vma=False
    )
```

time: 58.2 us -> 45.6 us (0.78)
  the two profiles are of different devices: /device:TPU:20 before, /device:TPU:1 now
where the time goes in v1:
time: 45.6 us; the launch traced here: 45.3 us
  Pallas kernels  24.1 us (53%)
  starting transfers between devices  8.22 us (18%)
  waiting for transfers between devices  6.05 us (13%)
  local copies, waits for them, and re-layouts  5.98 us (13%)
  other arithmetic  0.85 us (2%)
    pallas_call x3, Pallas kernels, incoming_rows(): pl.pallas_call(functools.partial(incoming_kernel, pieces=pieces, groups=g...  12 us
    pallas_call x1, Pallas kernels, per_device(): pl.pallas_call(functools.partial(own_kernel, group=4), out_shape=jax.Shap...  11.1 us
    ppermute x3, waiting for transfers between devices, per_device(): lax.ppermute(chunk(held), 'frames', ring('frames'))  6.04 us
    ppermute x3, starting transfers between devices, per_device(): lax.ppermute(chunk(held), 'frames', ring('frames'))  4.51 us
    ppermute x2, starting transfers between devices, neighbour_rows(): got = lax.ppermute(mine, 'rows', ring('rows'))  3.7 us
    slice x3, local copies, waits for them, and re-layouts, chunk(): return jnp.concatenate([last[a:b] for a, b in runs], axis=0)  3.23 us
    unnamed x10, local copies, waits for them, and re-layouts  2.75 us
    pallas_call x1, Pallas kernels, per_device(): pl.pallas_call(prepare_kernel, out_shape=(square, flat, bias, bias), in_s...  0.97 us
  transfers between devices with their start and end apart: 5, of which 1 were waited for; matrix products, arithmetic and copies ran while one was open for 4% of the time, Pallas kernels for 46%

profile of v1, /device:TPU:1, one launch (start us, length us, event | category | flops | bytes accessed | tf_op | source)
XLA Modules:
  0.0 45.3 jit_solution(3600910895917412241)
XLA Ops:
  0.0 0.0 copy-start
  0.0 0.0 copy-start.3
  0.0 0.0 copy-start.4
  0.0 1.2 %slice_bitcast_fusion.2 = (bf16[3,320,128]{2,1,0:T(8,128)(2,1)S(1)}, bf16[3,320,128]{2,1,0:T(8,128)(2,1)S(1)}) fusion(bf16[2,16,320,128]{3,2,1,0:T(8,128)(2,1)} %bitcast.12), kind=kLoop, calls=%fused_computation.3 | loop fusion | bytes 983040 | tf_op jit(solution)/shard_map/slice | solution.py:169
  1.3 0.8 %pad_maximum_fusion = bf16[6,320,128]{2,1,0:T(8,128)(2,1)} fusion(bf16[3,320,128]{2,1,0:T(8,128)(2,1)S(1)} %get-tuple-element.14, bf16[3,320,128]{2,1,0:T(8,128)(2,1)S(1)} %get-tuple-element.13), kind=kLoop, calls=%fused_computation.1 | loop fusion | flops 245760 | bytes 983040 | tf_op jit(solution)/shard_map/concatenate | solution.py:169
  2.1 2.0 %collective-permute-start.1 = (bf16[6,320,128]{2,1,0:T(8,128)(2,1)}, bf16[6,320,128]{2,1,0:T(8,128)(2,1)S(1)}, u32[]{:S(2)}, u32[]{:S(2)}) collective-permute-start(bf16[6,320,128]{2,1,0:T(8,128)(2,1)} %pad_maximum_fusion), channel_id=1, source_target_pairs={{0,8},{8,16},{16,24},{24,0},{1,9},{9,17},{17,25},{25,1},{2,10},{10... | collective-permute-start | bytes 1474568 | tf_op jit(solution)/shard_map/ppermute | solution.py:171
  4.1 2.0 %slice_bitcast_fusion = bf16[8,320,128]{2,1,0:T(8,128)(2,1)} fusion(bf16[2,16,320,128]{3,2,1,0:T(8,128)(2,1)} %bitcast.13), kind=kLoop, calls=%fused_computation | loop fusion | bytes 1310720 | tf_op jit(solution)/shard_map/slice | solution.py:169
  6.1 1.2 %collective-permute-start.3 = (bf16[8,320,128]{2,1,0:T(8,128)(2,1)}, bf16[8,320,128]{2,1,0:T(8,128)(2,1)}, u32[]{:S(2)}, u32[]{:S(2)}) collective-permute-start(bf16[8,320,128]{2,1,0:T(8,128)(2,1)} %slice_bitcast_fusion), channel_id=1, source_target_pairs={{0,8},{8,16},{16,24},{24,0},{1,9},{9,17},{17,25},{25,1},{2,10},{10... | collective-permute-start | bytes 1966088 | tf_op jit(solution)/shard_map/ppermute | solution.py:171
  7.3 0.0 copy-done
  7.3 1.3 %collective-permute-start.4 = (bf16[2,320,128]{2,1,0:T(8,128)(2,1)S(1)}, bf16[2,320,128]{2,1,0:T(8,128)(2,1)S(1)}, u32[]{:S(2)}, u32[]{:S(2)}) collective-permute-start(bf16[2,320,128]{2,1,0:T(8,128)(2,1)S(1)} %slice_bitcast_fusion.3), channel_id=1, source_target_pairs={{0,8},{8,16},{16,24},{24,0},{1,9},{9,17},{17,25},{25,1},{2,10},{10... | collective-permute-start | bytes 491528 | tf_op jit(solution)/shard_map/ppermute | solution.py:171
  8.6 1.6 %collective-permute-start = (bf16[2,1,320,128]{3,2,1,0:T(8,128)(2,1)S(1)}, bf16[2,1,320,128]{3,2,1,0:T(8,128)(2,1)S(1)}, u32[]{:S(2)}, u32[]{:S(2)}) collective-permute-start(bf16[2,1,320,128]{3,2,1,0:T(8,128)(2,1)S(1)} %slice_select_fusion), channel_id=1, source_target_pairs={{0,4},{4,0},{1,5},{5,1},{2,6},{6,2},{3,7},{7,3},{8,12},{12,8},{9,1... | collective-permute-start | bytes 491528 | tf_op jit(solution)/shard_map/ppermute | solution.py:26
  10.2 6.0 %collective-permute-done.1.refs_6_ = bf16[6,320,128]{2,1,0:T(8,128)(2,1)S(1)} collective-permute-done((bf16[6,320,128]{2,1,0:T(8,128)(2,1)}, bf16[6,320,128]{2,1,0:T(8,128)(2,1)S(1)}, u32[]{:S(2)}, u32[]{:S(2)}) %collective-permute-start.1) | collective-permute-done | bytes 491552 | tf_op jit(solution)/shard_map/ppermute | solution.py:171
  16.2 2.1 %collective-permute-start.2 = (bf16[1,320,128]{2,1,0:T(8,128)(2,1)S(1)}, bf16[1,320,128]{2,1,0:T(8,128)(2,1)S(1)}, u32[]{:S(2)}, u32[]{:S(2)}) collective-permute-start(bf16[1,320,128]{2,1,0:T(8,128)(2,1)S(1)} %slice_select_fusion.1), channel_id=1, source_target_pairs={{0,4},{4,0},{1,5},{5,1},{2,6},{6,2},{3,7},{7,3},{8,12},{12,8},{9,1... | collective-permute-start | bytes 245768 | tf_op jit(solution)/shard_map/ppermute | solution.py:26
  18.4 0.0 copy-done.3
  18.4 0.0 copy-done.4
  18.4 0.0 copy-start.1
  18.4 1.6 %copy-done.1 = bf16[3,3,320,320]{3,2,1,0:T(8,128)(2,1)S(1)} copy-done((bf16[3,3,320,320]{3,2,1,0:T(8,128)(2,1)S(1)}, bf16[3,3,320,320]{3,2,1,0:T(8,128)(2,1)}, u32[]{:S(2)}) %copy-start.1) | copy-done | bytes 1843224
  20.0 0.0 copy-start.2
  20.0 1.1 %copy-done.2 = bf16[3,320,320]{2,1,0:T(8,128)(2,1)S(1)} copy-done((bf16[3,320,320]{2,1,0:T(8,128)(2,1)S(1)}, bf16[3,320,320]{2,1,0:T(8,128)(2,1)}, u32[]{:S(2)}) %copy-start.2) | copy-done | bytes 614424
  21.1 1.0 %shard_map.55 = (bf16[960,960]{1,0:T(8,128)(2,1)S(1)}, bf16[320,960]{1,0:T(8,128)(2,1)S(1)}, f32[320,128]{1,0:T(8,128)S(1)}, f32[320,128]{1,0:T(8,128)S(1)}) custom-call(bf16[3,3,320,320]{3,2,1,0:T(8,128)(2,1)S(1)} %copy-done.1, f32[1,320]{1,0:T(1,128)S(1)} %reshape.10.bs_ref, bf16[3,320,320]{2,1,0:T(8,128)(2,1)S(1)} %copy-done.2, f32[1,320]{1,0:T(1,128)S(1)} %reshape.11.bt_ref), custom_call_target="tpu_custom_call" | custom-call | tf_op jit(solution)/shard_map/pallas_call | solution.py:178
  22.1 0.0 collective-permute-done.above_ref.below_ref
  22.1 11.1 %shard_map.56.refs_0_ = f32[16,320,128]{2,1,0:T(8,128)S(1)} custom-call(bf16[2,16,320,128]{3,2,1,0:T(8,128)(2,1)S(1)} %bitcast.16, bf16[2,1,320,128]{3,2,1,0:T(8,128)(2,1)S(1)} %collective-permute-done.above_ref.below_ref, bf16[2,1,320,128]{3,2,1,0:T(8,128)(2,1)S(1)} %collective-permute-done.above_ref.below_ref, ...), custom_call_target="tpu_custom_call" | custom-call | tf_op jit(solution)/shard_map/pallas_call | solution.py:186
  33.2 0.0 collective-permute-done.2.refs_4_.refs_5_
  33.2 3.6 %shard_map.57.refs_8_ = bf16[16,320,128]{2,1,0:T(8,128)(2,1)} custom-call(f32[16,320,128]{2,1,0:T(8,128)S(1)} %shard_map.56.refs_0_, bf16[960,960]{1,0:T(8,128)(2,1)S(1)} %get-tuple-element.9.conv_ref.refs_1_, bf16[320,960]{1,0:T(8,128)(2,1)S(1)} %get-tuple-element.10.mix_ref.refs_2_, f32[320,128]{1,0:T(8,128)S(1)} %get-tuple-element.11.cb_ref.refs_3_, ...), custom_call_target="tpu_custom_call" | custom-call | tf_op jit(solution)/shard_map/pallas_call | solution.py:141
  36.8 0.0 collective-permute-done.3.refs_7_
  36.9 5.0 %shard_map.58.refs_9_ = bf16[16,320,128]{2,1,0:T(8,128)(2,1)} custom-call(f32[16,320,128]{2,1,0:T(8,128)S(1)} %shard_map.56.refs_0_, bf16[960,960]{1,0:T(8,128)(2,1)S(1)} %get-tuple-element.9.conv_ref.refs_1_, bf16[320,960]{1,0:T(8,128)(2,1)S(1)} %get-tuple-element.10.mix_ref.refs_2_, ...), custom_call_target="tpu_custom_call", output_to_operand_aliasing={{}: (8, {})} | custom-call | tf_op jit(solution)/shard_map/pallas_call | solution.py:141
  41.8 0.0 collective-permute-done.4.refs_8_
  41.8 3.5 %shard_map.59 = bf16[16,320,128]{2,1,0:T(8,128)(2,1)} custom-call(f32[16,320,128]{2,1,0:T(8,128)S(1)} %shard_map.56.refs_0_, bf16[960,960]{1,0:T(8,128)(2,1)S(1)} %get-tuple-element.9.conv_ref.refs_1_, bf16[320,960]{1,0:T(8,128)(2,1)S(1)} %get-tuple-element.10.mix_ref.refs_2_, ...), custom_call_target="tpu_custom_call", output_to_operand_aliasing={{}: (9, {})} | custom-call | tf_op jit(solution)/shard_map/pallas_call | solution.py:141
  (5 shorter events, 0.0 us)
Async XLA Ops:
  0.0 7.3 %copy-start = (bf16[2,16,128,320]{2,3,1,0:T(8,128)(2,1)S(1)}, bf16[2,16,128,320]{2,3,1,0:T(8,128)(2,1)}, u32[]{:S(2)}) copy-start(bf16[2,16,128,320]{2,3,1,0:T(8,128)(2,1)} %param.5) | copy-start | bytes 7864324
  0.0 18.4 %copy-start.3 = (f32[320]{0:T(512)S(1)}, f32[320]{0:T(512)}, u32[]{:S(2)}) copy-start(f32[320]{0:T(512)} %param.7) | copy-start | bytes 3844
  0.0 18.4 %copy-start.4 = (f32[320]{0:T(512)S(1)}, f32[320]{0:T(512)}, u32[]{:S(2)}) copy-start(f32[320]{0:T(512)} %param.9) | copy-start | bytes 3844
  2.1 14.2 %collective-permute-start.1 = (bf16[6,320,128]{2,1,0:T(8,128)(2,1)}, bf16[6,320,128]{2,1,0:T(8,128)(2,1)S(1)}, u32[]{:S(2)}, u32[]{:S(2)}) collective-permute-start(bf16[6,320,128]{2,1,0:T(8,128)(2,1)} %pad_maximum_fusion), channel_id=1, source_target_pairs={{0,8},{8,16},{16,24},{24,0},{1,9},{9,17},{17,25},{25,1},{2,10},{10... | collective-permute-start | bytes 1474568 | tf_op jit(solution)/shard_map/ppermute | solution.py:171
  6.1 30.7 %collective-permute-start.3 = (bf16[8,320,128]{2,1,0:T(8,128)(2,1)}, bf16[8,320,128]{2,1,0:T(8,128)(2,1)}, u32[]{:S(2)}, u32[]{:S(2)}) collective-permute-start(bf16[8,320,128]{2,1,0:T(8,128)(2,1)} %slice_bitcast_fusion), channel_id=1, source_target_pairs={{0,8},{8,16},{16,24},{24,0},{1,9},{9,17},{17,25},{25,1},{2,10},{10... | collective-permute-start | bytes 1966088 | tf_op jit(solution)/shard_map/ppermute | solution.py:171
  7.3 34.5 %collective-permute-start.4 = (bf16[2,320,128]{2,1,0:T(8,128)(2,1)S(1)}, bf16[2,320,128]{2,1,0:T(8,128)(2,1)S(1)}, u32[]{:S(2)}, u32[]{:S(2)}) collective-permute-start(bf16[2,320,128]{2,1,0:T(8,128)(2,1)S(1)} %slice_bitcast_fusion.3), channel_id=1, source_target_pairs={{0,8},{8,16},{16,24},{24,0},{1,9},{9,17},{17,25},{25,1},{2,10},{10... | collective-permute-start | bytes 491528 | tf_op jit(solution)/shard_map/ppermute | solution.py:171
  8.6 13.5 %collective-permute-start = (bf16[2,1,320,128]{3,2,1,0:T(8,128)(2,1)S(1)}, bf16[2,1,320,128]{3,2,1,0:T(8,128)(2,1)S(1)}, u32[]{:S(2)}, u32[]{:S(2)}) collective-permute-start(bf16[2,1,320,128]{3,2,1,0:T(8,128)(2,1)S(1)} %slice_select_fusion), channel_id=1, source_target_pairs={{0,4},{4,0},{1,5},{5,1},{2,6},{6,2},{3,7},{7,3},{8,12},{12,8},{9,1... | collective-permute-start | bytes 491528 | tf_op jit(solution)/shard_map/ppermute | solution.py:26
  16.2 17.0 %collective-permute-start.2 = (bf16[1,320,128]{2,1,0:T(8,128)(2,1)S(1)}, bf16[1,320,128]{2,1,0:T(8,128)(2,1)S(1)}, u32[]{:S(2)}, u32[]{:S(2)}) collective-permute-start(bf16[1,320,128]{2,1,0:T(8,128)(2,1)S(1)} %slice_select_fusion.1), channel_id=1, source_target_pairs={{0,4},{4,0},{1,5},{5,1},{2,6},{6,2},{3,7},{7,3},{8,12},{12,8},{9,1... | collective-permute-start | bytes 245768 | tf_op jit(solution)/shard_map/ppermute | solution.py:26
  18.4 1.6 %copy-start.1 = (bf16[3,3,320,320]{3,2,1,0:T(8,128)(2,1)S(1)}, bf16[3,3,320,320]{3,2,1,0:T(8,128)(2,1)}, u32[]{:S(2)}) copy-start(bf16[3,3,320,320]{3,2,1,0:T(8,128)(2,1)} %ws_ref.1) | copy-start | bytes 5529604
  20.0 1.1 %copy-start.2 = (bf16[3,320,320]{2,1,0:T(8,128)(2,1)S(1)}, bf16[3,320,320]{2,1,0:T(8,128)(2,1)}, u32[]{:S(2)}) copy-start(bf16[3,320,320]{2,1,0:T(8,128)(2,1)} %wt_ref.1) | copy-start | bytes 1843204

commit v2 on v1

v2 whole, which is shorter than its diff:
```python
import functools

import jax
import jax.numpy as jnp
from jax import lax
from jax.experimental import pallas as pl
from jax.experimental.pallas import tpu as pltpu
from jax.sharding import PartitionSpec as P

F32 = jnp.float32
BF16 = jnp.bfloat16
VMEM = pl.BlockSpec(memory_space=pltpu.VMEM)
ANY = pl.BlockSpec(memory_space=pl.ANY)
HEAD_LIMIT = 62 * 2**20
PARAMS = pltpu.CompilerParams(vmem_limit_bytes=20 * 2**20)


def flipped():
    return lax.axis_index("rows") == 0


def first_row(place, size, rows):
    return jnp.where(flipped(), rows - place - size, place)


def ring(axis):
    count = lax.axis_size(axis)
    return [(i, (i + 1) % count) for i in range(count)]


def cost(flops, moved):
    return pl.CostEstimate(flops=flops, bytes_accessed=moved, transcendentals=0)


def silu(v):
    half = 0.5 * v
    return half + half * jnp.tanh(half)


def row_copies(x_ref, outs, spans, sem):
    rows = x_ref.shape[1]
    copies = []
    for k, (out, (frame, count, place, size)) in enumerate(zip(outs, spans)):
        source = x_ref.at[pl.ds(frame, count), pl.ds(first_row(place, size, rows), size)]
        copies.append(pltpu.make_async_copy(source, out, sem.at[k]))
    for copy in copies:
        copy.start()
    return copies


def row_shapes(x, spans):
    return [jax.ShapeDtypeStruct((count, size) + x.shape[2:], x.dtype) for _, count, _, size in spans]


def slice_kernel(x_ref, *refs, spans):
    for copy in row_copies(x_ref, refs[:-1], spans, refs[-1]):
        copy.wait()


def prepare_kernel(x_ref, ws_ref, bs_ref, wt_ref, bt_ref, conv_ref, mix_ref, cb_ref, mb_ref, piece_ref, sem, *, spans):
    copies = row_copies(x_ref, [piece_ref], spans, sem)
    taps, channels = ws_ref.shape[0], ws_ref.shape[2]
    for j in range(taps):
        blocks = [ws_ref[jnp.where(flipped(), taps - 1 - i, i), j] for i in range(taps)]
        conv_ref[j * channels : (j + 1) * channels, :] = jnp.concatenate(blocks, axis=0).T
    mix_ref[...] = wt_ref[...].reshape(taps * channels, channels).T
    width = cb_ref.shape[1]
    cb_ref[...] = jnp.broadcast_to(bs_ref[...], (width, channels)).T
    mb_ref[...] = jnp.broadcast_to(bt_ref[...], (width, channels)).T
    for copy in copies:
        copy.wait()


def conv_rows(columns, conv, bias, channels, width):
    stacked = jnp.concatenate(columns, axis=1)
    products = jnp.dot(conv, stacked, preferred_element_type=F32)
    lane = lax.broadcasted_iota(jnp.int32, (1, width), 1)
    rows = []
    for q in range(len(columns)):
        part = products[:, q * width : (q + 1) * width]
        left = jnp.where(lane == 0, 0.0, pltpu.roll(part[:channels], 1, 1))
        right = jnp.where(lane == width - 1, 0.0, pltpu.roll(part[2 * channels :], width - 1, 1))
        rows.append(silu(left + part[channels : 2 * channels] + right + bias).astype(BF16))
    return jnp.concatenate(rows, axis=1)


def own_kernel(x_ref, beside_ref, conv_ref, mix_ref, cb_ref, mb_ref, out_ref, piece_ref, xs, *, group, spans):
    frames, rows, channels, width = x_ref.shape
    ((frame, _, place, size),) = spans
    piece_ref[0] = x_ref[frame, pl.ds(first_row(place, size, rows), size)]
    for f in range(frames):
        xs[f, 0] = beside_ref[f, 0]
        xs[f, rows + 1] = jnp.zeros((channels, width), BF16)

    def fill(s, carry):
        for f in range(frames):
            xs[f, s + 1] = x_ref[f, first_row(s, 1, rows)]
        return carry

    lax.fori_loop(0, rows, fill, 0)

    def body(p, carry):
        h = p * group
        parts = []
        for f in range(frames):
            columns = [xs[f, pl.ds(h + q, 3)].reshape(3 * channels, width) for q in range(group)]
            parts.append(conv_rows(columns, conv_ref[...], cb_ref[...], channels, width))
        mixed = jnp.dot(mix_ref[:, channels:], jnp.concatenate(parts, axis=0), preferred_element_type=F32)
        for q in range(group):
            out_ref[h + q] = mixed[:, q * width : (q + 1) * width] + mb_ref[...]
        return carry

    lax.fori_loop(0, rows // group, body, 0)


def incoming_kernel(own_ref, conv_ref, mix_ref, cb_ref, kept_ref, piece_ref, *refs, low, place, group, aliased):
    refs = refs[1:] if aliased else refs
    out_ref, carry_ref, xs, stage, sem = refs
    rows, channels, width = own_ref.shape
    kept, size = kept_ref.shape[0], piece_ref.shape[1]
    count = stage.shape[0]
    flip = flipped()
    xs[0:kept] = kept_ref[...]
    for k in range(size):
        xs[kept + k] = piece_ref[0, jnp.where(flip, size - 1 - k, k)]
    if xs.shape[0] > kept + size:
        xs[kept + size] = jnp.zeros((channels, width), BF16)
    carry_ref[...] = xs[pl.ds(xs.shape[0] - 2, 2)]
    first = lax.axis_index("frames") == 0

    @pl.when(first)
    def _():
        for q in range(count):
            stage[jnp.where(flip, count - 1 - q, q)] = own_ref[low + q].astype(BF16)

    @pl.when(jnp.logical_not(first))
    def _():
        def body(p, carry):
            h = p * group
            columns = [xs[pl.ds(h + q, 3)].reshape(3 * channels, width) for q in range(group)]
            act = conv_rows(columns, conv_ref[...], cb_ref[...], channels, width)
            mixed = jnp.dot(mix_ref[:, :channels], act, preferred_element_type=F32)
            for q in range(group):
                total = own_ref[low + h + q] + mixed[:, q * width : (q + 1) * width]
                stage[jnp.where(flip, count - 1 - h - q, h + q)] = total.astype(BF16)
            return carry

        lax.fori_loop(0, count // group, body, 0)

    copy = pltpu.make_async_copy(stage, out_ref.at[pl.ds(first_row(low, count, rows), count)], sem)
    copy.start()
    copy.wait()


def incoming_rows(out, own, weights, kept, piece, low, place, last):
    conv, mix, cb = weights
    rows, channels, width = own.shape
    held = kept.shape[0] + piece.shape[1] + (1 if last else 0)
    count = held - 2
    group = next(g for g in (4, 3, 2, 1) if count % g == 0)
    operands = [own, conv, mix, cb, kept, piece]
    in_specs = [VMEM] * len(operands)
    aliases = {}
    if out is not None:
        aliases = {len(operands): 0}
        operands.append(out)
        in_specs.append(ANY)
    return pl.pallas_call(
        functools.partial(
            incoming_kernel, low=low, place=place, group=group, aliased=out is not None
        ),
        out_shape=(
            jax.ShapeDtypeStruct(own.shape, BF16),
            jax.ShapeDtypeStruct((2, channels, width), BF16),
        ),
        in_specs=in_specs,
        out_specs=(ANY, VMEM),
        input_output_aliases=aliases,
        scratch_shapes=[
            pltpu.VMEM((held, channels, width), BF16),
            pltpu.VMEM((count, channels, width), BF16),
            pltpu.SemaphoreType.DMA,
        ],
        compiler_params=PARAMS,
        cost_estimate=cost(0, 0),
    )(*operands)


def per_device(video, w_spatial, b_spatial, w_temporal, b_temporal):
    frames, rows, width, channels = video.shape
    x = jnp.transpose(video, (0, 1, 3, 2))
    sizes = [rows - rows // 4 - 1, rows // 4, 1]
    places = [sum(sizes[:k]) for k in range(len(sizes))]

    spans = [(frames - 1, 1, place, size) for place, size in zip(places, sizes)]

    head_spans = [spans[0], (0, frames, 0, 1)]
    head, boundary = pl.pallas_call(
        functools.partial(slice_kernel, spans=head_spans),
        out_shape=row_shapes(x, head_spans),
        in_specs=[ANY],
        out_specs=[ANY] * 2,
        scratch_shapes=[pltpu.SemaphoreType.DMA((2,))],
        compiler_params=pltpu.CompilerParams(vmem_limit_bytes=HEAD_LIMIT),
    )(x)
    arrived = [lax.ppermute(head, "frames", ring("frames"))]
    beside = lax.ppermute(boundary, "rows", ring("rows"))

    square = jax.ShapeDtypeStruct((3 * channels, 3 * channels), BF16)
    flat = jax.ShapeDtypeStruct((channels, 3 * channels), BF16)
    bias = jax.ShapeDtypeStruct((channels, width), F32)
    conv, mix, cb, mb, piece = pl.pallas_call(
        functools.partial(prepare_kernel, spans=spans[1:2]),
        out_shape=[square, flat, bias, bias] + row_shapes(x, spans[1:2]),
        in_specs=[ANY] + [VMEM] * 4,
        out_specs=[VMEM] * 4 + [ANY],
        scratch_shapes=[pltpu.SemaphoreType.DMA((1,))],
        compiler_params=PARAMS,
        cost_estimate=cost(0, 2 * 12 * channels * channels * 2),
    )(x, w_spatial, b_spatial.reshape(1, channels), w_temporal, b_temporal.reshape(1, channels))
    arrived.append(lax.ppermute(piece, "frames", ring("frames")))

    own, piece = pl.pallas_call(
        functools.partial(own_kernel, group=4, spans=spans[2:]),
        out_shape=[jax.ShapeDtypeStruct((rows, channels, width), F32)] + row_shapes(x, spans[2:]),
        in_specs=[VMEM] * 6,
        out_specs=[VMEM] * 2,
        scratch_shapes=[pltpu.VMEM((frames, rows + 2, channels, width), BF16)],
        compiler_params=PARAMS,
        cost_estimate=cost(2 * rows * width * channels * channels * 20, 8 * rows * channels * width),
    )(x, beside, conv, mix, cb, mb)
    arrived.append(lax.ppermute(piece, "frames", ring("frames")))

    own, arrived[0] = lax.optimization_barrier((own, arrived[0]))
    size = sizes[0]
    edge = jnp.where(flipped(), arrived[0][0, size - 1 :], arrived[0][0, :1])
    kept = lax.ppermute(edge, "rows", ring("rows"))

    weights = (conv, mix, cb)
    out, low = None, 0
    for k, piece in enumerate(arrived):
        last = k == len(arrived) - 1
        out, kept = incoming_rows(out, own, weights, kept, piece, low, places[k], last)
        low = places[k] + sizes[k] - 1
    return jnp.transpose(out[None], (0, 1, 3, 2))


def solution(mesh):
    in_specs = (P(("batch", "frames"), "rows", None, None), P(), P(), P(), P())
    out_specs = P(("batch", "frames"), "rows", None, None)
    return jax.shard_map(
        per_device, mesh=mesh, in_specs=in_specs, out_specs=out_specs, check_vma=False
    )
```

time: 45.6 us -> 73.5 us (1.61)
  the two profiles are of different devices: /device:TPU:1 before, /device:TPU:20 now
where the time goes in v2:
time: 73.5 us; the launch traced here: 72.6 us
  Pallas kernels  59.7 us (81%)
  local copies, waits for them, and re-layouts  6.69 us (9%)
  starting transfers between devices  2.81 us (4%)
  waiting for transfers between devices  2.35 us (3%)
  other arithmetic  0.94 us (1%)
    pallas_call x1, Pallas kernels, per_device(): pl.pallas_call(functools.partial(slice_kernel, spans=head_spans), out_sha...  33.4 us
    pallas_call x3, Pallas kernels, incoming_rows(): pl.pallas_call(functools.partial(incoming_kernel, low=low, place=place, g...  12.7 us
    pallas_call x1, Pallas kernels, per_device(): pl.pallas_call(functools.partial(own_kernel, group=4, spans=spans[2:]), o...  12 us
    unnamed x16, local copies, waits for them, and re-layouts  6.68 us
    ppermute x1, waiting for transfers between devices, per_device(): arrived = [lax.ppermute(head, 'frames', ring('frames'))]  1.72 us
    pallas_call x1, Pallas kernels, per_device(): pl.pallas_call(functools.partial(prepare_kernel, spans=spans[1:2]), out_s...  1.63 us
    ppermute x1, starting transfers between devices, per_device(): arrived = [lax.ppermute(head, 'frames', ring('frames'))]  1.54 us
  transfers between devices with their start and end apart: 5, of which 2 were waited for; matrix products, arithmetic and copies ran while one was open for 1% of the time, Pallas kernels for 33%

profile of v2, /device:TPU:20, one launch (start us, length us, event | category | flops | bytes accessed | tf_op | source)
XLA Modules:
  0.0 72.6 jit_solution(1156356847375663374)
XLA Ops:
  0.0 0.0 copy-start.6
  0.0 0.0 copy-start.7
  0.0 0.0 copy-start.3
  0.0 33.4 %shard_map.55 = (bf16[1,11,320,128]{3,2,1,0:T(8,128)(2,1)}, bf16[2,1,320,128]{3,2,1,0:T(8,128)(2,1)}) custom-call(bf16[2,16,320,128]{3,2,1,0:T(8,128)(2,1)} %bitcast.6), custom_call_target="tpu_custom_call" | custom-call | tf_op jit(solution)/shard_map/pallas_call | solution.py:198
  33.4 0.1 collective-permute-start
  33.5 1.5 %collective-permute-start.1 = (bf16[1,11,320,128]{3,2,1,0:T(8,128)(2,1)}, bf16[1,11,320,128]{3,2,1,0:T(8,128)(2,1)}, u32[]{:S(2)}, u32[]{:S(2)}) collective-permute-start(bf16[1,11,320,128]{3,2,1,0:T(8,128)(2,1)} %get-tuple-element.27), channel_id=1, source_target_pairs={{0,8},{8,16},{16,24},{24,0},{1,9},{9,17},{17,25},{25,1},{2,10},{10... | collective-permute-start | bytes 2703368 | tf_op jit(solution)/shard_map/ppermute | solution.py:206
  35.0 0.0 copy-done.6
  35.0 0.0 copy-done.7
  35.0 0.0 copy-done.3
  35.1 0.0 copy-start
  35.1 1.7 %copy-done = bf16[2,16,128,320]{2,3,1,0:T(8,128)(2,1)S(1)} copy-done((bf16[2,16,128,320]{2,3,1,0:T(8,128)(2,1)S(1)}, bf16[2,16,128,320]{2,3,1,0:T(8,128)(2,1)}, u32[]{:S(2)}) %copy-start) | copy-done | bytes 2621464
  36.8 0.0 copy-start.2
  36.8 1.6 %copy-done.2 = bf16[3,3,320,320]{3,2,1,0:T(8,128)(2,1)S(1)} copy-done((bf16[3,3,320,320]{3,2,1,0:T(8,128)(2,1)S(1)}, bf16[3,3,320,320]{3,2,1,0:T(8,128)(2,1)}, u32[]{:S(2)}) %copy-start.2) | copy-done | bytes 1843224
  38.4 1.6 %shard_map.56 = (bf16[960,960]{1,0:T(8,128)(2,1)S(1)}, bf16[320,960]{1,0:T(8,128)(2,1)S(1)}, f32[320,128]{1,0:T(8,128)S(1)}, f32[320,128]{1,0:T(8,128)S(1)}, bf16[1,4,320,128]{3,2,1,0:T(8,128)(2,1)}) custom-call(bf16[2,16,320,128]{3,2,1,0:T(8,128)(2,1)S(1)} %bitcast.7, bf16[3,3,320,320]{3,2,1,0:T(8,128)(2,1)S(1)} %copy-done.2, f32[1,320]{1,0:T(1,128)S(1)} %reshape.28.bs_ref, ...), custom_call_target="tpu_custom_call" | custom-call | bytes 4915200 | tf_op jit(solution)/shard_map/pallas_call | solution.py:212
  40.1 0.0 copy-start.4
  40.1 0.7 copy-done.4
  40.7 0.5 collective-permute-start.3
  41.2 0.0 collective-permute-done.beside_ref
  41.2 0.0 copy-start.1
  41.2 1.7 %copy-done.1 = bf16[2,16,128,320]{2,3,1,0:T(8,128)(2,1)S(1)} copy-done((bf16[2,16,128,320]{2,3,1,0:T(8,128)(2,1)S(1)}, bf16[2,16,128,320]{2,3,1,0:T(8,128)(2,1)}, u32[]{:S(2)}) %copy-start.1) | copy-done | bytes 2621464
  43.0 0.0 copy-start.5
  43.0 0.9 %copy-done.5 = f32[320,128]{1,0:T(8,128)S(1)} copy-done((f32[320,128]{1,0:T(8,128)S(1)}, f32[320,128]{1,0:T(8,128)}, u32[]{:S(2)}) %copy-start.5) | copy-done | bytes 163864
  43.9 12.0 %shard_map.57 = (f32[16,320,128]{2,1,0:T(8,128)S(1)}, bf16[1,1,320,128]{3,2,1,0:T(8,128)(2,1)S(1)}) custom-call(bf16[2,16,320,128]{3,2,1,0:T(8,128)(2,1)S(1)} %bitcast.8, bf16[2,1,320,128]{3,2,1,0:T(8,128)(2,1)} %collective-permute-done.beside_ref, bf16[960,960]{1,0:T(8,128)(2,1)S(1)} %get-tuple-element.22.conv_ref, ...), custom_call_target="tpu_custom_call" | custom-call | flops 8388608000 | bytes 5242880 | tf_op jit(solution)/shard_map/pallas_call | solution.py:223
  55.8 1.7 %collective-permute-done.1.piece_ref = bf16[1,11,320,128]{3,2,1,0:T(8,128)(2,1)} collective-permute-done((bf16[1,11,320,128]{3,2,1,0:T(8,128)(2,1)}, bf16[1,11,320,128]{3,2,1,0:T(8,128)(2,1)}, u32[]{:S(2)}, u32[]{:S(2)}) %collective-permute-start.1) | collective-permute-done | bytes 901152 | tf_op jit(solution)/shard_map/ppermute | solution.py:206
  57.6 0.9 %select_bitcast_fusion = bf16[1,320,128]{2,1,0:T(8,128)(2,1)S(1)} fusion(bf16[1,11,320,128]{3,2,1,0:T(8,128)(2,1)} %collective-permute-done.1.piece_ref, pred[]{:T(512)S(6)} %eq.3), kind=kLoop, calls=%fused_computation | loop fusion | flops 40960 | bytes 245761 | tf_op jit(solution)/shard_map/jit(_where)/select_n | solution.py:236
  58.5 0.1 collective-permute-start.2
  58.6 0.6 collective-permute-start.4
  59.2 0.6 collective-permute-done.2.kept_ref
  59.9 7.8 %shard_map.58 = (bf16[16,320,128]{2,1,0:T(8,128)(2,1)}, bf16[2,320,128]{2,1,0:T(8,128)(2,1)S(1)}) custom-call(f32[16,320,128]{2,1,0:T(8,128)S(1)} %get-tuple-element.28.own_ref, bf16[960,960]{1,0:T(8,128)(2,1)S(1)} %get-tuple-element.22.conv_ref, bf16[320,960]{1,0:T(8,128)(2,1)S(1)} %get-tuple-element.23.mix_ref, f32[320,128]{1,0:T(8,128)S(1)} %get-tuple-element.24.cb_ref, ...), custom_call_target="tpu_custom_call" | custom-call | tf_op jit(solution)/shard_map/pallas_call | solution.py:168
  67.6 0.0 collective-permute-done.3.piece_ref
  67.6 2.4 %shard_map.59 = (bf16[16,320,128]{2,1,0:T(8,128)(2,1)}, bf16[2,320,128]{2,1,0:T(8,128)(2,1)S(1)}) custom-call(f32[16,320,128]{2,1,0:T(8,128)S(1)} %get-tuple-element.28.own_ref, bf16[960,960]{1,0:T(8,128)(2,1)S(1)} %get-tuple-element.22.conv_ref, bf16[320,960]{1,0:T(8,128)(2,1)S(1)} %get-tuple-element.23.mix_ref, ...), custom_call_target="tpu_custom_call", output_to_operand_aliasing={{0}: (6, {})} | custom-call | tf_op jit(solution)/shard_map/pallas_call | solution.py:168
  70.1 0.0 collective-permute-done.4.piece_ref
  70.1 2.5 %shard_map.60 = (bf16[16,320,128]{2,1,0:T(8,128)(2,1)}, bf16[2,320,128]{2,1,0:T(8,128)(2,1)}) custom-call(f32[16,320,128]{2,1,0:T(8,128)S(1)} %get-tuple-element.28.own_ref, bf16[960,960]{1,0:T(8,128)(2,1)S(1)} %get-tuple-element.22.conv_ref, bf16[320,960]{1,0:T(8,128)(2,1)S(1)} %get-tuple-element.23.mix_ref, ...), custom_call_target="tpu_custom_call", output_to_operand_aliasing={{0}: (6, {})} | custom-call | tf_op jit(solution)/shard_map/pallas_call | solution.py:168
  (2 shorter events, 0.0 us)
Async XLA Ops:
  0.0 35.0 %copy-start.6 = (f32[320]{0:T(512)S(1)}, f32[320]{0:T(512)}, u32[]{:S(2)}) copy-start(f32[320]{0:T(512)} %param.7) | copy-start | bytes 3844
  0.0 35.0 %copy-start.7 = (f32[320]{0:T(512)S(1)}, f32[320]{0:T(512)}, u32[]{:S(2)}) copy-start(f32[320]{0:T(512)} %param.9) | copy-start | bytes 3844
  0.0 35.0 %copy-start.3 = (bf16[3,320,320]{2,1,0:T(8,128)(2,1)S(1)}, bf16[3,320,320]{2,1,0:T(8,128)(2,1)}, u32[]{:S(2)}) copy-start(bf16[3,320,320]{2,1,0:T(8,128)(2,1)} %wt_ref.1) | copy-start | bytes 1843204
  33.4 7.8 %collective-permute-start = (bf16[2,1,320,128]{3,2,1,0:T(8,128)(2,1)}, bf16[2,1,320,128]{3,2,1,0:T(8,128)(2,1)}, u32[]{:S(2)}, u32[]{:S(2)}) collective-permute-start(bf16[2,1,320,128]{3,2,1,0:T(8,128)(2,1)} %get-tuple-element.21), channel_id=1, source_target_pairs={{0,4},{4,0},{1,5},{5,1},{2,6},{6,2},{3,7},{7,3},{8,12},{12,8},{9,1... | collective-permute-start | bytes 491528 | tf_op jit(solution)/shard_map/ppermute | solution.py:207
  33.5 24.1 %collective-permute-start.1 = (bf16[1,11,320,128]{3,2,1,0:T(8,128)(2,1)}, bf16[1,11,320,128]{3,2,1,0:T(8,128)(2,1)}, u32[]{:S(2)}, u32[]{:S(2)}) collective-permute-start(bf16[1,11,320,128]{3,2,1,0:T(8,128)(2,1)} %get-tuple-element.27), channel_id=1, source_target_pairs={{0,8},{8,16},{16,24},{24,0},{1,9},{9,17},{17,25},{25,1},{2,10},{10... | collective-permute-start | bytes 2703368 | tf_op jit(solution)/shard_map/ppermute | solution.py:206
  35.1 1.7 %copy-start = (bf16[2,16,128,320]{2,3,1,0:T(8,128)(2,1)S(1)}, bf16[2,16,128,320]{2,3,1,0:T(8,128)(2,1)}, u32[]{:S(2)}) copy-start(bf16[2,16,128,320]{2,3,1,0:T(8,128)(2,1)} %param.5) | copy-start | bytes 7864324
  36.8 1.6 %copy-start.2 = (bf16[3,3,320,320]{3,2,1,0:T(8,128)(2,1)S(1)}, bf16[3,3,320,320]{3,2,1,0:T(8,128)(2,1)}, u32[]{:S(2)}) copy-start(bf16[3,3,320,320]{3,2,1,0:T(8,128)(2,1)} %ws_ref.1) | copy-start | bytes 5529604
  40.1 0.7 copy-start.4
  40.7 26.9 %collective-permute-start.3 = (bf16[1,4,320,128]{3,2,1,0:T(8,128)(2,1)}, bf16[1,4,320,128]{3,2,1,0:T(8,128)(2,1)S(1)}, u32[]{:S(2)}, u32[]{:S(2)}) collective-permute-start(bf16[1,4,320,128]{3,2,1,0:T(8,128)(2,1)} %get-tuple-element.31), channel_id=1, source_target_pairs={{0,8},{8,16},{16,24},{24,0},{1,9},{9,17},{17,25},{25,1},{2,10},{10... | collective-permute-start | bytes 983048 | tf_op jit(solution)/shard_map/ppermute | solution.py:221
  41.2 1.7 %copy-start.1 = (bf16[2,16,128,320]{2,3,1,0:T(8,128)(2,1)S(1)}, bf16[2,16,128,320]{2,3,1,0:T(8,128)(2,1)}, u32[]{:S(2)}) copy-start(bf16[2,16,128,320]{2,3,1,0:T(8,128)(2,1)} %param.5) | copy-start | bytes 7864324
  43.0 0.9 %copy-start.5 = (f32[320,128]{1,0:T(8,128)S(1)}, f32[320,128]{1,0:T(8,128)}, u32[]{:S(2)}) copy-start(f32[320,128]{1,0:T(8,128)} %copy-done.4) | copy-start | bytes 491524
  58.5 1.3 %collective-permute-start.2 = (bf16[1,320,128]{2,1,0:T(8,128)(2,1)S(1)}, bf16[1,320,128]{2,1,0:T(8,128)(2,1)S(1)}, u32[]{:S(2)}, u32[]{:S(2)}) collective-permute-start(bf16[1,320,128]{2,1,0:T(8,128)(2,1)S(1)} %select_bitcast_fusion), channel_id=1, source_target_pairs={{0,4},{4,0},{1,5},{5,1},{2,6},{6,2},{3,7},{7,3},{8,12},{12,8},{9,1... | collective-permute-start | bytes 245768 | tf_op jit(solution)/shard_map/ppermute | solution.py:237
  58.6 11.5 %collective-permute-start.4 = (bf16[1,1,320,128]{3,2,1,0:T(8,128)(2,1)S(1)}, bf16[1,1,320,128]{3,2,1,0:T(8,128)(2,1)S(1)}, u32[]{:S(2)}, u32[]{:S(2)}) collective-permute-start(bf16[1,1,320,128]{3,2,1,0:T(8,128)(2,1)S(1)} %get-tuple-element.34), channel_id=1, source_target_pairs={{0,8},{8,16},{16,24},{24,0},{1,9},{9,17},{17,25},{25,1},{2,10},{10... | collective-permute-start | bytes 245768 | tf_op jit(solution)/shard_map/ppermute | solution.py:232

commit v3 on v2

--- a/solution.py
+++ b/solution.py
@@ -11,7 +11,7 @@
 BF16 = jnp.bfloat16
 VMEM = pl.BlockSpec(memory_space=pltpu.VMEM)
 ANY = pl.BlockSpec(memory_space=pl.ANY)
-HEAD_LIMIT = 62 * 2**20
+HEAD_LIMIT = 53 * 2**20
 PARAMS = pltpu.CompilerParams(vmem_limit_bytes=20 * 2**20)
 
 
@@ -84,10 +84,11 @@
     return jnp.concatenate(rows, axis=1)
 
 
-def own_kernel(x_ref, beside_ref, conv_ref, mix_ref, cb_ref, mb_ref, out_ref, piece_ref, xs, *, group, spans):
+def own_kernel(x_ref, beside_ref, conv_ref, mix_ref, cb_ref, mb_ref, out_ref, *refs, group, spans):
+    piece_refs, xs = refs[:-1], refs[-1]
     frames, rows, channels, width = x_ref.shape
-    ((frame, _, place, size),) = spans
-    piece_ref[0] = x_ref[frame, pl.ds(first_row(place, size, rows), size)]
+    for ref, (frame, _, place, size) in zip(piece_refs, spans):
+        ref[0] = x_ref[frame, pl.ds(first_row(place, size, rows), size)]
     for f in range(frames):
         xs[f, 0] = beside_ref[f, 0]
         xs[f, rows + 1] = jnp.zeros((channels, width), BF16)
@@ -113,18 +114,21 @@
     lax.fori_loop(0, rows // group, body, 0)
 
 
-def incoming_kernel(own_ref, conv_ref, mix_ref, cb_ref, kept_ref, piece_ref, *refs, low, place, group, aliased):
-    refs = refs[1:] if aliased else refs
-    out_ref, carry_ref, xs, stage, sem = refs
+def incoming_kernel(own_ref, conv_ref, mix_ref, cb_ref, *refs, pieces, low, group):
+    kept_ref, piece_refs = refs[0], refs[1 : 1 + pieces]
+    out_ref, carry_ref, xs, stage, sem = refs[-5:]
     rows, channels, width = own_ref.shape
-    kept, size = kept_ref.shape[0], piece_ref.shape[1]
     count = stage.shape[0]
     flip = flipped()
-    xs[0:kept] = kept_ref[...]
-    for k in range(size):
-        xs[kept + k] = piece_ref[0, jnp.where(flip, size - 1 - k, k)]
-    if xs.shape[0] > kept + size:
-        xs[kept + size] = jnp.zeros((channels, width), BF16)
+    held = kept_ref.shape[0]
+    xs[0:held] = kept_ref[...]
+    for ref in piece_refs:
+        size = ref.shape[1]
+        for k in range(size):
+            xs[held + k] = ref[0, jnp.where(flip, size - 1 - k, k)]
+        held += size
+    if xs.shape[0] > held:
+        xs[held] = jnp.zeros((channels, width), BF16)
     carry_ref[...] = xs[pl.ds(xs.shape[0] - 2, 2)]
     first = lax.axis_index("frames") == 0
 
@@ -152,13 +156,13 @@
     copy.wait()
 
 
-def incoming_rows(out, own, weights, kept, piece, low, place, last):
+def incoming_rows(out, own, weights, kept, pieces, low, last):
     conv, mix, cb = weights
     rows, channels, width = own.shape
-    held = kept.shape[0] + piece.shape[1] + (1 if last else 0)
+    held = kept.shape[0] + sum(piece.shape[1] for piece in pieces) + (1 if last else 0)
     count = held - 2
-    group = next(g for g in (4, 3, 2, 1) if count % g == 0)
-    operands = [own, conv, mix, cb, kept, piece]
+    group = next(g for g in (5, 4, 3, 2, 1) if count % g == 0)
+    operands = [own, conv, mix, cb, kept, *pieces]
     in_specs = [VMEM] * len(operands)
     aliases = {}
     if out is not None:
@@ -166,9 +170,7 @@
         operands.append(out)
         in_specs.append(ANY)
     return pl.pallas_call(
-        functools.partial(
-            incoming_kernel, low=low, place=place, group=group, aliased=out is not None
-        ),
+        functools.partial(incoming_kernel, pieces=len(pieces), low=low, group=group),
         out_shape=(
             jax.ShapeDtypeStruct(own.shape, BF16),
             jax.ShapeDtypeStruct((2, channels, width), BF16),
@@ -189,9 +191,9 @@
 def per_device(video, w_spatial, b_spatial, w_temporal, b_temporal):
     frames, rows, width, channels = video.shape
     x = jnp.transpose(video, (0, 1, 3, 2))
-    sizes = [rows - rows // 4 - 1, rows // 4, 1]
+    sizes = [5, rows - 10, 4, 1]
+    steps = [(0, 2), (2, 3), (3, 4)]
     places = [sum(sizes[:k]) for k in range(len(sizes))]
-
     spans = [(frames - 1, 1, place, size) for place, size in zip(places, sizes)]
 
     head_spans = [spans[0], (0, frames, 0, 1)]
@@ -199,7 +201,7 @@
         functools.partial(slice_kernel, spans=head_spans),
         out_shape=row_shapes(x, head_spans),
         in_specs=[ANY],
-        out_specs=[ANY] * 2,
+        out_specs=[VMEM] * 2,
         scratch_shapes=[pltpu.SemaphoreType.DMA((2,))],
         compiler_params=pltpu.CompilerParams(vmem_limit_bytes=HEAD_LIMIT),
     )(x)
@@ -213,23 +215,23 @@
         functools.partial(prepare_kernel, spans=spans[1:2]),
         out_shape=[square, flat, bias, bias] + row_shapes(x, spans[1:2]),
         in_specs=[ANY] + [VMEM] * 4,
-        out_specs=[VMEM] * 4 + [ANY],
+        out_specs=[VMEM] * 5,
         scratch_shapes=[pltpu.SemaphoreType.DMA((1,))],
         compiler_params=PARAMS,
         cost_estimate=cost(0, 2 * 12 * channels * channels * 2),
     )(x, w_spatial, b_spatial.reshape(1, channels), w_temporal, b_temporal.reshape(1, channels))
     arrived.append(lax.ppermute(piece, "frames", ring("frames")))
 
-    own, piece = pl.pallas_call(
+    own, *pieces = pl.pallas_call(
         functools.partial(own_kernel, group=4, spans=spans[2:]),
         out_shape=[jax.ShapeDtypeStruct((rows, channels, width), F32)] + row_shapes(x, spans[2:]),
         in_specs=[VMEM] * 6,
-        out_specs=[VMEM] * 2,
+        out_specs=[VMEM] * (len(sizes) - 1),
         scratch_shapes=[pltpu.VMEM((frames, rows + 2, channels, width), BF16)],
         compiler_params=PARAMS,
         cost_estimate=cost(2 * rows * width * channels * channels * 20, 8 * rows * channels * width),
     )(x, beside, conv, mix, cb, mb)
-    arrived.append(lax.ppermute(piece, "frames", ring("frames")))
+    arrived += [lax.ppermute(piece, "frames", ring("frames")) for piece in pieces]
 
     own, arrived[0] = lax.optimization_barrier((own, arrived[0]))
     size = sizes[0]
@@ -238,10 +240,9 @@
 
     weights = (conv, mix, cb)
     out, low = None, 0
-    for k, piece in enumerate(arrived):
-        last = k == len(arrived) - 1
-        out, kept = incoming_rows(out, own, weights, kept, piece, low, places[k], last)
-        low = places[k] + sizes[k] - 1
+    for begin, end in steps:
+        out, kept = incoming_rows(out, own, weights, kept, arrived[begin:end], low, end == len(arrived))
+        low = places[end - 1] + sizes[end - 1] - 1
     return jnp.transpose(out[None], (0, 1, 3, 2))
 
 

time: 73.5 us -> 40.6 us (0.55)
  Pallas kernels: 59.7 us -> 27.8 us
  starting transfers between devices: 2.81 us -> 5.3 us
  local copies, waits for them, and re-layouts: 6.69 us -> 4.3 us
    pallas_call x1, Pallas kernels: 33.4 us -> 1.97 us  [per_device(): pl.pallas_call(functools.partial(slice_kernel, spans=head_spans), out_sha...]
    ppermute x0 -> x2, starting transfers between devices: none -> 3.09 us  [per_device(): lax.ppermute(piece, 'frames', ring('frames'))]
    unnamed x16 -> x14, local copies, waits for them, and re-layouts: 6.68 us -> 4.29 us
    ppermute x2 -> x1, waiting for transfers between devices: 0.01 us -> 1.86 us  [per_device(): arrived.append(lax.ppermute(piece, 'frames', ring('frames')))]
    ppermute x1, waiting for transfers between devices: 1.72 us -> 0.01 us  [per_device(): arrived = [lax.ppermute(head, 'frames', ring('frames'))]]
    pallas_call x1, Pallas kernels: 12 us -> 11.1 us  [per_device(): pl.pallas_call(functools.partial(own_kernel, group=4, spans=spans[2:]), o...]
  transfers between devices with their start and end apart: 5 -> 6, of which waited for: 2 -> 1; matrix products, arithmetic and copies ran while one was open for 1% -> 2% of each run, Pallas kernels for 33% -> 58%
where the time goes in v3:
time: 40.6 us; the launch traced here: 40.3 us
  Pallas kernels  27.8 us (68%)
  starting transfers between devices  5.3 us (13%)
  local copies, waits for them, and re-layouts  4.3 us (11%)
  waiting for transfers between devices  1.88 us (5%)
  other arithmetic  0.94 us (2%)
    pallas_call x3, Pallas kernels, incoming_rows(): pl.pallas_call(functools.partial(incoming_kernel, pieces=len(pieces), low...  12.6 us
    pallas_call x1, Pallas kernels, per_device(): pl.pallas_call(functools.partial(own_kernel, group=4, spans=spans[2:]), o...  11.1 us
    unnamed x14, local copies, waits for them, and re-layouts  4.29 us
    ppermute x2, starting transfers between devices, per_device(): lax.ppermute(piece, 'frames', ring('frames'))  3.09 us
    pallas_call x1, Pallas kernels, per_device(): pl.pallas_call(functools.partial(prepare_kernel, spans=spans[1:2]), out_s...  2.11 us
    pallas_call x1, Pallas kernels, per_device(): pl.pallas_call(functools.partial(slice_kernel, spans=head_spans), out_sha...  1.97 us
    ppermute x1, waiting for transfers between devices, per_device(): arrived.append(lax.ppermute(piece, 'frames', ring('frames')))  1.86 us
    ppermute x1, starting transfers between devices, per_device(): arrived = [lax.ppermute(head, 'frames', ring('frames'))]  1.54 us
  transfers between devices with their start and end apart: 6, of which 1 were waited for; matrix products, arithmetic and copies ran while one was open for 2% of the time, Pallas kernels for 58%

profile of v3, /device:TPU:20, one launch (start us, length us, event | category | flops | bytes accessed | tf_op | source)
XLA Modules:
  0.0 40.3 jit_solution(1186819406745000029)
XLA Ops:
  0.0 0.0 copy-start.2
  0.0 0.0 copy-start.5
  0.0 0.0 copy-start.6
  0.0 2.0 %shard_map.55 = (bf16[1,5,320,128]{3,2,1,0:T(8,128)(2,1)}, bf16[2,1,320,128]{3,2,1,0:T(8,128)(2,1)S(1)}) custom-call(bf16[2,16,320,128]{3,2,1,0:T(8,128)(2,1)} %bitcast.6), custom_call_target="tpu_custom_call" | custom-call | tf_op jit(solution)/shard_map/pallas_call | solution.py:200
  2.0 0.1 collective-permute-start
  2.1 1.5 %collective-permute-start.1 = (bf16[1,5,320,128]{3,2,1,0:T(8,128)(2,1)}, bf16[1,5,320,128]{3,2,1,0:T(8,128)(2,1)}, u32[]{:S(2)}, u32[]{:S(2)}) collective-permute-start(bf16[1,5,320,128]{3,2,1,0:T(8,128)(2,1)} %get-tuple-element.28), channel_id=1, source_target_pairs={{0,8},{8,16},{16,24},{24,0},{1,9},{9,17},{17,25},{25,1},{2,10},{10... | collective-permute-start | bytes 1228808 | tf_op jit(solution)/shard_map/ppermute | solution.py:208
  3.6 0.0 copy-done.5
  3.6 0.0 copy-done.6
  3.6 0.0 copy-done.2
  3.6 0.0 copy-start.3
  3.6 1.6 %copy-done.3 = bf16[3,3,320,320]{3,2,1,0:T(8,128)(2,1)S(1)} copy-done((bf16[3,3,320,320]{3,2,1,0:T(8,128)(2,1)S(1)}, bf16[3,3,320,320]{3,2,1,0:T(8,128)(2,1)}, u32[]{:S(2)}) %copy-start.3) | copy-done | bytes 1843224
  5.3 0.0 copy-start.4
  5.3 1.1 %copy-done.4 = bf16[3,320,320]{2,1,0:T(8,128)(2,1)S(1)} copy-done((bf16[3,320,320]{2,1,0:T(8,128)(2,1)S(1)}, bf16[3,320,320]{2,1,0:T(8,128)(2,1)}, u32[]{:S(2)}) %copy-start.4) | copy-done | bytes 614424
  6.4 2.1 %shard_map.56 = (bf16[960,960]{1,0:T(8,128)(2,1)S(1)}, bf16[320,960]{1,0:T(8,128)(2,1)S(1)}, f32[320,128]{1,0:T(8,128)S(1)}, f32[320,128]{1,0:T(8,128)S(1)}, bf16[1,6,320,128]{3,2,1,0:T(8,128)(2,1)}) custom-call(bf16[2,16,320,128]{3,2,1,0:T(8,128)(2,1)S(1)} %bitcast.7, bf16[3,3,320,320]{3,2,1,0:T(8,128)(2,1)S(1)} %copy-done.3, f32[1,320]{1,0:T(1,128)S(1)} %reshape.28.bs_ref, ...), custom_call_target="tpu_custom_call" | custom-call | bytes 4915200 | tf_op jit(solution)/shard_map/pallas_call | solution.py:214
  8.5 0.0 copy-start
  8.5 0.5 %collective-permute-start.3 = (bf16[1,6,320,128]{3,2,1,0:T(8,128)(2,1)}, bf16[1,6,320,128]{3,2,1,0:T(8,128)(2,1)}, u32[]{:S(2)}, u32[]{:S(2)}) collective-permute-start(bf16[1,6,320,128]{3,2,1,0:T(8,128)(2,1)} %get-tuple-element.31), channel_id=1, source_target_pairs={{0,8},{8,16},{16,24},{24,0},{1,9},{9,17},{17,25},{25,1},{2,10},{10... | collective-permute-start | bytes 1474568 | tf_op jit(solution)/shard_map/ppermute | solution.py:223
  9.0 0.0 collective-permute-done.beside_ref
  9.0 11.1 %shard_map.57 = (f32[16,320,128]{2,1,0:T(8,128)S(1)}, bf16[1,4,320,128]{3,2,1,0:T(8,128)(2,1)}, bf16[1,1,320,128]{3,2,1,0:T(8,128)(2,1)S(1)}) custom-call(bf16[2,16,320,128]{3,2,1,0:T(8,128)(2,1)S(1)} %bitcast.8, bf16[2,1,320,128]{3,2,1,0:T(8,128)(2,1)S(1)} %collective-permute-done.beside_ref, bf16[960,960]{1,0:T(8,128)(2,1)S(1)} %get-tuple-element.23.conv_ref, ...), custom_call_target="tpu_custom_call" | custom-call | flops 8388608000 | bytes 5242880 | tf_op jit(solution)/shard_map/pallas_call | solution.py:225
  20.1 0.0 copy-done
  20.2 1.5 %collective-permute-start.4 = (bf16[1,4,320,128]{3,2,1,0:T(8,128)(2,1)}, bf16[1,4,320,128]{3,2,1,0:T(8,128)(2,1)}, u32[]{:S(2)}, u32[]{:S(2)}) collective-permute-start(bf16[1,4,320,128]{3,2,1,0:T(8,128)(2,1)} %get-tuple-element.33), channel_id=1, source_target_pairs={{0,8},{8,16},{16,24},{24,0},{1,9},{9,17},{17,25},{25,1},{2,10},{10... | collective-permute-start | bytes 983048 | tf_op jit(solution)/shard_map/ppermute | solution.py:234
  21.7 0.0 collective-permute-done.1.refs_1_
  21.7 0.9 %select_bitcast_fusion = bf16[1,320,128]{2,1,0:T(8,128)(2,1)S(1)} fusion(bf16[1,5,320,128]{3,2,1,0:T(8,128)(2,1)} %collective-permute-done.1.refs_1_, pred[]{:T(512)S(6)} %eq.3), kind=kLoop, calls=%fused_computation | loop fusion | flops 40960 | bytes 245761 | tf_op jit(solution)/shard_map/jit(_where)/select_n | solution.py:238
  22.6 0.1 collective-permute-start.2
  22.7 1.5 %collective-permute-start.5 = (bf16[1,1,320,128]{3,2,1,0:T(8,128)(2,1)S(1)}, bf16[1,1,320,128]{3,2,1,0:T(8,128)(2,1)S(1)}, u32[]{:S(2)}, u32[]{:S(2)}) collective-permute-start(bf16[1,1,320,128]{3,2,1,0:T(8,128)(2,1)S(1)} %get-tuple-element.36), channel_id=1, source_target_pairs={{0,8},{8,16},{16,24},{24,0},{1,9},{9,17},{17,25},{25,1},{2,10},{10... | collective-permute-start | bytes 245768 | tf_op jit(solution)/shard_map/ppermute | solution.py:234
  24.3 0.0 collective-permute-done.2.refs_0_
  24.3 1.9 %collective-permute-done.3.refs_2_ = bf16[1,6,320,128]{3,2,1,0:T(8,128)(2,1)} collective-permute-done((bf16[1,6,320,128]{3,2,1,0:T(8,128)(2,1)}, bf16[1,6,320,128]{3,2,1,0:T(8,128)(2,1)}, u32[]{:S(2)}, u32[]{:S(2)}) %collective-permute-start.3) | collective-permute-done | bytes 491552 | tf_op jit(solution)/shard_map/ppermute | solution.py:223
  26.1 0.0 copy-start.1
  26.1 1.5 %copy-done.1 = bf16[960,960]{1,0:T(8,128)(2,1)S(1)} copy-done((bf16[960,960]{1,0:T(8,128)(2,1)S(1)}, bf16[960,960]{1,0:T(8,128)(2,1)}, u32[]{:S(2)}) %copy-start.1) | copy-done | bytes 1843224
  27.7 6.7 %shard_map.58 = (bf16[16,320,128]{2,1,0:T(8,128)(2,1)}, bf16[2,320,128]{2,1,0:T(8,128)(2,1)S(1)}) custom-call(f32[16,320,128]{2,1,0:T(8,128)S(1)} %get-tuple-element.29.own_ref, bf16[960,960]{1,0:T(8,128)(2,1)S(1)} %copy-done.1, bf16[320,960]{1,0:T(8,128)(2,1)S(1)} %get-tuple-element.24.mix_ref, f32[320,128]{1,0:T(8,128)S(1)} %get-tuple-element.25.cb_ref, ...), custom_call_target="tpu_custom_call" | custom-call | tf_op jit(solution)/shard_map/pallas_call | solution.py:172
  34.4 0.0 collective-permute-done.4.refs_1_
  34.4 3.4 %shard_map.59 = (bf16[16,320,128]{2,1,0:T(8,128)(2,1)}, bf16[2,320,128]{2,1,0:T(8,128)(2,1)S(1)}) custom-call(f32[16,320,128]{2,1,0:T(8,128)S(1)} %get-tuple-element.29.own_ref, bf16[960,960]{1,0:T(8,128)(2,1)S(1)} %copy-done.1, bf16[320,960]{1,0:T(8,128)(2,1)S(1)} %get-tuple-element.24.mix_ref, ...), custom_call_target="tpu_custom_call", output_to_operand_aliasing={{0}: (6, {})} | custom-call | tf_op jit(solution)/shard_map/pallas_call | solution.py:172
  37.8 0.0 collective-permute-done.5.refs_1_
  37.8 2.5 %shard_map.60 = (bf16[16,320,128]{2,1,0:T(8,128)(2,1)}, bf16[2,320,128]{2,1,0:T(8,128)(2,1)}) custom-call(f32[16,320,128]{2,1,0:T(8,128)S(1)} %get-tuple-element.29.own_ref, bf16[960,960]{1,0:T(8,128)(2,1)S(1)} %copy-done.1, bf16[320,960]{1,0:T(8,128)(2,1)S(1)} %get-tuple-element.24.mix_ref, ...), custom_call_target="tpu_custom_call", output_to_operand_aliasing={{0}: (6, {})} | custom-call | tf_op jit(solution)/shard_map/pallas_call | solution.py:172
  (2 shorter events, 0.0 us)
Async XLA Ops:
  0.0 3.6 %copy-start.2 = (bf16[2,16,128,320]{2,3,1,0:T(8,128)(2,1)S(1)}, bf16[2,16,128,320]{2,3,1,0:T(8,128)(2,1)}, u32[]{:S(2)}) copy-start(bf16[2,16,128,320]{2,3,1,0:T(8,128)(2,1)} %param.5) | copy-start | bytes 7864324
  0.0 3.6 %copy-start.5 = (f32[320]{0:T(512)S(1)}, f32[320]{0:T(512)}, u32[]{:S(2)}) copy-start(f32[320]{0:T(512)} %param.7) | copy-start | bytes 3844
  0.0 3.6 %copy-start.6 = (f32[320]{0:T(512)S(1)}, f32[320]{0:T(512)}, u32[]{:S(2)}) copy-start(f32[320]{0:T(512)} %param.9) | copy-start | bytes 3844
  2.0 7.1 %collective-permute-start = (bf16[2,1,320,128]{3,2,1,0:T(8,128)(2,1)S(1)}, bf16[2,1,320,128]{3,2,1,0:T(8,128)(2,1)S(1)}, u32[]{:S(2)}, u32[]{:S(2)}) collective-permute-start(bf16[2,1,320,128]{3,2,1,0:T(8,128)(2,1)S(1)} %get-tuple-element.22), channel_id=1, source_target_pairs={{0,4},{4,0},{1,5},{5,1},{2,6},{6,2},{3,7},{7,3},{8,12},{12,8},{9,1... | collective-permute-start | bytes 491528 | tf_op jit(solution)/shard_map/ppermute | solution.py:209
  2.1 19.6 %collective-permute-start.1 = (bf16[1,5,320,128]{3,2,1,0:T(8,128)(2,1)}, bf16[1,5,320,128]{3,2,1,0:T(8,128)(2,1)}, u32[]{:S(2)}, u32[]{:S(2)}) collective-permute-start(bf16[1,5,320,128]{3,2,1,0:T(8,128)(2,1)} %get-tuple-element.28), channel_id=1, source_target_pairs={{0,8},{8,16},{16,24},{24,0},{1,9},{9,17},{17,25},{25,1},{2,10},{10... | collective-permute-start | bytes 1228808 | tf_op jit(solution)/shard_map/ppermute | solution.py:208
  3.6 1.6 %copy-start.3 = (bf16[3,3,320,320]{3,2,1,0:T(8,128)(2,1)S(1)}, bf16[3,3,320,320]{3,2,1,0:T(8,128)(2,1)}, u32[]{:S(2)}) copy-start(bf16[3,3,320,320]{3,2,1,0:T(8,128)(2,1)} %ws_ref.1) | copy-start | bytes 5529604
  5.3 1.1 %copy-start.4 = (bf16[3,320,320]{2,1,0:T(8,128)(2,1)S(1)}, bf16[3,320,320]{2,1,0:T(8,128)(2,1)}, u32[]{:S(2)}) copy-start(bf16[3,320,320]{2,1,0:T(8,128)(2,1)} %wt_ref.1) | copy-start | bytes 1843204
  8.5 11.6 %copy-start = (bf16[960,960]{1,0:T(8,128)(2,1)}, bf16[960,960]{1,0:T(8,128)(2,1)S(1)}, u32[]{:S(2)}) copy-start(bf16[960,960]{1,0:T(8,128)(2,1)S(1)} %get-tuple-element.23.conv_ref) | copy-start | bytes 5529604
  8.5 17.6 %collective-permute-start.3 = (bf16[1,6,320,128]{3,2,1,0:T(8,128)(2,1)}, bf16[1,6,320,128]{3,2,1,0:T(8,128)(2,1)}, u32[]{:S(2)}, u32[]{:S(2)}) collective-permute-start(bf16[1,6,320,128]{3,2,1,0:T(8,128)(2,1)} %get-tuple-element.31), channel_id=1, source_target_pairs={{0,8},{8,16},{16,24},{24,0},{1,9},{9,17},{17,25},{25,1},{2,10},{10... | collective-permute-start | bytes 1474568 | tf_op jit(solution)/shard_map/ppermute | solution.py:223
  20.2 14.2 %collective-permute-start.4 = (bf16[1,4,320,128]{3,2,1,0:T(8,128)(2,1)}, bf16[1,4,320,128]{3,2,1,0:T(8,128)(2,1)}, u32[]{:S(2)}, u32[]{:S(2)}) collective-permute-start(bf16[1,4,320,128]{3,2,1,0:T(8,128)(2,1)} %get-tuple-element.33), channel_id=1, source_target_pairs={{0,8},{8,16},{16,24},{24,0},{1,9},{9,17},{17,25},{25,1},{2,10},{10... | collective-permute-start | bytes 983048 | tf_op jit(solution)/shard_map/ppermute | solution.py:234
  22.6 1.6 %collective-permute-start.2 = (bf16[1,320,128]{2,1,0:T(8,128)(2,1)S(1)}, bf16[1,320,128]{2,1,0:T(8,128)(2,1)S(1)}, u32[]{:S(2)}, u32[]{:S(2)}) collective-permute-start(bf16[1,320,128]{2,1,0:T(8,128)(2,1)S(1)} %select_bitcast_fusion), channel_id=1, source_target_pairs={{0,4},{4,0},{1,5},{5,1},{2,6},{6,2},{3,7},{7,3},{8,12},{12,8},{9,1... | collective-permute-start | bytes 245768 | tf_op jit(solution)/shard_map/ppermute | solution.py:239
  22.7 15.1 %collective-permute-start.5 = (bf16[1,1,320,128]{3,2,1,0:T(8,128)(2,1)S(1)}, bf16[1,1,320,128]{3,2,1,0:T(8,128)(2,1)S(1)}, u32[]{:S(2)}, u32[]{:S(2)}) collective-permute-start(bf16[1,1,320,128]{3,2,1,0:T(8,128)(2,1)S(1)} %get-tuple-element.36), channel_id=1, source_target_pairs={{0,8},{8,16},{16,24},{24,0},{1,9},{9,17},{17,25},{25,1},{2,10},{10... | collective-permute-start | bytes 245768 | tf_op jit(solution)/shard_map/ppermute | solution.py:234
  26.1 1.5 %copy-start.1 = (bf16[960,960]{1,0:T(8,128)(2,1)S(1)}, bf16[960,960]{1,0:T(8,128)(2,1)}, u32[]{:S(2)}) copy-start(bf16[960,960]{1,0:T(8,128)(2,1)} %copy-done) | copy-start | bytes 5529604

commit v4 on v3

--- a/solution.py
+++ b/solution.py
@@ -40,14 +40,21 @@
 def row_copies(x_ref, outs, spans, sem):
     rows = x_ref.shape[1]
     copies = []
-    for k, (out, (frame, count, place, size)) in enumerate(zip(outs, spans)):
-        source = x_ref.at[pl.ds(frame, count), pl.ds(first_row(place, size, rows), size)]
-        copies.append(pltpu.make_async_copy(source, out, sem.at[k]))
+    for out, (frame, count, place, size) in zip(outs, spans):
+        for q in range(size):
+            source = x_ref.at[pl.ds(frame, count), first_row(place + q, 1, rows)]
+            copies.append(pltpu.make_async_copy(source, out.at[:, q], sem.at[len(copies)]))
     for copy in copies:
         copy.start()
     return copies
 
 
+def keep_rows(x_ref, outs, spans):
+    for out, (frame, _, place, size) in zip(outs, spans):
+        for q in range(size):
+            out[0, q] = x_ref[frame, first_row(place + q, 1, x_ref.shape[1])]
+
+
 def row_shapes(x, spans):
     return [jax.ShapeDtypeStruct((count, size) + x.shape[2:], x.dtype) for _, count, _, size in spans]
 
@@ -57,8 +64,8 @@
         copy.wait()
 
 
-def prepare_kernel(x_ref, ws_ref, bs_ref, wt_ref, bt_ref, conv_ref, mix_ref, cb_ref, mb_ref, piece_ref, sem, *, spans):
-    copies = row_copies(x_ref, [piece_ref], spans, sem)
+def prepare_kernel(x_ref, ws_ref, bs_ref, wt_ref, bt_ref, conv_ref, mix_ref, cb_ref, mb_ref, *piece_refs, spans):
+    keep_rows(x_ref, piece_refs, spans)
     taps, channels = ws_ref.shape[0], ws_ref.shape[2]
     for j in range(taps):
         blocks = [ws_ref[jnp.where(flipped(), taps - 1 - i, i), j] for i in range(taps)]
@@ -67,8 +74,6 @@
     width = cb_ref.shape[1]
     cb_ref[...] = jnp.broadcast_to(bs_ref[...], (width, channels)).T
     mb_ref[...] = jnp.broadcast_to(bt_ref[...], (width, channels)).T
-    for copy in copies:
-        copy.wait()
 
 
 def conv_rows(columns, conv, bias, channels, width):
@@ -87,8 +92,7 @@
 def own_kernel(x_ref, beside_ref, conv_ref, mix_ref, cb_ref, mb_ref, out_ref, *refs, group, spans):
     piece_refs, xs = refs[:-1], refs[-1]
     frames, rows, channels, width = x_ref.shape
-    for ref, (frame, _, place, size) in zip(piece_refs, spans):
-        ref[0] = x_ref[frame, pl.ds(first_row(place, size, rows), size)]
+    keep_rows(x_ref, piece_refs, spans)
     for f in range(frames):
         xs[f, 0] = beside_ref[f, 0]
         xs[f, rows + 1] = jnp.zeros((channels, width), BF16)
@@ -114,9 +118,9 @@
     lax.fori_loop(0, rows // group, body, 0)
 
 
-def incoming_kernel(own_ref, conv_ref, mix_ref, cb_ref, *refs, pieces, low, group):
+def incoming_kernel(own_ref, conv_ref, mix_ref, cb_ref, *refs, pieces, carry, low, group):
     kept_ref, piece_refs = refs[0], refs[1 : 1 + pieces]
-    out_ref, carry_ref, xs, stage, sem = refs[-5:]
+    out_ref, carry_refs, (xs, stage, sem) = refs[-4 - carry], refs[-3 - carry : -3], refs[-3:]
     rows, channels, width = own_ref.shape
     count = stage.shape[0]
     flip = flipped()
@@ -124,12 +128,12 @@
     xs[0:held] = kept_ref[...]
     for ref in piece_refs:
         size = ref.shape[1]
-        for k in range(size):
-            xs[held + k] = ref[0, jnp.where(flip, size - 1 - k, k)]
+        xs[held : held + size] = ref[0]
         held += size
     if xs.shape[0] > held:
         xs[held] = jnp.zeros((channels, width), BF16)
-    carry_ref[...] = xs[pl.ds(xs.shape[0] - 2, 2)]
+    for ref in carry_refs:
+        ref[...] = xs[pl.ds(xs.shape[0] - 2, 2)]
     first = lax.axis_index("frames") == 0
 
     @pl.when(first)
@@ -164,19 +168,17 @@
     group = next(g for g in (5, 4, 3, 2, 1) if count % g == 0)
     operands = [own, conv, mix, cb, kept, *pieces]
     in_specs = [VMEM] * len(operands)
+    two_rows = jax.ShapeDtypeStruct((2, channels, width), BF16)
     aliases = {}
     if out is not None:
         aliases = {len(operands): 0}
         operands.append(out)
         in_specs.append(ANY)
     return pl.pallas_call(
-        functools.partial(incoming_kernel, pieces=len(pieces), low=low, group=group),
-        out_shape=(
-            jax.ShapeDtypeStruct(own.shape, BF16),
-            jax.ShapeDtypeStruct((2, channels, width), BF16),
-        ),
+        functools.partial(incoming_kernel, pieces=len(pieces), carry=0 if last else 1, low=low, group=group),
+        out_shape=[jax.ShapeDtypeStruct(own.shape, BF16)] + ([] if last else [two_rows]),
         in_specs=in_specs,
-        out_specs=(ANY, VMEM),
+        out_specs=[ANY] + ([] if last else [VMEM]),
         input_output_aliases=aliases,
         scratch_shapes=[
             pltpu.VMEM((held, channels, width), BF16),
@@ -202,7 +204,7 @@
         out_shape=row_shapes(x, head_spans),
         in_specs=[ANY],
         out_specs=[VMEM] * 2,
-        scratch_shapes=[pltpu.SemaphoreType.DMA((2,))],
+        scratch_shapes=[pltpu.SemaphoreType.DMA((sizes[0] + 1,))],
         compiler_params=pltpu.CompilerParams(vmem_limit_bytes=HEAD_LIMIT),
     )(x)
     arrived = [lax.ppermute(head, "frames", ring("frames"))]
@@ -214,9 +216,8 @@
     conv, mix, cb, mb, piece = pl.pallas_call(
         functools.partial(prepare_kernel, spans=spans[1:2]),
         out_shape=[square, flat, bias, bias] + row_shapes(x, spans[1:2]),
-        in_specs=[ANY] + [VMEM] * 4,
+        in_specs=[VMEM] * 5,
         out_specs=[VMEM] * 5,
-        scratch_shapes=[pltpu.SemaphoreType.DMA((1,))],
         compiler_params=PARAMS,
         cost_estimate=cost(0, 2 * 12 * channels * channels * 2),
     )(x, w_spatial, b_spatial.reshape(1, channels), w_temporal, b_temporal.reshape(1, channels))
@@ -234,14 +235,12 @@
     arrived += [lax.ppermute(piece, "frames", ring("frames")) for piece in pieces]
 
     own, arrived[0] = lax.optimization_barrier((own, arrived[0]))
-    size = sizes[0]
-    edge = jnp.where(flipped(), arrived[0][0, size - 1 :], arrived[0][0, :1])
-    kept = lax.ppermute(edge, "rows", ring("rows"))
+    kept = [lax.ppermute(arrived[0][0, :1], "rows", ring("rows"))]
 
     weights = (conv, mix, cb)
     out, low = None, 0
     for begin, end in steps:
-        out, kept = incoming_rows(out, own, weights, kept, arrived[begin:end], low, end == len(arrived))
+        out, *kept = incoming_rows(out, own, weights, kept[0], arrived[begin:end], low, end == len(arrived))
         low = places[end - 1] + sizes[end - 1] - 1
     return jnp.transpose(out[None], (0, 1, 3, 2))
 

time: 40.6 us -> 36.6 us (0.901)
  Pallas kernels: 27.8 us -> 23.2 us
  waiting for transfers between devices: 1.88 us -> 5.13 us
  local copies, waits for them, and re-layouts: 4.3 us -> 2.76 us
  other arithmetic: 0.94 us -> 0 us
    pallas_call x3, Pallas kernels: 12.6 us -> 9.76 us  [incoming_rows(): pl.pallas_call(functools.partial(incoming_kernel, pieces=len(pieces), car...]
    ppermute x1, waiting for transfers between devices: 1.86 us -> 3.63 us  [per_device(): arrived.append(lax.ppermute(piece, 'frames', ring('frames')))]
    unnamed x14 -> x10, local copies, waits for them, and re-layouts: 4.29 us -> 2.75 us
    ppermute x2, waiting for transfers between devices: 0.01 us -> 1.49 us  [per_device(): lax.ppermute(piece, 'frames', ring('frames'))]
    pallas_call x1, Pallas kernels: 2.11 us -> 1 us  [per_device(): pl.pallas_call(functools.partial(prepare_kernel, spans=spans[1:2]), out_s...]
    select_n x1 -> x0, other arithmetic: 0.94 us -> none  [per_device(): edge = jnp.where(flipped(), arrived[0][0, size - 1:], arrived[0][0, :1])]
    pallas_call x1, Pallas kernels: 1.97 us -> 1.33 us  [per_device(): pl.pallas_call(functools.partial(slice_kernel, spans=head_spans), out_sha...]
  transfers between devices with their start and end apart: 6 -> 6, of which waited for: 1 -> 2; matrix products, arithmetic and copies ran while one was open for 2% -> 0% of each run, Pallas kernels for 58% -> 55%
where the time goes in v4:
time: 36.6 us; the launch traced here: 36.5 us
  Pallas kernels  23.2 us (63%)
  starting transfers between devices  5.3 us (14%)
  waiting for transfers between devices  5.13 us (14%)
  local copies, waits for them, and re-layouts  2.76 us (8%)
    pallas_call x1, Pallas kernels, per_device(): pl.pallas_call(functools.partial(own_kernel, group=4, spans=spans[2:]), o...  11.1 us
    pallas_call x3, Pallas kernels, incoming_rows(): pl.pallas_call(functools.partial(incoming_kernel, pieces=len(pieces), car...  9.76 us
    ppermute x1, waiting for transfers between devices, per_device(): arrived.append(lax.ppermute(piece, 'frames', ring('frames')))  3.63 us
    ppermute x2, starting transfers between devices, per_device(): lax.ppermute(piece, 'frames', ring('frames'))  3.02 us
    unnamed x10, local copies, waits for them, and re-layouts  2.75 us
    ppermute x1, starting transfers between devices, per_device(): arrived = [lax.ppermute(head, 'frames', ring('frames'))]  1.54 us
    ppermute x2, waiting for transfers between devices, per_device(): lax.ppermute(piece, 'frames', ring('frames'))  1.49 us
    pallas_call x1, Pallas kernels, per_device(): pl.pallas_call(functools.partial(slice_kernel, spans=head_spans), out_sha...  1.33 us
  transfers between devices with their start and end apart: 6, of which 2 were waited for; matrix products, arithmetic and copies ran while one was open for 0% of the time, Pallas kernels for 55%

profile of v4, /device:TPU:20, one launch (start us, length us, event | category | flops | bytes accessed | tf_op | source)
XLA Modules:
  0.0 36.5 jit_solution(12888977915811503981)
XLA Ops:
  0.0 0.0 copy-start
  0.0 0.0 copy-start.3
  0.0 0.0 copy-start.4
  0.0 1.3 %shard_map.55 = (bf16[1,5,320,128]{3,2,1,0:T(8,128)(2,1)S(1)}, bf16[2,1,320,128]{3,2,1,0:T(8,128)(2,1)S(1)}) custom-call(bf16[2,16,320,128]{3,2,1,0:T(8,128)(2,1)} %bitcast.6), custom_call_target="tpu_custom_call" | custom-call | tf_op jit(solution)/shard_map/pallas_call | solution.py:202
  1.3 0.1 collective-permute-start
  1.4 1.5 %collective-permute-start.1 = (bf16[1,5,320,128]{3,2,1,0:T(8,128)(2,1)S(1)}, bf16[1,5,320,128]{3,2,1,0:T(8,128)(2,1)S(1)}, u32[]{:S(2)}, u32[]{:S(2)}) collective-permute-start(bf16[1,5,320,128]{3,2,1,0:T(8,128)(2,1)S(1)} %get-tuple-element.27), channel_id=1, source_target_pairs={{0,8},{8,16},{16,24},{24,0},{1,9},{9,17},{17,25},{25,1},{2,10},{10... | collective-permute-start | bytes 1228808 | tf_op jit(solution)/shard_map/ppermute | solution.py:210
  3.0 0.0 copy-done.3
  3.0 0.0 copy-done.4
  3.0 0.0 copy-done
  3.0 0.0 copy-start.1
  3.0 1.6 %copy-done.1 = bf16[3,3,320,320]{3,2,1,0:T(8,128)(2,1)S(1)} copy-done((bf16[3,3,320,320]{3,2,1,0:T(8,128)(2,1)S(1)}, bf16[3,3,320,320]{3,2,1,0:T(8,128)(2,1)}, u32[]{:S(2)}) %copy-start.1) | copy-done | bytes 1843224
  4.6 0.0 copy-start.2
  4.6 1.1 %copy-done.2 = bf16[3,320,320]{2,1,0:T(8,128)(2,1)S(1)} copy-done((bf16[3,320,320]{2,1,0:T(8,128)(2,1)S(1)}, bf16[3,320,320]{2,1,0:T(8,128)(2,1)}, u32[]{:S(2)}) %copy-start.2) | copy-done | bytes 614424
  5.7 1.0 %shard_map.56 = (bf16[960,960]{1,0:T(8,128)(2,1)S(1)}, bf16[320,960]{1,0:T(8,128)(2,1)S(1)}, f32[320,128]{1,0:T(8,128)S(1)}, f32[320,128]{1,0:T(8,128)S(1)}, bf16[1,6,320,128]{3,2,1,0:T(8,128)(2,1)S(1)}) custom-call(bf16[2,16,320,128]{3,2,1,0:T(8,128)(2,1)S(1)} %bitcast.7, bf16[3,3,320,320]{3,2,1,0:T(8,128)(2,1)S(1)} %copy-done.1, ...), custom_call_target="tpu_custom_call" | custom-call | bytes 4915200 | tf_op jit(solution)/shard_map/pallas_call | solution.py:216
  6.7 0.6 %collective-permute-start.3 = (bf16[1,6,320,128]{3,2,1,0:T(8,128)(2,1)S(1)}, bf16[1,6,320,128]{3,2,1,0:T(8,128)(2,1)S(1)}, u32[]{:S(2)}, u32[]{:S(2)}) collective-permute-start(bf16[1,6,320,128]{3,2,1,0:T(8,128)(2,1)S(1)} %get-tuple-element.30), channel_id=1, source_target_pairs={{0,8},{8,16},{16,24},{24,0},{1,9},{9,17},{17,25},{25,1},{2,10},{10... | collective-permute-start | bytes 1474568 | tf_op jit(solution)/shard_map/ppermute | solution.py:224
  7.3 0.0 collective-permute-done.beside_ref
  7.3 11.1 %shard_map.57 = (f32[16,320,128]{2,1,0:T(8,128)S(1)}, bf16[1,4,320,128]{3,2,1,0:T(8,128)(2,1)S(1)}, bf16[1,1,320,128]{3,2,1,0:T(8,128)(2,1)S(1)}) custom-call(bf16[2,16,320,128]{3,2,1,0:T(8,128)(2,1)S(1)} %bitcast.8, bf16[2,1,320,128]{3,2,1,0:T(8,128)(2,1)S(1)} %collective-permute-done.beside_ref, bf16[960,960]{1,0:T(8,128)(2,1)S(1)} %get-tuple-element.22.conv_ref, ...), custom_call_target="tpu_custom_call" | custom-call | flops 8388608000 | bytes 5242880 | tf_op jit(solution)/shard_map/pallas_call | solution.py:226
  18.4 1.5 %collective-permute-start.4 = (bf16[1,4,320,128]{3,2,1,0:T(8,128)(2,1)S(1)}, bf16[1,4,320,128]{3,2,1,0:T(8,128)(2,1)S(1)}, u32[]{:S(2)}, u32[]{:S(2)}) collective-permute-start(bf16[1,4,320,128]{3,2,1,0:T(8,128)(2,1)S(1)} %get-tuple-element.32), channel_id=1, source_target_pairs={{0,8},{8,16},{16,24},{24,0},{1,9},{9,17},{17,25},{25,1},{2,10},{10... | collective-permute-start | bytes 983048 | tf_op jit(solution)/shard_map/ppermute | solution.py:235
  19.9 0.0 collective-permute-done.1.refs_1_
  19.9 0.1 collective-permute-start.2
  20.0 1.5 %collective-permute-start.5 = (bf16[1,1,320,128]{3,2,1,0:T(8,128)(2,1)S(1)}, bf16[1,1,320,128]{3,2,1,0:T(8,128)(2,1)S(1)}, u32[]{:S(2)}, u32[]{:S(2)}) collective-permute-start(bf16[1,1,320,128]{3,2,1,0:T(8,128)(2,1)S(1)} %get-tuple-element.35), channel_id=1, source_target_pairs={{0,8},{8,16},{16,24},{24,0},{1,9},{9,17},{17,25},{25,1},{2,10},{10... | collective-permute-start | bytes 245768 | tf_op jit(solution)/shard_map/ppermute | solution.py:235
  21.5 0.0 collective-permute-done.2.refs_0_
  21.5 3.6 %collective-permute-done.3.refs_2_ = bf16[1,6,320,128]{3,2,1,0:T(8,128)(2,1)S(1)} collective-permute-done((bf16[1,6,320,128]{3,2,1,0:T(8,128)(2,1)S(1)}, bf16[1,6,320,128]{3,2,1,0:T(8,128)(2,1)S(1)}, u32[]{:S(2)}, u32[]{:S(2)}) %collective-permute-start.3) | collective-permute-done | bytes 491552 | tf_op jit(solution)/shard_map/ppermute | solution.py:224
  25.2 5.5 %shard_map.58 = (bf16[16,320,128]{2,1,0:T(8,128)(2,1)}, bf16[2,320,128]{2,1,0:T(8,128)(2,1)S(1)}) custom-call(f32[16,320,128]{2,1,0:T(8,128)S(1)} %get-tuple-element.28.own_ref, bf16[960,960]{1,0:T(8,128)(2,1)S(1)} %get-tuple-element.22.conv_ref, bf16[320,960]{1,0:T(8,128)(2,1)S(1)} %get-tuple-element.23.mix_ref, f32[320,128]{1,0:T(8,128)S(1)} %get-tuple-element.24.cb_ref, ...), custom_call_target="tpu_custom_call" | custom-call | tf_op jit(solution)/shard_map/pallas_call | solution.py:177
  30.7 1.5 %collective-permute-done.4.refs_1_ = bf16[1,4,320,128]{3,2,1,0:T(8,128)(2,1)S(1)} collective-permute-done((bf16[1,4,320,128]{3,2,1,0:T(8,128)(2,1)S(1)}, bf16[1,4,320,128]{3,2,1,0:T(8,128)(2,1)S(1)}, u32[]{:S(2)}, u32[]{:S(2)}) %collective-permute-start.4) | collective-permute-done | bytes 327712 | tf_op jit(solution)/shard_map/ppermute | solution.py:235
  32.2 2.4 %shard_map.59 = (bf16[16,320,128]{2,1,0:T(8,128)(2,1)}, bf16[2,320,128]{2,1,0:T(8,128)(2,1)S(1)}) custom-call(f32[16,320,128]{2,1,0:T(8,128)S(1)} %get-tuple-element.28.own_ref, bf16[960,960]{1,0:T(8,128)(2,1)S(1)} %get-tuple-element.22.conv_ref, bf16[320,960]{1,0:T(8,128)(2,1)S(1)} %get-tuple-element.23.mix_ref, ...), custom_call_target="tpu_custom_call", output_to_operand_aliasing={{0}: (6, {})} | custom-call | tf_op jit(solution)/shard_map/pallas_call | solution.py:177
  34.6 0.0 collective-permute-done.5.refs_1_
  34.6 1.8 %shard_map.60 = bf16[16,320,128]{2,1,0:T(8,128)(2,1)} custom-call(f32[16,320,128]{2,1,0:T(8,128)S(1)} %get-tuple-element.28.own_ref, bf16[960,960]{1,0:T(8,128)(2,1)S(1)} %get-tuple-element.22.conv_ref, bf16[320,960]{1,0:T(8,128)(2,1)S(1)} %get-tuple-element.23.mix_ref, f32[320,128]{1,0:T(8,128)S(1)} %get-tuple-element.24.cb_ref, ...), custom_call_target="tpu_custom_call", output_to_operand_aliasing={{}: (6, {})} | custom-call | tf_op jit(solution)/shard_map/pallas_call | solution.py:177
  (3 shorter events, 0.0 us)
Async XLA Ops:
  0.0 3.0 %copy-start = (bf16[2,16,128,320]{2,3,1,0:T(8,128)(2,1)S(1)}, bf16[2,16,128,320]{2,3,1,0:T(8,128)(2,1)}, u32[]{:S(2)}) copy-start(bf16[2,16,128,320]{2,3,1,0:T(8,128)(2,1)} %param.5) | copy-start | bytes 7864324
  0.0 3.0 %copy-start.3 = (f32[320]{0:T(512)S(1)}, f32[320]{0:T(512)}, u32[]{:S(2)}) copy-start(f32[320]{0:T(512)} %param.7) | copy-start | bytes 3844
  0.0 3.0 %copy-start.4 = (f32[320]{0:T(512)S(1)}, f32[320]{0:T(512)}, u32[]{:S(2)}) copy-start(f32[320]{0:T(512)} %param.9) | copy-start | bytes 3844
  1.3 6.0 %collective-permute-start = (bf16[2,1,320,128]{3,2,1,0:T(8,128)(2,1)S(1)}, bf16[2,1,320,128]{3,2,1,0:T(8,128)(2,1)S(1)}, u32[]{:S(2)}, u32[]{:S(2)}) collective-permute-start(bf16[2,1,320,128]{3,2,1,0:T(8,128)(2,1)S(1)} %get-tuple-element.21), channel_id=1, source_target_pairs={{0,4},{4,0},{1,5},{5,1},{2,6},{6,2},{3,7},{7,3},{8,12},{12,8},{9,1... | collective-permute-start | bytes 491528 | tf_op jit(solution)/shard_map/ppermute | solution.py:211
  1.4 18.5 %collective-permute-start.1 = (bf16[1,5,320,128]{3,2,1,0:T(8,128)(2,1)S(1)}, bf16[1,5,320,128]{3,2,1,0:T(8,128)(2,1)S(1)}, u32[]{:S(2)}, u32[]{:S(2)}) collective-permute-start(bf16[1,5,320,128]{3,2,1,0:T(8,128)(2,1)S(1)} %get-tuple-element.27), channel_id=1, source_target_pairs={{0,8},{8,16},{16,24},{24,0},{1,9},{9,17},{17,25},{25,1},{2,10},{10... | collective-permute-start | bytes 1228808 | tf_op jit(solution)/shard_map/ppermute | solution.py:210
  3.0 1.6 %copy-start.1 = (bf16[3,3,320,320]{3,2,1,0:T(8,128)(2,1)S(1)}, bf16[3,3,320,320]{3,2,1,0:T(8,128)(2,1)}, u32[]{:S(2)}) copy-start(bf16[3,3,320,320]{3,2,1,0:T(8,128)(2,1)} %ws_ref.1) | copy-start | bytes 5529604
  4.6 1.1 %copy-start.2 = (bf16[3,320,320]{2,1,0:T(8,128)(2,1)S(1)}, bf16[3,320,320]{2,1,0:T(8,128)(2,1)}, u32[]{:S(2)}) copy-start(bf16[3,320,320]{2,1,0:T(8,128)(2,1)} %wt_ref.1) | copy-start | bytes 1843204
  6.7 18.4 %collective-permute-start.3 = (bf16[1,6,320,128]{3,2,1,0:T(8,128)(2,1)S(1)}, bf16[1,6,320,128]{3,2,1,0:T(8,128)(2,1)S(1)}, u32[]{:S(2)}, u32[]{:S(2)}) collective-permute-start(bf16[1,6,320,128]{3,2,1,0:T(8,128)(2,1)S(1)} %get-tuple-element.30), channel_id=1, source_target_pairs={{0,8},{8,16},{16,24},{24,0},{1,9},{9,17},{17,25},{25,1},{2,10},{10... | collective-permute-start | bytes 1474568 | tf_op jit(solution)/shard_map/ppermute | solution.py:224
  18.4 13.8 %collective-permute-start.4 = (bf16[1,4,320,128]{3,2,1,0:T(8,128)(2,1)S(1)}, bf16[1,4,320,128]{3,2,1,0:T(8,128)(2,1)S(1)}, u32[]{:S(2)}, u32[]{:S(2)}) collective-permute-start(bf16[1,4,320,128]{3,2,1,0:T(8,128)(2,1)S(1)} %get-tuple-element.32), channel_id=1, source_target_pairs={{0,8},{8,16},{16,24},{24,0},{1,9},{9,17},{17,25},{25,1},{2,10},{10... | collective-permute-start | bytes 983048 | tf_op jit(solution)/shard_map/ppermute | solution.py:235
  19.9 1.6 %collective-permute-start.2 = (bf16[1,320,128]{2,1,0:T(8,128)(2,1)S(1)}, bf16[1,320,128]{2,1,0:T(8,128)(2,1)S(1)}, u32[]{:S(2)}, u32[]{:S(2)}) collective-permute-start(bf16[1,320,128]{2,1,0:T(8,128)(2,1)S(1)} %slice_bitcast_fusion), channel_id=1, source_target_pairs={{0,4},{4,0},{1,5},{5,1},{2,6},{6,2},{3,7},{7,3},{8,12},{12,8},{9,1... | collective-permute-start | bytes 245768 | tf_op jit(solution)/shard_map/ppermute | solution.py:238
  20.0 14.6 %collective-permute-start.5 = (bf16[1,1,320,128]{3,2,1,0:T(8,128)(2,1)S(1)}, bf16[1,1,320,128]{3,2,1,0:T(8,128)(2,1)S(1)}, u32[]{:S(2)}, u32[]{:S(2)}) collective-permute-start(bf16[1,1,320,128]{3,2,1,0:T(8,128)(2,1)S(1)} %get-tuple-element.35), channel_id=1, source_target_pairs={{0,8},{8,16},{16,24},{24,0},{1,9},{9,17},{17,25},{25,1},{2,10},{10... | collective-permute-start | bytes 245768 | tf_op jit(solution)/shard_map/ppermute | solution.py:235

commit v5 on v4

--- a/solution.py
+++ b/solution.py
@@ -37,31 +37,35 @@
     return half + half * jnp.tanh(half)
 
 
-def row_copies(x_ref, outs, spans, sem):
-    rows = x_ref.shape[1]
-    copies = []
-    for out, (frame, count, place, size) in zip(outs, spans):
-        for q in range(size):
-            source = x_ref.at[pl.ds(frame, count), first_row(place + q, 1, rows)]
-            copies.append(pltpu.make_async_copy(source, out.at[:, q], sem.at[len(copies)]))
+def span_of(x_ref, span):
+    frame, count, place, size = span
+    return x_ref.at[pl.ds(frame, count), pl.ds(first_row(place, size, x_ref.shape[1]), size)]
+
+
+def keep_rows(x_ref, outs, spans):
+    for out, span in zip(outs, spans):
+        out[...] = span_of(x_ref, span)[...]
+
+
+def row_shapes(x, spans):
+    return [jax.ShapeDtypeStruct((count, size) + x.shape[2:], x.dtype) for _, count, _, size in spans]
+
+
+def slice_kernel(x_ref, *refs, spans):
+    outs, sem = refs[:-1], refs[-1]
+    copies = [
+        pltpu.make_async_copy(span_of(x_ref, span), out, sem.at[k])
+        for k, (out, span) in enumerate(zip(outs, spans))
+    ]
     for copy in copies:
         copy.start()
-    return copies
-
-
-def keep_rows(x_ref, outs, spans):
-    for out, (frame, _, place, size) in zip(outs, spans):
-        for q in range(size):
-            out[0, q] = x_ref[frame, first_row(place + q, 1, x_ref.shape[1])]
-
-
-def row_shapes(x, spans):
-    return [jax.ShapeDtypeStruct((count, size) + x.shape[2:], x.dtype) for _, count, _, size in spans]
-
-
-def slice_kernel(x_ref, *refs, spans):
-    for copy in row_copies(x_ref, refs[:-1], spans, refs[-1]):
+    for copy in copies:
         copy.wait()
+
+
+def edge_kernel(piece_ref, out_ref):
+    size = piece_ref.shape[1]
+    out_ref[0] = piece_ref[0, jnp.where(flipped(), size - 1, 0)]
 
 
 def prepare_kernel(x_ref, ws_ref, bs_ref, wt_ref, bt_ref, conv_ref, mix_ref, cb_ref, mb_ref, *piece_refs, spans):
@@ -118,28 +122,37 @@
     lax.fori_loop(0, rows // group, body, 0)
 
 
-def incoming_kernel(own_ref, conv_ref, mix_ref, cb_ref, *refs, pieces, carry, low, group):
-    kept_ref, piece_refs = refs[0], refs[1 : 1 + pieces]
-    out_ref, carry_refs, (xs, stage, sem) = refs[-4 - carry], refs[-3 - carry : -3], refs[-3:]
+def incoming_kernel(own_ref, conv_ref, mix_ref, cb_ref, *refs, pieces, low, count, group, ready, last):
     rows, channels, width = own_ref.shape
-    count = stage.shape[0]
     flip = flipped()
+    kept_ref, piece_refs, refs = refs[0], refs[1 : 1 + pieces], refs[1 + pieces :]
+    copies = []
+    if ready:
+        ready_ref, refs = refs[0], refs[1:]
+        refs = refs[1:] if low > ready else refs
+        out_ref, refs = refs[0], refs[1:]
+        sem, refs = refs[-1], refs[:-1]
+        place = first_row(low - ready, ready, rows)
+        copies.append(pltpu.make_async_copy(ready_ref, out_ref.at[pl.ds(place, ready)], sem.at[0]))
+        copies[0].start()
+    made_ref, carry_refs, xs = (refs[1], [], refs[0]) if last else (refs[0], [refs[1]], refs[2])
     held = kept_ref.shape[0]
     xs[0:held] = kept_ref[...]
     for ref in piece_refs:
         size = ref.shape[1]
-        xs[held : held + size] = ref[0]
+        for k in range(size):
+            xs[held + k] = ref[0, jnp.where(flip, size - 1 - k, k)]
         held += size
-    if xs.shape[0] > held:
+    if last:
         xs[held] = jnp.zeros((channels, width), BF16)
     for ref in carry_refs:
-        ref[...] = xs[pl.ds(xs.shape[0] - 2, 2)]
+        ref[...] = xs[pl.ds(held - 2, 2)]
     first = lax.axis_index("frames") == 0
 
     @pl.when(first)
     def _():
         for q in range(count):
-            stage[jnp.where(flip, count - 1 - q, q)] = own_ref[low + q].astype(BF16)
+            made_ref[jnp.where(flip, count - 1 - q, q)] = own_ref[low + q].astype(BF16)
 
     @pl.when(jnp.logical_not(first))
     def _():
@@ -150,51 +163,72 @@
             mixed = jnp.dot(mix_ref[:, :channels], act, preferred_element_type=F32)
             for q in range(group):
                 total = own_ref[low + h + q] + mixed[:, q * width : (q + 1) * width]
-                stage[jnp.where(flip, count - 1 - h - q, h + q)] = total.astype(BF16)
+                made_ref[jnp.where(flip, count - 1 - h - q, h + q)] = total.astype(BF16)
             return carry
 
         lax.fori_loop(0, count // group, body, 0)
 
-    copy = pltpu.make_async_copy(stage, out_ref.at[pl.ds(first_row(low, count, rows), count)], sem)
-    copy.start()
-    copy.wait()
-
-
-def incoming_rows(out, own, weights, kept, pieces, low, last):
+    if last:
+        place = first_row(low, count, rows)
+        copies.append(pltpu.make_async_copy(made_ref, out_ref.at[pl.ds(place, count)], sem.at[1]))
+        copies[-1].start()
+    for copy in copies:
+        copy.wait()
+
+
+def incoming_rows(out, made, own, weights, kept, pieces, low, last):
     conv, mix, cb = weights
     rows, channels, width = own.shape
     held = kept.shape[0] + sum(piece.shape[1] for piece in pieces) + (1 if last else 0)
     count = held - 2
     group = next(g for g in (5, 4, 3, 2, 1) if count % g == 0)
+    row_array = lambda n: jax.ShapeDtypeStruct((n, channels, width), BF16)
     operands = [own, conv, mix, cb, kept, *pieces]
     in_specs = [VMEM] * len(operands)
-    two_rows = jax.ShapeDtypeStruct((2, channels, width), BF16)
-    aliases = {}
-    if out is not None:
-        aliases = {len(operands): 0}
-        operands.append(out)
-        in_specs.append(ANY)
-    return pl.pallas_call(
-        functools.partial(incoming_kernel, pieces=len(pieces), carry=0 if last else 1, low=low, group=group),
-        out_shape=[jax.ShapeDtypeStruct(own.shape, BF16)] + ([] if last else [two_rows]),
+    out_shape, out_specs, scratch, aliases = [], [], [pltpu.VMEM((held, channels, width), BF16)], {}
+    if made is not None:
+        operands.append(made)
+        in_specs.append(VMEM)
+        if out is not None:
+            aliases = {len(operands): 0}
+            operands.append(out)
+            in_specs.append(ANY)
+        out_shape.append(row_array(rows))
+        out_specs.append(ANY)
+    if last:
+        scratch.append(pltpu.VMEM((count, channels, width), BF16))
+    else:
+        out_shape += [row_array(count), row_array(2)]
+        out_specs += [VMEM] * 2
+    if made is not None:
+        scratch.append(pltpu.SemaphoreType.DMA((2,)))
+    results = pl.pallas_call(
+        functools.partial(
+            incoming_kernel,
+            pieces=len(pieces),
+            low=low,
+            count=count,
+            group=group,
+            ready=0 if made is None else made.shape[0],
+            last=last,
+        ),
+        out_shape=out_shape,
         in_specs=in_specs,
-        out_specs=[ANY] + ([] if last else [VMEM]),
+        out_specs=out_specs,
         input_output_aliases=aliases,
-        scratch_shapes=[
-            pltpu.VMEM((held, channels, width), BF16),
-            pltpu.VMEM((count, channels, width), BF16),
-            pltpu.SemaphoreType.DMA,
-        ],
+        scratch_shapes=scratch,
         compiler_params=PARAMS,
         cost_estimate=cost(0, 0),
     )(*operands)
+    if last:
+        return results[0], None, None
+    return (None if made is None else results[0]), results[-2], results[-1]
 
 
 def per_device(video, w_spatial, b_spatial, w_temporal, b_temporal):
     frames, rows, width, channels = video.shape
     x = jnp.transpose(video, (0, 1, 3, 2))
-    sizes = [5, rows - 10, 4, 1]
-    steps = [(0, 2), (2, 3), (3, 4)]
+    sizes, early, steps = [5, 4, 4, 2, 1], 2, [(0, 2), (2, 3), (3, 4), (4, 5)]
     places = [sum(sizes[:k]) for k in range(len(sizes))]
     spans = [(frames - 1, 1, place, size) for place, size in zip(places, sizes)]
 
@@ -204,7 +238,7 @@
         out_shape=row_shapes(x, head_spans),
         in_specs=[ANY],
         out_specs=[VMEM] * 2,
-        scratch_shapes=[pltpu.SemaphoreType.DMA((sizes[0] + 1,))],
+        scratch_shapes=[pltpu.SemaphoreType.DMA((2,))],
         compiler_params=pltpu.CompilerParams(vmem_limit_bytes=HEAD_LIMIT),
     )(x)
     arrived = [lax.ppermute(head, "frames", ring("frames"))]
@@ -213,21 +247,22 @@
     square = jax.ShapeDtypeStruct((3 * channels, 3 * channels), BF16)
     flat = jax.ShapeDtypeStruct((channels, 3 * channels), BF16)
     bias = jax.ShapeDtypeStruct((channels, width), F32)
-    conv, mix, cb, mb, piece = pl.pallas_call(
-        functools.partial(prepare_kernel, spans=spans[1:2]),
-        out_shape=[square, flat, bias, bias] + row_shapes(x, spans[1:2]),
+    late = spans[1 + early :]
+    conv, mix, cb, mb, *pieces = pl.pallas_call(
+        functools.partial(prepare_kernel, spans=spans[1 : 1 + early]),
+        out_shape=[square, flat, bias, bias] + row_shapes(x, spans[1 : 1 + early]),
         in_specs=[VMEM] * 5,
-        out_specs=[VMEM] * 5,
+        out_specs=[VMEM] * (4 + early),
         compiler_params=PARAMS,
         cost_estimate=cost(0, 2 * 12 * channels * channels * 2),
     )(x, w_spatial, b_spatial.reshape(1, channels), w_temporal, b_temporal.reshape(1, channels))
-    arrived.append(lax.ppermute(piece, "frames", ring("frames")))
+    arrived += [lax.ppermute(piece, "frames", ring("frames")) for piece in pieces]
 
     own, *pieces = pl.pallas_call(
-        functools.partial(own_kernel, group=4, spans=spans[2:]),
-        out_shape=[jax.ShapeDtypeStruct((rows, channels, width), F32)] + row_shapes(x, spans[2:]),
+        functools.partial(own_kernel, group=4, spans=late),
+        out_shape=[jax.ShapeDtypeStruct((rows, channels, width), F32)] + row_shapes(x, late),
         in_specs=[VMEM] * 6,
-        out_specs=[VMEM] * (len(sizes) - 1),
+        out_specs=[VMEM] * (1 + len(late)),
         scratch_shapes=[pltpu.VMEM((frames, rows + 2, channels, width), BF16)],
         compiler_params=PARAMS,
         cost_estimate=cost(2 * rows * width * channels * channels * 20, 8 * rows * channels * width),
@@ -235,12 +270,21 @@
     arrived += [lax.ppermute(piece, "frames", ring("frames")) for piece in pieces]
 
     own, arrived[0] = lax.optimization_barrier((own, arrived[0]))
-    kept = [lax.ppermute(arrived[0][0, :1], "rows", ring("rows"))]
+    edge = pl.pallas_call(
+        edge_kernel,
+        out_shape=jax.ShapeDtypeStruct((1, channels, width), BF16),
+        in_specs=[VMEM],
+        out_specs=VMEM,
+        compiler_params=PARAMS,
+        cost_estimate=cost(0, 0),
+    )(arrived[0])
+    kept = lax.ppermute(edge, "rows", ring("rows"))
 
     weights = (conv, mix, cb)
-    out, low = None, 0
+    out, made, low = None, None, 0
     for begin, end in steps:
-        out, *kept = incoming_rows(out, own, weights, kept[0], arrived[begin:end], low, end == len(arrived))
+        last = end == len(arrived)
+        out, made, kept = incoming_rows(out, made, own, weights, kept, arrived[begin:end], low, last)
         low = places[end - 1] + sizes[end - 1] - 1
     return jnp.transpose(out[None], (0, 1, 3, 2))
 

time: 36.6 us -> 35.6 us (0.973)
  Pallas kernels: 23.2 us -> 21.4 us
  starting transfers between devices: 5.3 us -> 6.81 us
  waiting for transfers between devices: 5.13 us -> 4.19 us
    ppermute x2 -> x1, waiting for transfers between devices: 3.63 us -> 0.01 us  [per_device(): kept = lax.ppermute(edge, 'rows', ring('rows'))]
    ppermute x2 -> x4, waiting for transfers between devices: 1.49 us -> 4.19 us  [per_device(): lax.ppermute(piece, 'frames', ring('frames'))]
    ppermute x2 -> x4, starting transfers between devices: 3.02 us -> 5.12 us  [per_device(): lax.ppermute(piece, 'frames', ring('frames'))]
    pallas_call x5 -> x7, Pallas kernels: 21.8 us -> 20.1 us  [the longest x1 11.1 us: per_device(): pl.pallas_call(functools.partial(own_kernel, group=4, spans=late), out_sh...]
    ppermute x2 -> x1, starting transfers between devices: 0.66 us -> 0.07 us  [per_device(): kept = lax.ppermute(edge, 'rows', ring('rows'))]
  transfers between devices with their start and end apart: 6 -> 7, of which waited for: 2 -> 3; matrix products, arithmetic and copies ran while one was open for 0% -> 0% of each run, Pallas kernels for 55% -> 52%
where the time goes in v5:
time: 35.6 us; the launch traced here: 35.2 us
  Pallas kernels  21.4 us (60%)
  starting transfers between devices  6.81 us (19%)
  waiting for transfers between devices  4.19 us (12%)
  local copies, waits for them, and re-layouts  2.75 us (8%)
    pallas_call x1, Pallas kernels, per_device(): pl.pallas_call(functools.partial(own_kernel, group=4, spans=late), out_sh...  11.1 us
    pallas_call x4, Pallas kernels, incoming_rows(): pl.pallas_call(functools.partial(incoming_kernel, pieces=len(pieces), low...  8.07 us
    ppermute x4, starting transfers between devices, per_device(): lax.ppermute(piece, 'frames', ring('frames'))  5.12 us
    ppermute x4, waiting for transfers between devices, per_device(): lax.ppermute(piece, 'frames', ring('frames'))  4.19 us
    unnamed x10, local copies, waits for them, and re-layouts  2.75 us
    ppermute x1, starting transfers between devices, per_device(): arrived = [lax.ppermute(head, 'frames', ring('frames'))]  1.54 us
    pallas_call x1, Pallas kernels, per_device(): pl.pallas_call(functools.partial(slice_kernel, spans=head_spans), out_sha...  1.22 us
    pallas_call x1, Pallas kernels, per_device(): pl.pallas_call(functools.partial(prepare_kernel, spans=spans[1:1 + early]...  1.01 us
  transfers between devices with their start and end apart: 7, of which 3 were waited for; matrix products, arithmetic and copies ran while one was open for 0% of the time, Pallas kernels for 52%

profile of v5, /device:TPU:20, one launch (start us, length us, event | category | flops | bytes accessed | tf_op | source)
XLA Modules:
  0.0 35.2 jit_solution(6477337151494104517)
XLA Ops:
  0.0 0.0 copy-start
  0.0 0.0 copy-start.3
  0.0 0.0 copy-start.4
  0.0 1.2 %shard_map.55 = (bf16[1,5,320,128]{3,2,1,0:T(8,128)(2,1)S(1)}, bf16[2,1,320,128]{3,2,1,0:T(8,128)(2,1)S(1)}) custom-call(bf16[2,16,320,128]{3,2,1,0:T(8,128)(2,1)} %bitcast.4), custom_call_target="tpu_custom_call" | custom-call | tf_op jit(solution)/shard_map/pallas_call | solution.py:236
  1.2 0.1 collective-permute-start
  1.3 1.5 %collective-permute-start.1 = (bf16[1,5,320,128]{3,2,1,0:T(8,128)(2,1)S(1)}, bf16[1,5,320,128]{3,2,1,0:T(8,128)(2,1)S(1)}, u32[]{:S(2)}, u32[]{:S(2)}) collective-permute-start(bf16[1,5,320,128]{3,2,1,0:T(8,128)(2,1)S(1)} %get-tuple-element.32), channel_id=1, source_target_pairs={{0,8},{8,16},{16,24},{24,0},{1,9},{9,17},{17,25},{25,1},{2,10},{10... | collective-permute-start | bytes 1228808 | tf_op jit(solution)/shard_map/ppermute | solution.py:244
  2.9 0.0 copy-done.3
  2.9 0.0 copy-done.4
  2.9 0.0 copy-done
  2.9 0.0 copy-start.1
  2.9 1.6 %copy-done.1 = bf16[3,3,320,320]{3,2,1,0:T(8,128)(2,1)S(1)} copy-done((bf16[3,3,320,320]{3,2,1,0:T(8,128)(2,1)S(1)}, bf16[3,3,320,320]{3,2,1,0:T(8,128)(2,1)}, u32[]{:S(2)}) %copy-start.1) | copy-done | bytes 1843224
  4.5 0.0 copy-start.2
  4.5 1.1 %copy-done.2 = bf16[3,320,320]{2,1,0:T(8,128)(2,1)S(1)} copy-done((bf16[3,320,320]{2,1,0:T(8,128)(2,1)S(1)}, bf16[3,320,320]{2,1,0:T(8,128)(2,1)}, u32[]{:S(2)}) %copy-start.2) | copy-done | bytes 614424
  5.6 1.0 %shard_map.56 = (bf16[960,960]{1,0:T(8,128)(2,1)S(1)}, bf16[320,960]{1,0:T(8,128)(2,1)S(1)}, f32[320,128]{1,0:T(8,128)S(1)}, f32[320,128]{1,0:T(8,128)S(1)}, bf1...) custom-call(bf16[2,16,320,128]{3,2,1,0:T(8,128)(2,1)S(1)} %bitcast.5, ...), custom_call_target="tpu_custom_call" | custom-call | bytes 4915200 | tf_op jit(solution)/shard_map/pallas_call | solution.py:251
  6.6 0.6 %collective-permute-start.3 = (bf16[1,4,320,128]{3,2,1,0:T(8,128)(2,1)S(1)}, bf16[1,4,320,128]{3,2,1,0:T(8,128)(2,1)S(1)}, u32[]{:S(2)}, u32[]{:S(2)}) collective-permute-start(bf16[1,4,320,128]{3,2,1,0:T(8,128)(2,1)S(1)} %get-tuple-element.35), channel_id=1, source_target_pairs={{0,8},{8,16},{16,24},{24,0},{1,9},{9,17},{17,25},{25,1},{2,10},{10... | collective-permute-start | bytes 983048 | tf_op jit(solution)/shard_map/ppermute | solution.py:259
  7.3 1.4 %collective-permute-start.4 = (bf16[1,4,320,128]{3,2,1,0:T(8,128)(2,1)S(1)}, bf16[1,4,320,128]{3,2,1,0:T(8,128)(2,1)S(1)}, u32[]{:S(2)}, u32[]{:S(2)}) collective-permute-start(bf16[1,4,320,128]{3,2,1,0:T(8,128)(2,1)S(1)} %get-tuple-element.37), channel_id=1, source_target_pairs={{0,8},{8,16},{16,24},{24,0},{1,9},{9,17},{17,25},{25,1},{2,10},{10... | collective-permute-start | bytes 983048 | tf_op jit(solution)/shard_map/ppermute | solution.py:259
  8.7 0.0 collective-permute-done.beside_ref
  8.7 11.1 %shard_map.57 = (f32[16,320,128]{2,1,0:T(8,128)S(1)}, bf16[1,2,320,128]{3,2,1,0:T(8,128)(2,1)S(1)}, bf16[1,1,320,128]{3,2,1,0:T(8,128)(2,1)S(1)}) custom-call(bf16[2,16,320,128]{3,2,1,0:T(8,128)(2,1)S(1)} %bitcast.6, bf16[2,1,320,128]{3,2,1,0:T(8,128)(2,1)S(1)} %collective-permute-done.beside_ref, bf16[960,960]{1,0:T(8,128)(2,1)S(1)} %get-tuple-element.27.conv_ref, ...), custom_call_target="tpu_custom_call" | custom-call | flops 8388608000 | bytes 5242880 | tf_op jit(solution)/shard_map/pallas_call | solution.py:261
  19.7 1.5 %collective-permute-start.5 = (bf16[1,2,320,128]{3,2,1,0:T(8,128)(2,1)S(1)}, bf16[1,2,320,128]{3,2,1,0:T(8,128)(2,1)S(1)}, u32[]{:S(2)}, u32[]{:S(2)}) collective-permute-start(bf16[1,2,320,128]{3,2,1,0:T(8,128)(2,1)S(1)} %get-tuple-element.40), channel_id=1, source_target_pairs={{0,8},{8,16},{16,24},{24,0},{1,9},{9,17},{17,25},{25,1},{2,10},{10... | collective-permute-start | bytes 491528 | tf_op jit(solution)/shard_map/ppermute | solution.py:270
  21.3 0.0 collective-permute-done.1.piece_ref.refs_1_
  21.3 0.1 collective-permute-start.2
  21.4 1.6 %collective-permute-start.6 = (bf16[1,1,320,128]{3,2,1,0:T(8,128)(2,1)S(1)}, bf16[1,1,320,128]{3,2,1,0:T(8,128)(2,1)S(1)}, u32[]{:S(2)}, u32[]{:S(2)}) collective-permute-start(bf16[1,1,320,128]{3,2,1,0:T(8,128)(2,1)S(1)} %get-tuple-element.44), channel_id=1, source_target_pairs={{0,8},{8,16},{16,24},{24,0},{1,9},{9,17},{17,25},{25,1},{2,10},{10... | collective-permute-start | bytes 245768 | tf_op jit(solution)/shard_map/ppermute | solution.py:270
  22.9 0.0 collective-permute-done.3.refs_2_
  22.9 0.0 collective-permute-done.2.refs_0_
  22.9 3.4 %shard_map.59 = (bf16[8,320,128]{2,1,0:T(8,128)(2,1)S(1)}, bf16[2,320,128]{2,1,0:T(8,128)(2,1)S(1)}) custom-call(f32[16,320,128]{2,1,0:T(8,128)S(1)} %get-tuple-element.33.own_ref, bf16[960,960]{1,0:T(8,128)(2,1)S(1)} %get-tuple-element.27.conv_ref, bf16[320,960]{1,0:T(8,128)(2,1)S(1)} %get-tuple-element.28.mix_ref, ...), custom_call_target="tpu_custom_call" | custom-call | tf_op jit(solution)/shard_map/pallas_call | solution.py:205
  26.3 2.3 %collective-permute-done.4.refs_1_ = bf16[1,4,320,128]{3,2,1,0:T(8,128)(2,1)S(1)} collective-permute-done((bf16[1,4,320,128]{3,2,1,0:T(8,128)(2,1)S(1)}, bf16[1,4,320,128]{3,2,1,0:T(8,128)(2,1)S(1)}, u32[]{:S(2)}, u32[]{:S(2)}) %collective-permute-start.4) | collective-permute-done | bytes 327712 | tf_op jit(solution)/shard_map/ppermute | solution.py:259
  28.6 1.7 %shard_map.60 = (bf16[16,320,128]{2,1,0:T(8,128)(2,1)}, bf16[4,320,128]{2,1,0:T(8,128)(2,1)S(1)}, bf16[2,320,128]{2,1,0:T(8,128)(2,1)S(1)}) custom-call(f32[16,320,128]{2,1,0:T(8,128)S(1)} %get-tuple-element.33.own_ref, bf16[960,960]{1,0:T(8,128)(2,1)S(1)} %get-tuple-element.27.conv_ref, bf16[320,960]{1,0:T(8,128)(2,1)S(1)} %get-tuple-element.28.mix_ref, ...), custom_call_target="tpu_custom_call" | custom-call | tf_op jit(solution)/shard_map/pallas_call | solution.py:205
  30.3 1.8 %collective-permute-done.5.refs_1_ = bf16[1,2,320,128]{3,2,1,0:T(8,128)(2,1)S(1)} collective-permute-done((bf16[1,2,320,128]{3,2,1,0:T(8,128)(2,1)S(1)}, bf16[1,2,320,128]{3,2,1,0:T(8,128)(2,1)S(1)}, u32[]{:S(2)}, u32[]{:S(2)}) %collective-permute-start.5) | collective-permute-done | bytes 163872 | tf_op jit(solution)/shard_map/ppermute | solution.py:270
  32.1 1.2 %shard_map.61 = (bf16[16,320,128]{2,1,0:T(8,128)(2,1)}, bf16[2,320,128]{2,1,0:T(8,128)(2,1)S(1)}, bf16[2,320,128]{2,1,0:T(8,128)(2,1)S(1)}) custom-call(f32[16,320,128]{2,1,0:T(8,128)S(1)} %get-tuple-element.33.own_ref, bf16[960,960]{1,0:T(8,128)(2,1)S(1)} %get-tuple-element.27.conv_ref, ...), custom_call_target="tpu_custom_call", output_to_operand_aliasing={{0}: (7, {})} | custom-call | tf_op jit(solution)/shard_map/pallas_call | solution.py:205
  33.3 0.1 collective-permute-done.6.refs_1_
  33.4 1.8 %shard_map.62 = bf16[16,320,128]{2,1,0:T(8,128)(2,1)} custom-call(f32[16,320,128]{2,1,0:T(8,128)S(1)} %get-tuple-element.33.own_ref, bf16[960,960]{1,0:T(8,128)(2,1)S(1)} %get-tuple-element.27.conv_ref, bf16[320,960]{1,0:T(8,128)(2,1)S(1)} %get-tuple-element.28.mix_ref, f32[320,128]{1,0:T(8,128)S(1)} %get-tuple-element.29.cb_ref, ...), custom_call_target="tpu_custom_call", output_to_operand_aliasing={{}: (7, {})} | custom-call | tf_op jit(solution)/shard_map/pallas_call | solution.py:205
  (3 shorter events, 0.0 us)
Async XLA Ops:
  0.0 2.9 %copy-start = (bf16[2,16,128,320]{2,3,1,0:T(8,128)(2,1)S(1)}, bf16[2,16,128,320]{2,3,1,0:T(8,128)(2,1)}, u32[]{:S(2)}) copy-start(bf16[2,16,128,320]{2,3,1,0:T(8,128)(2,1)} %param.5) | copy-start | bytes 7864324
  0.0 2.9 %copy-start.3 = (f32[320]{0:T(512)S(1)}, f32[320]{0:T(512)}, u32[]{:S(2)}) copy-start(f32[320]{0:T(512)} %param.7) | copy-start | bytes 3844
  0.0 2.9 %copy-start.4 = (f32[320]{0:T(512)S(1)}, f32[320]{0:T(512)}, u32[]{:S(2)}) copy-start(f32[320]{0:T(512)} %param.9) | copy-start | bytes 3844
  1.2 7.4 %collective-permute-start = (bf16[2,1,320,128]{3,2,1,0:T(8,128)(2,1)S(1)}, bf16[2,1,320,128]{3,2,1,0:T(8,128)(2,1)S(1)}, u32[]{:S(2)}, u32[]{:S(2)}) collective-permute-start(bf16[2,1,320,128]{3,2,1,0:T(8,128)(2,1)S(1)} %get-tuple-element.26), channel_id=1, source_target_pairs={{0,4},{4,0},{1,5},{5,1},{2,6},{6,2},{3,7},{7,3},{8,12},{12,8},{9,1... | collective-permute-start | bytes 491528 | tf_op jit(solution)/shard_map/ppermute | solution.py:245
  1.3 20.0 %collective-permute-start.1 = (bf16[1,5,320,128]{3,2,1,0:T(8,128)(2,1)S(1)}, bf16[1,5,320,128]{3,2,1,0:T(8,128)(2,1)S(1)}, u32[]{:S(2)}, u32[]{:S(2)}) collective-permute-start(bf16[1,5,320,128]{3,2,1,0:T(8,128)(2,1)S(1)} %get-tuple-element.32), channel_id=1, source_target_pairs={{0,8},{8,16},{16,24},{24,0},{1,9},{9,17},{17,25},{25,1},{2,10},{10... | collective-permute-start | bytes 1228808 | tf_op jit(solution)/shard_map/ppermute | solution.py:244
  2.9 1.6 %copy-start.1 = (bf16[3,3,320,320]{3,2,1,0:T(8,128)(2,1)S(1)}, bf16[3,3,320,320]{3,2,1,0:T(8,128)(2,1)}, u32[]{:S(2)}) copy-start(bf16[3,3,320,320]{3,2,1,0:T(8,128)(2,1)} %ws_ref.1) | copy-start | bytes 5529604
  4.5 1.1 %copy-start.2 = (bf16[3,320,320]{2,1,0:T(8,128)(2,1)S(1)}, bf16[3,320,320]{2,1,0:T(8,128)(2,1)}, u32[]{:S(2)}) copy-start(bf16[3,320,320]{2,1,0:T(8,128)(2,1)} %wt_ref.1) | copy-start | bytes 1843204
  6.6 16.3 %collective-permute-start.3 = (bf16[1,4,320,128]{3,2,1,0:T(8,128)(2,1)S(1)}, bf16[1,4,320,128]{3,2,1,0:T(8,128)(2,1)S(1)}, u32[]{:S(2)}, u32[]{:S(2)}) collective-permute-start(bf16[1,4,320,128]{3,2,1,0:T(8,128)(2,1)S(1)} %get-tuple-element.35), channel_id=1, source_target_pairs={{0,8},{8,16},{16,24},{24,0},{1,9},{9,17},{17,25},{25,1},{2,10},{10... | collective-permute-start | bytes 983048 | tf_op jit(solution)/shard_map/ppermute | solution.py:259
  7.3 21.3 %collective-permute-start.4 = (bf16[1,4,320,128]{3,2,1,0:T(8,128)(2,1)S(1)}, bf16[1,4,320,128]{3,2,1,0:T(8,128)(2,1)S(1)}, u32[]{:S(2)}, u32[]{:S(2)}) collective-permute-start(bf16[1,4,320,128]{3,2,1,0:T(8,128)(2,1)S(1)} %get-tuple-element.37), channel_id=1, source_target_pairs={{0,8},{8,16},{16,24},{24,0},{1,9},{9,17},{17,25},{25,1},{2,10},{10... | collective-permute-start | bytes 983048 | tf_op jit(solution)/shard_map/ppermute | solution.py:259
  19.7 12.3 %collective-permute-start.5 = (bf16[1,2,320,128]{3,2,1,0:T(8,128)(2,1)S(1)}, bf16[1,2,320,128]{3,2,1,0:T(8,128)(2,1)S(1)}, u32[]{:S(2)}, u32[]{:S(2)}) collective-permute-start(bf16[1,2,320,128]{3,2,1,0:T(8,128)(2,1)S(1)} %get-tuple-element.40), channel_id=1, source_target_pairs={{0,8},{8,16},{16,24},{24,0},{1,9},{9,17},{17,25},{25,1},{2,10},{10... | collective-permute-start | bytes 491528 | tf_op jit(solution)/shard_map/ppermute | solution.py:270
  21.3 1.6 %collective-permute-start.2 = (bf16[1,320,128]{2,1,0:T(8,128)(2,1)S(1)}, bf16[1,320,128]{2,1,0:T(8,128)(2,1)S(1)}, u32[]{:S(2)}, u32[]{:S(2)}) collective-permute-start(bf16[1,320,128]{2,1,0:T(8,128)(2,1)S(1)} %shard_map.58), channel_id=1, source_target_pairs={{0,4},{4,0},{1,5},{5,1},{2,6},{6,2},{3,7},{7,3},{8,12},{12,8},{9,1... | collective-permute-start | bytes 245768 | tf_op jit(solution)/shard_map/ppermute | solution.py:281
  21.4 12.0 %collective-permute-start.6 = (bf16[1,1,320,128]{3,2,1,0:T(8,128)(2,1)S(1)}, bf16[1,1,320,128]{3,2,1,0:T(8,128)(2,1)S(1)}, u32[]{:S(2)}, u32[]{:S(2)}) collective-permute-start(bf16[1,1,320,128]{3,2,1,0:T(8,128)(2,1)S(1)} %get-tuple-element.44), channel_id=1, source_target_pairs={{0,8},{8,16},{16,24},{24,0},{1,9},{9,17},{17,25},{25,1},{2,10},{10... | collective-permute-start | bytes 245768 | tf_op jit(solution)/shard_map/ppermute | solution.py:270

commit v6 on v5

--- a/solution.py
+++ b/solution.py
@@ -12,6 +12,7 @@
 VMEM = pl.BlockSpec(memory_space=pltpu.VMEM)
 ANY = pl.BlockSpec(memory_space=pl.ANY)
 HEAD_LIMIT = 53 * 2**20
+OPEN, CLOSING, LAST = range(3)
 PARAMS = pltpu.CompilerParams(vmem_limit_bytes=20 * 2**20)
 
 
@@ -122,40 +123,41 @@
     lax.fori_loop(0, rows // group, body, 0)
 
 
-def incoming_kernel(own_ref, conv_ref, mix_ref, cb_ref, *refs, pieces, low, count, group, ready, last):
+def incoming_kernel(own_ref, conv_ref, mix_ref, cb_ref, *refs, pieces, low, count, group, ready, stage):
     rows, channels, width = own_ref.shape
     flip = flipped()
+    first = lax.axis_index("frames") == 0
     kept_ref, piece_refs, refs = refs[0], refs[1 : 1 + pieces], refs[1 + pieces :]
-    copies = []
-    if ready:
-        ready_ref, refs = refs[0], refs[1:]
-        refs = refs[1:] if low > ready else refs
-        out_ref, refs = refs[0], refs[1:]
-        sem, refs = refs[-1], refs[:-1]
-        place = first_row(low - ready, ready, rows)
-        copies.append(pltpu.make_async_copy(ready_ref, out_ref.at[pl.ds(place, ready)], sem.at[0]))
-        copies[0].start()
-    made_ref, carry_refs, xs = (refs[1], [], refs[0]) if last else (refs[0], [refs[1]], refs[2])
-    held = kept_ref.shape[0]
-    xs[0:held] = kept_ref[...]
-    for ref in piece_refs:
-        size = ref.shape[1]
-        for k in range(size):
-            xs[held + k] = ref[0, jnp.where(flip, size - 1 - k, k)]
-        held += size
-    if last:
-        xs[held] = jnp.zeros((channels, width), BF16)
-    for ref in carry_refs:
-        ref[...] = xs[pl.ds(held - 2, 2)]
-    first = lax.axis_index("frames") == 0
-
-    @pl.when(first)
-    def _():
-        for q in range(count):
-            made_ref[jnp.where(flip, count - 1 - q, q)] = own_ref[low + q].astype(BF16)
-
-    @pl.when(jnp.logical_not(first))
-    def _():
+    ready_ref = out_ref = sem = None
+    if ready:
+        ready_ref, refs = refs[0], refs[1 + (low > ready) :]
+        out_ref, refs, sem = refs[0], refs[1:-1], refs[-1]
+    if stage == LAST:
+        xs, made_ref = refs
+    else:
+        made_ref, carry_ref, xs = refs[:3]
+
+    def to_output(source, place, size, k):
+        target = out_ref.at[pl.ds(first_row(place, size, rows), size)]
+        return pltpu.make_async_copy(source, target, sem.at[k])
+
+    def own_rows(target, size):
+        for q in range(size):
+            target[jnp.where(flip, size - 1 - q, q)] = own_ref[low + q].astype(BF16)
+
+    def convolve():
+        held = kept_ref.shape[0]
+        xs[0:held] = kept_ref[...]
+        for ref in piece_refs:
+            size = ref.shape[1]
+            for k in range(size):
+                xs[held + k] = ref[0, jnp.where(flip, size - 1 - k, k)]
+            held += size
+        if stage == LAST:
+            xs[held] = jnp.zeros((channels, width), BF16)
+        else:
+            carry_ref[...] = xs[pl.ds(held - 2, 2)]
+
         def body(p, carry):
             h = p * group
             columns = [xs[pl.ds(h + q, 3)].reshape(3 * channels, width) for q in range(group)]
@@ -168,25 +170,58 @@
 
         lax.fori_loop(0, count // group, body, 0)
 
-    if last:
-        place = first_row(low, count, rows)
-        copies.append(pltpu.make_async_copy(made_ref, out_ref.at[pl.ds(place, count)], sem.at[1]))
-        copies[-1].start()
-    for copy in copies:
-        copy.wait()
-
-
-def incoming_rows(out, made, own, weights, kept, pieces, low, last):
+    if stage == LAST:
+
+        @pl.when(jnp.logical_not(first))
+        def _():
+            before = to_output(ready_ref, low - ready, ready, 0)
+            before.start()
+            convolve()
+            after = to_output(made_ref, low, count, 1)
+            after.start()
+            before.wait()
+            after.wait()
+
+        return
+
+    before = to_output(ready_ref, low - ready, ready, 0) if ready else None
+    if ready:
+        before.start()
+
+    @pl.when(first)
+    def _():
+        if stage == CLOSING:
+            rest = refs[3]
+            own_rows(rest, rows - low)
+            after = to_output(rest, low, rows - low, 1)
+            after.start()
+            after.wait()
+        else:
+            own_rows(made_ref, count)
+
+    @pl.when(jnp.logical_not(first))
+    def _():
+        convolve()
+
+    if ready:
+        before.wait()
+
+
+def incoming_rows(out, made, own, weights, kept, pieces, low, stage):
     conv, mix, cb = weights
     rows, channels, width = own.shape
-    held = kept.shape[0] + sum(piece.shape[1] for piece in pieces) + (1 if last else 0)
+    held = kept.shape[0] + sum(piece.shape[1] for piece in pieces) + (stage == LAST)
     count = held - 2
+    ready = 0 if made is None else made.shape[0]
     group = next(g for g in (5, 4, 3, 2, 1) if count % g == 0)
-    row_array = lambda n: jax.ShapeDtypeStruct((n, channels, width), BF16)
+
+    def row_array(size):
+        return jax.ShapeDtypeStruct((size, channels, width), BF16)
+
     operands = [own, conv, mix, cb, kept, *pieces]
     in_specs = [VMEM] * len(operands)
-    out_shape, out_specs, scratch, aliases = [], [], [pltpu.VMEM((held, channels, width), BF16)], {}
-    if made is not None:
+    out_shape, out_specs, aliases = [], [], {}
+    if ready:
         operands.append(made)
         in_specs.append(VMEM)
         if out is not None:
@@ -195,22 +230,19 @@
             in_specs.append(ANY)
         out_shape.append(row_array(rows))
         out_specs.append(ANY)
-    if last:
-        scratch.append(pltpu.VMEM((count, channels, width), BF16))
-    else:
+    if stage != LAST:
         out_shape += [row_array(count), row_array(2)]
         out_specs += [VMEM] * 2
-    if made is not None:
+    scratch = [pltpu.VMEM((held, channels, width), BF16)]
+    if stage == LAST:
+        scratch.append(pltpu.VMEM((count, channels, width), BF16))
+    if stage == CLOSING:
+        scratch.append(pltpu.VMEM((rows - low, channels, width), BF16))
+    if ready:
         scratch.append(pltpu.SemaphoreType.DMA((2,)))
     results = pl.pallas_call(
         functools.partial(
-            incoming_kernel,
-            pieces=len(pieces),
-            low=low,
-            count=count,
-            group=group,
-            ready=0 if made is None else made.shape[0],
-            last=last,
+            incoming_kernel, pieces=len(pieces), low=low, count=count, group=group, ready=ready, stage=stage
         ),
         out_shape=out_shape,
         in_specs=in_specs,
@@ -220,9 +252,9 @@
         compiler_params=PARAMS,
         cost_estimate=cost(0, 0),
     )(*operands)
-    if last:
+    if stage == LAST:
         return results[0], None, None
-    return (None if made is None else results[0]), results[-2], results[-1]
+    return (results[0] if ready else None), results[-2], results[-1]
 
 
 def per_device(video, w_spatial, b_spatial, w_temporal, b_temporal):
@@ -283,8 +315,8 @@
     weights = (conv, mix, cb)
     out, made, low = None, None, 0
     for begin, end in steps:
-        last = end == len(arrived)
-        out, made, kept = incoming_rows(out, made, own, weights, kept, arrived[begin:end], low, last)
+        stage = {len(arrived): LAST, steps[-1][0]: CLOSING}.get(end, OPEN)
+        out, made, kept = incoming_rows(out, made, own, weights, kept, arrived[begin:end], low, stage)
         low = places[end - 1] + sizes[end - 1] - 1
     return jnp.transpose(out[None], (0, 1, 3, 2))
 

time: 35.6 us -> 35.4 us (level)
  no operation moved by 1% of the time
where the time goes in v6:
time: 35.4 us; the launch traced here: 35.2 us
  Pallas kernels  21.4 us (60%)
  starting transfers between devices  6.81 us (19%)
  waiting for transfers between devices  4.19 us (12%)
  local copies, waits for them, and re-layouts  2.75 us (8%)
    pallas_call x1, Pallas kernels, per_device(): pl.pallas_call(functools.partial(own_kernel, group=4, spans=late), out_sh...  11.1 us
    pallas_call x4, Pallas kernels, incoming_rows(): pl.pallas_call(functools.partial(incoming_kernel, pieces=len(pieces), low...  8.07 us
    ppermute x4, starting transfers between devices, per_device(): lax.ppermute(piece, 'frames', ring('frames'))  5.12 us
    ppermute x4, waiting for transfers between devices, per_device(): lax.ppermute(piece, 'frames', ring('frames'))  4.18 us
    unnamed x10, local copies, waits for them, and re-layouts  2.75 us
    ppermute x1, starting transfers between devices, per_device(): arrived = [lax.ppermute(head, 'frames', ring('frames'))]  1.54 us
    pallas_call x1, Pallas kernels, per_device(): pl.pallas_call(functools.partial(slice_kernel, spans=head_spans), out_sha...  1.22 us
    pallas_call x1, Pallas kernels, per_device(): pl.pallas_call(functools.partial(prepare_kernel, spans=spans[1:1 + early]...  1.01 us
  transfers between devices with their start and end apart: 7, of which 3 were waited for; matrix products, arithmetic and copies ran while one was open for 0% of the time, Pallas kernels for 52%

profile of v6, /device:TPU:20, one launch (start us, length us, event | category | flops | bytes accessed | tf_op | source)
XLA Modules:
  0.0 35.2 jit_solution(2008811733624576475)
XLA Ops:
  0.0 0.0 copy-start
  0.0 0.0 copy-start.3
  0.0 0.0 copy-start.4
  0.0 1.2 %shard_map.55 = (bf16[1,5,320,128]{3,2,1,0:T(8,128)(2,1)S(1)}, bf16[2,1,320,128]{3,2,1,0:T(8,128)(2,1)S(1)}) custom-call(bf16[2,16,320,128]{3,2,1,0:T(8,128)(2,1)} %bitcast.4), custom_call_target="tpu_custom_call" | custom-call | tf_op jit(solution)/shard_map/pallas_call | solution.py:268
  1.2 0.1 collective-permute-start
  1.3 1.5 %collective-permute-start.1 = (bf16[1,5,320,128]{3,2,1,0:T(8,128)(2,1)S(1)}, bf16[1,5,320,128]{3,2,1,0:T(8,128)(2,1)S(1)}, u32[]{:S(2)}, u32[]{:S(2)}) collective-permute-start(bf16[1,5,320,128]{3,2,1,0:T(8,128)(2,1)S(1)} %get-tuple-element.32), channel_id=1, source_target_pairs={{0,8},{8,16},{16,24},{24,0},{1,9},{9,17},{17,25},{25,1},{2,10},{10... | collective-permute-start | bytes 1228808 | tf_op jit(solution)/shard_map/ppermute | solution.py:276
  2.9 0.0 copy-done.3
  2.9 0.0 copy-done.4
  2.9 0.0 copy-done
  2.9 0.0 copy-start.1
  2.9 1.6 %copy-done.1 = bf16[3,3,320,320]{3,2,1,0:T(8,128)(2,1)S(1)} copy-done((bf16[3,3,320,320]{3,2,1,0:T(8,128)(2,1)S(1)}, bf16[3,3,320,320]{3,2,1,0:T(8,128)(2,1)}, u32[]{:S(2)}) %copy-start.1) | copy-done | bytes 1843224
  4.5 0.0 copy-start.2
  4.5 1.1 %copy-done.2 = bf16[3,320,320]{2,1,0:T(8,128)(2,1)S(1)} copy-done((bf16[3,320,320]{2,1,0:T(8,128)(2,1)S(1)}, bf16[3,320,320]{2,1,0:T(8,128)(2,1)}, u32[]{:S(2)}) %copy-start.2) | copy-done | bytes 614424
  5.6 1.0 %shard_map.56 = (bf16[960,960]{1,0:T(8,128)(2,1)S(1)}, bf16[320,960]{1,0:T(8,128)(2,1)S(1)}, f32[320,128]{1,0:T(8,128)S(1)}, f32[320,128]{1,0:T(8,128)S(1)}, bf1...) custom-call(bf16[2,16,320,128]{3,2,1,0:T(8,128)(2,1)S(1)} %bitcast.5, ...), custom_call_target="tpu_custom_call" | custom-call | bytes 4915200 | tf_op jit(solution)/shard_map/pallas_call | solution.py:283
  6.6 0.6 %collective-permute-start.3 = (bf16[1,4,320,128]{3,2,1,0:T(8,128)(2,1)S(1)}, bf16[1,4,320,128]{3,2,1,0:T(8,128)(2,1)S(1)}, u32[]{:S(2)}, u32[]{:S(2)}) collective-permute-start(bf16[1,4,320,128]{3,2,1,0:T(8,128)(2,1)S(1)} %get-tuple-element.35), channel_id=1, source_target_pairs={{0,8},{8,16},{16,24},{24,0},{1,9},{9,17},{17,25},{25,1},{2,10},{10... | collective-permute-start | bytes 983048 | tf_op jit(solution)/shard_map/ppermute | solution.py:291
  7.3 1.4 %collective-permute-start.4 = (bf16[1,4,320,128]{3,2,1,0:T(8,128)(2,1)S(1)}, bf16[1,4,320,128]{3,2,1,0:T(8,128)(2,1)S(1)}, u32[]{:S(2)}, u32[]{:S(2)}) collective-permute-start(bf16[1,4,320,128]{3,2,1,0:T(8,128)(2,1)S(1)} %get-tuple-element.37), channel_id=1, source_target_pairs={{0,8},{8,16},{16,24},{24,0},{1,9},{9,17},{17,25},{25,1},{2,10},{10... | collective-permute-start | bytes 983048 | tf_op jit(solution)/shard_map/ppermute | solution.py:291
  8.7 0.0 collective-permute-done.beside_ref
  8.7 11.1 %shard_map.57 = (f32[16,320,128]{2,1,0:T(8,128)S(1)}, bf16[1,2,320,128]{3,2,1,0:T(8,128)(2,1)S(1)}, bf16[1,1,320,128]{3,2,1,0:T(8,128)(2,1)S(1)}) custom-call(bf16[2,16,320,128]{3,2,1,0:T(8,128)(2,1)S(1)} %bitcast.6, bf16[2,1,320,128]{3,2,1,0:T(8,128)(2,1)S(1)} %collective-permute-done.beside_ref, bf16[960,960]{1,0:T(8,128)(2,1)S(1)} %get-tuple-element.27.conv_ref, ...), custom_call_target="tpu_custom_call" | custom-call | flops 8388608000 | bytes 5242880 | tf_op jit(solution)/shard_map/pallas_call | solution.py:293
  19.7 1.5 %collective-permute-start.5 = (bf16[1,2,320,128]{3,2,1,0:T(8,128)(2,1)S(1)}, bf16[1,2,320,128]{3,2,1,0:T(8,128)(2,1)S(1)}, u32[]{:S(2)}, u32[]{:S(2)}) collective-permute-start(bf16[1,2,320,128]{3,2,1,0:T(8,128)(2,1)S(1)} %get-tuple-element.40), channel_id=1, source_target_pairs={{0,8},{8,16},{16,24},{24,0},{1,9},{9,17},{17,25},{25,1},{2,10},{10... | collective-permute-start | bytes 491528 | tf_op jit(solution)/shard_map/ppermute | solution.py:302
  21.3 0.0 collective-permute-done.1.piece_ref.refs_1_
  21.3 0.1 collective-permute-start.2
  21.4 1.6 %collective-permute-start.6 = (bf16[1,1,320,128]{3,2,1,0:T(8,128)(2,1)S(1)}, bf16[1,1,320,128]{3,2,1,0:T(8,128)(2,1)S(1)}, u32[]{:S(2)}, u32[]{:S(2)}) collective-permute-start(bf16[1,1,320,128]{3,2,1,0:T(8,128)(2,1)S(1)} %get-tuple-element.44), channel_id=1, source_target_pairs={{0,8},{8,16},{16,24},{24,0},{1,9},{9,17},{17,25},{25,1},{2,10},{10... | collective-permute-start | bytes 245768 | tf_op jit(solution)/shard_map/ppermute | solution.py:302
  22.9 0.0 collective-permute-done.3.refs_2_
  22.9 0.0 collective-permute-done.2.refs_0_
  22.9 3.4 %shard_map.59 = (bf16[8,320,128]{2,1,0:T(8,128)(2,1)S(1)}, bf16[2,320,128]{2,1,0:T(8,128)(2,1)S(1)}) custom-call(f32[16,320,128]{2,1,0:T(8,128)S(1)} %get-tuple-element.33.own_ref, bf16[960,960]{1,0:T(8,128)(2,1)S(1)} %get-tuple-element.27.conv_ref, bf16[320,960]{1,0:T(8,128)(2,1)S(1)} %get-tuple-element.28.mix_ref, ...), custom_call_target="tpu_custom_call" | custom-call | tf_op jit(solution)/shard_map/pallas_call | solution.py:243
  26.3 2.3 %collective-permute-done.4.refs_1_ = bf16[1,4,320,128]{3,2,1,0:T(8,128)(2,1)S(1)} collective-permute-done((bf16[1,4,320,128]{3,2,1,0:T(8,128)(2,1)S(1)}, bf16[1,4,320,128]{3,2,1,0:T(8,128)(2,1)S(1)}, u32[]{:S(2)}, u32[]{:S(2)}) %collective-permute-start.4) | collective-permute-done | bytes 327712 | tf_op jit(solution)/shard_map/ppermute | solution.py:291
  28.6 1.7 %shard_map.60 = (bf16[16,320,128]{2,1,0:T(8,128)(2,1)}, bf16[4,320,128]{2,1,0:T(8,128)(2,1)S(1)}, bf16[2,320,128]{2,1,0:T(8,128)(2,1)S(1)}) custom-call(f32[16,320,128]{2,1,0:T(8,128)S(1)} %get-tuple-element.33.own_ref, bf16[960,960]{1,0:T(8,128)(2,1)S(1)} %get-tuple-element.27.conv_ref, bf16[320,960]{1,0:T(8,128)(2,1)S(1)} %get-tuple-element.28.mix_ref, ...), custom_call_target="tpu_custom_call" | custom-call | tf_op jit(solution)/shard_map/pallas_call | solution.py:243
  30.3 1.8 %collective-permute-done.5.refs_1_ = bf16[1,2,320,128]{3,2,1,0:T(8,128)(2,1)S(1)} collective-permute-done((bf16[1,2,320,128]{3,2,1,0:T(8,128)(2,1)S(1)}, bf16[1,2,320,128]{3,2,1,0:T(8,128)(2,1)S(1)}, u32[]{:S(2)}, u32[]{:S(2)}) %collective-permute-start.5) | collective-permute-done | bytes 163872 | tf_op jit(solution)/shard_map/ppermute | solution.py:302
  32.1 1.2 %shard_map.61 = (bf16[16,320,128]{2,1,0:T(8,128)(2,1)}, bf16[2,320,128]{2,1,0:T(8,128)(2,1)S(1)}, bf16[2,320,128]{2,1,0:T(8,128)(2,1)S(1)}) custom-call(f32[16,320,128]{2,1,0:T(8,128)S(1)} %get-tuple-element.33.own_ref, bf16[960,960]{1,0:T(8,128)(2,1)S(1)} %get-tuple-element.27.conv_ref, ...), custom_call_target="tpu_custom_call", output_to_operand_aliasing={{0}: (7, {})} | custom-call | tf_op jit(solution)/shard_map/pallas_call | solution.py:243
  33.3 0.1 collective-permute-done.6.refs_1_
  33.4 1.8 %shard_map.62 = bf16[16,320,128]{2,1,0:T(8,128)(2,1)} custom-call(f32[16,320,128]{2,1,0:T(8,128)S(1)} %get-tuple-element.33.own_ref, bf16[960,960]{1,0:T(8,128)(2,1)S(1)} %get-tuple-element.27.conv_ref, bf16[320,960]{1,0:T(8,128)(2,1)S(1)} %get-tuple-element.28.mix_ref, f32[320,128]{1,0:T(8,128)S(1)} %get-tuple-element.29.cb_ref, ...), custom_call_target="tpu_custom_call", output_to_operand_aliasing={{}: (7, {})} | custom-call | tf_op jit(solution)/shard_map/pallas_call | solution.py:243
  (3 shorter events, 0.0 us)
Async XLA Ops:
  0.0 2.9 %copy-start = (bf16[2,16,128,320]{2,3,1,0:T(8,128)(2,1)S(1)}, bf16[2,16,128,320]{2,3,1,0:T(8,128)(2,1)}, u32[]{:S(2)}) copy-start(bf16[2,16,128,320]{2,3,1,0:T(8,128)(2,1)} %param.5) | copy-start | bytes 7864324
  0.0 2.9 %copy-start.3 = (f32[320]{0:T(512)S(1)}, f32[320]{0:T(512)}, u32[]{:S(2)}) copy-start(f32[320]{0:T(512)} %param.7) | copy-start | bytes 3844
  0.0 2.9 %copy-start.4 = (f32[320]{0:T(512)S(1)}, f32[320]{0:T(512)}, u32[]{:S(2)}) copy-start(f32[320]{0:T(512)} %param.9) | copy-start | bytes 3844
  1.2 7.4 %collective-permute-start = (bf16[2,1,320,128]{3,2,1,0:T(8,128)(2,1)S(1)}, bf16[2,1,320,128]{3,2,1,0:T(8,128)(2,1)S(1)}, u32[]{:S(2)}, u32[]{:S(2)}) collective-permute-start(bf16[2,1,320,128]{3,2,1,0:T(8,128)(2,1)S(1)} %get-tuple-element.26), channel_id=1, source_target_pairs={{0,4},{4,0},{1,5},{5,1},{2,6},{6,2},{3,7},{7,3},{8,12},{12,8},{9,1... | collective-permute-start | bytes 491528 | tf_op jit(solution)/shard_map/ppermute | solution.py:277
  1.3 20.0 %collective-permute-start.1 = (bf16[1,5,320,128]{3,2,1,0:T(8,128)(2,1)S(1)}, bf16[1,5,320,128]{3,2,1,0:T(8,128)(2,1)S(1)}, u32[]{:S(2)}, u32[]{:S(2)}) collective-permute-start(bf16[1,5,320,128]{3,2,1,0:T(8,128)(2,1)S(1)} %get-tuple-element.32), channel_id=1, source_target_pairs={{0,8},{8,16},{16,24},{24,0},{1,9},{9,17},{17,25},{25,1},{2,10},{10... | collective-permute-start | bytes 1228808 | tf_op jit(solution)/shard_map/ppermute | solution.py:276
  2.9 1.6 %copy-start.1 = (bf16[3,3,320,320]{3,2,1,0:T(8,128)(2,1)S(1)}, bf16[3,3,320,320]{3,2,1,0:T(8,128)(2,1)}, u32[]{:S(2)}) copy-start(bf16[3,3,320,320]{3,2,1,0:T(8,128)(2,1)} %ws_ref.1) | copy-start | bytes 5529604
  4.5 1.1 %copy-start.2 = (bf16[3,320,320]{2,1,0:T(8,128)(2,1)S(1)}, bf16[3,320,320]{2,1,0:T(8,128)(2,1)}, u32[]{:S(2)}) copy-start(bf16[3,320,320]{2,1,0:T(8,128)(2,1)} %wt_ref.1) | copy-start | bytes 1843204
  6.6 16.3 %collective-permute-start.3 = (bf16[1,4,320,128]{3,2,1,0:T(8,128)(2,1)S(1)}, bf16[1,4,320,128]{3,2,1,0:T(8,128)(2,1)S(1)}, u32[]{:S(2)}, u32[]{:S(2)}) collective-permute-start(bf16[1,4,320,128]{3,2,1,0:T(8,128)(2,1)S(1)} %get-tuple-element.35), channel_id=1, source_target_pairs={{0,8},{8,16},{16,24},{24,0},{1,9},{9,17},{17,25},{25,1},{2,10},{10... | collective-permute-start | bytes 983048 | tf_op jit(solution)/shard_map/ppermute | solution.py:291
  7.3 21.3 %collective-permute-start.4 = (bf16[1,4,320,128]{3,2,1,0:T(8,128)(2,1)S(1)}, bf16[1,4,320,128]{3,2,1,0:T(8,128)(2,1)S(1)}, u32[]{:S(2)}, u32[]{:S(2)}) collective-permute-start(bf16[1,4,320,128]{3,2,1,0:T(8,128)(2,1)S(1)} %get-tuple-element.37), channel_id=1, source_target_pairs={{0,8},{8,16},{16,24},{24,0},{1,9},{9,17},{17,25},{25,1},{2,10},{10... | collective-permute-start | bytes 983048 | tf_op jit(solution)/shard_map/ppermute | solution.py:291
  19.7 12.3 %collective-permute-start.5 = (bf16[1,2,320,128]{3,2,1,0:T(8,128)(2,1)S(1)}, bf16[1,2,320,128]{3,2,1,0:T(8,128)(2,1)S(1)}, u32[]{:S(2)}, u32[]{:S(2)}) collective-permute-start(bf16[1,2,320,128]{3,2,1,0:T(8,128)(2,1)S(1)} %get-tuple-element.40), channel_id=1, source_target_pairs={{0,8},{8,16},{16,24},{24,0},{1,9},{9,17},{17,25},{25,1},{2,10},{10... | collective-permute-start | bytes 491528 | tf_op jit(solution)/shard_map/ppermute | solution.py:302
  21.3 1.6 %collective-permute-start.2 = (bf16[1,320,128]{2,1,0:T(8,128)(2,1)S(1)}, bf16[1,320,128]{2,1,0:T(8,128)(2,1)S(1)}, u32[]{:S(2)}, u32[]{:S(2)}) collective-permute-start(bf16[1,320,128]{2,1,0:T(8,128)(2,1)S(1)} %shard_map.58), channel_id=1, source_target_pairs={{0,4},{4,0},{1,5},{5,1},{2,6},{6,2},{3,7},{7,3},{8,12},{12,8},{9,1... | collective-permute-start | bytes 245768 | tf_op jit(solution)/shard_map/ppermute | solution.py:313
  21.4 12.0 %collective-permute-start.6 = (bf16[1,1,320,128]{3,2,1,0:T(8,128)(2,1)S(1)}, bf16[1,1,320,128]{3,2,1,0:T(8,128)(2,1)S(1)}, u32[]{:S(2)}, u32[]{:S(2)}) collective-permute-start(bf16[1,1,320,128]{3,2,1,0:T(8,128)(2,1)S(1)} %get-tuple-element.44), channel_id=1, source_target_pairs={{0,8},{8,16},{16,24},{24,0},{1,9},{9,17},{17,25},{25,1},{2,10},{10... | collective-permute-start | bytes 245768 | tf_op jit(solution)/shard_map/ppermute | solution.py:302

commit v7 on v6

--- a/solution.py
+++ b/solution.py
@@ -12,7 +12,8 @@
 VMEM = pl.BlockSpec(memory_space=pltpu.VMEM)
 ANY = pl.BlockSpec(memory_space=pl.ANY)
 HEAD_LIMIT = 53 * 2**20
-OPEN, CLOSING, LAST = range(3)
+LOAD_LIMIT = 50 * 2**20
+OPEN, CLOSING, LATE, LAST = range(4)
 PARAMS = pltpu.CompilerParams(vmem_limit_bytes=20 * 2**20)
 
 
@@ -27,6 +28,19 @@
 def ring(axis):
     count = lax.axis_size(axis)
     return [(i, (i + 1) % count) for i in range(count)]
+
+
+def next_odd(piece, axis):
+    count = lax.axis_size(axis)
+    if count % 2:
+        return piece
+    return lax.ppermute(piece, axis, [(i, (i + 2 * (i % 2)) % count) for i in range(count)])
+
+
+def within_pairs(piece, axis, keep):
+    count = lax.axis_size(axis)
+    route = ring(axis) if count % 2 else [(i, i ^ 1) for i in range(count)]
+    return lax.ppermute(piece, axis, [(a, b) for a, b in route if b or keep])
 
 
 def cost(flops, moved):
@@ -64,9 +78,13 @@
         copy.wait()
 
 
-def edge_kernel(piece_ref, out_ref):
+def edge_kernel(piece_ref, tail_ref, out_ref, *tail_out_refs):
     size = piece_ref.shape[1]
     out_ref[0] = piece_ref[0, jnp.where(flipped(), size - 1, 0)]
+    place, size = 0, tail_ref.shape[1]
+    for ref in tail_out_refs:
+        ref[...] = span_of(tail_ref, (0, 1, place, ref.shape[1]))[...]
+        place += ref.shape[1]
 
 
 def prepare_kernel(x_ref, ws_ref, bs_ref, wt_ref, bt_ref, conv_ref, mix_ref, cb_ref, mb_ref, *piece_refs, spans):
@@ -170,40 +188,39 @@
 
         lax.fori_loop(0, count // group, body, 0)
 
-    if stage == LAST:
+    if stage == OPEN:
+
+        @pl.when(first)
+        def _():
+            own_rows(made_ref, count)
 
         @pl.when(jnp.logical_not(first))
         def _():
-            before = to_output(ready_ref, low - ready, ready, 0)
+            convolve()
+
+        return
+
+    before = to_output(ready_ref, low - ready, ready, 0)
+    if stage == CLOSING:
+
+        @pl.when(first)
+        def _():
+            rest = refs[3]
+            own_rows(rest, rows - low)
+            after = to_output(rest, low, rows - low, 1)
             before.start()
-            convolve()
-            after = to_output(made_ref, low, count, 1)
             after.start()
             before.wait()
             after.wait()
 
-        return
-
-    before = to_output(ready_ref, low - ready, ready, 0) if ready else None
-    if ready:
+    @pl.when(jnp.logical_not(first))
+    def _():
         before.start()
-
-    @pl.when(first)
-    def _():
-        if stage == CLOSING:
-            rest = refs[3]
-            own_rows(rest, rows - low)
-            after = to_output(rest, low, rows - low, 1)
+        convolve()
+        if stage == LAST:
+            after = to_output(made_ref, low, count, 1)
             after.start()
             after.wait()
-        else:
-            own_rows(made_ref, count)
-
-    @pl.when(jnp.logical_not(first))
-    def _():
-        convolve()
-
-    if ready:
         before.wait()
 
 
@@ -273,13 +290,24 @@
         scratch_shapes=[pltpu.SemaphoreType.DMA((2,))],
         compiler_params=pltpu.CompilerParams(vmem_limit_bytes=HEAD_LIMIT),
     )(x)
+    whole = [(0, frames, 0, rows), (frames - 1, 1, places[-2], sizes[-2] + sizes[-1])]
+    x, tail = pl.pallas_call(
+        functools.partial(slice_kernel, spans=whole),
+        out_shape=row_shapes(x, whole),
+        in_specs=[ANY],
+        out_specs=[VMEM] * 2,
+        scratch_shapes=[pltpu.SemaphoreType.DMA((2,))],
+        compiler_params=pltpu.CompilerParams(vmem_limit_bytes=LOAD_LIMIT),
+        cost_estimate=cost(0, 0),
+    )(x)
     arrived = [lax.ppermute(head, "frames", ring("frames"))]
+    tail = next_odd(tail, "frames")
     beside = lax.ppermute(boundary, "rows", ring("rows"))
 
     square = jax.ShapeDtypeStruct((3 * channels, 3 * channels), BF16)
     flat = jax.ShapeDtypeStruct((channels, 3 * channels), BF16)
     bias = jax.ShapeDtypeStruct((channels, width), F32)
-    late = spans[1 + early :]
+    late = spans[1 + early : -2]
     conv, mix, cb, mb, *pieces = pl.pallas_call(
         functools.partial(prepare_kernel, spans=spans[1 : 1 + early]),
         out_shape=[square, flat, bias, bias] + row_shapes(x, spans[1 : 1 + early]),
@@ -290,7 +318,7 @@
     )(x, w_spatial, b_spatial.reshape(1, channels), w_temporal, b_temporal.reshape(1, channels))
     arrived += [lax.ppermute(piece, "frames", ring("frames")) for piece in pieces]
 
-    own, *pieces = pl.pallas_call(
+    (own,) = pl.pallas_call(
         functools.partial(own_kernel, group=4, spans=late),
         out_shape=[jax.ShapeDtypeStruct((rows, channels, width), F32)] + row_shapes(x, late),
         in_specs=[VMEM] * 6,
@@ -299,23 +327,22 @@
         compiler_params=PARAMS,
         cost_estimate=cost(2 * rows * width * channels * channels * 20, 8 * rows * channels * width),
     )(x, beside, conv, mix, cb, mb)
-    arrived += [lax.ppermute(piece, "frames", ring("frames")) for piece in pieces]
-
     own, arrived[0] = lax.optimization_barrier((own, arrived[0]))
-    edge = pl.pallas_call(
+    edge, *pieces = pl.pallas_call(
         edge_kernel,
-        out_shape=jax.ShapeDtypeStruct((1, channels, width), BF16),
-        in_specs=[VMEM],
-        out_specs=VMEM,
+        out_shape=[jax.ShapeDtypeStruct((1, channels, width), BF16)] + row_shapes(x, spans[-2:]),
+        in_specs=[VMEM] * 2,
+        out_specs=[VMEM] * 3,
         compiler_params=PARAMS,
         cost_estimate=cost(0, 0),
-    )(arrived[0])
+    )(arrived[0], tail)
+    arrived += [within_pairs(piece, "frames", piece is pieces[0]) for piece in pieces]
     kept = lax.ppermute(edge, "rows", ring("rows"))
 
     weights = (conv, mix, cb)
     out, made, low = None, None, 0
-    for begin, end in steps:
-        stage = {len(arrived): LAST, steps[-1][0]: CLOSING}.get(end, OPEN)
+    for k, (begin, end) in enumerate(steps):
+        stage = LAST if end == len(arrived) else min(k, LATE)
         out, made, kept = incoming_rows(out, made, own, weights, kept, arrived[begin:end], low, stage)
         low = places[end - 1] + sizes[end - 1] - 1
     return jnp.transpose(out[None], (0, 1, 3, 2))

time: 35.4 us -> 34.5 us (0.975)
  waiting for transfers between devices: 4.19 us -> 1.1 us
  starting transfers between devices: 6.81 us -> 9.63 us
  local copies, waits for them, and re-layouts: 2.75 us -> 0.02 us
  Pallas kernels: 21.4 us -> 23.3 us
    ppermute x0 -> x3, starting transfers between devices: none -> 4.66 us  [the longest x2 3.99 us: within_pairs(): return lax.ppermute(piece, axis, [(a, b) for a, b in route if b or keep])]
    ppermute x4 -> x2, waiting for transfers between devices: 4.18 us -> 0.12 us  [per_device(): lax.ppermute(piece, 'frames', ring('frames'))]
    unnamed x10 -> x8, local copies, waits for them, and re-layouts: 2.75 us -> 0.02 us
    pallas_call x1 -> x2, Pallas kernels: 0.01 us -> 1.79 us  [the longest x1 1.76 us: per_device(): pl.pallas_call(functools.partial(slice_kernel, spans=whole), out_shape=ro...]
    ppermute x4 -> x2, starting transfers between devices: 5.12 us -> 3.35 us  [per_device(): lax.ppermute(piece, 'frames', ring('frames'))]
    ppermute x0 -> x3, waiting for transfers between devices: none -> 0.97 us  [the longest x2 0.97 us: within_pairs(): return lax.ppermute(piece, axis, [(a, b) for a, b in route if b or keep])]
  transfers between devices with their start and end apart: 7 -> 8, of which waited for: 3 -> 3; matrix products, arithmetic and copies ran while one was open for 0% -> 0% of each run, Pallas kernels for 52% -> 59%
where the time goes in v7:
time: 34.5 us; the launch traced here: 34.3 us
  Pallas kernels  23.3 us (68%)
  starting transfers between devices  9.63 us (28%)
  waiting for transfers between devices  1.1 us (3%)
    pallas_call x1, Pallas kernels, per_device(): pl.pallas_call(functools.partial(own_kernel, group=4, spans=late), out_sh...  11.2 us
    pallas_call x4, Pallas kernels, incoming_rows(): pl.pallas_call(functools.partial(incoming_kernel, pieces=len(pieces), low...  8.08 us
    ppermute x2, starting transfers between devices, within_pairs(): return lax.ppermute(piece, axis, [(a, b) for a, b in route if b or keep])  3.99 us
    ppermute x2, starting transfers between devices, per_device(): lax.ppermute(piece, 'frames', ring('frames'))  3.35 us
    pallas_call x1, Pallas kernels, per_device(): pl.pallas_call(functools.partial(slice_kernel, spans=whole), out_shape=ro...  1.76 us
    ppermute x1, starting transfers between devices, per_device(): arrived = [lax.ppermute(head, 'frames', ring('frames'))]  1.54 us
    pallas_call x1, Pallas kernels, per_device(): pl.pallas_call(functools.partial(slice_kernel, spans=head_spans), out_sha...  1.22 us
    pallas_call x1, Pallas kernels, per_device(): pl.pallas_call(functools.partial(prepare_kernel, spans=spans[1:1 + early]...  1.03 us
  transfers between devices with their start and end apart: 8, of which 3 were waited for; matrix products, arithmetic and copies ran while one was open for 0% of the time, Pallas kernels for 59%

profile of v7, /device:TPU:20, one launch (start us, length us, event | category | flops | bytes accessed | tf_op | source)
XLA Modules:
  0.0 34.3 jit_solution(12503465186931144132)
XLA Ops:
  0.0 0.0 copy-start.2
  0.0 0.0 copy-start.3
  0.0 0.0 copy-start
  0.0 0.0 copy-start.1
  0.0 1.2 %shard_map.56 = (bf16[1,5,320,128]{3,2,1,0:T(8,128)(2,1)S(1)}, bf16[2,1,320,128]{3,2,1,0:T(8,128)(2,1)S(1)}) custom-call(bf16[2,16,320,128]{3,2,1,0:T(8,128)(2,1)} %bitcast.4), custom_call_target="tpu_custom_call" | custom-call | tf_op jit(solution)/shard_map/pallas_call | solution.py:285
  1.2 0.1 collective-permute-start
  1.3 1.5 %collective-permute-start.1 = (bf16[1,5,320,128]{3,2,1,0:T(8,128)(2,1)S(1)}, bf16[1,5,320,128]{3,2,1,0:T(8,128)(2,1)S(1)}, u32[]{:S(2)}, u32[]{:S(2)}) collective-permute-start(bf16[1,5,320,128]{3,2,1,0:T(8,128)(2,1)S(1)} %get-tuple-element.34), channel_id=1, source_target_pairs={{0,8},{8,16},{16,24},{24,0},{1,9},{9,17},{17,25},{25,1},{2,10},{10... | collective-permute-start | bytes 1228808 | tf_op jit(solution)/shard_map/ppermute | solution.py:303
  2.9 1.8 %shard_map.55 = (bf16[2,16,320,128]{3,2,1,0:T(8,128)(2,1)S(1)}, bf16[1,3,320,128]{3,2,1,0:T(8,128)(2,1)S(1)}) custom-call(bf16[2,16,320,128]{3,2,1,0:T(8,128)(2,1)} %bitcast.5), custom_call_target="tpu_custom_call" | custom-call | tf_op jit(solution)/shard_map/pallas_call | solution.py:294
  4.6 0.7 %collective-permute-start.2 = (bf16[1,3,320,128]{3,2,1,0:T(8,128)(2,1)S(1)}, bf16[1,3,320,128]{3,2,1,0:T(8,128)(2,1)S(1)}, u32[]{:S(2)}, u32[]{:S(2)}) collective-permute-start(bf16[1,3,320,128]{3,2,1,0:T(8,128)(2,1)S(1)} %get-tuple-element.37), channel_id=1, source_target_pairs={{0,0},{8,24},{16,16},{24,8},{1,1},{9,25},{17,17},{25,9},{2,2},{10,... | collective-permute-start | bytes 737288 | tf_op jit(solution)/shard_map/ppermute | solution.py:37
  5.3 0.0 copy-done.2
  5.3 0.0 copy-done.3
  5.4 0.0 copy-done
  5.4 0.0 copy-done.1
  5.4 1.0 %shard_map.57 = (bf16[960,960]{1,0:T(8,128)(2,1)S(1)}, bf16[320,960]{1,0:T(8,128)(2,1)S(1)}, f32[320,128]{1,0:T(8,128)S(1)}, f32[320,128]{1,0:T(8,128)S(1)}, bf1...) custom-call(bf16[2,16,320,128]{3,2,1,0:T(8,128)(2,1)S(1)} %get-tuple-element.28.x_ref, ...), custom_call_target="tpu_custom_call" | custom-call | bytes 4915200 | tf_op jit(solution)/shard_map/pallas_call | solution.py:311
  6.4 3.3 %collective-permute-start.4 = (bf16[1,4,320,128]{3,2,1,0:T(8,128)(2,1)S(1)}, bf16[1,4,320,128]{3,2,1,0:T(8,128)(2,1)S(1)}, u32[]{:S(2)}, u32[]{:S(2)}) collective-permute-start(bf16[1,4,320,128]{3,2,1,0:T(8,128)(2,1)S(1)} %get-tuple-element.39), channel_id=1, source_target_pairs={{0,8},{8,16},{16,24},{24,0},{1,9},{9,17},{17,25},{25,1},{2,10},{10... | collective-permute-start | bytes 983048 | tf_op jit(solution)/shard_map/ppermute | solution.py:319
  9.7 0.1 collective-permute-start.5
  9.8 0.0 collective-permute-done.beside_ref
  9.8 11.2 %shard_map.58.own_ref = f32[16,320,128]{2,1,0:T(8,128)S(1)} custom-call(bf16[2,16,320,128]{3,2,1,0:T(8,128)(2,1)S(1)} %get-tuple-element.28.x_ref, bf16[2,1,320,128]{3,2,1,0:T(8,128)(2,1)S(1)} %collective-permute-done.beside_ref, bf16[960,960]{1,0:T(8,128)(2,1)S(1)} %get-tuple-element.30.conv_ref, bf16[320,960]{1,0:T(8,128)(2,1)S(1)} %get-tuple-element.31.mix_ref, ...), custom_call_target="tpu_custom_call" | custom-call | flops 8388608000 | bytes 5242880 | tf_op jit(solution)/shard_map/pallas_call | solution.py:321
  21.0 0.0 collective-permute-done.1.piece_ref.refs_1_
  21.0 0.0 collective-permute-done.2.tail_ref
  21.1 2.0 %collective-permute-start.6 = (bf16[1,2,320,128]{3,2,1,0:T(8,128)(2,1)S(1)}, bf16[1,2,320,128]{3,2,1,0:T(8,128)(2,1)S(1)}, u32[]{:S(2)}, u32[]{:S(2)}) collective-permute-start(bf16[1,2,320,128]{3,2,1,0:T(8,128)(2,1)S(1)} %get-tuple-element.44), channel_id=1, source_target_pairs={{0,8},{8,0},{16,24},{24,16},{1,9},{9,1},{17,25},{25,17},{2,10},{10... | collective-permute-start | bytes 491528 | tf_op jit(solution)/shard_map/ppermute | solution.py:43
  23.0 0.0 collective-permute-start.3
  23.0 2.0 %collective-permute-start.7 = (bf16[1,1,320,128]{3,2,1,0:T(8,128)(2,1)S(1)}, bf16[1,1,320,128]{3,2,1,0:T(8,128)(2,1)S(1)}, u32[]{:S(2)}, u32[]{:S(2)}) collective-permute-start(bf16[1,1,320,128]{3,2,1,0:T(8,128)(2,1)S(1)} %get-tuple-element.48), channel_id=1, source_target_pairs={{0,8},{16,24},{24,16},{1,9},{17,25},{25,17},{2,10},{18,26},{26,18}... | collective-permute-start | bytes 245768 | tf_op jit(solution)/shard_map/ppermute | solution.py:43
  25.1 0.0 collective-permute-done.4.refs_2_
  25.1 0.0 collective-permute-done.3.refs_0_
  25.1 3.4 %shard_map.60 = (bf16[8,320,128]{2,1,0:T(8,128)(2,1)S(1)}, bf16[2,320,128]{2,1,0:T(8,128)(2,1)S(1)}) custom-call(f32[16,320,128]{2,1,0:T(8,128)S(1)} %shard_map.58.own_ref, bf16[960,960]{1,0:T(8,128)(2,1)S(1)} %get-tuple-element.30.conv_ref, bf16[320,960]{1,0:T(8,128)(2,1)S(1)} %get-tuple-element.31.mix_ref, f32[320,128]{1,0:T(8,128)S(1)} %get-tuple-element.32.cb_ref, ...), custom_call_target="tpu_custom_call" | custom-call | tf_op jit(solution)/shard_map/pallas_call | solution.py:260
  28.5 0.1 collective-permute-done.5.refs_1_
  28.6 1.7 %shard_map.61 = (bf16[16,320,128]{2,1,0:T(8,128)(2,1)}, bf16[4,320,128]{2,1,0:T(8,128)(2,1)S(1)}, bf16[2,320,128]{2,1,0:T(8,128)(2,1)S(1)}) custom-call(f32[16,320,128]{2,1,0:T(8,128)S(1)} %shard_map.58.own_ref, bf16[960,960]{1,0:T(8,128)(2,1)S(1)} %get-tuple-element.30.conv_ref, bf16[320,960]{1,0:T(8,128)(2,1)S(1)} %get-tuple-element.31.mix_ref, ...), custom_call_target="tpu_custom_call" | custom-call | tf_op jit(solution)/shard_map/pallas_call | solution.py:260
  30.3 0.8 %collective-permute-done.6.refs_1_ = bf16[1,2,320,128]{3,2,1,0:T(8,128)(2,1)S(1)} collective-permute-done((bf16[1,2,320,128]{3,2,1,0:T(8,128)(2,1)S(1)}, bf16[1,2,320,128]{3,2,1,0:T(8,128)(2,1)S(1)}, u32[]{:S(2)}, u32[]{:S(2)}) %collective-permute-start.6) | collective-permute-done | bytes 163872 | tf_op jit(solution)/shard_map/ppermute | solution.py:43
  31.1 1.2 %shard_map.62 = (bf16[16,320,128]{2,1,0:T(8,128)(2,1)}, bf16[2,320,128]{2,1,0:T(8,128)(2,1)S(1)}, bf16[2,320,128]{2,1,0:T(8,128)(2,1)S(1)}) custom-call(f32[16,320,128]{2,1,0:T(8,128)S(1)} %shard_map.58.own_ref, bf16[960,960]{1,0:T(8,128)(2,1)S(1)} %get-tuple-element.30.conv_ref, ...), custom_call_target="tpu_custom_call", output_to_operand_aliasing={{0}: (7, {})} | custom-call | tf_op jit(solution)/shard_map/pallas_call | solution.py:260
  32.3 0.1 collective-permute-done.7.refs_1_
  32.4 1.8 %shard_map.63 = bf16[16,320,128]{2,1,0:T(8,128)(2,1)} custom-call(f32[16,320,128]{2,1,0:T(8,128)S(1)} %shard_map.58.own_ref, bf16[960,960]{1,0:T(8,128)(2,1)S(1)} %get-tuple-element.30.conv_ref, bf16[320,960]{1,0:T(8,128)(2,1)S(1)} %get-tuple-element.31.mix_ref, f32[320,128]{1,0:T(8,128)S(1)} %get-tuple-element.32.cb_ref, ...), custom_call_target="tpu_custom_call", output_to_operand_aliasing={{}: (7, {})} | custom-call | tf_op jit(solution)/shard_map/pallas_call | solution.py:260
  (3 shorter events, 0.0 us)
Async XLA Ops:
  0.0 5.3 %copy-start.2 = (f32[320]{0:T(512)S(1)}, f32[320]{0:T(512)}, u32[]{:S(2)}) copy-start(f32[320]{0:T(512)} %param.7) | copy-start | bytes 3844
  0.0 5.3 %copy-start.3 = (f32[320]{0:T(512)S(1)}, f32[320]{0:T(512)}, u32[]{:S(2)}) copy-start(f32[320]{0:T(512)} %param.9) | copy-start | bytes 3844
  0.0 5.4 %copy-start = (bf16[3,3,320,320]{3,2,1,0:T(8,128)(2,1)S(1)}, bf16[3,3,320,320]{3,2,1,0:T(8,128)(2,1)}, u32[]{:S(2)}) copy-start(bf16[3,3,320,320]{3,2,1,0:T(8,128)(2,1)} %ws_ref.1) | copy-start | bytes 5529604
  0.0 5.4 %copy-start.1 = (bf16[3,320,320]{2,1,0:T(8,128)(2,1)S(1)}, bf16[3,320,320]{2,1,0:T(8,128)(2,1)}, u32[]{:S(2)}) copy-start(bf16[3,320,320]{2,1,0:T(8,128)(2,1)} %wt_ref.1) | copy-start | bytes 1843204
  1.2 8.5 %collective-permute-start = (bf16[2,1,320,128]{3,2,1,0:T(8,128)(2,1)S(1)}, bf16[2,1,320,128]{3,2,1,0:T(8,128)(2,1)S(1)}, u32[]{:S(2)}, u32[]{:S(2)}) collective-permute-start(bf16[2,1,320,128]{3,2,1,0:T(8,128)(2,1)S(1)} %get-tuple-element.29), channel_id=1, source_target_pairs={{0,4},{4,0},{1,5},{5,1},{2,6},{6,2},{3,7},{7,3},{8,12},{12,8},{9,1... | collective-permute-start | bytes 491528 | tf_op jit(solution)/shard_map/ppermute | solution.py:305
  1.3 19.7 %collective-permute-start.1 = (bf16[1,5,320,128]{3,2,1,0:T(8,128)(2,1)S(1)}, bf16[1,5,320,128]{3,2,1,0:T(8,128)(2,1)S(1)}, u32[]{:S(2)}, u32[]{:S(2)}) collective-permute-start(bf16[1,5,320,128]{3,2,1,0:T(8,128)(2,1)S(1)} %get-tuple-element.34), channel_id=1, source_target_pairs={{0,8},{8,16},{16,24},{24,0},{1,9},{9,17},{17,25},{25,1},{2,10},{10... | collective-permute-start | bytes 1228808 | tf_op jit(solution)/shard_map/ppermute | solution.py:303
  4.6 16.4 %collective-permute-start.2 = (bf16[1,3,320,128]{3,2,1,0:T(8,128)(2,1)S(1)}, bf16[1,3,320,128]{3,2,1,0:T(8,128)(2,1)S(1)}, u32[]{:S(2)}, u32[]{:S(2)}) collective-permute-start(bf16[1,3,320,128]{3,2,1,0:T(8,128)(2,1)S(1)} %get-tuple-element.37), channel_id=1, source_target_pairs={{0,0},{8,24},{16,16},{24,8},{1,1},{9,25},{17,17},{25,9},{2,2},{10,... | collective-permute-start | bytes 737288 | tf_op jit(solution)/shard_map/ppermute | solution.py:37
  6.4 18.6 %collective-permute-start.4 = (bf16[1,4,320,128]{3,2,1,0:T(8,128)(2,1)S(1)}, bf16[1,4,320,128]{3,2,1,0:T(8,128)(2,1)S(1)}, u32[]{:S(2)}, u32[]{:S(2)}) collective-permute-start(bf16[1,4,320,128]{3,2,1,0:T(8,128)(2,1)S(1)} %get-tuple-element.39), channel_id=1, source_target_pairs={{0,8},{8,16},{16,24},{24,0},{1,9},{9,17},{17,25},{25,1},{2,10},{10... | collective-permute-start | bytes 983048 | tf_op jit(solution)/shard_map/ppermute | solution.py:319
  9.7 18.9 %collective-permute-start.5 = (bf16[1,4,320,128]{3,2,1,0:T(8,128)(2,1)S(1)}, bf16[1,4,320,128]{3,2,1,0:T(8,128)(2,1)S(1)}, u32[]{:S(2)}, u32[]{:S(2)}) collective-permute-start(bf16[1,4,320,128]{3,2,1,0:T(8,128)(2,1)S(1)} %get-tuple-element.41), channel_id=1, source_target_pairs={{0,8},{8,16},{16,24},{24,0},{1,9},{9,17},{17,25},{25,1},{2,10},{10... | collective-permute-start | bytes 983048 | tf_op jit(solution)/shard_map/ppermute | solution.py:319
  21.1 10.1 %collective-permute-start.6 = (bf16[1,2,320,128]{3,2,1,0:T(8,128)(2,1)S(1)}, bf16[1,2,320,128]{3,2,1,0:T(8,128)(2,1)S(1)}, u32[]{:S(2)}, u32[]{:S(2)}) collective-permute-start(bf16[1,2,320,128]{3,2,1,0:T(8,128)(2,1)S(1)} %get-tuple-element.44), channel_id=1, source_target_pairs={{0,8},{8,0},{16,24},{24,16},{1,9},{9,1},{17,25},{25,17},{2,10},{10... | collective-permute-start | bytes 491528 | tf_op jit(solution)/shard_map/ppermute | solution.py:43
  23.0 2.0 %collective-permute-start.3 = (bf16[1,320,128]{2,1,0:T(8,128)(2,1)S(1)}, bf16[1,320,128]{2,1,0:T(8,128)(2,1)S(1)}, u32[]{:S(2)}, u32[]{:S(2)}) collective-permute-start(bf16[1,320,128]{2,1,0:T(8,128)(2,1)S(1)} %get-tuple-element.38), channel_id=1, source_target_pairs={{0,4},{4,0},{1,5},{5,1},{2,6},{6,2},{3,7},{7,3},{8,12},{12,8},{9,1... | collective-permute-start | bytes 245768 | tf_op jit(solution)/shard_map/ppermute | solution.py:340
  23.0 9.4 %collective-permute-start.7 = (bf16[1,1,320,128]{3,2,1,0:T(8,128)(2,1)S(1)}, bf16[1,1,320,128]{3,2,1,0:T(8,128)(2,1)S(1)}, u32[]{:S(2)}, u32[]{:S(2)}) collective-permute-start(bf16[1,1,320,128]{3,2,1,0:T(8,128)(2,1)S(1)} %get-tuple-element.48), channel_id=1, source_target_pairs={{0,8},{16,24},{24,16},{1,9},{17,25},{25,17},{2,10},{18,26},{26,18}... | collective-permute-start | bytes 245768 | tf_op jit(solution)/shard_map/ppermute | solution.py:43

commit v8 on v7

--- a/solution.py
+++ b/solution.py
@@ -60,6 +60,10 @@
 def keep_rows(x_ref, outs, spans):
     for out, span in zip(outs, spans):
         out[...] = span_of(x_ref, span)[...]
+
+
+def keep_kernel(x_ref, *outs, spans):
+    keep_rows(x_ref, outs, spans)
 
 
 def row_shapes(x, spans):
@@ -290,14 +294,23 @@
         scratch_shapes=[pltpu.SemaphoreType.DMA((2,))],
         compiler_params=pltpu.CompilerParams(vmem_limit_bytes=HEAD_LIMIT),
     )(x)
-    whole = [(0, frames, 0, rows), (frames - 1, 1, places[-2], sizes[-2] + sizes[-1])]
-    x, tail = pl.pallas_call(
+    whole = [(0, frames, 0, rows)]
+    (x,) = pl.pallas_call(
         functools.partial(slice_kernel, spans=whole),
         out_shape=row_shapes(x, whole),
         in_specs=[ANY],
-        out_specs=[VMEM] * 2,
-        scratch_shapes=[pltpu.SemaphoreType.DMA((2,))],
+        out_specs=[VMEM],
+        scratch_shapes=[pltpu.SemaphoreType.DMA((1,))],
         compiler_params=pltpu.CompilerParams(vmem_limit_bytes=LOAD_LIMIT),
+        cost_estimate=cost(0, 0),
+    )(x)
+    ending = [(frames - 1, 1, places[-2], sizes[-2] + sizes[-1])]
+    (tail,) = pl.pallas_call(
+        functools.partial(keep_kernel, spans=ending),
+        out_shape=row_shapes(x, ending),
+        in_specs=[VMEM],
+        out_specs=[VMEM],
+        compiler_params=PARAMS,
         cost_estimate=cost(0, 0),
     )(x)
     arrived = [lax.ppermute(head, "frames", ring("frames"))]

time: 34.5 us -> 34.3 us (level)
  local copies, waits for them, and re-layouts: 0.02 us -> 0.75 us
  starting transfers between devices: 9.63 us -> 9.06 us
    unnamed x8, local copies, waits for them, and re-layouts: 0.02 us -> 0.75 us
    ppermute x2, starting transfers between devices: 3.35 us -> 2.65 us  [per_device(): lax.ppermute(piece, 'frames', ring('frames'))]
  transfers between devices with their start and end apart: 8 -> 8, of which waited for: 3 -> 2; matrix products, arithmetic and copies ran while one was open for 0% -> 0% of each run, Pallas kernels for 59% -> 60%
where the time goes in v8:
time: 34.3 us; the launch traced here: 34.1 us
  Pallas kernels  23.3 us (68%)
  starting transfers between devices  9.06 us (26%)
  waiting for transfers between devices  0.81 us (2%)
  local copies, waits for them, and re-layouts  0.75 us (2%)
    pallas_call x1, Pallas kernels, per_device(): pl.pallas_call(functools.partial(own_kernel, group=4, spans=late), out_sh...  11.2 us
    pallas_call x4, Pallas kernels, incoming_rows(): pl.pallas_call(functools.partial(incoming_kernel, pieces=len(pieces), low...  8.11 us
    ppermute x2, starting transfers between devices, within_pairs(): return lax.ppermute(piece, axis, [(a, b) for a, b in route if b or keep])  3.99 us
    ppermute x2, starting transfers between devices, per_device(): lax.ppermute(piece, 'frames', ring('frames'))  2.65 us
    pallas_call x1, Pallas kernels, per_device(): pl.pallas_call(functools.partial(slice_kernel, spans=whole), out_shape=ro...  1.82 us
    ppermute x1, starting transfers between devices, per_device(): arrived = [lax.ppermute(head, 'frames', ring('frames'))]  1.54 us
    pallas_call x1, Pallas kernels, per_device(): pl.pallas_call(functools.partial(slice_kernel, spans=head_spans), out_sha...  1.06 us
    pallas_call x1, Pallas kernels, per_device(): pl.pallas_call(functools.partial(prepare_kernel, spans=spans[1:1 + early]...  1.01 us
  transfers between devices with their start and end apart: 8, of which 2 were waited for; matrix products, arithmetic and copies ran while one was open for 0% of the time, Pallas kernels for 60%

profile of v8, /device:TPU:20, one launch (start us, length us, event | category | flops | bytes accessed | tf_op | source)
XLA Modules:
  0.0 34.1 jit_solution(2891168182155193294)
XLA Ops:
  0.0 1.1 %shard_map.56 = (bf16[1,5,320,128]{3,2,1,0:T(8,128)(2,1)S(1)}, bf16[2,1,320,128]{3,2,1,0:T(8,128)(2,1)S(1)}) custom-call(bf16[2,16,320,128]{3,2,1,0:T(8,128)(2,1)} %bitcast.4), custom_call_target="tpu_custom_call" | custom-call | tf_op jit(solution)/shard_map/pallas_call | solution.py:289
  1.1 0.1 collective-permute-start
  1.1 1.5 %collective-permute-start.1 = (bf16[1,5,320,128]{3,2,1,0:T(8,128)(2,1)S(1)}, bf16[1,5,320,128]{3,2,1,0:T(8,128)(2,1)S(1)}, u32[]{:S(2)}, u32[]{:S(2)}) collective-permute-start(bf16[1,5,320,128]{3,2,1,0:T(8,128)(2,1)S(1)} %get-tuple-element.31), channel_id=1, source_target_pairs={{0,8},{8,16},{16,24},{24,0},{1,9},{9,17},{17,25},{25,1},{2,10},{10... | collective-permute-start | bytes 1228808 | tf_op jit(solution)/shard_map/ppermute | solution.py:316
  2.7 0.0 copy-start.1
  2.7 1.8 %shard_map.55.x_ref = bf16[2,16,320,128]{3,2,1,0:T(8,128)(2,1)S(1)} custom-call(bf16[2,16,320,128]{3,2,1,0:T(8,128)(2,1)} %bitcast.5), custom_call_target="tpu_custom_call" | custom-call | tf_op jit(solution)/shard_map/pallas_call | solution.py:298
  4.5 0.0 copy-start.2
  4.5 0.0 copy-start.3
  4.5 0.0 copy-start
  4.6 0.8 %collective-permute-start.2 = (bf16[1,3,320,128]{3,2,1,0:T(8,128)(2,1)S(1)}, bf16[1,3,320,128]{3,2,1,0:T(8,128)(2,1)S(1)}, u32[]{:S(2)}, u32[]{:S(2)}) collective-permute-start(bf16[1,3,320,128]{3,2,1,0:T(8,128)(2,1)S(1)} %shard_map.59), channel_id=1, source_target_pairs={{0,0},{8,24},{16,16},{24,8},{1,1},{9,25},{17,17},{25,9},{2,2},{10,... | collective-permute-start | bytes 737288 | tf_op jit(solution)/shard_map/ppermute | solution.py:37
  5.4 0.0 copy-done.2
  5.4 0.0 copy-done.3
  5.4 0.0 copy-done.1
  5.5 0.7 %copy-done = bf16[3,3,320,320]{3,2,1,0:T(8,128)(2,1)S(1)} copy-done((bf16[3,3,320,320]{3,2,1,0:T(8,128)(2,1)S(1)}, bf16[3,3,320,320]{3,2,1,0:T(8,128)(2,1)}, u32[]{:S(2)}) %copy-start) | copy-done | bytes 1843224
  6.2 1.0 %shard_map.57 = (bf16[960,960]{1,0:T(8,128)(2,1)S(1)}, bf16[320,960]{1,0:T(8,128)(2,1)S(1)}, f32[320,128]{1,0:T(8,128)S(1)}, f32[320,128]{1,0:T(8,128)S(1)}, bf1...) custom-call(bf16[2,16,320,128]{3,2,1,0:T(8,128)(2,1)S(1)} %shard_map.55.x_ref, ...), custom_call_target="tpu_custom_call" | custom-call | bytes 4915200 | tf_op jit(solution)/shard_map/pallas_call | solution.py:324
  7.2 2.6 %collective-permute-start.4 = (bf16[1,4,320,128]{3,2,1,0:T(8,128)(2,1)S(1)}, bf16[1,4,320,128]{3,2,1,0:T(8,128)(2,1)S(1)}, u32[]{:S(2)}, u32[]{:S(2)}) collective-permute-start(bf16[1,4,320,128]{3,2,1,0:T(8,128)(2,1)S(1)} %get-tuple-element.35), channel_id=1, source_target_pairs={{0,8},{8,16},{16,24},{24,0},{1,9},{9,17},{17,25},{25,1},{2,10},{10... | collective-permute-start | bytes 983048 | tf_op jit(solution)/shard_map/ppermute | solution.py:332
  9.8 0.1 collective-permute-start.5
  9.9 0.0 collective-permute-done.beside_ref
  9.9 11.2 %shard_map.58.own_ref = f32[16,320,128]{2,1,0:T(8,128)S(1)} custom-call(bf16[2,16,320,128]{3,2,1,0:T(8,128)(2,1)S(1)} %shard_map.55.x_ref, bf16[2,1,320,128]{3,2,1,0:T(8,128)(2,1)S(1)} %collective-permute-done.beside_ref, bf16[960,960]{1,0:T(8,128)(2,1)S(1)} %get-tuple-element.27.conv_ref, bf16[320,960]{1,0:T(8,128)(2,1)S(1)} %get-tuple-element.28.mix_ref, ...), custom_call_target="tpu_custom_call" | custom-call | flops 8388608000 | bytes 5242880 | tf_op jit(solution)/shard_map/pallas_call | solution.py:334
  21.1 0.0 collective-permute-done.1.piece_ref.refs_1_
  21.1 0.0 collective-permute-done.2.tail_ref
  21.1 2.0 %collective-permute-start.6 = (bf16[1,2,320,128]{3,2,1,0:T(8,128)(2,1)S(1)}, bf16[1,2,320,128]{3,2,1,0:T(8,128)(2,1)S(1)}, u32[]{:S(2)}, u32[]{:S(2)}) collective-permute-start(bf16[1,2,320,128]{3,2,1,0:T(8,128)(2,1)S(1)} %get-tuple-element.40), channel_id=1, source_target_pairs={{0,8},{8,0},{16,24},{24,16},{1,9},{9,1},{17,25},{25,17},{2,10},{10... | collective-permute-start | bytes 491528 | tf_op jit(solution)/shard_map/ppermute | solution.py:43
  23.1 0.0 collective-permute-start.3
  23.1 2.0 %collective-permute-start.7 = (bf16[1,1,320,128]{3,2,1,0:T(8,128)(2,1)S(1)}, bf16[1,1,320,128]{3,2,1,0:T(8,128)(2,1)S(1)}, u32[]{:S(2)}, u32[]{:S(2)}) collective-permute-start(bf16[1,1,320,128]{3,2,1,0:T(8,128)(2,1)S(1)} %get-tuple-element.44), channel_id=1, source_target_pairs={{0,8},{16,24},{24,16},{1,9},{17,25},{25,17},{2,10},{18,26},{26,18}... | collective-permute-start | bytes 245768 | tf_op jit(solution)/shard_map/ppermute | solution.py:43
  25.1 0.0 collective-permute-done.4.refs_2_
  25.2 0.0 collective-permute-done.3.refs_0_
  25.2 3.4 %shard_map.61 = (bf16[8,320,128]{2,1,0:T(8,128)(2,1)S(1)}, bf16[2,320,128]{2,1,0:T(8,128)(2,1)S(1)}) custom-call(f32[16,320,128]{2,1,0:T(8,128)S(1)} %shard_map.58.own_ref, bf16[960,960]{1,0:T(8,128)(2,1)S(1)} %get-tuple-element.27.conv_ref, bf16[320,960]{1,0:T(8,128)(2,1)S(1)} %get-tuple-element.28.mix_ref, f32[320,128]{1,0:T(8,128)S(1)} %get-tuple-element.29.cb_ref, ...), custom_call_target="tpu_custom_call" | custom-call | tf_op jit(solution)/shard_map/pallas_call | solution.py:264
  28.6 0.0 collective-permute-done.5.refs_1_
  28.6 1.7 %shard_map.62 = (bf16[16,320,128]{2,1,0:T(8,128)(2,1)}, bf16[4,320,128]{2,1,0:T(8,128)(2,1)S(1)}, bf16[2,320,128]{2,1,0:T(8,128)(2,1)S(1)}) custom-call(f32[16,320,128]{2,1,0:T(8,128)S(1)} %shard_map.58.own_ref, bf16[960,960]{1,0:T(8,128)(2,1)S(1)} %get-tuple-element.27.conv_ref, bf16[320,960]{1,0:T(8,128)(2,1)S(1)} %get-tuple-element.28.mix_ref, ...), custom_call_target="tpu_custom_call" | custom-call | tf_op jit(solution)/shard_map/pallas_call | solution.py:264
  30.3 0.7 %collective-permute-done.6.refs_1_ = bf16[1,2,320,128]{3,2,1,0:T(8,128)(2,1)S(1)} collective-permute-done((bf16[1,2,320,128]{3,2,1,0:T(8,128)(2,1)S(1)}, bf16[1,2,320,128]{3,2,1,0:T(8,128)(2,1)S(1)}, u32[]{:S(2)}, u32[]{:S(2)}) %collective-permute-start.6) | collective-permute-done | bytes 163872 | tf_op jit(solution)/shard_map/ppermute | solution.py:43
  31.0 1.2 %shard_map.63 = (bf16[16,320,128]{2,1,0:T(8,128)(2,1)}, bf16[2,320,128]{2,1,0:T(8,128)(2,1)S(1)}, bf16[2,320,128]{2,1,0:T(8,128)(2,1)S(1)}) custom-call(f32[16,320,128]{2,1,0:T(8,128)S(1)} %shard_map.58.own_ref, bf16[960,960]{1,0:T(8,128)(2,1)S(1)} %get-tuple-element.27.conv_ref, ...), custom_call_target="tpu_custom_call", output_to_operand_aliasing={{0}: (7, {})} | custom-call | tf_op jit(solution)/shard_map/pallas_call | solution.py:264
  32.1 0.1 collective-permute-done.7.refs_1_
  32.3 1.8 %shard_map.64 = bf16[16,320,128]{2,1,0:T(8,128)(2,1)} custom-call(f32[16,320,128]{2,1,0:T(8,128)S(1)} %shard_map.58.own_ref, bf16[960,960]{1,0:T(8,128)(2,1)S(1)} %get-tuple-element.27.conv_ref, bf16[320,960]{1,0:T(8,128)(2,1)S(1)} %get-tuple-element.28.mix_ref, f32[320,128]{1,0:T(8,128)S(1)} %get-tuple-element.29.cb_ref, ...), custom_call_target="tpu_custom_call", output_to_operand_aliasing={{}: (7, {})} | custom-call | tf_op jit(solution)/shard_map/pallas_call | solution.py:264
  (4 shorter events, 0.1 us)
Async XLA Ops:
  1.1 8.8 %collective-permute-start = (bf16[2,1,320,128]{3,2,1,0:T(8,128)(2,1)S(1)}, bf16[2,1,320,128]{3,2,1,0:T(8,128)(2,1)S(1)}, u32[]{:S(2)}, u32[]{:S(2)}) collective-permute-start(bf16[2,1,320,128]{3,2,1,0:T(8,128)(2,1)S(1)} %get-tuple-element.26), channel_id=1, source_target_pairs={{0,4},{4,0},{1,5},{5,1},{2,6},{6,2},{3,7},{7,3},{8,12},{12,8},{9,1... | collective-permute-start | bytes 491528 | tf_op jit(solution)/shard_map/ppermute | solution.py:318
  1.1 19.9 %collective-permute-start.1 = (bf16[1,5,320,128]{3,2,1,0:T(8,128)(2,1)S(1)}, bf16[1,5,320,128]{3,2,1,0:T(8,128)(2,1)S(1)}, u32[]{:S(2)}, u32[]{:S(2)}) collective-permute-start(bf16[1,5,320,128]{3,2,1,0:T(8,128)(2,1)S(1)} %get-tuple-element.31), channel_id=1, source_target_pairs={{0,8},{8,16},{16,24},{24,0},{1,9},{9,17},{17,25},{25,1},{2,10},{10... | collective-permute-start | bytes 1228808 | tf_op jit(solution)/shard_map/ppermute | solution.py:316
  2.7 2.8 %copy-start.1 = (bf16[3,320,320]{2,1,0:T(8,128)(2,1)S(1)}, bf16[3,320,320]{2,1,0:T(8,128)(2,1)}, u32[]{:S(2)}) copy-start(bf16[3,320,320]{2,1,0:T(8,128)(2,1)} %wt_ref.1) | copy-start | bytes 1843204
  4.5 0.9 %copy-start.2 = (f32[320]{0:T(512)S(1)}, f32[320]{0:T(512)}, u32[]{:S(2)}) copy-start(f32[320]{0:T(512)} %param.7) | copy-start | bytes 3844
  4.5 0.9 %copy-start.3 = (f32[320]{0:T(512)S(1)}, f32[320]{0:T(512)}, u32[]{:S(2)}) copy-start(f32[320]{0:T(512)} %param.9) | copy-start | bytes 3844
  4.5 1.6 %copy-start = (bf16[3,3,320,320]{3,2,1,0:T(8,128)(2,1)S(1)}, bf16[3,3,320,320]{3,2,1,0:T(8,128)(2,1)}, u32[]{:S(2)}) copy-start(bf16[3,3,320,320]{3,2,1,0:T(8,128)(2,1)} %ws_ref.1) | copy-start | bytes 5529604
  4.6 16.5 %collective-permute-start.2 = (bf16[1,3,320,128]{3,2,1,0:T(8,128)(2,1)S(1)}, bf16[1,3,320,128]{3,2,1,0:T(8,128)(2,1)S(1)}, u32[]{:S(2)}, u32[]{:S(2)}) collective-permute-start(bf16[1,3,320,128]{3,2,1,0:T(8,128)(2,1)S(1)} %shard_map.59), channel_id=1, source_target_pairs={{0,0},{8,24},{16,16},{24,8},{1,1},{9,25},{17,17},{25,9},{2,2},{10,... | collective-permute-start | bytes 737288 | tf_op jit(solution)/shard_map/ppermute | solution.py:37
  7.2 17.9 %collective-permute-start.4 = (bf16[1,4,320,128]{3,2,1,0:T(8,128)(2,1)S(1)}, bf16[1,4,320,128]{3,2,1,0:T(8,128)(2,1)S(1)}, u32[]{:S(2)}, u32[]{:S(2)}) collective-permute-start(bf16[1,4,320,128]{3,2,1,0:T(8,128)(2,1)S(1)} %get-tuple-element.35), channel_id=1, source_target_pairs={{0,8},{8,16},{16,24},{24,0},{1,9},{9,17},{17,25},{25,1},{2,10},{10... | collective-permute-start | bytes 983048 | tf_op jit(solution)/shard_map/ppermute | solution.py:332
  9.8 18.8 %collective-permute-start.5 = (bf16[1,4,320,128]{3,2,1,0:T(8,128)(2,1)S(1)}, bf16[1,4,320,128]{3,2,1,0:T(8,128)(2,1)S(1)}, u32[]{:S(2)}, u32[]{:S(2)}) collective-permute-start(bf16[1,4,320,128]{3,2,1,0:T(8,128)(2,1)S(1)} %get-tuple-element.37), channel_id=1, source_target_pairs={{0,8},{8,16},{16,24},{24,0},{1,9},{9,17},{17,25},{25,1},{2,10},{10... | collective-permute-start | bytes 983048 | tf_op jit(solution)/shard_map/ppermute | solution.py:332
  21.1 9.8 %collective-permute-start.6 = (bf16[1,2,320,128]{3,2,1,0:T(8,128)(2,1)S(1)}, bf16[1,2,320,128]{3,2,1,0:T(8,128)(2,1)S(1)}, u32[]{:S(2)}, u32[]{:S(2)}) collective-permute-start(bf16[1,2,320,128]{3,2,1,0:T(8,128)(2,1)S(1)} %get-tuple-element.40), channel_id=1, source_target_pairs={{0,8},{8,0},{16,24},{24,16},{1,9},{9,1},{17,25},{25,17},{2,10},{10... | collective-permute-start | bytes 491528 | tf_op jit(solution)/shard_map/ppermute | solution.py:43
  23.1 2.0 %collective-permute-start.3 = (bf16[1,320,128]{2,1,0:T(8,128)(2,1)S(1)}, bf16[1,320,128]{2,1,0:T(8,128)(2,1)S(1)}, u32[]{:S(2)}, u32[]{:S(2)}) collective-permute-start(bf16[1,320,128]{2,1,0:T(8,128)(2,1)S(1)} %get-tuple-element.34), channel_id=1, source_target_pairs={{0,4},{4,0},{1,5},{5,1},{2,6},{6,2},{3,7},{7,3},{8,12},{12,8},{9,1... | collective-permute-start | bytes 245768 | tf_op jit(solution)/shard_map/ppermute | solution.py:353
  23.1 9.2 %collective-permute-start.7 = (bf16[1,1,320,128]{3,2,1,0:T(8,128)(2,1)S(1)}, bf16[1,1,320,128]{3,2,1,0:T(8,128)(2,1)S(1)}, u32[]{:S(2)}, u32[]{:S(2)}) collective-permute-start(bf16[1,1,320,128]{3,2,1,0:T(8,128)(2,1)S(1)} %get-tuple-element.44), channel_id=1, source_target_pairs={{0,8},{16,24},{24,16},{1,9},{17,25},{25,17},{2,10},{18,26},{26,18}... | collective-permute-start | bytes 245768 | tf_op jit(solution)/shard_map/ppermute | solution.py:43

commit v9 on v8

--- a/solution.py
+++ b/solution.py
@@ -32,9 +32,7 @@
 
 def next_odd(piece, axis):
     count = lax.axis_size(axis)
-    if count % 2:
-        return piece
-    return lax.ppermute(piece, axis, [(i, (i + 2 * (i % 2)) % count) for i in range(count)])
+    return lax.ppermute(piece, axis, [(i, (i + 2) % count) for i in range(1, count, 2)])
 
 
 def within_pairs(piece, axis, keep):
@@ -82,13 +80,20 @@
         copy.wait()
 
 
-def edge_kernel(piece_ref, tail_ref, out_ref, *tail_out_refs):
+def edge_kernel(piece_ref, tail_ref, relayed_ref, out_ref, *tail_out_refs):
     size = piece_ref.shape[1]
     out_ref[0] = piece_ref[0, jnp.where(flipped(), size - 1, 0)]
-    place, size = 0, tail_ref.shape[1]
-    for ref in tail_out_refs:
-        ref[...] = span_of(tail_ref, (0, 1, place, ref.shape[1]))[...]
-        place += ref.shape[1]
+    count = lax.axis_size("frames")
+    relay = jnp.logical_and(count % 2 == 0, lax.rem(lax.axis_index("frames"), 2) == 1)
+
+    def cut(source_ref):
+        place = 0
+        for ref in tail_out_refs:
+            ref[...] = span_of(source_ref, (0, 1, place, ref.shape[1]))[...]
+            place += ref.shape[1]
+
+    pl.when(relay)(lambda: cut(relayed_ref))
+    pl.when(jnp.logical_not(relay))(lambda: cut(tail_ref))
 
 
 def prepare_kernel(x_ref, ws_ref, bs_ref, wt_ref, bt_ref, conv_ref, mix_ref, cb_ref, mb_ref, *piece_refs, spans):
@@ -116,10 +121,8 @@
     return jnp.concatenate(rows, axis=1)
 
 
-def own_kernel(x_ref, beside_ref, conv_ref, mix_ref, cb_ref, mb_ref, out_ref, *refs, group, spans):
-    piece_refs, xs = refs[:-1], refs[-1]
+def own_kernel(x_ref, beside_ref, conv_ref, mix_ref, cb_ref, mb_ref, out_ref, xs, *, group):
     frames, rows, channels, width = x_ref.shape
-    keep_rows(x_ref, piece_refs, spans)
     for f in range(frames):
         xs[f, 0] = beside_ref[f, 0]
         xs[f, rows + 1] = jnp.zeros((channels, width), BF16)
@@ -281,7 +284,7 @@
 def per_device(video, w_spatial, b_spatial, w_temporal, b_temporal):
     frames, rows, width, channels = video.shape
     x = jnp.transpose(video, (0, 1, 3, 2))
-    sizes, early, steps = [5, 4, 4, 2, 1], 2, [(0, 2), (2, 3), (3, 4), (4, 5)]
+    sizes, steps = [rows - 11, 4, 4, 2, 1], [(0, 2), (2, 3), (3, 4), (4, 5)]
     places = [sum(sizes[:k]) for k in range(len(sizes))]
     spans = [(frames - 1, 1, place, size) for place, size in zip(places, sizes)]
 
@@ -314,28 +317,27 @@
         cost_estimate=cost(0, 0),
     )(x)
     arrived = [lax.ppermute(head, "frames", ring("frames"))]
-    tail = next_odd(tail, "frames")
+    relayed = next_odd(tail, "frames")
     beside = lax.ppermute(boundary, "rows", ring("rows"))
 
     square = jax.ShapeDtypeStruct((3 * channels, 3 * channels), BF16)
     flat = jax.ShapeDtypeStruct((channels, 3 * channels), BF16)
     bias = jax.ShapeDtypeStruct((channels, width), F32)
-    late = spans[1 + early : -2]
     conv, mix, cb, mb, *pieces = pl.pallas_call(
-        functools.partial(prepare_kernel, spans=spans[1 : 1 + early]),
-        out_shape=[square, flat, bias, bias] + row_shapes(x, spans[1 : 1 + early]),
+        functools.partial(prepare_kernel, spans=spans[1:3]),
+        out_shape=[square, flat, bias, bias] + row_shapes(x, spans[1:3]),
         in_specs=[VMEM] * 5,
-        out_specs=[VMEM] * (4 + early),
+        out_specs=[VMEM] * 6,
         compiler_params=PARAMS,
         cost_estimate=cost(0, 2 * 12 * channels * channels * 2),
     )(x, w_spatial, b_spatial.reshape(1, channels), w_temporal, b_temporal.reshape(1, channels))
     arrived += [lax.ppermute(piece, "frames", ring("frames")) for piece in pieces]
 
-    (own,) = pl.pallas_call(
-        functools.partial(own_kernel, group=4, spans=late),
-        out_shape=[jax.ShapeDtypeStruct((rows, channels, width), F32)] + row_shapes(x, late),
+    own = pl.pallas_call(
+        functools.partial(own_kernel, group=next(g for g in (4, 3, 2, 1) if rows % g == 0)),
+        out_shape=jax.ShapeDtypeStruct((rows, channels, width), F32),
         in_specs=[VMEM] * 6,
-        out_specs=[VMEM] * (1 + len(late)),
+        out_specs=VMEM,
         scratch_shapes=[pltpu.VMEM((frames, rows + 2, channels, width), BF16)],
         compiler_params=PARAMS,
         cost_estimate=cost(2 * rows * width * channels * channels * 20, 8 * rows * channels * width),
@@ -344,12 +346,12 @@
     edge, *pieces = pl.pallas_call(
         edge_kernel,
         out_shape=[jax.ShapeDtypeStruct((1, channels, width), BF16)] + row_shapes(x, spans[-2:]),
-        in_specs=[VMEM] * 2,
+        in_specs=[VMEM] * 3,
         out_specs=[VMEM] * 3,
         compiler_params=PARAMS,
         cost_estimate=cost(0, 0),
-    )(arrived[0], tail)
-    arrived += [within_pairs(piece, "frames", piece is pieces[0]) for piece in pieces]
+    )(arrived[0], tail, relayed)
+    arrived += [within_pairs(pieces[0], "frames", True), within_pairs(pieces[1], "frames", False)]
     kept = lax.ppermute(edge, "rows", ring("rows"))
 
     weights = (conv, mix, cb)

time: 34.3 us -> 34.3 us (level)
  no operation moved by 1% of the time
where the time goes in v9:
time: 34.3 us; the launch traced here: 34.1 us
  Pallas kernels  23.3 us (68%)
  starting transfers between devices  9.06 us (26%)
  waiting for transfers between devices  0.81 us (2%)
  local copies, waits for them, and re-layouts  0.75 us (2%)
    pallas_call x1, Pallas kernels, per_device(): pl.pallas_call(functools.partial(own_kernel, group=next((g for g in (4, 3...  11.2 us
    pallas_call x4, Pallas kernels, incoming_rows(): pl.pallas_call(functools.partial(incoming_kernel, pieces=len(pieces), low...  8.1 us
    ppermute x2, starting transfers between devices, within_pairs(): return lax.ppermute(piece, axis, [(a, b) for a, b in route if b or keep])  3.99 us
    ppermute x2, starting transfers between devices, per_device(): lax.ppermute(piece, 'frames', ring('frames'))  2.65 us
    pallas_call x1, Pallas kernels, per_device(): pl.pallas_call(functools.partial(slice_kernel, spans=whole), out_shape=ro...  1.82 us
    ppermute x1, starting transfers between devices, per_device(): arrived = [lax.ppermute(head, 'frames', ring('frames'))]  1.54 us
    pallas_call x1, Pallas kernels, per_device(): pl.pallas_call(functools.partial(slice_kernel, spans=head_spans), out_sha...  1.06 us
    pallas_call x1, Pallas kernels, per_device(): pl.pallas_call(functools.partial(prepare_kernel, spans=spans[1:3]), out_s...  1.01 us
  transfers between devices with their start and end apart: 8, of which 2 were waited for; matrix products, arithmetic and copies ran while one was open for 0% of the time, Pallas kernels for 60%

profile of v9, /device:TPU:20, one launch (start us, length us, event | category | flops | bytes accessed | tf_op | source)
XLA Modules:
  0.0 34.1 jit_solution(10274490797226772203)
XLA Ops:
  0.0 1.1 %shard_map.56 = (bf16[1,5,320,128]{3,2,1,0:T(8,128)(2,1)S(1)}, bf16[2,1,320,128]{3,2,1,0:T(8,128)(2,1)S(1)}) custom-call(bf16[2,16,320,128]{3,2,1,0:T(8,128)(2,1)} %bitcast.4), custom_call_target="tpu_custom_call" | custom-call | tf_op jit(solution)/shard_map/pallas_call | solution.py:292
  1.1 0.1 collective-permute-start
  1.1 1.5 %collective-permute-start.1 = (bf16[1,5,320,128]{3,2,1,0:T(8,128)(2,1)S(1)}, bf16[1,5,320,128]{3,2,1,0:T(8,128)(2,1)S(1)}, u32[]{:S(2)}, u32[]{:S(2)}) collective-permute-start(bf16[1,5,320,128]{3,2,1,0:T(8,128)(2,1)S(1)} %get-tuple-element.31), channel_id=1, source_target_pairs={{0,8},{8,16},{16,24},{24,0},{1,9},{9,17},{17,25},{25,1},{2,10},{10... | collective-permute-start | bytes 1228808 | tf_op jit(solution)/shard_map/ppermute | solution.py:319
  2.7 0.0 copy-start.1
  2.7 1.8 %shard_map.55.x_ref = bf16[2,16,320,128]{3,2,1,0:T(8,128)(2,1)S(1)} custom-call(bf16[2,16,320,128]{3,2,1,0:T(8,128)(2,1)} %bitcast.5), custom_call_target="tpu_custom_call" | custom-call | tf_op jit(solution)/shard_map/pallas_call | solution.py:301
  4.5 0.0 copy-start.2
  4.5 0.0 copy-start.3
  4.5 0.0 copy-start
  4.6 0.8 %collective-permute-start.2 = (bf16[1,3,320,128]{3,2,1,0:T(8,128)(2,1)S(1)}, bf16[1,3,320,128]{3,2,1,0:T(8,128)(2,1)S(1)}, u32[]{:S(2)}, u32[]{:S(2)}) collective-permute-start(bf16[1,3,320,128]{3,2,1,0:T(8,128)(2,1)S(1)} %shard_map.59.tail_ref), channel_id=1, source_target_pairs={{8,24},{24,8},{9,25},{25,9},{10,26},{26,10},{11,27},{27,11},{12,28... | collective-permute-start | bytes 737288 | tf_op jit(solution)/shard_map/ppermute | solution.py:35
  5.4 0.0 copy-done.2
  5.4 0.0 copy-done.3
  5.4 0.0 copy-done.1
  5.5 0.7 %copy-done = bf16[3,3,320,320]{3,2,1,0:T(8,128)(2,1)S(1)} copy-done((bf16[3,3,320,320]{3,2,1,0:T(8,128)(2,1)S(1)}, bf16[3,3,320,320]{3,2,1,0:T(8,128)(2,1)}, u32[]{:S(2)}) %copy-start) | copy-done | bytes 1843224
  6.2 1.0 %shard_map.57 = (bf16[960,960]{1,0:T(8,128)(2,1)S(1)}, bf16[320,960]{1,0:T(8,128)(2,1)S(1)}, f32[320,128]{1,0:T(8,128)S(1)}, f32[320,128]{1,0:T(8,128)S(1)}, bf1...) custom-call(bf16[2,16,320,128]{3,2,1,0:T(8,128)(2,1)S(1)} %shard_map.55.x_ref, ...), custom_call_target="tpu_custom_call" | custom-call | bytes 4915200 | tf_op jit(solution)/shard_map/pallas_call | solution.py:326
  7.2 2.6 %collective-permute-start.4 = (bf16[1,4,320,128]{3,2,1,0:T(8,128)(2,1)S(1)}, bf16[1,4,320,128]{3,2,1,0:T(8,128)(2,1)S(1)}, u32[]{:S(2)}, u32[]{:S(2)}) collective-permute-start(bf16[1,4,320,128]{3,2,1,0:T(8,128)(2,1)S(1)} %get-tuple-element.35), channel_id=1, source_target_pairs={{0,8},{8,16},{16,24},{24,0},{1,9},{9,17},{17,25},{25,1},{2,10},{10... | collective-permute-start | bytes 983048 | tf_op jit(solution)/shard_map/ppermute | solution.py:334
  9.8 0.1 collective-permute-start.5
  9.9 0.0 collective-permute-done.beside_ref
  9.9 11.2 %shard_map.58.own_ref = f32[16,320,128]{2,1,0:T(8,128)S(1)} custom-call(bf16[2,16,320,128]{3,2,1,0:T(8,128)(2,1)S(1)} %shard_map.55.x_ref, bf16[2,1,320,128]{3,2,1,0:T(8,128)(2,1)S(1)} %collective-permute-done.beside_ref, bf16[960,960]{1,0:T(8,128)(2,1)S(1)} %get-tuple-element.27.conv_ref, bf16[320,960]{1,0:T(8,128)(2,1)S(1)} %get-tuple-element.28.mix_ref, ...), custom_call_target="tpu_custom_call" | custom-call | flops 8388608000 | bytes 5242880 | tf_op jit(solution)/shard_map/pallas_call | solution.py:336
  21.1 0.0 collective-permute-done.1.piece_ref.refs_1_
  21.1 0.0 collective-permute-done.2.relayed_ref
  21.1 2.0 %collective-permute-start.6 = (bf16[1,2,320,128]{3,2,1,0:T(8,128)(2,1)S(1)}, bf16[1,2,320,128]{3,2,1,0:T(8,128)(2,1)S(1)}, u32[]{:S(2)}, u32[]{:S(2)}) collective-permute-start(bf16[1,2,320,128]{3,2,1,0:T(8,128)(2,1)S(1)} %get-tuple-element.40), channel_id=1, source_target_pairs={{0,8},{8,0},{16,24},{24,16},{1,9},{9,1},{17,25},{25,17},{2,10},{10... | collective-permute-start | bytes 491528 | tf_op jit(solution)/shard_map/ppermute | solution.py:41
  23.1 0.0 collective-permute-start.3
  23.1 2.0 %collective-permute-start.7 = (bf16[1,1,320,128]{3,2,1,0:T(8,128)(2,1)S(1)}, bf16[1,1,320,128]{3,2,1,0:T(8,128)(2,1)S(1)}, u32[]{:S(2)}, u32[]{:S(2)}) collective-permute-start(bf16[1,1,320,128]{3,2,1,0:T(8,128)(2,1)S(1)} %get-tuple-element.44), channel_id=1, source_target_pairs={{0,8},{16,24},{24,16},{1,9},{17,25},{25,17},{2,10},{18,26},{26,18}... | collective-permute-start | bytes 245768 | tf_op jit(solution)/shard_map/ppermute | solution.py:41
  25.1 0.0 collective-permute-done.4.refs_2_
  25.2 0.0 collective-permute-done.3.refs_0_
  25.2 3.4 %shard_map.61 = (bf16[8,320,128]{2,1,0:T(8,128)(2,1)S(1)}, bf16[2,320,128]{2,1,0:T(8,128)(2,1)S(1)}) custom-call(f32[16,320,128]{2,1,0:T(8,128)S(1)} %shard_map.58.own_ref, bf16[960,960]{1,0:T(8,128)(2,1)S(1)} %get-tuple-element.27.conv_ref, bf16[320,960]{1,0:T(8,128)(2,1)S(1)} %get-tuple-element.28.mix_ref, f32[320,128]{1,0:T(8,128)S(1)} %get-tuple-element.29.cb_ref, ...), custom_call_target="tpu_custom_call" | custom-call | tf_op jit(solution)/shard_map/pallas_call | solution.py:267
  28.6 0.0 collective-permute-done.5.refs_1_
  28.6 1.7 %shard_map.62 = (bf16[16,320,128]{2,1,0:T(8,128)(2,1)}, bf16[4,320,128]{2,1,0:T(8,128)(2,1)S(1)}, bf16[2,320,128]{2,1,0:T(8,128)(2,1)S(1)}) custom-call(f32[16,320,128]{2,1,0:T(8,128)S(1)} %shard_map.58.own_ref, bf16[960,960]{1,0:T(8,128)(2,1)S(1)} %get-tuple-element.27.conv_ref, bf16[320,960]{1,0:T(8,128)(2,1)S(1)} %get-tuple-element.28.mix_ref, ...), custom_call_target="tpu_custom_call" | custom-call | tf_op jit(solution)/shard_map/pallas_call | solution.py:267
  30.3 0.7 %collective-permute-done.6.refs_1_ = bf16[1,2,320,128]{3,2,1,0:T(8,128)(2,1)S(1)} collective-permute-done((bf16[1,2,320,128]{3,2,1,0:T(8,128)(2,1)S(1)}, bf16[1,2,320,128]{3,2,1,0:T(8,128)(2,1)S(1)}, u32[]{:S(2)}, u32[]{:S(2)}) %collective-permute-start.6) | collective-permute-done | bytes 163872 | tf_op jit(solution)/shard_map/ppermute | solution.py:41
  31.0 1.2 %shard_map.63 = (bf16[16,320,128]{2,1,0:T(8,128)(2,1)}, bf16[2,320,128]{2,1,0:T(8,128)(2,1)S(1)}, bf16[2,320,128]{2,1,0:T(8,128)(2,1)S(1)}) custom-call(f32[16,320,128]{2,1,0:T(8,128)S(1)} %shard_map.58.own_ref, bf16[960,960]{1,0:T(8,128)(2,1)S(1)} %get-tuple-element.27.conv_ref, ...), custom_call_target="tpu_custom_call", output_to_operand_aliasing={{0}: (7, {})} | custom-call | tf_op jit(solution)/shard_map/pallas_call | solution.py:267
  32.1 0.1 collective-permute-done.7.refs_1_
  32.3 1.8 %shard_map.64 = bf16[16,320,128]{2,1,0:T(8,128)(2,1)} custom-call(f32[16,320,128]{2,1,0:T(8,128)S(1)} %shard_map.58.own_ref, bf16[960,960]{1,0:T(8,128)(2,1)S(1)} %get-tuple-element.27.conv_ref, bf16[320,960]{1,0:T(8,128)(2,1)S(1)} %get-tuple-element.28.mix_ref, f32[320,128]{1,0:T(8,128)S(1)} %get-tuple-element.29.cb_ref, ...), custom_call_target="tpu_custom_call", output_to_operand_aliasing={{}: (7, {})} | custom-call | tf_op jit(solution)/shard_map/pallas_call | solution.py:267
  (4 shorter events, 0.1 us)
Async XLA Ops:
  1.1 8.8 %collective-permute-start = (bf16[2,1,320,128]{3,2,1,0:T(8,128)(2,1)S(1)}, bf16[2,1,320,128]{3,2,1,0:T(8,128)(2,1)S(1)}, u32[]{:S(2)}, u32[]{:S(2)}) collective-permute-start(bf16[2,1,320,128]{3,2,1,0:T(8,128)(2,1)S(1)} %get-tuple-element.26), channel_id=1, source_target_pairs={{0,4},{4,0},{1,5},{5,1},{2,6},{6,2},{3,7},{7,3},{8,12},{12,8},{9,1... | collective-permute-start | bytes 491528 | tf_op jit(solution)/shard_map/ppermute | solution.py:321
  1.1 19.9 %collective-permute-start.1 = (bf16[1,5,320,128]{3,2,1,0:T(8,128)(2,1)S(1)}, bf16[1,5,320,128]{3,2,1,0:T(8,128)(2,1)S(1)}, u32[]{:S(2)}, u32[]{:S(2)}) collective-permute-start(bf16[1,5,320,128]{3,2,1,0:T(8,128)(2,1)S(1)} %get-tuple-element.31), channel_id=1, source_target_pairs={{0,8},{8,16},{16,24},{24,0},{1,9},{9,17},{17,25},{25,1},{2,10},{10... | collective-permute-start | bytes 1228808 | tf_op jit(solution)/shard_map/ppermute | solution.py:319
  2.7 2.8 %copy-start.1 = (bf16[3,320,320]{2,1,0:T(8,128)(2,1)S(1)}, bf16[3,320,320]{2,1,0:T(8,128)(2,1)}, u32[]{:S(2)}) copy-start(bf16[3,320,320]{2,1,0:T(8,128)(2,1)} %wt_ref.1) | copy-start | bytes 1843204
  4.5 0.9 %copy-start.2 = (f32[320]{0:T(512)S(1)}, f32[320]{0:T(512)}, u32[]{:S(2)}) copy-start(f32[320]{0:T(512)} %param.7) | copy-start | bytes 3844
  4.5 0.9 %copy-start.3 = (f32[320]{0:T(512)S(1)}, f32[320]{0:T(512)}, u32[]{:S(2)}) copy-start(f32[320]{0:T(512)} %param.9) | copy-start | bytes 3844
  4.5 1.6 %copy-start = (bf16[3,3,320,320]{3,2,1,0:T(8,128)(2,1)S(1)}, bf16[3,3,320,320]{3,2,1,0:T(8,128)(2,1)}, u32[]{:S(2)}) copy-start(bf16[3,3,320,320]{3,2,1,0:T(8,128)(2,1)} %ws_ref.1) | copy-start | bytes 5529604
  4.6 16.5 %collective-permute-start.2 = (bf16[1,3,320,128]{3,2,1,0:T(8,128)(2,1)S(1)}, bf16[1,3,320,128]{3,2,1,0:T(8,128)(2,1)S(1)}, u32[]{:S(2)}, u32[]{:S(2)}) collective-permute-start(bf16[1,3,320,128]{3,2,1,0:T(8,128)(2,1)S(1)} %shard_map.59.tail_ref), channel_id=1, source_target_pairs={{8,24},{24,8},{9,25},{25,9},{10,26},{26,10},{11,27},{27,11},{12,28... | collective-permute-start | bytes 737288 | tf_op jit(solution)/shard_map/ppermute | solution.py:35
  7.2 17.9 %collective-permute-start.4 = (bf16[1,4,320,128]{3,2,1,0:T(8,128)(2,1)S(1)}, bf16[1,4,320,128]{3,2,1,0:T(8,128)(2,1)S(1)}, u32[]{:S(2)}, u32[]{:S(2)}) collective-permute-start(bf16[1,4,320,128]{3,2,1,0:T(8,128)(2,1)S(1)} %get-tuple-element.35), channel_id=1, source_target_pairs={{0,8},{8,16},{16,24},{24,0},{1,9},{9,17},{17,25},{25,1},{2,10},{10... | collective-permute-start | bytes 983048 | tf_op jit(solution)/shard_map/ppermute | solution.py:334
  9.8 18.8 %collective-permute-start.5 = (bf16[1,4,320,128]{3,2,1,0:T(8,128)(2,1)S(1)}, bf16[1,4,320,128]{3,2,1,0:T(8,128)(2,1)S(1)}, u32[]{:S(2)}, u32[]{:S(2)}) collective-permute-start(bf16[1,4,320,128]{3,2,1,0:T(8,128)(2,1)S(1)} %get-tuple-element.37), channel_id=1, source_target_pairs={{0,8},{8,16},{16,24},{24,0},{1,9},{9,17},{17,25},{25,1},{2,10},{10... | collective-permute-start | bytes 983048 | tf_op jit(solution)/shard_map/ppermute | solution.py:334
  21.1 9.8 %collective-permute-start.6 = (bf16[1,2,320,128]{3,2,1,0:T(8,128)(2,1)S(1)}, bf16[1,2,320,128]{3,2,1,0:T(8,128)(2,1)S(1)}, u32[]{:S(2)}, u32[]{:S(2)}) collective-permute-start(bf16[1,2,320,128]{3,2,1,0:T(8,128)(2,1)S(1)} %get-tuple-element.40), channel_id=1, source_target_pairs={{0,8},{8,0},{16,24},{24,16},{1,9},{9,1},{17,25},{25,17},{2,10},{10... | collective-permute-start | bytes 491528 | tf_op jit(solution)/shard_map/ppermute | solution.py:41
  23.1 2.0 %collective-permute-start.3 = (bf16[1,320,128]{2,1,0:T(8,128)(2,1)S(1)}, bf16[1,320,128]{2,1,0:T(8,128)(2,1)S(1)}, u32[]{:S(2)}, u32[]{:S(2)}) collective-permute-start(bf16[1,320,128]{2,1,0:T(8,128)(2,1)S(1)} %get-tuple-element.34), channel_id=1, source_target_pairs={{0,4},{4,0},{1,5},{5,1},{2,6},{6,2},{3,7},{7,3},{8,12},{12,8},{9,1... | collective-permute-start | bytes 245768 | tf_op jit(solution)/shard_map/ppermute | solution.py:355
  23.1 9.1 %collective-permute-start.7 = (bf16[1,1,320,128]{3,2,1,0:T(8,128)(2,1)S(1)}, bf16[1,1,320,128]{3,2,1,0:T(8,128)(2,1)S(1)}, u32[]{:S(2)}, u32[]{:S(2)}) collective-permute-start(bf16[1,1,320,128]{3,2,1,0:T(8,128)(2,1)S(1)} %get-tuple-element.44), channel_id=1, source_target_pairs={{0,8},{16,24},{24,16},{1,9},{17,25},{25,17},{2,10},{18,26},{26,18}... | collective-permute-start | bytes 245768 | tf_op jit(solution)/shard_map/ppermute | solution.py:41

commit v10 on v9

--- a/solution.py
+++ b/solution.py
@@ -334,7 +334,7 @@
     arrived += [lax.ppermute(piece, "frames", ring("frames")) for piece in pieces]
 
     own = pl.pallas_call(
-        functools.partial(own_kernel, group=next(g for g in (4, 3, 2, 1) if rows % g == 0)),
+        functools.partial(own_kernel, group=next(g for g in (8, 4, 3, 2, 1) if rows % g == 0)),
         out_shape=jax.ShapeDtypeStruct((rows, channels, width), F32),
         in_specs=[VMEM] * 6,
         out_specs=VMEM,

time: 34.3 us -> 34.3 us (level)
  waiting for transfers between devices: 0.81 us -> 1.62 us
  Pallas kernels: 23.3 us -> 22.5 us
    pallas_call x1, Pallas kernels: 11.2 us -> 10.4 us  [per_device(): pl.pallas_call(functools.partial(own_kernel, group=next((g for g in (8, 4...]
    ppermute x2, waiting for transfers between devices: 0.01 us -> 0.64 us  [per_device(): lax.ppermute(piece, 'frames', ring('frames'))]
  transfers between devices with their start and end apart: 8 -> 8, of which waited for: 2 -> 3; matrix products, arithmetic and copies ran while one was open for 0% -> 0% of each run, Pallas kernels for 60% -> 57%
where the time goes in v10:
time: 34.3 us; the launch traced here: 34.1 us
  Pallas kernels  22.5 us (66%)
  starting transfers between devices  9.06 us (26%)
  waiting for transfers between devices  1.62 us (5%)
  local copies, waits for them, and re-layouts  0.75 us (2%)
    pallas_call x1, Pallas kernels, per_device(): pl.pallas_call(functools.partial(own_kernel, group=next((g for g in (8, 4...  10.4 us
    pallas_call x4, Pallas kernels, incoming_rows(): pl.pallas_call(functools.partial(incoming_kernel, pieces=len(pieces), low...  8.08 us
    ppermute x2, starting transfers between devices, within_pairs(): return lax.ppermute(piece, axis, [(a, b) for a, b in route if b or keep])  3.99 us
    ppermute x2, starting transfers between devices, per_device(): lax.ppermute(piece, 'frames', ring('frames'))  2.65 us
    pallas_call x1, Pallas kernels, per_device(): pl.pallas_call(functools.partial(slice_kernel, spans=whole), out_shape=ro...  1.82 us
    ppermute x1, starting transfers between devices, per_device(): arrived = [lax.ppermute(head, 'frames', ring('frames'))]  1.54 us
    pallas_call x1, Pallas kernels, per_device(): pl.pallas_call(functools.partial(slice_kernel, spans=head_spans), out_sha...  1.06 us
    pallas_call x1, Pallas kernels, per_device(): pl.pallas_call(functools.partial(prepare_kernel, spans=spans[1:3]), out_s...  1.01 us
  transfers between devices with their start and end apart: 8, of which 3 were waited for; matrix products, arithmetic and copies ran while one was open for 0% of the time, Pallas kernels for 57%

profile of v10, /device:TPU:20, one launch (start us, length us, event | category | flops | bytes accessed | tf_op | source)
XLA Modules:
  0.0 34.1 jit_solution(2949332687352645349)
XLA Ops:
  0.0 1.1 %shard_map.56 = (bf16[1,5,320,128]{3,2,1,0:T(8,128)(2,1)S(1)}, bf16[2,1,320,128]{3,2,1,0:T(8,128)(2,1)S(1)}) custom-call(bf16[2,16,320,128]{3,2,1,0:T(8,128)(2,1)} %bitcast.4), custom_call_target="tpu_custom_call" | custom-call | tf_op jit(solution)/shard_map/pallas_call | solution.py:292
  1.1 0.1 collective-permute-start
  1.1 1.5 %collective-permute-start.1 = (bf16[1,5,320,128]{3,2,1,0:T(8,128)(2,1)S(1)}, bf16[1,5,320,128]{3,2,1,0:T(8,128)(2,1)S(1)}, u32[]{:S(2)}, u32[]{:S(2)}) collective-permute-start(bf16[1,5,320,128]{3,2,1,0:T(8,128)(2,1)S(1)} %get-tuple-element.31), channel_id=1, source_target_pairs={{0,8},{8,16},{16,24},{24,0},{1,9},{9,17},{17,25},{25,1},{2,10},{10... | collective-permute-start | bytes 1228808 | tf_op jit(solution)/shard_map/ppermute | solution.py:319
  2.7 0.0 copy-start.1
  2.7 1.8 %shard_map.55.x_ref = bf16[2,16,320,128]{3,2,1,0:T(8,128)(2,1)S(1)} custom-call(bf16[2,16,320,128]{3,2,1,0:T(8,128)(2,1)} %bitcast.5), custom_call_target="tpu_custom_call" | custom-call | tf_op jit(solution)/shard_map/pallas_call | solution.py:301
  4.5 0.0 copy-start.2
  4.5 0.0 copy-start.3
  4.5 0.0 copy-start
  4.6 0.8 %collective-permute-start.2 = (bf16[1,3,320,128]{3,2,1,0:T(8,128)(2,1)S(1)}, bf16[1,3,320,128]{3,2,1,0:T(8,128)(2,1)S(1)}, u32[]{:S(2)}, u32[]{:S(2)}) collective-permute-start(bf16[1,3,320,128]{3,2,1,0:T(8,128)(2,1)S(1)} %shard_map.59.tail_ref), channel_id=1, source_target_pairs={{8,24},{24,8},{9,25},{25,9},{10,26},{26,10},{11,27},{27,11},{12,28... | collective-permute-start | bytes 737288 | tf_op jit(solution)/shard_map/ppermute | solution.py:35
  5.4 0.0 copy-done.2
  5.4 0.0 copy-done.3
  5.4 0.0 copy-done.1
  5.5 0.7 %copy-done = bf16[3,3,320,320]{3,2,1,0:T(8,128)(2,1)S(1)} copy-done((bf16[3,3,320,320]{3,2,1,0:T(8,128)(2,1)S(1)}, bf16[3,3,320,320]{3,2,1,0:T(8,128)(2,1)}, u32[]{:S(2)}) %copy-start) | copy-done | bytes 1843224
  6.2 1.0 %shard_map.57 = (bf16[960,960]{1,0:T(8,128)(2,1)S(1)}, bf16[320,960]{1,0:T(8,128)(2,1)S(1)}, f32[320,128]{1,0:T(8,128)S(1)}, f32[320,128]{1,0:T(8,128)S(1)}, bf1...) custom-call(bf16[2,16,320,128]{3,2,1,0:T(8,128)(2,1)S(1)} %shard_map.55.x_ref, ...), custom_call_target="tpu_custom_call" | custom-call | bytes 4915200 | tf_op jit(solution)/shard_map/pallas_call | solution.py:326
  7.2 2.6 %collective-permute-start.4 = (bf16[1,4,320,128]{3,2,1,0:T(8,128)(2,1)S(1)}, bf16[1,4,320,128]{3,2,1,0:T(8,128)(2,1)S(1)}, u32[]{:S(2)}, u32[]{:S(2)}) collective-permute-start(bf16[1,4,320,128]{3,2,1,0:T(8,128)(2,1)S(1)} %get-tuple-element.35), channel_id=1, source_target_pairs={{0,8},{8,16},{16,24},{24,0},{1,9},{9,17},{17,25},{25,1},{2,10},{10... | collective-permute-start | bytes 983048 | tf_op jit(solution)/shard_map/ppermute | solution.py:334
  9.8 0.1 collective-permute-start.5
  9.9 0.0 collective-permute-done.beside_ref
  9.9 10.4 %shard_map.58.own_ref = f32[16,320,128]{2,1,0:T(8,128)S(1)} custom-call(bf16[2,16,320,128]{3,2,1,0:T(8,128)(2,1)S(1)} %shard_map.55.x_ref, bf16[2,1,320,128]{3,2,1,0:T(8,128)(2,1)S(1)} %collective-permute-done.beside_ref, bf16[960,960]{1,0:T(8,128)(2,1)S(1)} %get-tuple-element.27.conv_ref, bf16[320,960]{1,0:T(8,128)(2,1)S(1)} %get-tuple-element.28.mix_ref, ...), custom_call_target="tpu_custom_call" | custom-call | flops 8388608000 | bytes 5242880 | tf_op jit(solution)/shard_map/pallas_call | solution.py:336
  20.3 0.0 collective-permute-done.1.piece_ref.refs_1_
  20.3 0.0 collective-permute-done.2.relayed_ref
  20.4 2.0 %collective-permute-start.6 = (bf16[1,2,320,128]{3,2,1,0:T(8,128)(2,1)S(1)}, bf16[1,2,320,128]{3,2,1,0:T(8,128)(2,1)S(1)}, u32[]{:S(2)}, u32[]{:S(2)}) collective-permute-start(bf16[1,2,320,128]{3,2,1,0:T(8,128)(2,1)S(1)} %get-tuple-element.40), channel_id=1, source_target_pairs={{0,8},{8,0},{16,24},{24,16},{1,9},{9,1},{17,25},{25,17},{2,10},{10... | collective-permute-start | bytes 491528 | tf_op jit(solution)/shard_map/ppermute | solution.py:41
  22.3 0.0 collective-permute-start.3
  22.3 2.0 %collective-permute-start.7 = (bf16[1,1,320,128]{3,2,1,0:T(8,128)(2,1)S(1)}, bf16[1,1,320,128]{3,2,1,0:T(8,128)(2,1)S(1)}, u32[]{:S(2)}, u32[]{:S(2)}) collective-permute-start(bf16[1,1,320,128]{3,2,1,0:T(8,128)(2,1)S(1)} %get-tuple-element.44), channel_id=1, source_target_pairs={{0,8},{16,24},{24,16},{1,9},{17,25},{25,17},{2,10},{18,26},{26,18}... | collective-permute-start | bytes 245768 | tf_op jit(solution)/shard_map/ppermute | solution.py:41
  24.4 0.0 collective-permute-done.4.refs_2_
  24.4 0.0 collective-permute-done.3.refs_0_
  24.4 3.4 %shard_map.61 = (bf16[8,320,128]{2,1,0:T(8,128)(2,1)S(1)}, bf16[2,320,128]{2,1,0:T(8,128)(2,1)S(1)}) custom-call(f32[16,320,128]{2,1,0:T(8,128)S(1)} %shard_map.58.own_ref, bf16[960,960]{1,0:T(8,128)(2,1)S(1)} %get-tuple-element.27.conv_ref, bf16[320,960]{1,0:T(8,128)(2,1)S(1)} %get-tuple-element.28.mix_ref, f32[320,128]{1,0:T(8,128)S(1)} %get-tuple-element.29.cb_ref, ...), custom_call_target="tpu_custom_call" | custom-call | tf_op jit(solution)/shard_map/pallas_call | solution.py:267
  27.8 0.6 %collective-permute-done.5.refs_1_ = bf16[1,4,320,128]{3,2,1,0:T(8,128)(2,1)S(1)} collective-permute-done((bf16[1,4,320,128]{3,2,1,0:T(8,128)(2,1)S(1)}, bf16[1,4,320,128]{3,2,1,0:T(8,128)(2,1)S(1)}, u32[]{:S(2)}, u32[]{:S(2)}) %collective-permute-start.5) | collective-permute-done | bytes 327712 | tf_op jit(solution)/shard_map/ppermute | solution.py:334
  28.4 1.7 %shard_map.62 = (bf16[16,320,128]{2,1,0:T(8,128)(2,1)}, bf16[4,320,128]{2,1,0:T(8,128)(2,1)S(1)}, bf16[2,320,128]{2,1,0:T(8,128)(2,1)S(1)}) custom-call(f32[16,320,128]{2,1,0:T(8,128)S(1)} %shard_map.58.own_ref, bf16[960,960]{1,0:T(8,128)(2,1)S(1)} %get-tuple-element.27.conv_ref, bf16[320,960]{1,0:T(8,128)(2,1)S(1)} %get-tuple-element.28.mix_ref, ...), custom_call_target="tpu_custom_call" | custom-call | tf_op jit(solution)/shard_map/pallas_call | solution.py:267
  30.1 0.8 %collective-permute-done.6.refs_1_ = bf16[1,2,320,128]{3,2,1,0:T(8,128)(2,1)S(1)} collective-permute-done((bf16[1,2,320,128]{3,2,1,0:T(8,128)(2,1)S(1)}, bf16[1,2,320,128]{3,2,1,0:T(8,128)(2,1)S(1)}, u32[]{:S(2)}, u32[]{:S(2)}) %collective-permute-start.6) | collective-permute-done | bytes 163872 | tf_op jit(solution)/shard_map/ppermute | solution.py:41
  31.0 1.2 %shard_map.63 = (bf16[16,320,128]{2,1,0:T(8,128)(2,1)}, bf16[2,320,128]{2,1,0:T(8,128)(2,1)S(1)}, bf16[2,320,128]{2,1,0:T(8,128)(2,1)S(1)}) custom-call(f32[16,320,128]{2,1,0:T(8,128)S(1)} %shard_map.58.own_ref, bf16[960,960]{1,0:T(8,128)(2,1)S(1)} %get-tuple-element.27.conv_ref, ...), custom_call_target="tpu_custom_call", output_to_operand_aliasing={{0}: (7, {})} | custom-call | tf_op jit(solution)/shard_map/pallas_call | solution.py:267
  32.1 0.1 collective-permute-done.7.refs_1_
  32.3 1.8 %shard_map.64 = bf16[16,320,128]{2,1,0:T(8,128)(2,1)} custom-call(f32[16,320,128]{2,1,0:T(8,128)S(1)} %shard_map.58.own_ref, bf16[960,960]{1,0:T(8,128)(2,1)S(1)} %get-tuple-element.27.conv_ref, bf16[320,960]{1,0:T(8,128)(2,1)S(1)} %get-tuple-element.28.mix_ref, f32[320,128]{1,0:T(8,128)S(1)} %get-tuple-element.29.cb_ref, ...), custom_call_target="tpu_custom_call", output_to_operand_aliasing={{}: (7, {})} | custom-call | tf_op jit(solution)/shard_map/pallas_call | solution.py:267
  (4 shorter events, 0.1 us)
Async XLA Ops:
  1.1 8.8 %collective-permute-start = (bf16[2,1,320,128]{3,2,1,0:T(8,128)(2,1)S(1)}, bf16[2,1,320,128]{3,2,1,0:T(8,128)(2,1)S(1)}, u32[]{:S(2)}, u32[]{:S(2)}) collective-permute-start(bf16[2,1,320,128]{3,2,1,0:T(8,128)(2,1)S(1)} %get-tuple-element.26), channel_id=1, source_target_pairs={{0,4},{4,0},{1,5},{5,1},{2,6},{6,2},{3,7},{7,3},{8,12},{12,8},{9,1... | collective-permute-start | bytes 491528 | tf_op jit(solution)/shard_map/ppermute | solution.py:321
  1.1 19.2 %collective-permute-start.1 = (bf16[1,5,320,128]{3,2,1,0:T(8,128)(2,1)S(1)}, bf16[1,5,320,128]{3,2,1,0:T(8,128)(2,1)S(1)}, u32[]{:S(2)}, u32[]{:S(2)}) collective-permute-start(bf16[1,5,320,128]{3,2,1,0:T(8,128)(2,1)S(1)} %get-tuple-element.31), channel_id=1, source_target_pairs={{0,8},{8,16},{16,24},{24,0},{1,9},{9,17},{17,25},{25,1},{2,10},{10... | collective-permute-start | bytes 1228808 | tf_op jit(solution)/shard_map/ppermute | solution.py:319
  2.7 2.8 %copy-start.1 = (bf16[3,320,320]{2,1,0:T(8,128)(2,1)S(1)}, bf16[3,320,320]{2,1,0:T(8,128)(2,1)}, u32[]{:S(2)}) copy-start(bf16[3,320,320]{2,1,0:T(8,128)(2,1)} %wt_ref.1) | copy-start | bytes 1843204
  4.5 0.9 %copy-start.2 = (f32[320]{0:T(512)S(1)}, f32[320]{0:T(512)}, u32[]{:S(2)}) copy-start(f32[320]{0:T(512)} %param.7) | copy-start | bytes 3844
  4.5 0.9 %copy-start.3 = (f32[320]{0:T(512)S(1)}, f32[320]{0:T(512)}, u32[]{:S(2)}) copy-start(f32[320]{0:T(512)} %param.9) | copy-start | bytes 3844
  4.5 1.6 %copy-start = (bf16[3,3,320,320]{3,2,1,0:T(8,128)(2,1)S(1)}, bf16[3,3,320,320]{3,2,1,0:T(8,128)(2,1)}, u32[]{:S(2)}) copy-start(bf16[3,3,320,320]{3,2,1,0:T(8,128)(2,1)} %ws_ref.1) | copy-start | bytes 5529604
  4.6 15.7 %collective-permute-start.2 = (bf16[1,3,320,128]{3,2,1,0:T(8,128)(2,1)S(1)}, bf16[1,3,320,128]{3,2,1,0:T(8,128)(2,1)S(1)}, u32[]{:S(2)}, u32[]{:S(2)}) collective-permute-start(bf16[1,3,320,128]{3,2,1,0:T(8,128)(2,1)S(1)} %shard_map.59.tail_ref), channel_id=1, source_target_pairs={{8,24},{24,8},{9,25},{25,9},{10,26},{26,10},{11,27},{27,11},{12,28... | collective-permute-start | bytes 737288 | tf_op jit(solution)/shard_map/ppermute | solution.py:35
  7.2 17.2 %collective-permute-start.4 = (bf16[1,4,320,128]{3,2,1,0:T(8,128)(2,1)S(1)}, bf16[1,4,320,128]{3,2,1,0:T(8,128)(2,1)S(1)}, u32[]{:S(2)}, u32[]{:S(2)}) collective-permute-start(bf16[1,4,320,128]{3,2,1,0:T(8,128)(2,1)S(1)} %get-tuple-element.35), channel_id=1, source_target_pairs={{0,8},{8,16},{16,24},{24,0},{1,9},{9,17},{17,25},{25,1},{2,10},{10... | collective-permute-start | bytes 983048 | tf_op jit(solution)/shard_map/ppermute | solution.py:334
  9.8 18.6 %collective-permute-start.5 = (bf16[1,4,320,128]{3,2,1,0:T(8,128)(2,1)S(1)}, bf16[1,4,320,128]{3,2,1,0:T(8,128)(2,1)S(1)}, u32[]{:S(2)}, u32[]{:S(2)}) collective-permute-start(bf16[1,4,320,128]{3,2,1,0:T(8,128)(2,1)S(1)} %get-tuple-element.37), channel_id=1, source_target_pairs={{0,8},{8,16},{16,24},{24,0},{1,9},{9,17},{17,25},{25,1},{2,10},{10... | collective-permute-start | bytes 983048 | tf_op jit(solution)/shard_map/ppermute | solution.py:334
  20.4 10.6 %collective-permute-start.6 = (bf16[1,2,320,128]{3,2,1,0:T(8,128)(2,1)S(1)}, bf16[1,2,320,128]{3,2,1,0:T(8,128)(2,1)S(1)}, u32[]{:S(2)}, u32[]{:S(2)}) collective-permute-start(bf16[1,2,320,128]{3,2,1,0:T(8,128)(2,1)S(1)} %get-tuple-element.40), channel_id=1, source_target_pairs={{0,8},{8,0},{16,24},{24,16},{1,9},{9,1},{17,25},{25,17},{2,10},{10... | collective-permute-start | bytes 491528 | tf_op jit(solution)/shard_map/ppermute | solution.py:41
  22.3 2.0 %collective-permute-start.3 = (bf16[1,320,128]{2,1,0:T(8,128)(2,1)S(1)}, bf16[1,320,128]{2,1,0:T(8,128)(2,1)S(1)}, u32[]{:S(2)}, u32[]{:S(2)}) collective-permute-start(bf16[1,320,128]{2,1,0:T(8,128)(2,1)S(1)} %get-tuple-element.34), channel_id=1, source_target_pairs={{0,4},{4,0},{1,5},{5,1},{2,6},{6,2},{3,7},{7,3},{8,12},{12,8},{9,1... | collective-permute-start | bytes 245768 | tf_op jit(solution)/shard_map/ppermute | solution.py:355
  22.3 9.9 %collective-permute-start.7 = (bf16[1,1,320,128]{3,2,1,0:T(8,128)(2,1)S(1)}, bf16[1,1,320,128]{3,2,1,0:T(8,128)(2,1)S(1)}, u32[]{:S(2)}, u32[]{:S(2)}) collective-permute-start(bf16[1,1,320,128]{3,2,1,0:T(8,128)(2,1)S(1)} %get-tuple-element.44), channel_id=1, source_target_pairs={{0,8},{16,24},{24,16},{1,9},{17,25},{25,17},{2,10},{18,26},{26,18}... | collective-permute-start | bytes 245768 | tf_op jit(solution)/shard_map/ppermute | solution.py:41

commit v11 on v10

--- a/solution.py
+++ b/solution.py
@@ -96,11 +96,15 @@
     pl.when(jnp.logical_not(relay))(lambda: cut(tail_ref))
 
 
-def prepare_kernel(x_ref, ws_ref, bs_ref, wt_ref, bt_ref, conv_ref, mix_ref, cb_ref, mb_ref, *piece_refs, spans):
+def prepare_kernel(x_ref, ws_ref, bs_ref, wt_ref, bt_ref, conv_ref, wide_ref, mix_ref, cb_ref, mb_ref, *piece_refs, spans):
     keep_rows(x_ref, piece_refs, spans)
     taps, channels = ws_ref.shape[0], ws_ref.shape[2]
+    wide = []
+    for i in range(taps):
+        wide.append(ws_ref[jnp.where(flipped(), taps - 1 - i, i)].reshape(taps * channels, channels))
+    wide_ref[...] = jnp.concatenate(wide, axis=0).T
     for j in range(taps):
-        blocks = [ws_ref[jnp.where(flipped(), taps - 1 - i, i), j] for i in range(taps)]
+        blocks = [part[j * channels : (j + 1) * channels] for part in wide]
         conv_ref[j * channels : (j + 1) * channels, :] = jnp.concatenate(blocks, axis=0).T
     mix_ref[...] = wt_ref[...].reshape(taps * channels, channels).T
     width = cb_ref.shape[1]
@@ -121,6 +125,15 @@
     return jnp.concatenate(rows, axis=1)
 
 
+def shifted_rows(row):
+    width = row.shape[-1]
+    lane = lax.broadcasted_iota(jnp.int32, (1, width), 1)
+    wide = row.astype(F32)
+    left = jnp.where(lane == 0, 0.0, pltpu.roll(wide, 1, 1)).astype(BF16)
+    right = jnp.where(lane == width - 1, 0.0, pltpu.roll(wide, width - 1, 1)).astype(BF16)
+    return jnp.concatenate([left, row, right], axis=0)
+
+
 def own_kernel(x_ref, beside_ref, conv_ref, mix_ref, cb_ref, mb_ref, out_ref, xs, *, group):
     frames, rows, channels, width = x_ref.shape
     for f in range(frames):
@@ -148,7 +161,7 @@
     lax.fori_loop(0, rows // group, body, 0)
 
 
-def incoming_kernel(own_ref, conv_ref, mix_ref, cb_ref, *refs, pieces, low, count, group, ready, stage):
+def incoming_kernel(own_ref, wide_ref, mix_ref, cb_ref, *refs, pieces, low, count, ready, stage):
     rows, channels, width = own_ref.shape
     flip = flipped()
     first = lax.axis_index("frames") == 0
@@ -171,29 +184,31 @@
             target[jnp.where(flip, size - 1 - q, q)] = own_ref[low + q].astype(BF16)
 
     def convolve():
-        held = kept_ref.shape[0]
-        xs[0:held] = kept_ref[...]
+        slots = [] if stage == OPEN else [kept_ref.at[k] for k in range(kept_ref.shape[0])]
+        fresh = [kept_ref.at[0]] if stage == OPEN else []
         for ref in piece_refs:
             size = ref.shape[1]
-            for k in range(size):
-                xs[held + k] = ref[0, jnp.where(flip, size - 1 - k, k)]
-            held += size
+            fresh += [ref.at[0, jnp.where(flip, size - 1 - k, k)] for k in range(size)]
+        total = len(slots) + len(fresh)
+        for k, ref in enumerate(fresh):
+            place = len(slots)
+            slot = xs.at[k] if stage == LAST or place < total - 2 else carry_ref.at[place - total + 2]
+            slot[...] = shifted_rows(ref[...])
+            slots.append(slot)
         if stage == LAST:
-            xs[held] = jnp.zeros((channels, width), BF16)
-        else:
-            carry_ref[...] = xs[pl.ds(held - 2, 2)]
-
-        def body(p, carry):
-            h = p * group
-            columns = [xs[pl.ds(h + q, 3)].reshape(3 * channels, width) for q in range(group)]
-            act = conv_rows(columns, conv_ref[...], cb_ref[...], channels, width)
-            mixed = jnp.dot(mix_ref[:, :channels], act, preferred_element_type=F32)
-            for q in range(group):
-                total = own_ref[low + h + q] + mixed[:, q * width : (q + 1) * width]
-                made_ref[jnp.where(flip, count - 1 - h - q, h + q)] = total.astype(BF16)
-            return carry
-
-        lax.fori_loop(0, count // group, body, 0)
+            xs[len(fresh)] = jnp.zeros((3 * channels, width), BF16)
+            slots.append(xs.at[len(fresh)])
+        for h in range(0, count, 8):
+            group = range(h, min(h + 8, count))
+            columns = [jnp.concatenate([slots[q + i][...] for i in range(3)], axis=0) for q in group]
+            summed = jnp.dot(wide_ref[...], jnp.concatenate(columns, axis=1), preferred_element_type=F32)
+            act = [
+                silu(summed[:, (q - h) * width : (q - h + 1) * width] + cb_ref[...]).astype(BF16) for q in group
+            ]
+            mixed = jnp.dot(mix_ref[:, :channels], jnp.concatenate(act, axis=1), preferred_element_type=F32)
+            for q in group:
+                term = mixed[:, (q - h) * width : (q - h + 1) * width]
+                made_ref[jnp.where(flip, count - 1 - q, q)] = (own_ref[low + q] + term).astype(BF16)
 
     if stage == OPEN:
 
@@ -232,17 +247,16 @@
 
 
 def incoming_rows(out, made, own, weights, kept, pieces, low, stage):
-    conv, mix, cb = weights
+    wide, mix, cb = weights
     rows, channels, width = own.shape
     held = kept.shape[0] + sum(piece.shape[1] for piece in pieces) + (stage == LAST)
     count = held - 2
     ready = 0 if made is None else made.shape[0]
-    group = next(g for g in (5, 4, 3, 2, 1) if count % g == 0)
 
     def row_array(size):
         return jax.ShapeDtypeStruct((size, channels, width), BF16)
 
-    operands = [own, conv, mix, cb, kept, *pieces]
+    operands = [own, wide, mix, cb, kept, *pieces]
     in_specs = [VMEM] * len(operands)
     out_shape, out_specs, aliases = [], [], {}
     if ready:
@@ -255,9 +269,9 @@
         out_shape.append(row_array(rows))
         out_specs.append(ANY)
     if stage != LAST:
-        out_shape += [row_array(count), row_array(2)]
+        out_shape += [row_array(count), jax.ShapeDtypeStruct((2, 3 * channels, width), BF16)]
         out_specs += [VMEM] * 2
-    scratch = [pltpu.VMEM((held, channels, width), BF16)]
+    scratch = [pltpu.VMEM((held, 3 * channels, width), BF16)]
     if stage == LAST:
         scratch.append(pltpu.VMEM((count, channels, width), BF16))
     if stage == CLOSING:
@@ -266,7 +280,7 @@
         scratch.append(pltpu.SemaphoreType.DMA((2,)))
     results = pl.pallas_call(
         functools.partial(
-            incoming_kernel, pieces=len(pieces), low=low, count=count, group=group, ready=ready, stage=stage
+            incoming_kernel, pieces=len(pieces), low=low, count=count, ready=ready, stage=stage
         ),
         out_shape=out_shape,
         in_specs=in_specs,
@@ -321,13 +335,14 @@
     beside = lax.ppermute(boundary, "rows", ring("rows"))
 
     square = jax.ShapeDtypeStruct((3 * channels, 3 * channels), BF16)
+    broad = jax.ShapeDtypeStruct((channels, 9 * channels), BF16)
     flat = jax.ShapeDtypeStruct((channels, 3 * channels), BF16)
     bias = jax.ShapeDtypeStruct((channels, width), F32)
-    conv, mix, cb, mb, *pieces = pl.pallas_call(
+    conv, wide, mix, cb, mb, *pieces = pl.pallas_call(
         functools.partial(prepare_kernel, spans=spans[1:3]),
-        out_shape=[square, flat, bias, bias] + row_shapes(x, spans[1:3]),
+        out_shape=[square, broad, flat, bias, bias] + row_shapes(x, spans[1:3]),
         in_specs=[VMEM] * 5,
-        out_specs=[VMEM] * 6,
+        out_specs=[VMEM] * 7,
         compiler_params=PARAMS,
         cost_estimate=cost(0, 2 * 12 * channels * channels * 2),
     )(x, w_spatial, b_spatial.reshape(1, channels), w_temporal, b_temporal.reshape(1, channels))
@@ -354,7 +369,7 @@
     arrived += [within_pairs(pieces[0], "frames", True), within_pairs(pieces[1], "frames", False)]
     kept = lax.ppermute(edge, "rows", ring("rows"))
 
-    weights = (conv, mix, cb)
+    weights = (wide, mix, cb)
     out, made, low = None, None, 0
     for k, (begin, end) in enumerate(steps):
         stage = LAST if end == len(arrived) else min(k, LATE)

time: 34.3 us -> 34.3 us (level)
  Pallas kernels: 22.5 us -> 22.1 us
    pallas_call x4, Pallas kernels: 8.08 us -> 7.42 us  [incoming_rows(): pl.pallas_call(functools.partial(incoming_kernel, pieces=len(pieces), low...]
where the time goes in v11:
time: 34.3 us; the launch traced here: 34 us
  Pallas kernels  22.1 us (64%)
  starting transfers between devices  9.06 us (26%)
  waiting for transfers between devices  1.94 us (6%)
  local copies, waits for them, and re-layouts  0.75 us (2%)
    pallas_call x1, Pallas kernels, per_device(): pl.pallas_call(functools.partial(own_kernel, group=next((g for g in (8, 4...  10.4 us
    pallas_call x4, Pallas kernels, incoming_rows(): pl.pallas_call(functools.partial(incoming_kernel, pieces=len(pieces), low...  7.42 us
    ppermute x2, starting transfers between devices, within_pairs(): return lax.ppermute(piece, axis, [(a, b) for a, b in route if b or keep])  3.99 us
    ppermute x2, starting transfers between devices, per_device(): lax.ppermute(piece, 'frames', ring('frames'))  2.65 us
    pallas_call x1, Pallas kernels, per_device(): pl.pallas_call(functools.partial(slice_kernel, spans=whole), out_shape=ro...  1.82 us
    ppermute x1, starting transfers between devices, per_device(): arrived = [lax.ppermute(head, 'frames', ring('frames'))]  1.54 us
    pallas_call x1, Pallas kernels, per_device(): pl.pallas_call(functools.partial(prepare_kernel, spans=spans[1:3]), out_s...  1.29 us
    ppermute x2, waiting for transfers between devices, within_pairs(): return lax.ppermute(piece, axis, [(a, b) for a, b in route if b or keep])  1.13 us
  transfers between devices with their start and end apart: 8, of which 3 were waited for; matrix products, arithmetic and copies ran while one was open for 0% of the time, Pallas kernels for 57%

profile of v11, /device:TPU:20, one launch (start us, length us, event | category | flops | bytes accessed | tf_op | source)
XLA Modules:
  0.0 34.0 jit_solution(10890688835965956504)
XLA Ops:
  0.0 1.1 %shard_map.56 = (bf16[1,5,320,128]{3,2,1,0:T(8,128)(2,1)S(1)}, bf16[2,1,320,128]{3,2,1,0:T(8,128)(2,1)S(1)}) custom-call(bf16[2,16,320,128]{3,2,1,0:T(8,128)(2,1)} %bitcast.4), custom_call_target="tpu_custom_call" | custom-call | tf_op jit(solution)/shard_map/pallas_call | solution.py:306
  1.1 0.1 collective-permute-start
  1.1 1.5 %collective-permute-start.1 = (bf16[1,5,320,128]{3,2,1,0:T(8,128)(2,1)S(1)}, bf16[1,5,320,128]{3,2,1,0:T(8,128)(2,1)S(1)}, u32[]{:S(2)}, u32[]{:S(2)}) collective-permute-start(bf16[1,5,320,128]{3,2,1,0:T(8,128)(2,1)S(1)} %get-tuple-element.32), channel_id=1, source_target_pairs={{0,8},{8,16},{16,24},{24,0},{1,9},{9,17},{17,25},{25,1},{2,10},{10... | collective-permute-start | bytes 1228808 | tf_op jit(solution)/shard_map/ppermute | solution.py:333
  2.7 0.0 copy-start.1
  2.7 1.8 %shard_map.55.x_ref = bf16[2,16,320,128]{3,2,1,0:T(8,128)(2,1)S(1)} custom-call(bf16[2,16,320,128]{3,2,1,0:T(8,128)(2,1)} %bitcast.5), custom_call_target="tpu_custom_call" | custom-call | tf_op jit(solution)/shard_map/pallas_call | solution.py:315
  4.5 0.0 copy-start.2
  4.5 0.0 copy-start.3
  4.5 0.0 copy-start
  4.6 0.8 %collective-permute-start.2 = (bf16[1,3,320,128]{3,2,1,0:T(8,128)(2,1)S(1)}, bf16[1,3,320,128]{3,2,1,0:T(8,128)(2,1)S(1)}, u32[]{:S(2)}, u32[]{:S(2)}) collective-permute-start(bf16[1,3,320,128]{3,2,1,0:T(8,128)(2,1)S(1)} %shard_map.59.tail_ref), channel_id=1, source_target_pairs={{8,24},{24,8},{9,25},{25,9},{10,26},{26,10},{11,27},{27,11},{12,28... | collective-permute-start | bytes 737288 | tf_op jit(solution)/shard_map/ppermute | solution.py:35
  5.4 0.0 copy-done.2
  5.4 0.0 copy-done.3
  5.4 0.0 copy-done.1
  5.5 0.7 %copy-done = bf16[3,3,320,320]{3,2,1,0:T(8,128)(2,1)S(1)} copy-done((bf16[3,3,320,320]{3,2,1,0:T(8,128)(2,1)S(1)}, bf16[3,3,320,320]{3,2,1,0:T(8,128)(2,1)}, u32[]{:S(2)}) %copy-start) | copy-done | bytes 1843224
  6.2 1.3 %shard_map.57 = (bf16[960,960]{1,0:T(8,128)(2,1)S(1)}, bf16[320,2880]{1,0:T(8,128)(2,1)S(1)}, bf16[320,960]{1,0:T(8,128)(2,1)S(1)}, f32[320,128]{1,0:T(8,128)S(1...) custom-call(bf16[2,16,320,128]{3,2,1,0:T(8,128)(2,1)S(1)} %shard_map.55.x_ref,, ...), custom_call_target="tpu_custom_call" | custom-call | bytes 4915200 | tf_op jit(solution)/shard_map/pallas_call | solution.py:341
  7.5 2.6 %collective-permute-start.4 = (bf16[1,4,320,128]{3,2,1,0:T(8,128)(2,1)S(1)}, bf16[1,4,320,128]{3,2,1,0:T(8,128)(2,1)S(1)}, u32[]{:S(2)}, u32[]{:S(2)}) collective-permute-start(bf16[1,4,320,128]{3,2,1,0:T(8,128)(2,1)S(1)} %get-tuple-element.37), channel_id=1, source_target_pairs={{0,8},{8,16},{16,24},{24,0},{1,9},{9,17},{17,25},{25,1},{2,10},{10... | collective-permute-start | bytes 983048 | tf_op jit(solution)/shard_map/ppermute | solution.py:349
  10.1 0.1 collective-permute-start.5
  10.1 0.0 collective-permute-done.beside_ref
  10.1 10.4 %shard_map.58.own_ref = f32[16,320,128]{2,1,0:T(8,128)S(1)} custom-call(bf16[2,16,320,128]{3,2,1,0:T(8,128)(2,1)S(1)} %shard_map.55.x_ref, bf16[2,1,320,128]{3,2,1,0:T(8,128)(2,1)S(1)} %collective-permute-done.beside_ref, bf16[960,960]{1,0:T(8,128)(2,1)S(1)} %get-tuple-element.28.conv_ref, bf16[320,960]{1,0:T(8,128)(2,1)S(1)} %get-tuple-element.29.mix_ref, ...), custom_call_target="tpu_custom_call" | custom-call | flops 8388608000 | bytes 5242880 | tf_op jit(solution)/shard_map/pallas_call | solution.py:351
  20.6 0.0 collective-permute-done.1.piece_ref.refs_1_
  20.6 0.0 collective-permute-done.2.relayed_ref
  20.6 2.0 %collective-permute-start.6 = (bf16[1,2,320,128]{3,2,1,0:T(8,128)(2,1)S(1)}, bf16[1,2,320,128]{3,2,1,0:T(8,128)(2,1)S(1)}, u32[]{:S(2)}, u32[]{:S(2)}) collective-permute-start(bf16[1,2,320,128]{3,2,1,0:T(8,128)(2,1)S(1)} %get-tuple-element.42), channel_id=1, source_target_pairs={{0,8},{8,0},{16,24},{24,16},{1,9},{9,1},{17,25},{25,17},{2,10},{10... | collective-permute-start | bytes 491528 | tf_op jit(solution)/shard_map/ppermute | solution.py:41
  22.6 0.0 collective-permute-start.3
  22.6 2.0 %collective-permute-start.7 = (bf16[1,1,320,128]{3,2,1,0:T(8,128)(2,1)S(1)}, bf16[1,1,320,128]{3,2,1,0:T(8,128)(2,1)S(1)}, u32[]{:S(2)}, u32[]{:S(2)}) collective-permute-start(bf16[1,1,320,128]{3,2,1,0:T(8,128)(2,1)S(1)} %get-tuple-element.46), channel_id=1, source_target_pairs={{0,8},{16,24},{24,16},{1,9},{17,25},{25,17},{2,10},{18,26},{26,18}... | collective-permute-start | bytes 245768 | tf_op jit(solution)/shard_map/ppermute | solution.py:41
  24.6 0.0 collective-permute-done.4.refs_2_
  24.6 0.0 collective-permute-done.3.refs_0_
  24.7 2.9 %shard_map.61 = (bf16[8,320,128]{2,1,0:T(8,128)(2,1)S(1)}, bf16[2,960,128]{2,1,0:T(8,128)(2,1)S(1)}) custom-call(f32[16,320,128]{2,1,0:T(8,128)S(1)} %shard_map.58.own_ref, bf16[320,2880]{1,0:T(8,128)(2,1)S(1)} %get-tuple-element.34.wide_ref, bf16[320,960]{1,0:T(8,128)(2,1)S(1)} %get-tuple-element.29.mix_ref, f32[320,128]{1,0:T(8,128)S(1)} %get-tuple-element.30.cb_ref, ...), custom_call_target="tpu_custom_call" | custom-call | tf_op jit(solution)/shard_map/pallas_call | solution.py:281
  27.6 0.8 %collective-permute-done.5.refs_1_ = bf16[1,4,320,128]{3,2,1,0:T(8,128)(2,1)S(1)} collective-permute-done((bf16[1,4,320,128]{3,2,1,0:T(8,128)(2,1)S(1)}, bf16[1,4,320,128]{3,2,1,0:T(8,128)(2,1)S(1)}, u32[]{:S(2)}, u32[]{:S(2)}) %collective-permute-start.5) | collective-permute-done | bytes 327712 | tf_op jit(solution)/shard_map/ppermute | solution.py:349
  28.4 1.6 %shard_map.62 = (bf16[16,320,128]{2,1,0:T(8,128)(2,1)}, bf16[4,320,128]{2,1,0:T(8,128)(2,1)S(1)}, bf16[2,960,128]{2,1,0:T(8,128)(2,1)S(1)}) custom-call(f32[16,320,128]{2,1,0:T(8,128)S(1)} %shard_map.58.own_ref, bf16[320,2880]{1,0:T(8,128)(2,1)S(1)} %get-tuple-element.34.wide_ref, bf16[320,960]{1,0:T(8,128)(2,1)S(1)} %get-tuple-element.29.mix_ref, ...), custom_call_target="tpu_custom_call" | custom-call | tf_op jit(solution)/shard_map/pallas_call | solution.py:281
  30.0 0.9 %collective-permute-done.6.refs_1_ = bf16[1,2,320,128]{3,2,1,0:T(8,128)(2,1)S(1)} collective-permute-done((bf16[1,2,320,128]{3,2,1,0:T(8,128)(2,1)S(1)}, bf16[1,2,320,128]{3,2,1,0:T(8,128)(2,1)S(1)}, u32[]{:S(2)}, u32[]{:S(2)}) %collective-permute-start.6) | collective-permute-done | bytes 163872 | tf_op jit(solution)/shard_map/ppermute | solution.py:41
  31.0 1.1 %shard_map.63 = (bf16[16,320,128]{2,1,0:T(8,128)(2,1)}, bf16[2,320,128]{2,1,0:T(8,128)(2,1)S(1)}, bf16[2,960,128]{2,1,0:T(8,128)(2,1)S(1)}) custom-call(f32[16,320,128]{2,1,0:T(8,128)S(1)} %shard_map.58.own_ref, bf16[320,2880]{1,0:T(8,128)(2,1)S(1)} %get-tuple-element.34.wide_ref, ...), custom_call_target="tpu_custom_call", output_to_operand_aliasing={{0}: (7, {})} | custom-call | tf_op jit(solution)/shard_map/pallas_call | solution.py:281
  32.1 0.2 collective-permute-done.7.refs_1_
  32.3 1.8 %shard_map.64 = bf16[16,320,128]{2,1,0:T(8,128)(2,1)} custom-call(f32[16,320,128]{2,1,0:T(8,128)S(1)} %shard_map.58.own_ref, bf16[320,2880]{1,0:T(8,128)(2,1)S(1)} %get-tuple-element.34.wide_ref, bf16[320,960]{1,0:T(8,128)(2,1)S(1)} %get-tuple-element.29.mix_ref, f32[320,128]{1,0:T(8,128)S(1)} %get-tuple-element.30.cb_ref, ...), custom_call_target="tpu_custom_call", output_to_operand_aliasing={{}: (7, {})} | custom-call | tf_op jit(solution)/shard_map/pallas_call | solution.py:281
  (4 shorter events, 0.1 us)
Async XLA Ops:
  1.1 9.1 %collective-permute-start = (bf16[2,1,320,128]{3,2,1,0:T(8,128)(2,1)S(1)}, bf16[2,1,320,128]{3,2,1,0:T(8,128)(2,1)S(1)}, u32[]{:S(2)}, u32[]{:S(2)}) collective-permute-start(bf16[2,1,320,128]{3,2,1,0:T(8,128)(2,1)S(1)} %get-tuple-element.27), channel_id=1, source_target_pairs={{0,4},{4,0},{1,5},{5,1},{2,6},{6,2},{3,7},{7,3},{8,12},{12,8},{9,1... | collective-permute-start | bytes 491528 | tf_op jit(solution)/shard_map/ppermute | solution.py:335
  1.1 19.4 %collective-permute-start.1 = (bf16[1,5,320,128]{3,2,1,0:T(8,128)(2,1)S(1)}, bf16[1,5,320,128]{3,2,1,0:T(8,128)(2,1)S(1)}, u32[]{:S(2)}, u32[]{:S(2)}) collective-permute-start(bf16[1,5,320,128]{3,2,1,0:T(8,128)(2,1)S(1)} %get-tuple-element.32), channel_id=1, source_target_pairs={{0,8},{8,16},{16,24},{24,0},{1,9},{9,17},{17,25},{25,1},{2,10},{10... | collective-permute-start | bytes 1228808 | tf_op jit(solution)/shard_map/ppermute | solution.py:333
  2.7 2.8 %copy-start.1 = (bf16[3,320,320]{2,1,0:T(8,128)(2,1)S(1)}, bf16[3,320,320]{2,1,0:T(8,128)(2,1)}, u32[]{:S(2)}) copy-start(bf16[3,320,320]{2,1,0:T(8,128)(2,1)} %wt_ref.1) | copy-start | bytes 1843204
  4.5 0.9 %copy-start.2 = (f32[320]{0:T(512)S(1)}, f32[320]{0:T(512)}, u32[]{:S(2)}) copy-start(f32[320]{0:T(512)} %param.7) | copy-start | bytes 3844
  4.5 0.9 %copy-start.3 = (f32[320]{0:T(512)S(1)}, f32[320]{0:T(512)}, u32[]{:S(2)}) copy-start(f32[320]{0:T(512)} %param.9) | copy-start | bytes 3844
  4.5 1.6 %copy-start = (bf16[3,3,320,320]{3,2,1,0:T(8,128)(2,1)S(1)}, bf16[3,3,320,320]{3,2,1,0:T(8,128)(2,1)}, u32[]{:S(2)}) copy-start(bf16[3,3,320,320]{3,2,1,0:T(8,128)(2,1)} %ws_ref.1) | copy-start | bytes 5529604
  4.6 16.0 %collective-permute-start.2 = (bf16[1,3,320,128]{3,2,1,0:T(8,128)(2,1)S(1)}, bf16[1,3,320,128]{3,2,1,0:T(8,128)(2,1)S(1)}, u32[]{:S(2)}, u32[]{:S(2)}) collective-permute-start(bf16[1,3,320,128]{3,2,1,0:T(8,128)(2,1)S(1)} %shard_map.59.tail_ref), channel_id=1, source_target_pairs={{8,24},{24,8},{9,25},{25,9},{10,26},{26,10},{11,27},{27,11},{12,28... | collective-permute-start | bytes 737288 | tf_op jit(solution)/shard_map/ppermute | solution.py:35
  7.5 17.2 %collective-permute-start.4 = (bf16[1,4,320,128]{3,2,1,0:T(8,128)(2,1)S(1)}, bf16[1,4,320,128]{3,2,1,0:T(8,128)(2,1)S(1)}, u32[]{:S(2)}, u32[]{:S(2)}) collective-permute-start(bf16[1,4,320,128]{3,2,1,0:T(8,128)(2,1)S(1)} %get-tuple-element.37), channel_id=1, source_target_pairs={{0,8},{8,16},{16,24},{24,0},{1,9},{9,17},{17,25},{25,1},{2,10},{10... | collective-permute-start | bytes 983048 | tf_op jit(solution)/shard_map/ppermute | solution.py:349
  10.1 18.3 %collective-permute-start.5 = (bf16[1,4,320,128]{3,2,1,0:T(8,128)(2,1)S(1)}, bf16[1,4,320,128]{3,2,1,0:T(8,128)(2,1)S(1)}, u32[]{:S(2)}, u32[]{:S(2)}) collective-permute-start(bf16[1,4,320,128]{3,2,1,0:T(8,128)(2,1)S(1)} %get-tuple-element.39), channel_id=1, source_target_pairs={{0,8},{8,16},{16,24},{24,0},{1,9},{9,17},{17,25},{25,1},{2,10},{10... | collective-permute-start | bytes 983048 | tf_op jit(solution)/shard_map/ppermute | solution.py:349
  20.6 10.3 %collective-permute-start.6 = (bf16[1,2,320,128]{3,2,1,0:T(8,128)(2,1)S(1)}, bf16[1,2,320,128]{3,2,1,0:T(8,128)(2,1)S(1)}, u32[]{:S(2)}, u32[]{:S(2)}) collective-permute-start(bf16[1,2,320,128]{3,2,1,0:T(8,128)(2,1)S(1)} %get-tuple-element.42), channel_id=1, source_target_pairs={{0,8},{8,0},{16,24},{24,16},{1,9},{9,1},{17,25},{25,17},{2,10},{10... | collective-permute-start | bytes 491528 | tf_op jit(solution)/shard_map/ppermute | solution.py:41
  22.6 2.0 %collective-permute-start.3 = (bf16[1,320,128]{2,1,0:T(8,128)(2,1)S(1)}, bf16[1,320,128]{2,1,0:T(8,128)(2,1)S(1)}, u32[]{:S(2)}, u32[]{:S(2)}) collective-permute-start(bf16[1,320,128]{2,1,0:T(8,128)(2,1)S(1)} %get-tuple-element.36), channel_id=1, source_target_pairs={{0,4},{4,0},{1,5},{5,1},{2,6},{6,2},{3,7},{7,3},{8,12},{12,8},{9,1... | collective-permute-start | bytes 245768 | tf_op jit(solution)/shard_map/ppermute | solution.py:370
  22.6 9.7 %collective-permute-start.7 = (bf16[1,1,320,128]{3,2,1,0:T(8,128)(2,1)S(1)}, bf16[1,1,320,128]{3,2,1,0:T(8,128)(2,1)S(1)}, u32[]{:S(2)}, u32[]{:S(2)}) collective-permute-start(bf16[1,1,320,128]{3,2,1,0:T(8,128)(2,1)S(1)} %get-tuple-element.46), channel_id=1, source_target_pairs={{0,8},{16,24},{24,16},{1,9},{17,25},{25,17},{2,10},{18,26},{26,18}... | collective-permute-start | bytes 245768 | tf_op jit(solution)/shard_map/ppermute | solution.py:41

commit v12 on v11

--- a/solution.py
+++ b/solution.py
@@ -58,6 +58,10 @@
 def keep_rows(x_ref, outs, spans):
     for out, span in zip(outs, spans):
         out[...] = span_of(x_ref, span)[...]
+
+
+def load_kernel(x_ref, head_ref, *refs, spans):
+    slice_kernel(x_ref, *refs, spans=spans)
 
 
 def keep_kernel(x_ref, *outs, spans):
@@ -80,7 +84,7 @@
         copy.wait()
 
 
-def edge_kernel(piece_ref, tail_ref, relayed_ref, out_ref, *tail_out_refs):
+def edge_kernel(piece_ref, tail_ref, relayed_ref, second_ref, out_ref, *tail_out_refs):
     size = piece_ref.shape[1]
     out_ref[0] = piece_ref[0, jnp.where(flipped(), size - 1, 0)]
     count = lax.axis_size("frames")
@@ -134,7 +138,7 @@
     return jnp.concatenate([left, row, right], axis=0)
 
 
-def own_kernel(x_ref, beside_ref, conv_ref, mix_ref, cb_ref, mb_ref, out_ref, xs, *, group):
+def own_kernel(x_ref, beside_ref, conv_ref, mix_ref, cb_ref, mb_ref, early_ref, out_ref, xs, *, group):
     frames, rows, channels, width = x_ref.shape
     for f in range(frames):
         xs[f, 0] = beside_ref[f, 0]
@@ -298,39 +302,38 @@
 def per_device(video, w_spatial, b_spatial, w_temporal, b_temporal):
     frames, rows, width, channels = video.shape
     x = jnp.transpose(video, (0, 1, 3, 2))
-    sizes, steps = [rows - 11, 4, 4, 2, 1], [(0, 2), (2, 3), (3, 4), (4, 5)]
+    sizes, steps = [3, rows - 10, 4, 2, 1], [(0, 2), (2, 3), (3, 4), (4, 5)]
     places = [sum(sizes[:k]) for k in range(len(sizes))]
     spans = [(frames - 1, 1, place, size) for place, size in zip(places, sizes)]
 
-    head_spans = [spans[0], (0, frames, 0, 1)]
-    head, boundary = pl.pallas_call(
-        functools.partial(slice_kernel, spans=head_spans),
-        out_shape=row_shapes(x, head_spans),
+    (head,) = pl.pallas_call(
+        functools.partial(slice_kernel, spans=spans[:1]),
+        out_shape=row_shapes(x, spans[:1]),
         in_specs=[ANY],
-        out_specs=[VMEM] * 2,
-        scratch_shapes=[pltpu.SemaphoreType.DMA((2,))],
+        out_specs=[VMEM],
+        scratch_shapes=[pltpu.SemaphoreType.DMA((1,))],
         compiler_params=pltpu.CompilerParams(vmem_limit_bytes=HEAD_LIMIT),
     )(x)
     whole = [(0, frames, 0, rows)]
     (x,) = pl.pallas_call(
-        functools.partial(slice_kernel, spans=whole),
+        functools.partial(load_kernel, spans=whole),
         out_shape=row_shapes(x, whole),
-        in_specs=[ANY],
+        in_specs=[ANY] * 2,
         out_specs=[VMEM],
         scratch_shapes=[pltpu.SemaphoreType.DMA((1,))],
         compiler_params=pltpu.CompilerParams(vmem_limit_bytes=LOAD_LIMIT),
         cost_estimate=cost(0, 0),
-    )(x)
-    ending = [(frames - 1, 1, places[-2], sizes[-2] + sizes[-1])]
-    (tail,) = pl.pallas_call(
-        functools.partial(keep_kernel, spans=ending),
-        out_shape=row_shapes(x, ending),
+    )(x, head)
+    kept_spans = [(0, frames, 0, 1), (frames - 1, 1, places[-2], sizes[-2] + sizes[-1]), spans[1]]
+    boundary, tail, second = pl.pallas_call(
+        functools.partial(keep_kernel, spans=kept_spans),
+        out_shape=row_shapes(x, kept_spans),
         in_specs=[VMEM],
-        out_specs=[VMEM],
+        out_specs=[VMEM] * 3,
         compiler_params=PARAMS,
         cost_estimate=cost(0, 0),
     )(x)
-    arrived = [lax.ppermute(head, "frames", ring("frames"))]
+    arrived = [lax.ppermute(piece, "frames", ring("frames")) for piece in (head, second)]
     relayed = next_odd(tail, "frames")
     beside = lax.ppermute(boundary, "rows", ring("rows"))
 
@@ -339,10 +342,10 @@
     flat = jax.ShapeDtypeStruct((channels, 3 * channels), BF16)
     bias = jax.ShapeDtypeStruct((channels, width), F32)
     conv, wide, mix, cb, mb, *pieces = pl.pallas_call(
-        functools.partial(prepare_kernel, spans=spans[1:3]),
-        out_shape=[square, broad, flat, bias, bias] + row_shapes(x, spans[1:3]),
+        functools.partial(prepare_kernel, spans=spans[2:3]),
+        out_shape=[square, broad, flat, bias, bias] + row_shapes(x, spans[2:3]),
         in_specs=[VMEM] * 5,
-        out_specs=[VMEM] * 7,
+        out_specs=[VMEM] * 6,
         compiler_params=PARAMS,
         cost_estimate=cost(0, 2 * 12 * channels * channels * 2),
     )(x, w_spatial, b_spatial.reshape(1, channels), w_temporal, b_temporal.reshape(1, channels))
@@ -351,21 +354,21 @@
     own = pl.pallas_call(
         functools.partial(own_kernel, group=next(g for g in (8, 4, 3, 2, 1) if rows % g == 0)),
         out_shape=jax.ShapeDtypeStruct((rows, channels, width), F32),
-        in_specs=[VMEM] * 6,
+        in_specs=[VMEM] * 6 + [ANY],
         out_specs=VMEM,
         scratch_shapes=[pltpu.VMEM((frames, rows + 2, channels, width), BF16)],
         compiler_params=PARAMS,
         cost_estimate=cost(2 * rows * width * channels * channels * 20, 8 * rows * channels * width),
-    )(x, beside, conv, mix, cb, mb)
+    )(x, beside, conv, mix, cb, mb, arrived[0])
     own, arrived[0] = lax.optimization_barrier((own, arrived[0]))
     edge, *pieces = pl.pallas_call(
         edge_kernel,
         out_shape=[jax.ShapeDtypeStruct((1, channels, width), BF16)] + row_shapes(x, spans[-2:]),
-        in_specs=[VMEM] * 3,
+        in_specs=[VMEM] * 3 + [ANY],
         out_specs=[VMEM] * 3,
         compiler_params=PARAMS,
         cost_estimate=cost(0, 0),
-    )(arrived[0], tail, relayed)
+    )(arrived[0], tail, relayed, arrived[1])
     arrived += [within_pairs(pieces[0], "frames", True), within_pairs(pieces[1], "frames", False)]
     kept = lax.ppermute(edge, "rows", ring("rows"))
 

time: 34.3 us -> 34 us (level)
  starting transfers between devices: 9.06 us -> 10.9 us
  waiting for transfers between devices: 1.94 us -> 0.12 us
  local copies, waits for them, and re-layouts: 0.75 us -> 0.24 us
    ppermute x2 -> x3, starting transfers between devices: 2.65 us -> 6.18 us  [per_device(): lax.ppermute(piece, 'frames', ring('frames'))]
    ppermute x1 -> x0, starting transfers between devices: 1.54 us -> none  [per_device(): arrived = [lax.ppermute(head, 'frames', ring('frames'))]]
    ppermute x2, waiting for transfers between devices: 1.13 us -> 0.1 us  [within_pairs(): return lax.ppermute(piece, axis, [(a, b) for a, b in route if b or keep])]
    ppermute x2 -> x3, waiting for transfers between devices: 0.8 us -> 0.01 us  [per_device(): lax.ppermute(piece, 'frames', ring('frames'))]
    unnamed x8, local copies, waits for them, and re-layouts: 0.75 us -> 0.24 us
  transfers between devices with their start and end apart: 8 -> 8, of which waited for: 3 -> 1; matrix products, arithmetic and copies ran while one was open for 0% -> 0% of each run, Pallas kernels for 57% -> 58%
where the time goes in v12:
time: 34 us; the launch traced here: 33.5 us
  Pallas kernels  22.1 us (65%)
  starting transfers between devices  10.9 us (32%)
    pallas_call x1, Pallas kernels, per_device(): pl.pallas_call(functools.partial(own_kernel, group=next((g for g in (8, 4...  10.4 us
    pallas_call x4, Pallas kernels, incoming_rows(): pl.pallas_call(functools.partial(incoming_kernel, pieces=len(pieces), low...  7.46 us
    ppermute x3, starting transfers between devices, per_device(): lax.ppermute(piece, 'frames', ring('frames'))  6.18 us
    ppermute x2, starting transfers between devices, within_pairs(): return lax.ppermute(piece, axis, [(a, b) for a, b in route if b or keep])  3.93 us
    pallas_call x1, Pallas kernels, per_device(): pl.pallas_call(functools.partial(load_kernel, spans=whole), out_shape=row...  1.82 us
    pallas_call x1, Pallas kernels, per_device(): pl.pallas_call(functools.partial(prepare_kernel, spans=spans[2:3]), out_s...  1.27 us
    pallas_call x1, Pallas kernels, per_device(): pl.pallas_call(functools.partial(slice_kernel, spans=spans[:1]), out_shap...  0.95 us
  transfers between devices with their start and end apart: 8, of which 1 were waited for; matrix products, arithmetic and copies ran while one was open for 0% of the time, Pallas kernels for 58%

profile of v12, /device:TPU:20, one launch (start us, length us, event | category | flops | bytes accessed | tf_op | source)
XLA Modules:
  0.0 33.5 jit_solution(13855235594361082718)
XLA Ops:
  0.0 1.0 %shard_map.55.head_ref = bf16[1,3,320,128]{3,2,1,0:T(8,128)(2,1)S(1)} custom-call(bf16[2,16,320,128]{3,2,1,0:T(8,128)(2,1)} %bitcast.4), custom_call_target="tpu_custom_call" | custom-call | tf_op jit(solution)/shard_map/pallas_call | solution.py:309
  1.0 1.5 %collective-permute-start.1 = (bf16[1,3,320,128]{3,2,1,0:T(8,128)(2,1)S(1)}, bf16[1,3,320,128]{3,2,1,0:T(8,128)(2,1)S(1)}, u32[]{:S(2)}, u32[]{:S(2)}) collective-permute-start(bf16[1,3,320,128]{3,2,1,0:T(8,128)(2,1)S(1)} %shard_map.55.head_ref), channel_id=1, source_target_pairs={{0,8},{8,16},{16,24},{24,0},{1,9},{9,17},{17,25},{25,1},{2,10},{10... | collective-permute-start | bytes 737288 | tf_op jit(solution)/shard_map/ppermute | solution.py:336
  2.5 0.0 copy-start.1
  2.5 1.8 %shard_map.56.x_ref = bf16[2,16,320,128]{3,2,1,0:T(8,128)(2,1)S(1)} custom-call(bf16[2,16,320,128]{3,2,1,0:T(8,128)(2,1)} %bitcast.5, bf16[1,3,320,128]{3,2,1,0:T(8,128)(2,1)S(1)} %shard_map.55.head_ref), custom_call_target="tpu_custom_call" | custom-call | tf_op jit(solution)/shard_map/pallas_call | solution.py:318
  4.3 0.0 copy-start.2
  4.3 0.0 copy-start.3
  4.4 0.0 copy-start
  4.4 0.1 shard_map.57
  4.5 0.1 collective-permute-start
  4.5 0.5 %collective-permute-start.3 = (bf16[1,6,320,128]{3,2,1,0:T(8,128)(2,1)S(1)}, bf16[1,6,320,128]{3,2,1,0:T(8,128)(2,1)S(1)}, u32[]{:S(2)}, u32[]{:S(2)}) collective-permute-start(bf16[1,6,320,128]{3,2,1,0:T(8,128)(2,1)S(1)} %get-tuple-element.36), channel_id=1, source_target_pairs={{0,8},{8,16},{16,24},{24,0},{1,9},{9,17},{17,25},{25,1},{2,10},{10... | collective-permute-start | bytes 1474568 | tf_op jit(solution)/shard_map/ppermute | solution.py:336
  5.1 0.7 %collective-permute-start.2 = (bf16[1,3,320,128]{3,2,1,0:T(8,128)(2,1)S(1)}, bf16[1,3,320,128]{3,2,1,0:T(8,128)(2,1)S(1)}, u32[]{:S(2)}, u32[]{:S(2)}) collective-permute-start(bf16[1,3,320,128]{3,2,1,0:T(8,128)(2,1)S(1)} %get-tuple-element.35.tail_ref), channel_id=1, source_target_pairs={{8,24},{24,8},{9,25},{25,9},{10,26},{26,10},{11,27},{27,11},{12,28... | collective-permute-start | bytes 737288 | tf_op jit(solution)/shard_map/ppermute | solution.py:35
  5.7 0.0 copy-done.2
  5.8 0.0 copy-done.3
  5.8 0.0 copy-done.1
  5.8 0.2 copy-done
  6.0 1.3 %shard_map.58 = (bf16[960,960]{1,0:T(8,128)(2,1)S(1)}, bf16[320,2880]{1,0:T(8,128)(2,1)S(1)}, bf16[320,960]{1,0:T(8,128)(2,1)S(1)}, f32[320,128]{1,0:T(8,128)S(1...) custom-call(bf16[2,16,320,128]{3,2,1,0:T(8,128)(2,1)S(1)} %shard_map.56.x_ref, ...), custom_call_target="tpu_custom_call" | custom-call | bytes 4915200 | tf_op jit(solution)/shard_map/pallas_call | solution.py:344
  7.3 4.1 %collective-permute-start.5 = (bf16[1,4,320,128]{3,2,1,0:T(8,128)(2,1)S(1)}, bf16[1,4,320,128]{3,2,1,0:T(8,128)(2,1)S(1)}, u32[]{:S(2)}, u32[]{:S(2)}) collective-permute-start(bf16[1,4,320,128]{3,2,1,0:T(8,128)(2,1)S(1)} %get-tuple-element.39), channel_id=1, source_target_pairs={{0,8},{8,16},{16,24},{24,0},{1,9},{9,17},{17,25},{25,1},{2,10},{10... | collective-permute-start | bytes 983048 | tf_op jit(solution)/shard_map/ppermute | solution.py:352
  11.4 0.0 collective-permute-done.beside_ref
  11.4 0.0 collective-permute-done.1.early_ref.piece_ref.refs_1_
  11.4 10.4 %shard_map.59.own_ref = f32[16,320,128]{2,1,0:T(8,128)S(1)} custom-call(bf16[2,16,320,128]{3,2,1,0:T(8,128)(2,1)S(1)} %shard_map.56.x_ref, bf16[2,1,320,128]{3,2,1,0:T(8,128)(2,1)S(1)} %collective-permute-done.beside_ref, bf16[960,960]{1,0:T(8,128)(2,1)S(1)} %get-tuple-element.28.conv_ref, bf16[320,960]{1,0:T(8,128)(2,1)S(1)} %get-tuple-element.29.mix_ref, ...), custom_call_target="tpu_custom_call" | custom-call | flops 8388608000 | bytes 5242880 | tf_op jit(solution)/shard_map/pallas_call | solution.py:354
  21.8 0.0 collective-permute-done.2.relayed_ref
  21.8 0.0 collective-permute-done.3.second_ref.refs_2_
  21.9 0.1 collective-permute-start.6
  22.0 0.1 collective-permute-start.4
  22.1 3.8 %collective-permute-start.7 = (bf16[1,1,320,128]{3,2,1,0:T(8,128)(2,1)S(1)}, bf16[1,1,320,128]{3,2,1,0:T(8,128)(2,1)S(1)}, u32[]{:S(2)}, u32[]{:S(2)}) collective-permute-start(bf16[1,1,320,128]{3,2,1,0:T(8,128)(2,1)S(1)} %get-tuple-element.46), channel_id=1, source_target_pairs={{0,8},{16,24},{24,16},{1,9},{17,25},{25,17},{2,10},{18,26},{26,18}... | collective-permute-start | bytes 245768 | tf_op jit(solution)/shard_map/ppermute | solution.py:41
  25.9 0.0 collective-permute-done.4.refs_0_
  25.9 2.9 %shard_map.61 = (bf16[8,320,128]{2,1,0:T(8,128)(2,1)S(1)}, bf16[2,960,128]{2,1,0:T(8,128)(2,1)S(1)}) custom-call(f32[16,320,128]{2,1,0:T(8,128)S(1)} %shard_map.59.own_ref, bf16[320,2880]{1,0:T(8,128)(2,1)S(1)} %get-tuple-element.33.wide_ref, bf16[320,960]{1,0:T(8,128)(2,1)S(1)} %get-tuple-element.29.mix_ref, f32[320,128]{1,0:T(8,128)S(1)} %get-tuple-element.30.cb_ref, ...), custom_call_target="tpu_custom_call" | custom-call | tf_op jit(solution)/shard_map/pallas_call | solution.py:285
  28.9 0.0 collective-permute-done.5.refs_1_
  28.9 1.6 %shard_map.62 = (bf16[16,320,128]{2,1,0:T(8,128)(2,1)}, bf16[4,320,128]{2,1,0:T(8,128)(2,1)S(1)}, bf16[2,960,128]{2,1,0:T(8,128)(2,1)S(1)}) custom-call(f32[16,320,128]{2,1,0:T(8,128)S(1)} %shard_map.59.own_ref, bf16[320,2880]{1,0:T(8,128)(2,1)S(1)} %get-tuple-element.33.wide_ref, bf16[320,960]{1,0:T(8,128)(2,1)S(1)} %get-tuple-element.29.mix_ref, ...), custom_call_target="tpu_custom_call" | custom-call | tf_op jit(solution)/shard_map/pallas_call | solution.py:285
  30.5 0.1 collective-permute-done.6.refs_1_
  30.6 1.1 %shard_map.63 = (bf16[16,320,128]{2,1,0:T(8,128)(2,1)}, bf16[2,320,128]{2,1,0:T(8,128)(2,1)S(1)}, bf16[2,960,128]{2,1,0:T(8,128)(2,1)S(1)}) custom-call(f32[16,320,128]{2,1,0:T(8,128)S(1)} %shard_map.59.own_ref, bf16[320,2880]{1,0:T(8,128)(2,1)S(1)} %get-tuple-element.33.wide_ref, ...), custom_call_target="tpu_custom_call", output_to_operand_aliasing={{0}: (7, {})} | custom-call | tf_op jit(solution)/shard_map/pallas_call | solution.py:285
  31.7 0.0 collective-permute-done.7.refs_1_
  31.7 1.8 %shard_map.64 = bf16[16,320,128]{2,1,0:T(8,128)(2,1)} custom-call(f32[16,320,128]{2,1,0:T(8,128)S(1)} %shard_map.59.own_ref, bf16[320,2880]{1,0:T(8,128)(2,1)S(1)} %get-tuple-element.33.wide_ref, bf16[320,960]{1,0:T(8,128)(2,1)S(1)} %get-tuple-element.29.mix_ref, f32[320,128]{1,0:T(8,128)S(1)} %get-tuple-element.30.cb_ref, ...), custom_call_target="tpu_custom_call", output_to_operand_aliasing={{}: (7, {})} | custom-call | tf_op jit(solution)/shard_map/pallas_call | solution.py:285
  (3 shorter events, 0.0 us)
Async XLA Ops:
  1.0 10.4 %collective-permute-start.1 = (bf16[1,3,320,128]{3,2,1,0:T(8,128)(2,1)S(1)}, bf16[1,3,320,128]{3,2,1,0:T(8,128)(2,1)S(1)}, u32[]{:S(2)}, u32[]{:S(2)}) collective-permute-start(bf16[1,3,320,128]{3,2,1,0:T(8,128)(2,1)S(1)} %shard_map.55.head_ref), channel_id=1, source_target_pairs={{0,8},{8,16},{16,24},{24,0},{1,9},{9,17},{17,25},{25,1},{2,10},{10... | collective-permute-start | bytes 737288 | tf_op jit(solution)/shard_map/ppermute | solution.py:336
  2.5 3.3 %copy-start.1 = (bf16[3,320,320]{2,1,0:T(8,128)(2,1)S(1)}, bf16[3,320,320]{2,1,0:T(8,128)(2,1)}, u32[]{:S(2)}) copy-start(bf16[3,320,320]{2,1,0:T(8,128)(2,1)} %wt_ref.1) | copy-start | bytes 1843204
  4.3 1.4 %copy-start.2 = (f32[320]{0:T(512)S(1)}, f32[320]{0:T(512)}, u32[]{:S(2)}) copy-start(f32[320]{0:T(512)} %param.7) | copy-start | bytes 3844
  4.3 1.4 %copy-start.3 = (f32[320]{0:T(512)S(1)}, f32[320]{0:T(512)}, u32[]{:S(2)}) copy-start(f32[320]{0:T(512)} %param.9) | copy-start | bytes 3844
  4.4 1.6 %copy-start = (bf16[3,3,320,320]{3,2,1,0:T(8,128)(2,1)S(1)}, bf16[3,3,320,320]{3,2,1,0:T(8,128)(2,1)}, u32[]{:S(2)}) copy-start(bf16[3,3,320,320]{3,2,1,0:T(8,128)(2,1)} %ws_ref.1) | copy-start | bytes 5529604
  4.5 6.9 %collective-permute-start = (bf16[2,1,320,128]{3,2,1,0:T(8,128)(2,1)S(1)}, bf16[2,1,320,128]{3,2,1,0:T(8,128)(2,1)S(1)}, u32[]{:S(2)}, u32[]{:S(2)}) collective-permute-start(bf16[2,1,320,128]{3,2,1,0:T(8,128)(2,1)S(1)} %get-tuple-element.27), channel_id=1, source_target_pairs={{0,4},{4,0},{1,5},{5,1},{2,6},{6,2},{3,7},{7,3},{8,12},{12,8},{9,1... | collective-permute-start | bytes 491528 | tf_op jit(solution)/shard_map/ppermute | solution.py:338
  4.5 17.3 %collective-permute-start.3 = (bf16[1,6,320,128]{3,2,1,0:T(8,128)(2,1)S(1)}, bf16[1,6,320,128]{3,2,1,0:T(8,128)(2,1)S(1)}, u32[]{:S(2)}, u32[]{:S(2)}) collective-permute-start(bf16[1,6,320,128]{3,2,1,0:T(8,128)(2,1)S(1)} %get-tuple-element.36), channel_id=1, source_target_pairs={{0,8},{8,16},{16,24},{24,0},{1,9},{9,17},{17,25},{25,1},{2,10},{10... | collective-permute-start | bytes 1474568 | tf_op jit(solution)/shard_map/ppermute | solution.py:336
  5.1 16.8 %collective-permute-start.2 = (bf16[1,3,320,128]{3,2,1,0:T(8,128)(2,1)S(1)}, bf16[1,3,320,128]{3,2,1,0:T(8,128)(2,1)S(1)}, u32[]{:S(2)}, u32[]{:S(2)}) collective-permute-start(bf16[1,3,320,128]{3,2,1,0:T(8,128)(2,1)S(1)} %get-tuple-element.35.tail_ref), channel_id=1, source_target_pairs={{8,24},{24,8},{9,25},{25,9},{10,26},{26,10},{11,27},{27,11},{12,28... | collective-permute-start | bytes 737288 | tf_op jit(solution)/shard_map/ppermute | solution.py:35
  7.3 21.6 %collective-permute-start.5 = (bf16[1,4,320,128]{3,2,1,0:T(8,128)(2,1)S(1)}, bf16[1,4,320,128]{3,2,1,0:T(8,128)(2,1)S(1)}, u32[]{:S(2)}, u32[]{:S(2)}) collective-permute-start(bf16[1,4,320,128]{3,2,1,0:T(8,128)(2,1)S(1)} %get-tuple-element.39), channel_id=1, source_target_pairs={{0,8},{8,16},{16,24},{24,0},{1,9},{9,17},{17,25},{25,1},{2,10},{10... | collective-permute-start | bytes 983048 | tf_op jit(solution)/shard_map/ppermute | solution.py:352
  21.9 8.7 %collective-permute-start.6 = (bf16[1,2,320,128]{3,2,1,0:T(8,128)(2,1)S(1)}, bf16[1,2,320,128]{3,2,1,0:T(8,128)(2,1)S(1)}, u32[]{:S(2)}, u32[]{:S(2)}) collective-permute-start(bf16[1,2,320,128]{3,2,1,0:T(8,128)(2,1)S(1)} %get-tuple-element.42), channel_id=1, source_target_pairs={{0,8},{8,0},{16,24},{24,16},{1,9},{9,1},{17,25},{25,17},{2,10},{10... | collective-permute-start | bytes 491528 | tf_op jit(solution)/shard_map/ppermute | solution.py:41
  22.0 3.9 %collective-permute-start.4 = (bf16[1,320,128]{2,1,0:T(8,128)(2,1)S(1)}, bf16[1,320,128]{2,1,0:T(8,128)(2,1)S(1)}, u32[]{:S(2)}, u32[]{:S(2)}) collective-permute-start(bf16[1,320,128]{2,1,0:T(8,128)(2,1)S(1)} %get-tuple-element.37), channel_id=1, source_target_pairs={{0,4},{4,0},{1,5},{5,1},{2,6},{6,2},{3,7},{7,3},{8,12},{12,8},{9,1... | collective-permute-start | bytes 245768 | tf_op jit(solution)/shard_map/ppermute | solution.py:373
  22.1 9.7 %collective-permute-start.7 = (bf16[1,1,320,128]{3,2,1,0:T(8,128)(2,1)S(1)}, bf16[1,1,320,128]{3,2,1,0:T(8,128)(2,1)S(1)}, u32[]{:S(2)}, u32[]{:S(2)}) collective-permute-start(bf16[1,1,320,128]{3,2,1,0:T(8,128)(2,1)S(1)} %get-tuple-element.46), channel_id=1, source_target_pairs={{0,8},{16,24},{24,16},{1,9},{17,25},{25,17},{2,10},{18,26},{26,18}... | collective-permute-start | bytes 245768 | tf_op jit(solution)/shard_map/ppermute | solution.py:41

commit v13 on v12

--- a/solution.py
+++ b/solution.py
@@ -324,32 +324,33 @@
         compiler_params=pltpu.CompilerParams(vmem_limit_bytes=LOAD_LIMIT),
         cost_estimate=cost(0, 0),
     )(x, head)
-    kept_spans = [(0, frames, 0, 1), (frames - 1, 1, places[-2], sizes[-2] + sizes[-1]), spans[1]]
-    boundary, tail, second = pl.pallas_call(
+    ending = (frames - 1, 1, places[-2], sizes[-2] + sizes[-1])
+    kept_spans = [(0, frames, 0, 1), spans[1]]
+    boundary, second = pl.pallas_call(
         functools.partial(keep_kernel, spans=kept_spans),
         out_shape=row_shapes(x, kept_spans),
         in_specs=[VMEM],
-        out_specs=[VMEM] * 3,
+        out_specs=[VMEM] * 2,
         compiler_params=PARAMS,
         cost_estimate=cost(0, 0),
     )(x)
     arrived = [lax.ppermute(piece, "frames", ring("frames")) for piece in (head, second)]
-    relayed = next_odd(tail, "frames")
     beside = lax.ppermute(boundary, "rows", ring("rows"))
 
     square = jax.ShapeDtypeStruct((3 * channels, 3 * channels), BF16)
     broad = jax.ShapeDtypeStruct((channels, 9 * channels), BF16)
     flat = jax.ShapeDtypeStruct((channels, 3 * channels), BF16)
     bias = jax.ShapeDtypeStruct((channels, width), F32)
-    conv, wide, mix, cb, mb, *pieces = pl.pallas_call(
-        functools.partial(prepare_kernel, spans=spans[2:3]),
-        out_shape=[square, broad, flat, bias, bias] + row_shapes(x, spans[2:3]),
+    conv, wide, mix, cb, mb, piece, tail = pl.pallas_call(
+        functools.partial(prepare_kernel, spans=[spans[2], ending]),
+        out_shape=[square, broad, flat, bias, bias] + row_shapes(x, [spans[2], ending]),
         in_specs=[VMEM] * 5,
-        out_specs=[VMEM] * 6,
+        out_specs=[VMEM] * 7,
         compiler_params=PARAMS,
         cost_estimate=cost(0, 2 * 12 * channels * channels * 2),
     )(x, w_spatial, b_spatial.reshape(1, channels), w_temporal, b_temporal.reshape(1, channels))
-    arrived += [lax.ppermute(piece, "frames", ring("frames")) for piece in pieces]
+    arrived.append(lax.ppermute(piece, "frames", ring("frames")))
+    relayed = next_odd(tail, "frames")
 
     own = pl.pallas_call(
         functools.partial(own_kernel, group=next(g for g in (8, 4, 3, 2, 1) if rows % g == 0)),
@@ -369,7 +370,7 @@
         compiler_params=PARAMS,
         cost_estimate=cost(0, 0),
     )(arrived[0], tail, relayed, arrived[1])
-    arrived += [within_pairs(pieces[0], "frames", True), within_pairs(pieces[1], "frames", False)]
+    arrived += [within_pairs(pieces[0], "frames", True), within_pairs(pieces[1], "frames", True)]
     kept = lax.ppermute(edge, "rows", ring("rows"))
 
     weights = (wide, mix, cb)

time: 34 us -> 34.1 us (level)
  starting transfers between devices: 10.9 us -> 8.29 us
  waiting for transfers between devices: 0.12 us -> 2.1 us
  local copies, waits for them, and re-layouts: 0.24 us -> 0.96 us
    ppermute x3 -> x2, starting transfers between devices: 6.18 us -> 2.07 us  [per_device(): lax.ppermute(piece, 'frames', ring('frames'))]
    ppermute x0 -> x1, starting transfers between devices: none -> 3.39 us  [per_device(): arrived.append(lax.ppermute(piece, 'frames', ring('frames')))]
    ppermute x2, starting transfers between devices: 3.93 us -> 2.04 us  [within_pairs(): return lax.ppermute(piece, axis, [(a, b) for a, b in route if b or keep])]
    ppermute x0 -> x1, waiting for transfers between devices: none -> 1.3 us  [per_device(): arrived.append(lax.ppermute(piece, 'frames', ring('frames')))]
    unnamed x8, local copies, waits for them, and re-layouts: 0.24 us -> 0.95 us
    ppermute x2, waiting for transfers between devices: 0.1 us -> 0.79 us  [within_pairs(): return lax.ppermute(piece, axis, [(a, b) for a, b in route if b or keep])]
  transfers between devices with their start and end apart: 8 -> 8, of which waited for: 1 -> 2; matrix products, arithmetic and copies ran while one was open for 0% -> 0% of each run, Pallas kernels for 58% -> 58%
where the time goes in v13:
time: 34.1 us; the launch traced here: 33.5 us
  Pallas kernels  22 us (65%)
  starting transfers between devices  8.29 us (24%)
  waiting for transfers between devices  2.1 us (6%)
  local copies, waits for them, and re-layouts  0.96 us (3%)
    pallas_call x1, Pallas kernels, per_device(): pl.pallas_call(functools.partial(own_kernel, group=next((g for g in (8, 4...  10.4 us
    pallas_call x4, Pallas kernels, incoming_rows(): pl.pallas_call(functools.partial(incoming_kernel, pieces=len(pieces), low...  7.42 us
    ppermute x1, starting transfers between devices, per_device(): arrived.append(lax.ppermute(piece, 'frames', ring('frames')))  3.39 us
    ppermute x2, starting transfers between devices, per_device(): lax.ppermute(piece, 'frames', ring('frames'))  2.07 us
    ppermute x2, starting transfers between devices, within_pairs(): return lax.ppermute(piece, axis, [(a, b) for a, b in route if b or keep])  2.04 us
    pallas_call x1, Pallas kernels, per_device(): pl.pallas_call(functools.partial(load_kernel, spans=whole), out_shape=row...  1.82 us
    ppermute x1, waiting for transfers between devices, per_device(): arrived.append(lax.ppermute(piece, 'frames', ring('frames')))  1.3 us
    pallas_call x1, Pallas kernels, per_device(): pl.pallas_call(functools.partial(prepare_kernel, spans=[spans[2], ending]...  1.29 us
  transfers between devices with their start and end apart: 8, of which 2 were waited for; matrix products, arithmetic and copies ran while one was open for 0% of the time, Pallas kernels for 58%

profile of v13, /device:TPU:20, one launch (start us, length us, event | category | flops | bytes accessed | tf_op | source)
XLA Modules:
  0.0 33.5 jit_solution(10043699164147899377)
XLA Ops:
  0.0 1.0 %shard_map.55.head_ref = bf16[1,3,320,128]{3,2,1,0:T(8,128)(2,1)S(1)} custom-call(bf16[2,16,320,128]{3,2,1,0:T(8,128)(2,1)} %bitcast.4), custom_call_target="tpu_custom_call" | custom-call | tf_op jit(solution)/shard_map/pallas_call | solution.py:309
  1.0 1.5 %collective-permute-start.1 = (bf16[1,3,320,128]{3,2,1,0:T(8,128)(2,1)S(1)}, bf16[1,3,320,128]{3,2,1,0:T(8,128)(2,1)S(1)}, u32[]{:S(2)}, u32[]{:S(2)}) collective-permute-start(bf16[1,3,320,128]{3,2,1,0:T(8,128)(2,1)S(1)} %shard_map.55.head_ref), channel_id=1, source_target_pairs={{0,8},{8,16},{16,24},{24,0},{1,9},{9,17},{17,25},{25,1},{2,10},{10... | collective-permute-start | bytes 737288 | tf_op jit(solution)/shard_map/ppermute | solution.py:337
  2.5 0.0 copy-start.1
  2.5 1.8 %shard_map.56.x_ref = bf16[2,16,320,128]{3,2,1,0:T(8,128)(2,1)S(1)} custom-call(bf16[2,16,320,128]{3,2,1,0:T(8,128)(2,1)} %bitcast.5, bf16[1,3,320,128]{3,2,1,0:T(8,128)(2,1)S(1)} %shard_map.55.head_ref), custom_call_target="tpu_custom_call" | custom-call | tf_op jit(solution)/shard_map/pallas_call | solution.py:318
  4.3 0.0 copy-start.2
  4.3 0.0 copy-start.3
  4.4 0.0 copy-start
  4.4 0.1 shard_map.57
  4.4 0.1 collective-permute-start
  4.5 0.5 %collective-permute-start.3 = (bf16[1,6,320,128]{3,2,1,0:T(8,128)(2,1)S(1)}, bf16[1,6,320,128]{3,2,1,0:T(8,128)(2,1)S(1)}, u32[]{:S(2)}, u32[]{:S(2)}) collective-permute-start(bf16[1,6,320,128]{3,2,1,0:T(8,128)(2,1)S(1)} %get-tuple-element.36), channel_id=1, source_target_pairs={{0,8},{8,16},{16,24},{24,0},{1,9},{9,17},{17,25},{25,1},{2,10},{10... | collective-permute-start | bytes 1474568 | tf_op jit(solution)/shard_map/ppermute | solution.py:337
  5.0 0.0 copy-done.2
  5.0 0.0 copy-done.3
  5.1 0.0 copy-done.1
  5.1 0.9 %copy-done = bf16[3,3,320,320]{3,2,1,0:T(8,128)(2,1)S(1)} copy-done((bf16[3,3,320,320]{3,2,1,0:T(8,128)(2,1)S(1)}, bf16[3,3,320,320]{3,2,1,0:T(8,128)(2,1)}, u32[]{:S(2)}) %copy-start) | copy-done | bytes 1843224
  6.0 1.3 %shard_map.58 = (bf16[960,960]{1,0:T(8,128)(2,1)S(1)}, bf16[320,2880]{1,0:T(8,128)(2,1)S(1)}, bf16[320,960]{1,0:T(8,128)(2,1)S(1)}, f32[320,128]{1,0:T(8,128)S(1...) custom-call(bf16[2,16,320,128]{3,2,1,0:T(8,128)(2,1)S(1)} %shard_map.56.x_ref,, ...), custom_call_target="tpu_custom_call" | custom-call | bytes 4915200 | tf_op jit(solution)/shard_map/pallas_call | solution.py:344
  7.3 0.7 %collective-permute-start.2 = (bf16[1,3,320,128]{3,2,1,0:T(8,128)(2,1)S(1)}, bf16[1,3,320,128]{3,2,1,0:T(8,128)(2,1)S(1)}, u32[]{:S(2)}, u32[]{:S(2)}) collective-permute-start(bf16[1,3,320,128]{3,2,1,0:T(8,128)(2,1)S(1)} %get-tuple-element.35.tail_ref), channel_id=1, source_target_pairs={{8,24},{24,8},{9,25},{25,9},{10,26},{26,10},{11,27},{27,11},{12,28... | collective-permute-start | bytes 737288 | tf_op jit(solution)/shard_map/ppermute | solution.py:35
  8.0 3.4 %collective-permute-start.5 = (bf16[1,4,320,128]{3,2,1,0:T(8,128)(2,1)S(1)}, bf16[1,4,320,128]{3,2,1,0:T(8,128)(2,1)S(1)}, u32[]{:S(2)}, u32[]{:S(2)}) collective-permute-start(bf16[1,4,320,128]{3,2,1,0:T(8,128)(2,1)S(1)} %get-tuple-element.39), channel_id=1, source_target_pairs={{0,8},{8,16},{16,24},{24,0},{1,9},{9,17},{17,25},{25,1},{2,10},{10... | collective-permute-start | bytes 983048 | tf_op jit(solution)/shard_map/ppermute | solution.py:352
  11.4 0.0 collective-permute-done.beside_ref
  11.4 0.0 collective-permute-done.1.early_ref.piece_ref.refs_1_
  11.4 10.4 %shard_map.59.own_ref = f32[16,320,128]{2,1,0:T(8,128)S(1)} custom-call(bf16[2,16,320,128]{3,2,1,0:T(8,128)(2,1)S(1)} %shard_map.56.x_ref, bf16[2,1,320,128]{3,2,1,0:T(8,128)(2,1)S(1)} %collective-permute-done.beside_ref, bf16[960,960]{1,0:T(8,128)(2,1)S(1)} %get-tuple-element.28.conv_ref, bf16[320,960]{1,0:T(8,128)(2,1)S(1)} %get-tuple-element.29.mix_ref, ...), custom_call_target="tpu_custom_call" | custom-call | flops 8388608000 | bytes 5242880 | tf_op jit(solution)/shard_map/pallas_call | solution.py:355
  21.8 0.0 collective-permute-done.2.relayed_ref
  21.8 0.0 collective-permute-done.3.second_ref.refs_2_
  21.9 0.1 collective-permute-start.6
  22.0 0.0 collective-permute-start.4
  22.0 1.9 %collective-permute-start.7 = (bf16[1,1,320,128]{3,2,1,0:T(8,128)(2,1)S(1)}, bf16[1,1,320,128]{3,2,1,0:T(8,128)(2,1)S(1)}, u32[]{:S(2)}, u32[]{:S(2)}) collective-permute-start(bf16[1,1,320,128]{3,2,1,0:T(8,128)(2,1)S(1)} %get-tuple-element.46), channel_id=1, source_target_pairs={{0,8},{8,0},{16,24},{24,16},{1,9},{9,1},{17,25},{25,17},{2,10},{10... | collective-permute-start | bytes 245768 | tf_op jit(solution)/shard_map/ppermute | solution.py:41
  24.0 0.0 collective-permute-done.4.refs_0_
  24.0 2.9 %shard_map.61 = (bf16[8,320,128]{2,1,0:T(8,128)(2,1)S(1)}, bf16[2,960,128]{2,1,0:T(8,128)(2,1)S(1)}) custom-call(f32[16,320,128]{2,1,0:T(8,128)S(1)} %shard_map.59.own_ref, bf16[320,2880]{1,0:T(8,128)(2,1)S(1)} %get-tuple-element.33.wide_ref, bf16[320,960]{1,0:T(8,128)(2,1)S(1)} %get-tuple-element.29.mix_ref, f32[320,128]{1,0:T(8,128)S(1)} %get-tuple-element.30.cb_ref, ...), custom_call_target="tpu_custom_call" | custom-call | tf_op jit(solution)/shard_map/pallas_call | solution.py:285
  26.9 1.3 %collective-permute-done.5.refs_1_ = bf16[1,4,320,128]{3,2,1,0:T(8,128)(2,1)S(1)} collective-permute-done((bf16[1,4,320,128]{3,2,1,0:T(8,128)(2,1)S(1)}, bf16[1,4,320,128]{3,2,1,0:T(8,128)(2,1)S(1)}, u32[]{:S(2)}, u32[]{:S(2)}) %collective-permute-start.5) | collective-permute-done | bytes 327712 | tf_op jit(solution)/shard_map/ppermute | solution.py:352
  28.2 1.6 %shard_map.62 = (bf16[16,320,128]{2,1,0:T(8,128)(2,1)}, bf16[4,320,128]{2,1,0:T(8,128)(2,1)S(1)}, bf16[2,960,128]{2,1,0:T(8,128)(2,1)S(1)}) custom-call(f32[16,320,128]{2,1,0:T(8,128)S(1)} %shard_map.59.own_ref, bf16[320,2880]{1,0:T(8,128)(2,1)S(1)} %get-tuple-element.33.wide_ref, bf16[320,960]{1,0:T(8,128)(2,1)S(1)} %get-tuple-element.29.mix_ref, ...), custom_call_target="tpu_custom_call" | custom-call | tf_op jit(solution)/shard_map/pallas_call | solution.py:285
  29.8 0.8 %collective-permute-done.6.refs_1_ = bf16[1,2,320,128]{3,2,1,0:T(8,128)(2,1)S(1)} collective-permute-done((bf16[1,2,320,128]{3,2,1,0:T(8,128)(2,1)S(1)}, bf16[1,2,320,128]{3,2,1,0:T(8,128)(2,1)S(1)}, u32[]{:S(2)}, u32[]{:S(2)}) %collective-permute-start.6) | collective-permute-done | bytes 163872 | tf_op jit(solution)/shard_map/ppermute | solution.py:41
  30.6 1.1 %shard_map.63 = (bf16[16,320,128]{2,1,0:T(8,128)(2,1)}, bf16[2,320,128]{2,1,0:T(8,128)(2,1)S(1)}, bf16[2,960,128]{2,1,0:T(8,128)(2,1)S(1)}) custom-call(f32[16,320,128]{2,1,0:T(8,128)S(1)} %shard_map.59.own_ref, bf16[320,2880]{1,0:T(8,128)(2,1)S(1)} %get-tuple-element.33.wide_ref, ...), custom_call_target="tpu_custom_call", output_to_operand_aliasing={{0}: (7, {})} | custom-call | tf_op jit(solution)/shard_map/pallas_call | solution.py:285
  31.7 0.0 collective-permute-done.7.refs_1_
  31.7 1.8 %shard_map.64 = bf16[16,320,128]{2,1,0:T(8,128)(2,1)} custom-call(f32[16,320,128]{2,1,0:T(8,128)S(1)} %shard_map.59.own_ref, bf16[320,2880]{1,0:T(8,128)(2,1)S(1)} %get-tuple-element.33.wide_ref, bf16[320,960]{1,0:T(8,128)(2,1)S(1)} %get-tuple-element.29.mix_ref, f32[320,128]{1,0:T(8,128)S(1)} %get-tuple-element.30.cb_ref, ...), custom_call_target="tpu_custom_call", output_to_operand_aliasing={{}: (7, {})} | custom-call | tf_op jit(solution)/shard_map/pallas_call | solution.py:285
  (3 shorter events, 0.0 us)
Async XLA Ops:
  1.0 10.4 %collective-permute-start.1 = (bf16[1,3,320,128]{3,2,1,0:T(8,128)(2,1)S(1)}, bf16[1,3,320,128]{3,2,1,0:T(8,128)(2,1)S(1)}, u32[]{:S(2)}, u32[]{:S(2)}) collective-permute-start(bf16[1,3,320,128]{3,2,1,0:T(8,128)(2,1)S(1)} %shard_map.55.head_ref), channel_id=1, source_target_pairs={{0,8},{8,16},{16,24},{24,0},{1,9},{9,17},{17,25},{25,1},{2,10},{10... | collective-permute-start | bytes 737288 | tf_op jit(solution)/shard_map/ppermute | solution.py:337
  2.5 2.6 %copy-start.1 = (bf16[3,320,320]{2,1,0:T(8,128)(2,1)S(1)}, bf16[3,320,320]{2,1,0:T(8,128)(2,1)}, u32[]{:S(2)}) copy-start(bf16[3,320,320]{2,1,0:T(8,128)(2,1)} %wt_ref.1) | copy-start | bytes 1843204
  4.3 0.7 %copy-start.2 = (f32[320]{0:T(512)S(1)}, f32[320]{0:T(512)}, u32[]{:S(2)}) copy-start(f32[320]{0:T(512)} %param.7) | copy-start | bytes 3844
  4.3 0.7 %copy-start.3 = (f32[320]{0:T(512)S(1)}, f32[320]{0:T(512)}, u32[]{:S(2)}) copy-start(f32[320]{0:T(512)} %param.9) | copy-start | bytes 3844
  4.4 1.6 %copy-start = (bf16[3,3,320,320]{3,2,1,0:T(8,128)(2,1)S(1)}, bf16[3,3,320,320]{3,2,1,0:T(8,128)(2,1)}, u32[]{:S(2)}) copy-start(bf16[3,3,320,320]{3,2,1,0:T(8,128)(2,1)} %ws_ref.1) | copy-start | bytes 5529604
  4.4 6.9 %collective-permute-start = (bf16[2,1,320,128]{3,2,1,0:T(8,128)(2,1)S(1)}, bf16[2,1,320,128]{3,2,1,0:T(8,128)(2,1)S(1)}, u32[]{:S(2)}, u32[]{:S(2)}) collective-permute-start(bf16[2,1,320,128]{3,2,1,0:T(8,128)(2,1)S(1)} %get-tuple-element.27), channel_id=1, source_target_pairs={{0,4},{4,0},{1,5},{5,1},{2,6},{6,2},{3,7},{7,3},{8,12},{12,8},{9,1... | collective-permute-start | bytes 491528 | tf_op jit(solution)/shard_map/ppermute | solution.py:338
  4.5 17.3 %collective-permute-start.3 = (bf16[1,6,320,128]{3,2,1,0:T(8,128)(2,1)S(1)}, bf16[1,6,320,128]{3,2,1,0:T(8,128)(2,1)S(1)}, u32[]{:S(2)}, u32[]{:S(2)}) collective-permute-start(bf16[1,6,320,128]{3,2,1,0:T(8,128)(2,1)S(1)} %get-tuple-element.36), channel_id=1, source_target_pairs={{0,8},{8,16},{16,24},{24,0},{1,9},{9,17},{17,25},{25,1},{2,10},{10... | collective-permute-start | bytes 1474568 | tf_op jit(solution)/shard_map/ppermute | solution.py:337
  7.3 14.5 %collective-permute-start.2 = (bf16[1,3,320,128]{3,2,1,0:T(8,128)(2,1)S(1)}, bf16[1,3,320,128]{3,2,1,0:T(8,128)(2,1)S(1)}, u32[]{:S(2)}, u32[]{:S(2)}) collective-permute-start(bf16[1,3,320,128]{3,2,1,0:T(8,128)(2,1)S(1)} %get-tuple-element.35.tail_ref), channel_id=1, source_target_pairs={{8,24},{24,8},{9,25},{25,9},{10,26},{26,10},{11,27},{27,11},{12,28... | collective-permute-start | bytes 737288 | tf_op jit(solution)/shard_map/ppermute | solution.py:35
  8.0 20.2 %collective-permute-start.5 = (bf16[1,4,320,128]{3,2,1,0:T(8,128)(2,1)S(1)}, bf16[1,4,320,128]{3,2,1,0:T(8,128)(2,1)S(1)}, u32[]{:S(2)}, u32[]{:S(2)}) collective-permute-start(bf16[1,4,320,128]{3,2,1,0:T(8,128)(2,1)S(1)} %get-tuple-element.39), channel_id=1, source_target_pairs={{0,8},{8,16},{16,24},{24,0},{1,9},{9,17},{17,25},{25,1},{2,10},{10... | collective-permute-start | bytes 983048 | tf_op jit(solution)/shard_map/ppermute | solution.py:352
  21.9 8.7 %collective-permute-start.6 = (bf16[1,2,320,128]{3,2,1,0:T(8,128)(2,1)S(1)}, bf16[1,2,320,128]{3,2,1,0:T(8,128)(2,1)S(1)}, u32[]{:S(2)}, u32[]{:S(2)}) collective-permute-start(bf16[1,2,320,128]{3,2,1,0:T(8,128)(2,1)S(1)} %get-tuple-element.42), channel_id=1, source_target_pairs={{0,8},{8,0},{16,24},{24,16},{1,9},{9,1},{17,25},{25,17},{2,10},{10... | collective-permute-start | bytes 491528 | tf_op jit(solution)/shard_map/ppermute | solution.py:41
  22.0 2.0 %collective-permute-start.4 = (bf16[1,320,128]{2,1,0:T(8,128)(2,1)S(1)}, bf16[1,320,128]{2,1,0:T(8,128)(2,1)S(1)}, u32[]{:S(2)}, u32[]{:S(2)}) collective-permute-start(bf16[1,320,128]{2,1,0:T(8,128)(2,1)S(1)} %get-tuple-element.37), channel_id=1, source_target_pairs={{0,4},{4,0},{1,5},{5,1},{2,6},{6,2},{3,7},{7,3},{8,12},{12,8},{9,1... | collective-permute-start | bytes 245768 | tf_op jit(solution)/shard_map/ppermute | solution.py:374
  22.0 9.7 %collective-permute-start.7 = (bf16[1,1,320,128]{3,2,1,0:T(8,128)(2,1)S(1)}, bf16[1,1,320,128]{3,2,1,0:T(8,128)(2,1)S(1)}, u32[]{:S(2)}, u32[]{:S(2)}) collective-permute-start(bf16[1,1,320,128]{3,2,1,0:T(8,128)(2,1)S(1)} %get-tuple-element.46), channel_id=1, source_target_pairs={{0,8},{8,0},{16,24},{24,16},{1,9},{9,1},{17,25},{25,17},{2,10},{10... | collective-permute-start | bytes 245768 | tf_op jit(solution)/shard_map/ppermute | solution.py:41

commit v14 on v13

--- a/solution.py
+++ b/solution.py
@@ -370,7 +370,7 @@
         compiler_params=PARAMS,
         cost_estimate=cost(0, 0),
     )(arrived[0], tail, relayed, arrived[1])
-    arrived += [within_pairs(pieces[0], "frames", True), within_pairs(pieces[1], "frames", True)]
+    arrived += [within_pairs(pieces[0], "frames", True), within_pairs(pieces[1], "frames", False)]
     kept = lax.ppermute(edge, "rows", ring("rows"))
 
     weights = (wide, mix, cb)

time: 34.1 us -> 34 us (level)
  waiting for transfers between devices: 2.1 us -> 0.14 us
  starting transfers between devices: 8.29 us -> 10.2 us
    ppermute x2, starting transfers between devices: 2.04 us -> 3.93 us  [within_pairs(): return lax.ppermute(piece, axis, [(a, b) for a, b in route if b or keep])]
    ppermute x1, waiting for transfers between devices: 1.3 us -> 0.01 us  [per_device(): arrived.append(lax.ppermute(piece, 'frames', ring('frames')))]
    ppermute x2, waiting for transfers between devices: 0.79 us -> 0.12 us  [within_pairs(): return lax.ppermute(piece, axis, [(a, b) for a, b in route if b or keep])]
  transfers between devices with their start and end apart: 8 -> 8, of which waited for: 2 -> 1; matrix products, arithmetic and copies ran while one was open for 0% -> 0% of each run, Pallas kernels for 58% -> 58%
where the time goes in v14:
time: 34 us; the launch traced here: 33.5 us
  Pallas kernels  22 us (65%)
  starting transfers between devices  10.2 us (30%)
  local copies, waits for them, and re-layouts  0.96 us (3%)
    pallas_call x1, Pallas kernels, per_device(): pl.pallas_call(functools.partial(own_kernel, group=next((g for g in (8, 4...  10.4 us
    pallas_call x4, Pallas kernels, incoming_rows(): pl.pallas_call(functools.partial(incoming_kernel, pieces=len(pieces), low...  7.46 us
    ppermute x2, starting transfers between devices, within_pairs(): return lax.ppermute(piece, axis, [(a, b) for a, b in route if b or keep])  3.93 us
    ppermute x1, starting transfers between devices, per_device(): arrived.append(lax.ppermute(piece, 'frames', ring('frames')))  3.39 us
    ppermute x2, starting transfers between devices, per_device(): lax.ppermute(piece, 'frames', ring('frames'))  2.07 us
    pallas_call x1, Pallas kernels, per_device(): pl.pallas_call(functools.partial(load_kernel, spans=whole), out_shape=row...  1.82 us
    pallas_call x1, Pallas kernels, per_device(): pl.pallas_call(functools.partial(prepare_kernel, spans=[spans[2], ending]...  1.29 us
    unnamed x8, local copies, waits for them, and re-layouts  0.95 us
  transfers between devices with their start and end apart: 8, of which 1 were waited for; matrix products, arithmetic and copies ran while one was open for 0% of the time, Pallas kernels for 58%

profile of v14, /device:TPU:20, one launch (start us, length us, event | category | flops | bytes accessed | tf_op | source)
XLA Modules:
  0.0 33.5 jit_solution(11515694529877291666)
XLA Ops:
  0.0 1.0 %shard_map.55.head_ref = bf16[1,3,320,128]{3,2,1,0:T(8,128)(2,1)S(1)} custom-call(bf16[2,16,320,128]{3,2,1,0:T(8,128)(2,1)} %bitcast.4), custom_call_target="tpu_custom_call" | custom-call | tf_op jit(solution)/shard_map/pallas_call | solution.py:309
  1.0 1.5 %collective-permute-start.1 = (bf16[1,3,320,128]{3,2,1,0:T(8,128)(2,1)S(1)}, bf16[1,3,320,128]{3,2,1,0:T(8,128)(2,1)S(1)}, u32[]{:S(2)}, u32[]{:S(2)}) collective-permute-start(bf16[1,3,320,128]{3,2,1,0:T(8,128)(2,1)S(1)} %shard_map.55.head_ref), channel_id=1, source_target_pairs={{0,8},{8,16},{16,24},{24,0},{1,9},{9,17},{17,25},{25,1},{2,10},{10... | collective-permute-start | bytes 737288 | tf_op jit(solution)/shard_map/ppermute | solution.py:337
  2.5 0.0 copy-start.1
  2.5 1.8 %shard_map.56.x_ref = bf16[2,16,320,128]{3,2,1,0:T(8,128)(2,1)S(1)} custom-call(bf16[2,16,320,128]{3,2,1,0:T(8,128)(2,1)} %bitcast.5, bf16[1,3,320,128]{3,2,1,0:T(8,128)(2,1)S(1)} %shard_map.55.head_ref), custom_call_target="tpu_custom_call" | custom-call | tf_op jit(solution)/shard_map/pallas_call | solution.py:318
  4.3 0.0 copy-start.2
  4.3 0.0 copy-start.3
  4.4 0.0 copy-start
  4.4 0.1 shard_map.57
  4.4 0.1 collective-permute-start
  4.5 0.5 %collective-permute-start.3 = (bf16[1,6,320,128]{3,2,1,0:T(8,128)(2,1)S(1)}, bf16[1,6,320,128]{3,2,1,0:T(8,128)(2,1)S(1)}, u32[]{:S(2)}, u32[]{:S(2)}) collective-permute-start(bf16[1,6,320,128]{3,2,1,0:T(8,128)(2,1)S(1)} %get-tuple-element.36), channel_id=1, source_target_pairs={{0,8},{8,16},{16,24},{24,0},{1,9},{9,17},{17,25},{25,1},{2,10},{10... | collective-permute-start | bytes 1474568 | tf_op jit(solution)/shard_map/ppermute | solution.py:337
  5.0 0.0 copy-done.2
  5.0 0.0 copy-done.3
  5.1 0.0 copy-done.1
  5.1 0.9 %copy-done = bf16[3,3,320,320]{3,2,1,0:T(8,128)(2,1)S(1)} copy-done((bf16[3,3,320,320]{3,2,1,0:T(8,128)(2,1)S(1)}, bf16[3,3,320,320]{3,2,1,0:T(8,128)(2,1)}, u32[]{:S(2)}) %copy-start) | copy-done | bytes 1843224
  6.0 1.3 %shard_map.58 = (bf16[960,960]{1,0:T(8,128)(2,1)S(1)}, bf16[320,2880]{1,0:T(8,128)(2,1)S(1)}, bf16[320,960]{1,0:T(8,128)(2,1)S(1)}, f32[320,128]{1,0:T(8,128)S(1...) custom-call(bf16[2,16,320,128]{3,2,1,0:T(8,128)(2,1)S(1)} %shard_map.56.x_ref,, ...), custom_call_target="tpu_custom_call" | custom-call | bytes 4915200 | tf_op jit(solution)/shard_map/pallas_call | solution.py:344
  7.3 0.7 %collective-permute-start.2 = (bf16[1,3,320,128]{3,2,1,0:T(8,128)(2,1)S(1)}, bf16[1,3,320,128]{3,2,1,0:T(8,128)(2,1)S(1)}, u32[]{:S(2)}, u32[]{:S(2)}) collective-permute-start(bf16[1,3,320,128]{3,2,1,0:T(8,128)(2,1)S(1)} %get-tuple-element.35.tail_ref), channel_id=1, source_target_pairs={{8,24},{24,8},{9,25},{25,9},{10,26},{26,10},{11,27},{27,11},{12,28... | collective-permute-start | bytes 737288 | tf_op jit(solution)/shard_map/ppermute | solution.py:35
  8.0 3.4 %collective-permute-start.5 = (bf16[1,4,320,128]{3,2,1,0:T(8,128)(2,1)S(1)}, bf16[1,4,320,128]{3,2,1,0:T(8,128)(2,1)S(1)}, u32[]{:S(2)}, u32[]{:S(2)}) collective-permute-start(bf16[1,4,320,128]{3,2,1,0:T(8,128)(2,1)S(1)} %get-tuple-element.39), channel_id=1, source_target_pairs={{0,8},{8,16},{16,24},{24,0},{1,9},{9,17},{17,25},{25,1},{2,10},{10... | collective-permute-start | bytes 983048 | tf_op jit(solution)/shard_map/ppermute | solution.py:352
  11.4 0.0 collective-permute-done.beside_ref
  11.4 0.0 collective-permute-done.1.early_ref.piece_ref.refs_1_
  11.4 10.4 %shard_map.59.own_ref = f32[16,320,128]{2,1,0:T(8,128)S(1)} custom-call(bf16[2,16,320,128]{3,2,1,0:T(8,128)(2,1)S(1)} %shard_map.56.x_ref, bf16[2,1,320,128]{3,2,1,0:T(8,128)(2,1)S(1)} %collective-permute-done.beside_ref, bf16[960,960]{1,0:T(8,128)(2,1)S(1)} %get-tuple-element.28.conv_ref, bf16[320,960]{1,0:T(8,128)(2,1)S(1)} %get-tuple-element.29.mix_ref, ...), custom_call_target="tpu_custom_call" | custom-call | flops 8388608000 | bytes 5242880 | tf_op jit(solution)/shard_map/pallas_call | solution.py:355
  21.8 0.0 collective-permute-done.2.relayed_ref
  21.8 0.0 collective-permute-done.3.second_ref.refs_2_
  21.9 0.1 collective-permute-start.6
  22.0 0.0 collective-permute-start.4
  22.0 3.8 %collective-permute-start.7 = (bf16[1,1,320,128]{3,2,1,0:T(8,128)(2,1)S(1)}, bf16[1,1,320,128]{3,2,1,0:T(8,128)(2,1)S(1)}, u32[]{:S(2)}, u32[]{:S(2)}) collective-permute-start(bf16[1,1,320,128]{3,2,1,0:T(8,128)(2,1)S(1)} %get-tuple-element.46), channel_id=1, source_target_pairs={{0,8},{16,24},{24,16},{1,9},{17,25},{25,17},{2,10},{18,26},{26,18}... | collective-permute-start | bytes 245768 | tf_op jit(solution)/shard_map/ppermute | solution.py:41
  25.9 0.0 collective-permute-done.4.refs_0_
  25.9 2.9 %shard_map.61 = (bf16[8,320,128]{2,1,0:T(8,128)(2,1)S(1)}, bf16[2,960,128]{2,1,0:T(8,128)(2,1)S(1)}) custom-call(f32[16,320,128]{2,1,0:T(8,128)S(1)} %shard_map.59.own_ref, bf16[320,2880]{1,0:T(8,128)(2,1)S(1)} %get-tuple-element.33.wide_ref, bf16[320,960]{1,0:T(8,128)(2,1)S(1)} %get-tuple-element.29.mix_ref, f32[320,128]{1,0:T(8,128)S(1)} %get-tuple-element.30.cb_ref, ...), custom_call_target="tpu_custom_call" | custom-call | tf_op jit(solution)/shard_map/pallas_call | solution.py:285
  28.8 0.0 collective-permute-done.5.refs_1_
  28.8 1.6 %shard_map.62 = (bf16[16,320,128]{2,1,0:T(8,128)(2,1)}, bf16[4,320,128]{2,1,0:T(8,128)(2,1)S(1)}, bf16[2,960,128]{2,1,0:T(8,128)(2,1)S(1)}) custom-call(f32[16,320,128]{2,1,0:T(8,128)S(1)} %shard_map.59.own_ref, bf16[320,2880]{1,0:T(8,128)(2,1)S(1)} %get-tuple-element.33.wide_ref, bf16[320,960]{1,0:T(8,128)(2,1)S(1)} %get-tuple-element.29.mix_ref, ...), custom_call_target="tpu_custom_call" | custom-call | tf_op jit(solution)/shard_map/pallas_call | solution.py:285
  30.5 0.1 collective-permute-done.6.refs_1_
  30.6 1.1 %shard_map.63 = (bf16[16,320,128]{2,1,0:T(8,128)(2,1)}, bf16[2,320,128]{2,1,0:T(8,128)(2,1)S(1)}, bf16[2,960,128]{2,1,0:T(8,128)(2,1)S(1)}) custom-call(f32[16,320,128]{2,1,0:T(8,128)S(1)} %shard_map.59.own_ref, bf16[320,2880]{1,0:T(8,128)(2,1)S(1)} %get-tuple-element.33.wide_ref, ...), custom_call_target="tpu_custom_call", output_to_operand_aliasing={{0}: (7, {})} | custom-call | tf_op jit(solution)/shard_map/pallas_call | solution.py:285
  31.7 0.0 collective-permute-done.7.refs_1_
  31.7 1.8 %shard_map.64 = bf16[16,320,128]{2,1,0:T(8,128)(2,1)} custom-call(f32[16,320,128]{2,1,0:T(8,128)S(1)} %shard_map.59.own_ref, bf16[320,2880]{1,0:T(8,128)(2,1)S(1)} %get-tuple-element.33.wide_ref, bf16[320,960]{1,0:T(8,128)(2,1)S(1)} %get-tuple-element.29.mix_ref, f32[320,128]{1,0:T(8,128)S(1)} %get-tuple-element.30.cb_ref, ...), custom_call_target="tpu_custom_call", output_to_operand_aliasing={{}: (7, {})} | custom-call | tf_op jit(solution)/shard_map/pallas_call | solution.py:285
  (3 shorter events, 0.0 us)
Async XLA Ops:
  1.0 10.4 %collective-permute-start.1 = (bf16[1,3,320,128]{3,2,1,0:T(8,128)(2,1)S(1)}, bf16[1,3,320,128]{3,2,1,0:T(8,128)(2,1)S(1)}, u32[]{:S(2)}, u32[]{:S(2)}) collective-permute-start(bf16[1,3,320,128]{3,2,1,0:T(8,128)(2,1)S(1)} %shard_map.55.head_ref), channel_id=1, source_target_pairs={{0,8},{8,16},{16,24},{24,0},{1,9},{9,17},{17,25},{25,1},{2,10},{10... | collective-permute-start | bytes 737288 | tf_op jit(solution)/shard_map/ppermute | solution.py:337
  2.5 2.6 %copy-start.1 = (bf16[3,320,320]{2,1,0:T(8,128)(2,1)S(1)}, bf16[3,320,320]{2,1,0:T(8,128)(2,1)}, u32[]{:S(2)}) copy-start(bf16[3,320,320]{2,1,0:T(8,128)(2,1)} %wt_ref.1) | copy-start | bytes 1843204
  4.3 0.7 %copy-start.2 = (f32[320]{0:T(512)S(1)}, f32[320]{0:T(512)}, u32[]{:S(2)}) copy-start(f32[320]{0:T(512)} %param.7) | copy-start | bytes 3844
  4.3 0.7 %copy-start.3 = (f32[320]{0:T(512)S(1)}, f32[320]{0:T(512)}, u32[]{:S(2)}) copy-start(f32[320]{0:T(512)} %param.9) | copy-start | bytes 3844
  4.4 1.6 %copy-start = (bf16[3,3,320,320]{3,2,1,0:T(8,128)(2,1)S(1)}, bf16[3,3,320,320]{3,2,1,0:T(8,128)(2,1)}, u32[]{:S(2)}) copy-start(bf16[3,3,320,320]{3,2,1,0:T(8,128)(2,1)} %ws_ref.1) | copy-start | bytes 5529604
  4.4 6.9 %collective-permute-start = (bf16[2,1,320,128]{3,2,1,0:T(8,128)(2,1)S(1)}, bf16[2,1,320,128]{3,2,1,0:T(8,128)(2,1)S(1)}, u32[]{:S(2)}, u32[]{:S(2)}) collective-permute-start(bf16[2,1,320,128]{3,2,1,0:T(8,128)(2,1)S(1)} %get-tuple-element.27), channel_id=1, source_target_pairs={{0,4},{4,0},{1,5},{5,1},{2,6},{6,2},{3,7},{7,3},{8,12},{12,8},{9,1... | collective-permute-start | bytes 491528 | tf_op jit(solution)/shard_map/ppermute | solution.py:338
  4.5 17.3 %collective-permute-start.3 = (bf16[1,6,320,128]{3,2,1,0:T(8,128)(2,1)S(1)}, bf16[1,6,320,128]{3,2,1,0:T(8,128)(2,1)S(1)}, u32[]{:S(2)}, u32[]{:S(2)}) collective-permute-start(bf16[1,6,320,128]{3,2,1,0:T(8,128)(2,1)S(1)} %get-tuple-element.36), channel_id=1, source_target_pairs={{0,8},{8,16},{16,24},{24,0},{1,9},{9,17},{17,25},{25,1},{2,10},{10... | collective-permute-start | bytes 1474568 | tf_op jit(solution)/shard_map/ppermute | solution.py:337
  7.3 14.5 %collective-permute-start.2 = (bf16[1,3,320,128]{3,2,1,0:T(8,128)(2,1)S(1)}, bf16[1,3,320,128]{3,2,1,0:T(8,128)(2,1)S(1)}, u32[]{:S(2)}, u32[]{:S(2)}) collective-permute-start(bf16[1,3,320,128]{3,2,1,0:T(8,128)(2,1)S(1)} %get-tuple-element.35.tail_ref), channel_id=1, source_target_pairs={{8,24},{24,8},{9,25},{25,9},{10,26},{26,10},{11,27},{27,11},{12,28... | collective-permute-start | bytes 737288 | tf_op jit(solution)/shard_map/ppermute | solution.py:35
  8.0 20.9 %collective-permute-start.5 = (bf16[1,4,320,128]{3,2,1,0:T(8,128)(2,1)S(1)}, bf16[1,4,320,128]{3,2,1,0:T(8,128)(2,1)S(1)}, u32[]{:S(2)}, u32[]{:S(2)}) collective-permute-start(bf16[1,4,320,128]{3,2,1,0:T(8,128)(2,1)S(1)} %get-tuple-element.39), channel_id=1, source_target_pairs={{0,8},{8,16},{16,24},{24,0},{1,9},{9,17},{17,25},{25,1},{2,10},{10... | collective-permute-start | bytes 983048 | tf_op jit(solution)/shard_map/ppermute | solution.py:352
  21.9 8.7 %collective-permute-start.6 = (bf16[1,2,320,128]{3,2,1,0:T(8,128)(2,1)S(1)}, bf16[1,2,320,128]{3,2,1,0:T(8,128)(2,1)S(1)}, u32[]{:S(2)}, u32[]{:S(2)}) collective-permute-start(bf16[1,2,320,128]{3,2,1,0:T(8,128)(2,1)S(1)} %get-tuple-element.42), channel_id=1, source_target_pairs={{0,8},{8,0},{16,24},{24,16},{1,9},{9,1},{17,25},{25,17},{2,10},{10... | collective-permute-start | bytes 491528 | tf_op jit(solution)/shard_map/ppermute | solution.py:41
  22.0 3.9 %collective-permute-start.4 = (bf16[1,320,128]{2,1,0:T(8,128)(2,1)S(1)}, bf16[1,320,128]{2,1,0:T(8,128)(2,1)S(1)}, u32[]{:S(2)}, u32[]{:S(2)}) collective-permute-start(bf16[1,320,128]{2,1,0:T(8,128)(2,1)S(1)} %get-tuple-element.37), channel_id=1, source_target_pairs={{0,4},{4,0},{1,5},{5,1},{2,6},{6,2},{3,7},{7,3},{8,12},{12,8},{9,1... | collective-permute-start | bytes 245768 | tf_op jit(solution)/shard_map/ppermute | solution.py:374
  22.0 9.7 %collective-permute-start.7 = (bf16[1,1,320,128]{3,2,1,0:T(8,128)(2,1)S(1)}, bf16[1,1,320,128]{3,2,1,0:T(8,128)(2,1)S(1)}, u32[]{:S(2)}, u32[]{:S(2)}) collective-permute-start(bf16[1,1,320,128]{3,2,1,0:T(8,128)(2,1)S(1)} %get-tuple-element.46), channel_id=1, source_target_pairs={{0,8},{16,24},{24,16},{1,9},{17,25},{25,17},{2,10},{18,26},{26,18}... | collective-permute-start | bytes 245768 | tf_op jit(solution)/shard_map/ppermute | solution.py:41

commit v15 on v13

--- a/solution.py
+++ b/solution.py
@@ -302,7 +302,7 @@
 def per_device(video, w_spatial, b_spatial, w_temporal, b_temporal):
     frames, rows, width, channels = video.shape
     x = jnp.transpose(video, (0, 1, 3, 2))
-    sizes, steps = [3, rows - 10, 4, 2, 1], [(0, 2), (2, 3), (3, 4), (4, 5)]
+    sizes, steps = [4, rows - 11, 4, 2, 1], [(0, 2), (2, 3), (3, 4), (4, 5)]
     places = [sum(sizes[:k]) for k in range(len(sizes))]
     spans = [(frames - 1, 1, place, size) for place, size in zip(places, sizes)]
 

time: 34.1 us -> 34.1 us (level)
    ppermute x2, waiting for transfers between devices: 0.01 us -> 1.15 us  [per_device(): lax.ppermute(piece, 'frames', ring('frames'))]
    ppermute x1, waiting for transfers between devices: 1.3 us -> 0.27 us  [per_device(): arrived.append(lax.ppermute(piece, 'frames', ring('frames')))]
  transfers between devices with their start and end apart: 8 -> 8, of which waited for: 2 -> 3; matrix products, arithmetic and copies ran while one was open for 0% -> 0% of each run, Pallas kernels for 58% -> 58%
where the time goes in v15:
time: 34.1 us; the launch traced here: 33.5 us
  Pallas kernels  22 us (65%)
  starting transfers between devices  8.3 us (24%)
  waiting for transfers between devices  2.1 us (6%)
  local copies, waits for them, and re-layouts  0.96 us (3%)
    pallas_call x1, Pallas kernels, per_device(): pl.pallas_call(functools.partial(own_kernel, group=next((g for g in (8, 4...  10.4 us
    pallas_call x4, Pallas kernels, incoming_rows(): pl.pallas_call(functools.partial(incoming_kernel, pieces=len(pieces), low...  7.42 us
    ppermute x1, starting transfers between devices, per_device(): arrived.append(lax.ppermute(piece, 'frames', ring('frames')))  3.38 us
    ppermute x2, starting transfers between devices, within_pairs(): return lax.ppermute(piece, axis, [(a, b) for a, b in route if b or keep])  2.09 us
    ppermute x2, starting transfers between devices, per_device(): lax.ppermute(piece, 'frames', ring('frames'))  2.07 us
    pallas_call x1, Pallas kernels, per_device(): pl.pallas_call(functools.partial(load_kernel, spans=whole), out_shape=row...  1.82 us
    pallas_call x1, Pallas kernels, per_device(): pl.pallas_call(functools.partial(prepare_kernel, spans=[spans[2], ending]...  1.29 us
    ppermute x2, waiting for transfers between devices, per_device(): lax.ppermute(piece, 'frames', ring('frames'))  1.15 us
  transfers between devices with their start and end apart: 8, of which 3 were waited for; matrix products, arithmetic and copies ran while one was open for 0% of the time, Pallas kernels for 58%

profile of v15, /device:TPU:20, one launch (start us, length us, event | category | flops | bytes accessed | tf_op | source)
XLA Modules:
  0.0 33.5 jit_solution(88326253580586887)
XLA Ops:
  0.0 1.0 %shard_map.55.head_ref = bf16[1,4,320,128]{3,2,1,0:T(8,128)(2,1)S(1)} custom-call(bf16[2,16,320,128]{3,2,1,0:T(8,128)(2,1)} %bitcast.4), custom_call_target="tpu_custom_call" | custom-call | tf_op jit(solution)/shard_map/pallas_call | solution.py:309
  1.0 1.5 %collective-permute-start.1 = (bf16[1,4,320,128]{3,2,1,0:T(8,128)(2,1)S(1)}, bf16[1,4,320,128]{3,2,1,0:T(8,128)(2,1)S(1)}, u32[]{:S(2)}, u32[]{:S(2)}) collective-permute-start(bf16[1,4,320,128]{3,2,1,0:T(8,128)(2,1)S(1)} %shard_map.55.head_ref), channel_id=1, source_target_pairs={{0,8},{8,16},{16,24},{24,0},{1,9},{9,17},{17,25},{25,1},{2,10},{10... | collective-permute-start | bytes 983048 | tf_op jit(solution)/shard_map/ppermute | solution.py:337
  2.5 0.0 copy-start.1
  2.5 1.8 %shard_map.56.x_ref = bf16[2,16,320,128]{3,2,1,0:T(8,128)(2,1)S(1)} custom-call(bf16[2,16,320,128]{3,2,1,0:T(8,128)(2,1)} %bitcast.5, bf16[1,4,320,128]{3,2,1,0:T(8,128)(2,1)S(1)} %shard_map.55.head_ref), custom_call_target="tpu_custom_call" | custom-call | tf_op jit(solution)/shard_map/pallas_call | solution.py:318
  4.4 0.0 copy-start.2
  4.4 0.0 copy-start.3
  4.4 0.0 copy-start
  4.4 0.1 shard_map.57
  4.5 0.1 collective-permute-start
  4.5 0.5 %collective-permute-start.3 = (bf16[1,5,320,128]{3,2,1,0:T(8,128)(2,1)S(1)}, bf16[1,5,320,128]{3,2,1,0:T(8,128)(2,1)S(1)}, u32[]{:S(2)}, u32[]{:S(2)}) collective-permute-start(bf16[1,5,320,128]{3,2,1,0:T(8,128)(2,1)S(1)} %get-tuple-element.36), channel_id=1, source_target_pairs={{0,8},{8,16},{16,24},{24,0},{1,9},{9,17},{17,25},{25,1},{2,10},{10... | collective-permute-start | bytes 1228808 | tf_op jit(solution)/shard_map/ppermute | solution.py:337
  5.1 0.0 copy-done.2
  5.1 0.0 copy-done.3
  5.1 0.0 copy-done.1
  5.1 0.9 %copy-done = bf16[3,3,320,320]{3,2,1,0:T(8,128)(2,1)S(1)} copy-done((bf16[3,3,320,320]{3,2,1,0:T(8,128)(2,1)S(1)}, bf16[3,3,320,320]{3,2,1,0:T(8,128)(2,1)}, u32[]{:S(2)}) %copy-start) | copy-done | bytes 1843224
  6.0 1.3 %shard_map.58 = (bf16[960,960]{1,0:T(8,128)(2,1)S(1)}, bf16[320,2880]{1,0:T(8,128)(2,1)S(1)}, bf16[320,960]{1,0:T(8,128)(2,1)S(1)}, f32[320,128]{1,0:T(8,128)S(1...) custom-call(bf16[2,16,320,128]{3,2,1,0:T(8,128)(2,1)S(1)} %shard_map.56.x_ref,, ...), custom_call_target="tpu_custom_call" | custom-call | bytes 4915200 | tf_op jit(solution)/shard_map/pallas_call | solution.py:344
  7.3 0.7 %collective-permute-start.2 = (bf16[1,3,320,128]{3,2,1,0:T(8,128)(2,1)S(1)}, bf16[1,3,320,128]{3,2,1,0:T(8,128)(2,1)S(1)}, u32[]{:S(2)}, u32[]{:S(2)}) collective-permute-start(bf16[1,3,320,128]{3,2,1,0:T(8,128)(2,1)S(1)} %get-tuple-element.35.tail_ref), channel_id=1, source_target_pairs={{8,24},{24,8},{9,25},{25,9},{10,26},{26,10},{11,27},{27,11},{12,28... | collective-permute-start | bytes 737288 | tf_op jit(solution)/shard_map/ppermute | solution.py:35
  8.0 3.4 %collective-permute-start.5 = (bf16[1,4,320,128]{3,2,1,0:T(8,128)(2,1)S(1)}, bf16[1,4,320,128]{3,2,1,0:T(8,128)(2,1)S(1)}, u32[]{:S(2)}, u32[]{:S(2)}) collective-permute-start(bf16[1,4,320,128]{3,2,1,0:T(8,128)(2,1)S(1)} %get-tuple-element.39), channel_id=1, source_target_pairs={{0,8},{8,16},{16,24},{24,0},{1,9},{9,17},{17,25},{25,1},{2,10},{10... | collective-permute-start | bytes 983048 | tf_op jit(solution)/shard_map/ppermute | solution.py:352
  11.4 0.0 collective-permute-done.beside_ref
  11.4 1.1 %collective-permute-done.1.early_ref.piece_ref.refs_1_ = bf16[1,4,320,128]{3,2,1,0:T(8,128)(2,1)S(1)} collective-permute-done((bf16[1,4,320,128]{3,2,1,0:T(8,128)(2,1)S(1)}, bf16[1,4,320,128]{3,2,1,0:T(8,128)(2,1)S(1)}, u32[]{:S(2)}, u32[]{:S(2)}) %collective-permute-start.1) | collective-permute-done | bytes 327712 | tf_op jit(solution)/shard_map/ppermute | solution.py:337
  12.5 10.4 %shard_map.59.own_ref = f32[16,320,128]{2,1,0:T(8,128)S(1)} custom-call(bf16[2,16,320,128]{3,2,1,0:T(8,128)(2,1)S(1)} %shard_map.56.x_ref, bf16[2,1,320,128]{3,2,1,0:T(8,128)(2,1)S(1)} %collective-permute-done.beside_ref, bf16[960,960]{1,0:T(8,128)(2,1)S(1)} %get-tuple-element.28.conv_ref, bf16[320,960]{1,0:T(8,128)(2,1)S(1)} %get-tuple-element.29.mix_ref, ...), custom_call_target="tpu_custom_call" | custom-call | flops 8388608000 | bytes 5242880 | tf_op jit(solution)/shard_map/pallas_call | solution.py:355
  23.0 0.0 collective-permute-done.2.relayed_ref
  23.0 0.0 collective-permute-done.3.second_ref.refs_2_
  23.0 0.7 %collective-permute-start.6 = (bf16[1,2,320,128]{3,2,1,0:T(8,128)(2,1)S(1)}, bf16[1,2,320,128]{3,2,1,0:T(8,128)(2,1)S(1)}, u32[]{:S(2)}, u32[]{:S(2)}) collective-permute-start(bf16[1,2,320,128]{3,2,1,0:T(8,128)(2,1)S(1)} %get-tuple-element.42), channel_id=1, source_target_pairs={{0,8},{8,0},{16,24},{24,16},{1,9},{9,1},{17,25},{25,17},{2,10},{10... | collective-permute-start | bytes 491528 | tf_op jit(solution)/shard_map/ppermute | solution.py:41
  23.7 0.0 collective-permute-start.4
  23.7 1.4 %collective-permute-start.7 = (bf16[1,1,320,128]{3,2,1,0:T(8,128)(2,1)S(1)}, bf16[1,1,320,128]{3,2,1,0:T(8,128)(2,1)S(1)}, u32[]{:S(2)}, u32[]{:S(2)}) collective-permute-start(bf16[1,1,320,128]{3,2,1,0:T(8,128)(2,1)S(1)} %get-tuple-element.46), channel_id=1, source_target_pairs={{0,8},{8,0},{16,24},{24,16},{1,9},{9,1},{17,25},{25,17},{2,10},{10... | collective-permute-start | bytes 245768 | tf_op jit(solution)/shard_map/ppermute | solution.py:41
  25.1 0.0 collective-permute-done.4.refs_0_
  25.1 2.9 %shard_map.61 = (bf16[8,320,128]{2,1,0:T(8,128)(2,1)S(1)}, bf16[2,960,128]{2,1,0:T(8,128)(2,1)S(1)}) custom-call(f32[16,320,128]{2,1,0:T(8,128)S(1)} %shard_map.59.own_ref, bf16[320,2880]{1,0:T(8,128)(2,1)S(1)} %get-tuple-element.33.wide_ref, bf16[320,960]{1,0:T(8,128)(2,1)S(1)} %get-tuple-element.29.mix_ref, f32[320,128]{1,0:T(8,128)S(1)} %get-tuple-element.30.cb_ref, ...), custom_call_target="tpu_custom_call" | custom-call | tf_op jit(solution)/shard_map/pallas_call | solution.py:285
  28.1 0.3 collective-permute-done.5.refs_1_
  28.3 1.6 %shard_map.62 = (bf16[16,320,128]{2,1,0:T(8,128)(2,1)}, bf16[4,320,128]{2,1,0:T(8,128)(2,1)S(1)}, bf16[2,960,128]{2,1,0:T(8,128)(2,1)S(1)}) custom-call(f32[16,320,128]{2,1,0:T(8,128)S(1)} %shard_map.59.own_ref, bf16[320,2880]{1,0:T(8,128)(2,1)S(1)} %get-tuple-element.33.wide_ref, bf16[320,960]{1,0:T(8,128)(2,1)S(1)} %get-tuple-element.29.mix_ref, ...), custom_call_target="tpu_custom_call" | custom-call | tf_op jit(solution)/shard_map/pallas_call | solution.py:285
  29.9 0.7 %collective-permute-done.6.refs_1_ = bf16[1,2,320,128]{3,2,1,0:T(8,128)(2,1)S(1)} collective-permute-done((bf16[1,2,320,128]{3,2,1,0:T(8,128)(2,1)S(1)}, bf16[1,2,320,128]{3,2,1,0:T(8,128)(2,1)S(1)}, u32[]{:S(2)}, u32[]{:S(2)}) %collective-permute-start.6) | collective-permute-done | bytes 163872 | tf_op jit(solution)/shard_map/ppermute | solution.py:41
  30.6 1.1 %shard_map.63 = (bf16[16,320,128]{2,1,0:T(8,128)(2,1)}, bf16[2,320,128]{2,1,0:T(8,128)(2,1)S(1)}, bf16[2,960,128]{2,1,0:T(8,128)(2,1)S(1)}) custom-call(f32[16,320,128]{2,1,0:T(8,128)S(1)} %shard_map.59.own_ref, bf16[320,2880]{1,0:T(8,128)(2,1)S(1)} %get-tuple-element.33.wide_ref, ...), custom_call_target="tpu_custom_call", output_to_operand_aliasing={{0}: (7, {})} | custom-call | tf_op jit(solution)/shard_map/pallas_call | solution.py:285
  31.7 0.0 collective-permute-done.7.refs_1_
  31.8 1.8 %shard_map.64 = bf16[16,320,128]{2,1,0:T(8,128)(2,1)} custom-call(f32[16,320,128]{2,1,0:T(8,128)S(1)} %shard_map.59.own_ref, bf16[320,2880]{1,0:T(8,128)(2,1)S(1)} %get-tuple-element.33.wide_ref, bf16[320,960]{1,0:T(8,128)(2,1)S(1)} %get-tuple-element.29.mix_ref, f32[320,128]{1,0:T(8,128)S(1)} %get-tuple-element.30.cb_ref, ...), custom_call_target="tpu_custom_call", output_to_operand_aliasing={{}: (7, {})} | custom-call | tf_op jit(solution)/shard_map/pallas_call | solution.py:285
  (3 shorter events, 0.0 us)
Async XLA Ops:
  1.0 11.5 %collective-permute-start.1 = (bf16[1,4,320,128]{3,2,1,0:T(8,128)(2,1)S(1)}, bf16[1,4,320,128]{3,2,1,0:T(8,128)(2,1)S(1)}, u32[]{:S(2)}, u32[]{:S(2)}) collective-permute-start(bf16[1,4,320,128]{3,2,1,0:T(8,128)(2,1)S(1)} %shard_map.55.head_ref), channel_id=1, source_target_pairs={{0,8},{8,16},{16,24},{24,0},{1,9},{9,17},{17,25},{25,1},{2,10},{10... | collective-permute-start | bytes 983048 | tf_op jit(solution)/shard_map/ppermute | solution.py:337
  2.5 2.6 %copy-start.1 = (bf16[3,320,320]{2,1,0:T(8,128)(2,1)S(1)}, bf16[3,320,320]{2,1,0:T(8,128)(2,1)}, u32[]{:S(2)}) copy-start(bf16[3,320,320]{2,1,0:T(8,128)(2,1)} %wt_ref.1) | copy-start | bytes 1843204
  4.4 0.7 %copy-start.2 = (f32[320]{0:T(512)S(1)}, f32[320]{0:T(512)}, u32[]{:S(2)}) copy-start(f32[320]{0:T(512)} %param.7) | copy-start | bytes 3844
  4.4 0.7 %copy-start.3 = (f32[320]{0:T(512)S(1)}, f32[320]{0:T(512)}, u32[]{:S(2)}) copy-start(f32[320]{0:T(512)} %param.9) | copy-start | bytes 3844
  4.4 1.6 %copy-start = (bf16[3,3,320,320]{3,2,1,0:T(8,128)(2,1)S(1)}, bf16[3,3,320,320]{3,2,1,0:T(8,128)(2,1)}, u32[]{:S(2)}) copy-start(bf16[3,3,320,320]{3,2,1,0:T(8,128)(2,1)} %ws_ref.1) | copy-start | bytes 5529604
  4.5 6.9 %collective-permute-start = (bf16[2,1,320,128]{3,2,1,0:T(8,128)(2,1)S(1)}, bf16[2,1,320,128]{3,2,1,0:T(8,128)(2,1)S(1)}, u32[]{:S(2)}, u32[]{:S(2)}) collective-permute-start(bf16[2,1,320,128]{3,2,1,0:T(8,128)(2,1)S(1)} %get-tuple-element.27), channel_id=1, source_target_pairs={{0,4},{4,0},{1,5},{5,1},{2,6},{6,2},{3,7},{7,3},{8,12},{12,8},{9,1... | collective-permute-start | bytes 491528 | tf_op jit(solution)/shard_map/ppermute | solution.py:338
  4.5 18.5 %collective-permute-start.3 = (bf16[1,5,320,128]{3,2,1,0:T(8,128)(2,1)S(1)}, bf16[1,5,320,128]{3,2,1,0:T(8,128)(2,1)S(1)}, u32[]{:S(2)}, u32[]{:S(2)}) collective-permute-start(bf16[1,5,320,128]{3,2,1,0:T(8,128)(2,1)S(1)} %get-tuple-element.36), channel_id=1, source_target_pairs={{0,8},{8,16},{16,24},{24,0},{1,9},{9,17},{17,25},{25,1},{2,10},{10... | collective-permute-start | bytes 1228808 | tf_op jit(solution)/shard_map/ppermute | solution.py:337
  7.3 15.7 %collective-permute-start.2 = (bf16[1,3,320,128]{3,2,1,0:T(8,128)(2,1)S(1)}, bf16[1,3,320,128]{3,2,1,0:T(8,128)(2,1)S(1)}, u32[]{:S(2)}, u32[]{:S(2)}) collective-permute-start(bf16[1,3,320,128]{3,2,1,0:T(8,128)(2,1)S(1)} %get-tuple-element.35.tail_ref), channel_id=1, source_target_pairs={{8,24},{24,8},{9,25},{25,9},{10,26},{26,10},{11,27},{27,11},{12,28... | collective-permute-start | bytes 737288 | tf_op jit(solution)/shard_map/ppermute | solution.py:35
  8.0 20.3 %collective-permute-start.5 = (bf16[1,4,320,128]{3,2,1,0:T(8,128)(2,1)S(1)}, bf16[1,4,320,128]{3,2,1,0:T(8,128)(2,1)S(1)}, u32[]{:S(2)}, u32[]{:S(2)}) collective-permute-start(bf16[1,4,320,128]{3,2,1,0:T(8,128)(2,1)S(1)} %get-tuple-element.39), channel_id=1, source_target_pairs={{0,8},{8,16},{16,24},{24,0},{1,9},{9,17},{17,25},{25,1},{2,10},{10... | collective-permute-start | bytes 983048 | tf_op jit(solution)/shard_map/ppermute | solution.py:352
  23.0 7.6 %collective-permute-start.6 = (bf16[1,2,320,128]{3,2,1,0:T(8,128)(2,1)S(1)}, bf16[1,2,320,128]{3,2,1,0:T(8,128)(2,1)S(1)}, u32[]{:S(2)}, u32[]{:S(2)}) collective-permute-start(bf16[1,2,320,128]{3,2,1,0:T(8,128)(2,1)S(1)} %get-tuple-element.42), channel_id=1, source_target_pairs={{0,8},{8,0},{16,24},{24,16},{1,9},{9,1},{17,25},{25,17},{2,10},{10... | collective-permute-start | bytes 491528 | tf_op jit(solution)/shard_map/ppermute | solution.py:41
  23.7 1.4 %collective-permute-start.4 = (bf16[1,320,128]{2,1,0:T(8,128)(2,1)S(1)}, bf16[1,320,128]{2,1,0:T(8,128)(2,1)S(1)}, u32[]{:S(2)}, u32[]{:S(2)}) collective-permute-start(bf16[1,320,128]{2,1,0:T(8,128)(2,1)S(1)} %get-tuple-element.37), channel_id=1, source_target_pairs={{0,4},{4,0},{1,5},{5,1},{2,6},{6,2},{3,7},{7,3},{8,12},{12,8},{9,1... | collective-permute-start | bytes 245768 | tf_op jit(solution)/shard_map/ppermute | solution.py:374
  23.7 8.0 %collective-permute-start.7 = (bf16[1,1,320,128]{3,2,1,0:T(8,128)(2,1)S(1)}, bf16[1,1,320,128]{3,2,1,0:T(8,128)(2,1)S(1)}, u32[]{:S(2)}, u32[]{:S(2)}) collective-permute-start(bf16[1,1,320,128]{3,2,1,0:T(8,128)(2,1)S(1)} %get-tuple-element.46), channel_id=1, source_target_pairs={{0,8},{8,0},{16,24},{24,16},{1,9},{9,1},{17,25},{25,17},{2,10},{10... | collective-permute-start | bytes 245768 | tf_op jit(solution)/shard_map/ppermute | solution.py:41

commit v16 on v13

--- a/solution.py
+++ b/solution.py
@@ -241,11 +241,13 @@
 
     @pl.when(jnp.logical_not(first))
     def _():
-        before.start()
+        if stage != LAST:
+            before.start()
         convolve()
         if stage == LAST:
             after = to_output(made_ref, low, count, 1)
             after.start()
+            before.start()
             after.wait()
         before.wait()
 

time: 34.1 us -> 34.1 us (level)
  transfers between devices with their start and end apart: 8 -> 8, of which waited for: 2 -> 2; matrix products, arithmetic and copies ran while one was open for 0% -> 0% of each run, Pallas kernels for 58% -> 57%
where the time goes in v16:
time: 34.1 us; the launch traced here: 33.6 us
  Pallas kernels  22.1 us (65%)
  starting transfers between devices  8.29 us (24%)
  waiting for transfers between devices  2.1 us (6%)
  local copies, waits for them, and re-layouts  0.96 us (3%)
    pallas_call x1, Pallas kernels, per_device(): pl.pallas_call(functools.partial(own_kernel, group=next((g for g in (8, 4...  10.4 us
    pallas_call x4, Pallas kernels, incoming_rows(): pl.pallas_call(functools.partial(incoming_kernel, pieces=len(pieces), low...  7.47 us
    ppermute x1, starting transfers between devices, per_device(): arrived.append(lax.ppermute(piece, 'frames', ring('frames')))  3.39 us
    ppermute x2, starting transfers between devices, per_device(): lax.ppermute(piece, 'frames', ring('frames'))  2.07 us
    ppermute x2, starting transfers between devices, within_pairs(): return lax.ppermute(piece, axis, [(a, b) for a, b in route if b or keep])  2.04 us
    pallas_call x1, Pallas kernels, per_device(): pl.pallas_call(functools.partial(load_kernel, spans=whole), out_shape=row...  1.82 us
    ppermute x1, waiting for transfers between devices, per_device(): arrived.append(lax.ppermute(piece, 'frames', ring('frames')))  1.3 us
    pallas_call x1, Pallas kernels, per_device(): pl.pallas_call(functools.partial(prepare_kernel, spans=[spans[2], ending]...  1.29 us
  transfers between devices with their start and end apart: 8, of which 2 were waited for; matrix products, arithmetic and copies ran while one was open for 0% of the time, Pallas kernels for 57%

profile of v16, /device:TPU:20, one launch (start us, length us, event | category | flops | bytes accessed | tf_op | source)
XLA Modules:
  0.0 33.6 jit_solution(1583730773066683708)
XLA Ops:
  0.0 1.0 %shard_map.55.head_ref = bf16[1,3,320,128]{3,2,1,0:T(8,128)(2,1)S(1)} custom-call(bf16[2,16,320,128]{3,2,1,0:T(8,128)(2,1)} %bitcast.4), custom_call_target="tpu_custom_call" | custom-call | tf_op jit(solution)/shard_map/pallas_call | solution.py:311
  1.0 1.5 %collective-permute-start.1 = (bf16[1,3,320,128]{3,2,1,0:T(8,128)(2,1)S(1)}, bf16[1,3,320,128]{3,2,1,0:T(8,128)(2,1)S(1)}, u32[]{:S(2)}, u32[]{:S(2)}) collective-permute-start(bf16[1,3,320,128]{3,2,1,0:T(8,128)(2,1)S(1)} %shard_map.55.head_ref), channel_id=1, source_target_pairs={{0,8},{8,16},{16,24},{24,0},{1,9},{9,17},{17,25},{25,1},{2,10},{10... | collective-permute-start | bytes 737288 | tf_op jit(solution)/shard_map/ppermute | solution.py:339
  2.5 0.0 copy-start.1
  2.5 1.8 %shard_map.56.x_ref = bf16[2,16,320,128]{3,2,1,0:T(8,128)(2,1)S(1)} custom-call(bf16[2,16,320,128]{3,2,1,0:T(8,128)(2,1)} %bitcast.5, bf16[1,3,320,128]{3,2,1,0:T(8,128)(2,1)S(1)} %shard_map.55.head_ref), custom_call_target="tpu_custom_call" | custom-call | tf_op jit(solution)/shard_map/pallas_call | solution.py:320
  4.3 0.0 copy-start.2
  4.3 0.0 copy-start.3
  4.4 0.0 copy-start
  4.4 0.1 shard_map.57
  4.4 0.1 collective-permute-start
  4.5 0.5 %collective-permute-start.3 = (bf16[1,6,320,128]{3,2,1,0:T(8,128)(2,1)S(1)}, bf16[1,6,320,128]{3,2,1,0:T(8,128)(2,1)S(1)}, u32[]{:S(2)}, u32[]{:S(2)}) collective-permute-start(bf16[1,6,320,128]{3,2,1,0:T(8,128)(2,1)S(1)} %get-tuple-element.36), channel_id=1, source_target_pairs={{0,8},{8,16},{16,24},{24,0},{1,9},{9,17},{17,25},{25,1},{2,10},{10... | collective-permute-start | bytes 1474568 | tf_op jit(solution)/shard_map/ppermute | solution.py:339
  5.0 0.0 copy-done.2
  5.0 0.0 copy-done.3
  5.1 0.0 copy-done.1
  5.1 0.9 %copy-done = bf16[3,3,320,320]{3,2,1,0:T(8,128)(2,1)S(1)} copy-done((bf16[3,3,320,320]{3,2,1,0:T(8,128)(2,1)S(1)}, bf16[3,3,320,320]{3,2,1,0:T(8,128)(2,1)}, u32[]{:S(2)}) %copy-start) | copy-done | bytes 1843224
  6.0 1.3 %shard_map.58 = (bf16[960,960]{1,0:T(8,128)(2,1)S(1)}, bf16[320,2880]{1,0:T(8,128)(2,1)S(1)}, bf16[320,960]{1,0:T(8,128)(2,1)S(1)}, f32[320,128]{1,0:T(8,128)S(1...) custom-call(bf16[2,16,320,128]{3,2,1,0:T(8,128)(2,1)S(1)} %shard_map.56.x_ref,, ...), custom_call_target="tpu_custom_call" | custom-call | bytes 4915200 | tf_op jit(solution)/shard_map/pallas_call | solution.py:346
  7.3 0.7 %collective-permute-start.2 = (bf16[1,3,320,128]{3,2,1,0:T(8,128)(2,1)S(1)}, bf16[1,3,320,128]{3,2,1,0:T(8,128)(2,1)S(1)}, u32[]{:S(2)}, u32[]{:S(2)}) collective-permute-start(bf16[1,3,320,128]{3,2,1,0:T(8,128)(2,1)S(1)} %get-tuple-element.35.tail_ref), channel_id=1, source_target_pairs={{8,24},{24,8},{9,25},{25,9},{10,26},{26,10},{11,27},{27,11},{12,28... | collective-permute-start | bytes 737288 | tf_op jit(solution)/shard_map/ppermute | solution.py:35
  8.0 3.4 %collective-permute-start.5 = (bf16[1,4,320,128]{3,2,1,0:T(8,128)(2,1)S(1)}, bf16[1,4,320,128]{3,2,1,0:T(8,128)(2,1)S(1)}, u32[]{:S(2)}, u32[]{:S(2)}) collective-permute-start(bf16[1,4,320,128]{3,2,1,0:T(8,128)(2,1)S(1)} %get-tuple-element.39), channel_id=1, source_target_pairs={{0,8},{8,16},{16,24},{24,0},{1,9},{9,17},{17,25},{25,1},{2,10},{10... | collective-permute-start | bytes 983048 | tf_op jit(solution)/shard_map/ppermute | solution.py:354
  11.4 0.0 collective-permute-done.beside_ref
  11.4 0.0 collective-permute-done.1.early_ref.piece_ref.refs_1_
  11.4 10.4 %shard_map.59.own_ref = f32[16,320,128]{2,1,0:T(8,128)S(1)} custom-call(bf16[2,16,320,128]{3,2,1,0:T(8,128)(2,1)S(1)} %shard_map.56.x_ref, bf16[2,1,320,128]{3,2,1,0:T(8,128)(2,1)S(1)} %collective-permute-done.beside_ref, bf16[960,960]{1,0:T(8,128)(2,1)S(1)} %get-tuple-element.28.conv_ref, bf16[320,960]{1,0:T(8,128)(2,1)S(1)} %get-tuple-element.29.mix_ref, ...), custom_call_target="tpu_custom_call" | custom-call | flops 8388608000 | bytes 5242880 | tf_op jit(solution)/shard_map/pallas_call | solution.py:357
  21.8 0.0 collective-permute-done.2.relayed_ref
  21.8 0.0 collective-permute-done.3.second_ref.refs_2_
  21.9 0.1 collective-permute-start.6
  22.0 0.0 collective-permute-start.4
  22.0 1.9 %collective-permute-start.7 = (bf16[1,1,320,128]{3,2,1,0:T(8,128)(2,1)S(1)}, bf16[1,1,320,128]{3,2,1,0:T(8,128)(2,1)S(1)}, u32[]{:S(2)}, u32[]{:S(2)}) collective-permute-start(bf16[1,1,320,128]{3,2,1,0:T(8,128)(2,1)S(1)} %get-tuple-element.46), channel_id=1, source_target_pairs={{0,8},{8,0},{16,24},{24,16},{1,9},{9,1},{17,25},{25,17},{2,10},{10... | collective-permute-start | bytes 245768 | tf_op jit(solution)/shard_map/ppermute | solution.py:41
  24.0 0.0 collective-permute-done.4.refs_0_
  24.0 2.9 %shard_map.61 = (bf16[8,320,128]{2,1,0:T(8,128)(2,1)S(1)}, bf16[2,960,128]{2,1,0:T(8,128)(2,1)S(1)}) custom-call(f32[16,320,128]{2,1,0:T(8,128)S(1)} %shard_map.59.own_ref, bf16[320,2880]{1,0:T(8,128)(2,1)S(1)} %get-tuple-element.33.wide_ref, bf16[320,960]{1,0:T(8,128)(2,1)S(1)} %get-tuple-element.29.mix_ref, f32[320,128]{1,0:T(8,128)S(1)} %get-tuple-element.30.cb_ref, ...), custom_call_target="tpu_custom_call" | custom-call | tf_op jit(solution)/shard_map/pallas_call | solution.py:287
  26.9 1.3 %collective-permute-done.5.refs_1_ = bf16[1,4,320,128]{3,2,1,0:T(8,128)(2,1)S(1)} collective-permute-done((bf16[1,4,320,128]{3,2,1,0:T(8,128)(2,1)S(1)}, bf16[1,4,320,128]{3,2,1,0:T(8,128)(2,1)S(1)}, u32[]{:S(2)}, u32[]{:S(2)}) %collective-permute-start.5) | collective-permute-done | bytes 327712 | tf_op jit(solution)/shard_map/ppermute | solution.py:354
  28.2 1.6 %shard_map.62 = (bf16[16,320,128]{2,1,0:T(8,128)(2,1)}, bf16[4,320,128]{2,1,0:T(8,128)(2,1)S(1)}, bf16[2,960,128]{2,1,0:T(8,128)(2,1)S(1)}) custom-call(f32[16,320,128]{2,1,0:T(8,128)S(1)} %shard_map.59.own_ref, bf16[320,2880]{1,0:T(8,128)(2,1)S(1)} %get-tuple-element.33.wide_ref, bf16[320,960]{1,0:T(8,128)(2,1)S(1)} %get-tuple-element.29.mix_ref, ...), custom_call_target="tpu_custom_call" | custom-call | tf_op jit(solution)/shard_map/pallas_call | solution.py:287
  29.8 0.8 %collective-permute-done.6.refs_1_ = bf16[1,2,320,128]{3,2,1,0:T(8,128)(2,1)S(1)} collective-permute-done((bf16[1,2,320,128]{3,2,1,0:T(8,128)(2,1)S(1)}, bf16[1,2,320,128]{3,2,1,0:T(8,128)(2,1)S(1)}, u32[]{:S(2)}, u32[]{:S(2)}) %collective-permute-start.6) | collective-permute-done | bytes 163872 | tf_op jit(solution)/shard_map/ppermute | solution.py:41
  30.6 1.1 %shard_map.63 = (bf16[16,320,128]{2,1,0:T(8,128)(2,1)}, bf16[2,320,128]{2,1,0:T(8,128)(2,1)S(1)}, bf16[2,960,128]{2,1,0:T(8,128)(2,1)S(1)}) custom-call(f32[16,320,128]{2,1,0:T(8,128)S(1)} %shard_map.59.own_ref, bf16[320,2880]{1,0:T(8,128)(2,1)S(1)} %get-tuple-element.33.wide_ref, ...), custom_call_target="tpu_custom_call", output_to_operand_aliasing={{0}: (7, {})} | custom-call | tf_op jit(solution)/shard_map/pallas_call | solution.py:287
  31.7 0.0 collective-permute-done.7.refs_1_
  31.7 1.8 %shard_map.64 = bf16[16,320,128]{2,1,0:T(8,128)(2,1)} custom-call(f32[16,320,128]{2,1,0:T(8,128)S(1)} %shard_map.59.own_ref, bf16[320,2880]{1,0:T(8,128)(2,1)S(1)} %get-tuple-element.33.wide_ref, bf16[320,960]{1,0:T(8,128)(2,1)S(1)} %get-tuple-element.29.mix_ref, f32[320,128]{1,0:T(8,128)S(1)} %get-tuple-element.30.cb_ref, ...), custom_call_target="tpu_custom_call", output_to_operand_aliasing={{}: (7, {})} | custom-call | tf_op jit(solution)/shard_map/pallas_call | solution.py:287
  (3 shorter events, 0.0 us)
Async XLA Ops:
  1.0 10.4 %collective-permute-start.1 = (bf16[1,3,320,128]{3,2,1,0:T(8,128)(2,1)S(1)}, bf16[1,3,320,128]{3,2,1,0:T(8,128)(2,1)S(1)}, u32[]{:S(2)}, u32[]{:S(2)}) collective-permute-start(bf16[1,3,320,128]{3,2,1,0:T(8,128)(2,1)S(1)} %shard_map.55.head_ref), channel_id=1, source_target_pairs={{0,8},{8,16},{16,24},{24,0},{1,9},{9,17},{17,25},{25,1},{2,10},{10... | collective-permute-start | bytes 737288 | tf_op jit(solution)/shard_map/ppermute | solution.py:339
  2.5 2.6 %copy-start.1 = (bf16[3,320,320]{2,1,0:T(8,128)(2,1)S(1)}, bf16[3,320,320]{2,1,0:T(8,128)(2,1)}, u32[]{:S(2)}) copy-start(bf16[3,320,320]{2,1,0:T(8,128)(2,1)} %wt_ref.1) | copy-start | bytes 1843204
  4.3 0.7 %copy-start.2 = (f32[320]{0:T(512)S(1)}, f32[320]{0:T(512)}, u32[]{:S(2)}) copy-start(f32[320]{0:T(512)} %param.7) | copy-start | bytes 3844
  4.3 0.7 %copy-start.3 = (f32[320]{0:T(512)S(1)}, f32[320]{0:T(512)}, u32[]{:S(2)}) copy-start(f32[320]{0:T(512)} %param.9) | copy-start | bytes 3844
  4.4 1.6 %copy-start = (bf16[3,3,320,320]{3,2,1,0:T(8,128)(2,1)S(1)}, bf16[3,3,320,320]{3,2,1,0:T(8,128)(2,1)}, u32[]{:S(2)}) copy-start(bf16[3,3,320,320]{3,2,1,0:T(8,128)(2,1)} %ws_ref.1) | copy-start | bytes 5529604
  4.4 6.9 %collective-permute-start = (bf16[2,1,320,128]{3,2,1,0:T(8,128)(2,1)S(1)}, bf16[2,1,320,128]{3,2,1,0:T(8,128)(2,1)S(1)}, u32[]{:S(2)}, u32[]{:S(2)}) collective-permute-start(bf16[2,1,320,128]{3,2,1,0:T(8,128)(2,1)S(1)} %get-tuple-element.27), channel_id=1, source_target_pairs={{0,4},{4,0},{1,5},{5,1},{2,6},{6,2},{3,7},{7,3},{8,12},{12,8},{9,1... | collective-permute-start | bytes 491528 | tf_op jit(solution)/shard_map/ppermute | solution.py:340
  4.5 17.3 %collective-permute-start.3 = (bf16[1,6,320,128]{3,2,1,0:T(8,128)(2,1)S(1)}, bf16[1,6,320,128]{3,2,1,0:T(8,128)(2,1)S(1)}, u32[]{:S(2)}, u32[]{:S(2)}) collective-permute-start(bf16[1,6,320,128]{3,2,1,0:T(8,128)(2,1)S(1)} %get-tuple-element.36), channel_id=1, source_target_pairs={{0,8},{8,16},{16,24},{24,0},{1,9},{9,17},{17,25},{25,1},{2,10},{10... | collective-permute-start | bytes 1474568 | tf_op jit(solution)/shard_map/ppermute | solution.py:339
  7.3 14.5 %collective-permute-start.2 = (bf16[1,3,320,128]{3,2,1,0:T(8,128)(2,1)S(1)}, bf16[1,3,320,128]{3,2,1,0:T(8,128)(2,1)S(1)}, u32[]{:S(2)}, u32[]{:S(2)}) collective-permute-start(bf16[1,3,320,128]{3,2,1,0:T(8,128)(2,1)S(1)} %get-tuple-element.35.tail_ref), channel_id=1, source_target_pairs={{8,24},{24,8},{9,25},{25,9},{10,26},{26,10},{11,27},{27,11},{12,28... | collective-permute-start | bytes 737288 | tf_op jit(solution)/shard_map/ppermute | solution.py:35
  8.0 20.2 %collective-permute-start.5 = (bf16[1,4,320,128]{3,2,1,0:T(8,128)(2,1)S(1)}, bf16[1,4,320,128]{3,2,1,0:T(8,128)(2,1)S(1)}, u32[]{:S(2)}, u32[]{:S(2)}) collective-permute-start(bf16[1,4,320,128]{3,2,1,0:T(8,128)(2,1)S(1)} %get-tuple-element.39), channel_id=1, source_target_pairs={{0,8},{8,16},{16,24},{24,0},{1,9},{9,17},{17,25},{25,1},{2,10},{10... | collective-permute-start | bytes 983048 | tf_op jit(solution)/shard_map/ppermute | solution.py:354
  21.9 8.7 %collective-permute-start.6 = (bf16[1,2,320,128]{3,2,1,0:T(8,128)(2,1)S(1)}, bf16[1,2,320,128]{3,2,1,0:T(8,128)(2,1)S(1)}, u32[]{:S(2)}, u32[]{:S(2)}) collective-permute-start(bf16[1,2,320,128]{3,2,1,0:T(8,128)(2,1)S(1)} %get-tuple-element.42), channel_id=1, source_target_pairs={{0,8},{8,0},{16,24},{24,16},{1,9},{9,1},{17,25},{25,17},{2,10},{10... | collective-permute-start | bytes 491528 | tf_op jit(solution)/shard_map/ppermute | solution.py:41
  22.0 2.0 %collective-permute-start.4 = (bf16[1,320,128]{2,1,0:T(8,128)(2,1)S(1)}, bf16[1,320,128]{2,1,0:T(8,128)(2,1)S(1)}, u32[]{:S(2)}, u32[]{:S(2)}) collective-permute-start(bf16[1,320,128]{2,1,0:T(8,128)(2,1)S(1)} %get-tuple-element.37), channel_id=1, source_target_pairs={{0,4},{4,0},{1,5},{5,1},{2,6},{6,2},{3,7},{7,3},{8,12},{12,8},{9,1... | collective-permute-start | bytes 245768 | tf_op jit(solution)/shard_map/ppermute | solution.py:376
  22.0 9.7 %collective-permute-start.7 = (bf16[1,1,320,128]{3,2,1,0:T(8,128)(2,1)S(1)}, bf16[1,1,320,128]{3,2,1,0:T(8,128)(2,1)S(1)}, u32[]{:S(2)}, u32[]{:S(2)}) collective-permute-start(bf16[1,1,320,128]{3,2,1,0:T(8,128)(2,1)S(1)} %get-tuple-element.46), channel_id=1, source_target_pairs={{0,8},{8,0},{16,24},{24,16},{1,9},{9,1},{17,25},{25,17},{2,10},{10... | collective-permute-start | bytes 245768 | tf_op jit(solution)/shard_map/ppermute | solution.py:41
